TPU v7x, 32 devices: a whole 2x2x4 slice. The times are simulated.
32 devices in a mesh: case: 2 (over y), gx: 4 (over z), gy: 4 (over x, core).
Axes of the slice: x: 2, y: 2, z: 4, core: 2. Of those that a mesh axis runs over, the one named last changes fastest.
Arguments:
- features: bfloat16 [10, 512, 1024], P(None, ('case', 'gx'), 'gy'), parts along dimension 1, may hold values from -6 to 6
- source: bfloat16 [5, 512, 1024], P(None, ('case', 'gx'), 'gy'), parts along dimension 1, may hold values from -4.2 to 5.6
- coupling: bfloat16 [4, 512, 1024], P(None, ('case', 'gx'), 'gy'), parts along dimension 1, may hold values from 0.16992188 to 0.33984375
- diagonal: float32 [512, 1024], P(('case', 'gx'), 'gy'), parts along dimension 0, may hold values from 0.8 to 1
- production: float32 [512, 1024], P(('case', 'gx'), 'gy'), parts along dimension 0, may hold values from -6 to 6
- bc_code: int32 [512, 1024], P(('case', 'gx'), 'gy'), parts along dimension 0, may hold values from 0 to 2, as said below
- mixing: float32 [5, 5], replicated, may hold values from -0.15 to 0.9
- weight_in: bfloat16 [10, 64], replicated, may hold values from -2 to 2
- weight_mid: bfloat16 [64, 64], replicated, may hold values from -0.75 to 0.75
- weight_top: bfloat16 [64, 64], replicated, may hold values from -0.75 to 0.75
- weight_out: float32 [64], replicated, may hold values from -0.75 to 0.75
- biases: float32 [3, 64], replicated, may hold values from -3 to 3
Outputs:
- adjoint: float32 [5, 512, 1024], P(None, ('case', 'gx'), 'gy'), parts along dimension 1
- beta_field: float32 [512, 1024], P(('case', 'gx'), 'gy'), parts along dimension 0
- grad_in: float32 [20, 64], P('case'), parts along dimension 0
- grad_mid: float32 [128, 64], P('case'), parts along dimension 0
- grad_top: float32 [128, 64], P('case'), parts along dimension 0
- grad_out: float32 [128], P('case'), parts along dimension 0
- grad_bias: float32 [6, 64], P('case'), parts along dimension 0
There are 2 independent parts, one for each index of `case`. A program takes and returns all parts, laid end to end along the dimension named above; an argument that names none is the same for every part. Nothing has to cross between parts.
Inputs may be any that keep to these rules, and one draw needn't show every extreme that they name: `bc_code`: 0 marks an interior cell, 1 a wall cell, 2 a far-field cell.
All inputs are finite; a program needn't handle non-finite values.
Results may differ from a plain program's by a relative error of at most 0.0038.
Values sent between devices are 32-bit elements; how exact they have to be, the bound alone decides.
No kernel may reach another device: no remote copies, remote signals or barrier semaphores. Data moves between devices by JAX's collectives and lax.ppermute only.
A program may use at most 64 MiB of HBM per device.

v0:
```python
import functools

import jax
import jax.numpy as jnp
from jax import lax
from jax.experimental import pallas as pl
from jax.experimental.pallas import tpu as pltpu
from jax.sharding import PartitionSpec as P

SWEEPS = 6
WALL_EXTRA = 0.2
FAR_EXTRA = 0.6
REG_WEIGHT = 0.5
CLIP_NORM = 64.0
EDGE = 8
SUB, LANE = 8, 128
F32, BF16 = jnp.float32, jnp.bfloat16
NT = (((1,), (1,)), ((), ()))
TN = (((0,), (0,)), ((), ()))
VMEM_BYTES = 48 * 1024 * 1024


def whole(shape):
    return pl.BlockSpec(shape, lambda *_: (0,) * len(shape))


def params():
    return pltpu.CompilerParams(vmem_limit_bytes=VMEM_BYTES)


def inverse_diag(diag, code):
    total = diag + jnp.where(code == 1, WALL_EXTRA, 0.0) + jnp.where(code == 2, FAR_EXTRA, 0.0)
    return 1.0 / total


def rows_kernel(src_t, src_b, cpl_t, cpl_b, dia_t, dia_b, bc_t, bc_b, top_ref, bottom_ref):
    nv, nc = src_t.shape[0], cpl_t.shape[0]
    last = src_b.shape[1] - EDGE
    for v in range(nv):
        top_ref[v] = src_t[v].astype(F32)[:EDGE]
        bottom_ref[v] = src_b[v].astype(F32)[last:]
    for d in range(nc):
        top_ref[nv + d] = cpl_t[d].astype(F32)[:EDGE]
        bottom_ref[nv + d] = cpl_b[d].astype(F32)[last:]
    top_ref[nv + nc] = inverse_diag(dia_t[...], bc_t[...])
    bottom_ref[nv + nc] = inverse_diag(dia_b[...], bc_b[...])


def row_slabs(source, coupling, diagonal, bc_code):
    nv, rows, cols = source.shape
    nc = coupling.shape[0]
    slab = jax.ShapeDtypeStruct((nv + nc + 1, EDGE, cols), F32)
    tall = rows // 16 - 1

    def pair(count):
        return [
            pl.BlockSpec((count, 16, cols), lambda i: (0, 0, 0)),
            pl.BlockSpec((count, 16, cols), lambda i: (0, tall, 0)),
        ]

    flat = [
        pl.BlockSpec((EDGE, cols), lambda i: (0, 0)),
        pl.BlockSpec((EDGE, cols), lambda i: (rows // EDGE - 1, 0)),
    ]
    return pl.pallas_call(
        rows_kernel,
        grid=(1,),
        in_specs=pair(nv) + pair(nc) + flat + flat,
        out_specs=[whole(slab.shape)] * 2,
        out_shape=[slab, slab],
        compiler_params=params(),
        name="row_slabs",
    )(source, source, coupling, coupling, diagonal, diagonal, bc_code, bc_code)


def cols_kernel(src_w, src_e, cpl_w, cpl_e, dia_w, dia_e, bc_w, bc_e, north, south, west_ref, east_ref):
    nv, rows, _ = src_w.shape
    nc = cpl_w.shape[0]
    cols = north.shape[2]
    lane = lax.broadcasted_iota(jnp.int32, (rows, LANE), 1) // EDGE
    lane_h = lane[:EDGE]
    sides = (
        (west_ref, src_w, cpl_w, dia_w, bc_w, slice(0, LANE), 0),
        (east_ref, src_e, cpl_e, dia_e, bc_e, slice(cols - LANE, cols), EDGE),
    )
    for out, src, cpl, dia, bc, window, extra in sides:
        mid = jnp.zeros((rows, LANE), F32)
        up = jnp.zeros((EDGE, LANE), F32)
        down = jnp.zeros((EDGE, LANE), F32)
        for f in range(nv + nc + 1):
            if f < nv:
                x = src[f].astype(F32)
            elif f < nv + nc:
                x = cpl[f - nv].astype(F32)
            else:
                x = inverse_diag(dia[...], bc[...])
            shift = (EDGE * f + extra) % LANE
            mid = jnp.where(lane == f, pltpu.roll(x, shift, 1), mid)
            up = jnp.where(lane_h == f, pltpu.roll(north[f, :, window], shift, 1), up)
            down = jnp.where(lane_h == f, pltpu.roll(south[f, :, window], shift, 1), down)
        out[0:EDGE] = up
        out[EDGE : EDGE + rows] = mid
        out[EDGE + rows :] = down


def col_slabs(source, coupling, diagonal, bc_code, north, south):
    nv, rows, cols = source.shape
    nc = coupling.shape[0]
    slab = jax.ShapeDtypeStruct((rows + 2 * EDGE, LANE), F32)
    wide = cols // LANE - 1

    def pair(count):
        return [
            pl.BlockSpec((count, rows, LANE), lambda i: (0, 0, 0)),
            pl.BlockSpec((count, rows, LANE), lambda i: (0, 0, wide)),
        ]

    flat = [
        pl.BlockSpec((rows, LANE), lambda i: (0, 0)),
        pl.BlockSpec((rows, LANE), lambda i: (0, wide)),
    ]
    return pl.pallas_call(
        cols_kernel,
        grid=(1,),
        in_specs=pair(nv) + pair(nc) + flat + flat + [whole(north.shape)] * 2,
        out_specs=[whole(slab.shape)] * 2,
        out_shape=[slab, slab],
        compiler_params=params(),
        name="col_slabs",
    )(source, source, coupling, coupling, diagonal, diagonal, bc_code, bc_code, north, south)


def column_of(row):
    hidden = row.shape[1]
    wide = jnp.concatenate([row, jnp.zeros((1, LANE - hidden), F32)], axis=1)
    return jnp.transpose(jnp.broadcast_to(wide, (LANE, LANE)))[:hidden]


def across(block, width):
    return jnp.concatenate([block] * (width // LANE), axis=1)


def forward_kernel(
    feat_ref, win_ref, wmid_ref, wtop_ref, wout_ref, bias_ref,
    acts_ref, beta_ref,
    w1, x1, w2, w3, cst,
):
    nf, rows, cols = feat_ref.shape
    hidden = wmid_ref.shape[0]
    step_rows = hidden + 16

    @pl.when(pl.program_id(0) == 0)
    def _():
        depth = x1.shape[0]
        x1[...] = jnp.zeros(x1.shape, BF16)
        feat_of = lax.broadcasted_iota(jnp.int32, (nf, depth), 1) // rows
        pick = (feat_of == lax.broadcasted_iota(jnp.int32, (nf, depth), 0)).astype(F32).astype(BF16)
        spread = lax.dot_general(win_ref[...], pick, TN, preferred_element_type=F32)
        col = lax.broadcasted_iota(jnp.int32, (hidden, depth), 1)
        col_f = lax.broadcasted_iota(jnp.int32, (16, depth), 1)
        row_f = lax.broadcasted_iota(jnp.int32, (16, depth), 0)
        for r in range(rows):
            base = r * step_rows
            w1[base : base + hidden] = jnp.where(col % rows == r, spread, 0.0).astype(BF16)
            same = jnp.logical_and(col_f == row_f * rows + r, row_f < nf)
            w1[base + hidden : base + step_rows] = jnp.where(same, 1.0, 0.0).astype(BF16)
        w2[...] = jnp.transpose(wmid_ref[...].astype(F32)).astype(BF16)
        w3[...] = jnp.transpose(wtop_ref[...].astype(F32)).astype(BF16)
        for k in range(3):
            cst[k] = column_of(bias_ref[k : k + 1, :])
        cst[3] = column_of(wout_ref[...])

    x1[0 : nf * rows] = feat_ref[...].reshape(nf * rows, cols)
    per = 2
    b1, b2, b3, wo = (across(cst[k], cols) for k in range(4))
    for g in range(rows // per):
        lo = g * per * step_rows
        first = jnp.dot(w1[lo : lo + per * step_rows], x1[...], preferred_element_type=F32)
        ones = []
        for q in range(per):
            part = first[q * step_rows : (q + 1) * step_rows]
            one = jnp.tanh(part[:hidden] + b1).astype(BF16)
            acts_ref[g * per + q, 0:hidden] = one
            acts_ref[g * per + q, 3 * hidden :] = part[hidden:].astype(BF16)
            ones.append(one)
        second = jnp.dot(w2[...], jnp.concatenate(ones, axis=1), preferred_element_type=F32)
        twos = []
        for q in range(per):
            two = jnp.tanh(second[:, q * cols : (q + 1) * cols] + b2).astype(BF16)
            acts_ref[g * per + q, hidden : 2 * hidden] = two
            twos.append(two)
        third = jnp.dot(w3[...], jnp.concatenate(twos, axis=1), preferred_element_type=F32)
        for q in range(per):
            three = jnp.tanh(third[:, q * cols : (q + 1) * cols] + b3).astype(BF16)
            acts_ref[g * per + q, 2 * hidden : 3 * hidden] = three
            total = jnp.sum(three.astype(F32) * wo, axis=0, keepdims=True)
            beta_ref[g * per + q : g * per + q + 1, :] = 1.0 + total


def forward(features, weight_in, weight_mid, weight_top, weight_out, biases):
    nf, rows, cols = features.shape
    hidden = weight_mid.shape[0]
    blk = 16
    high = 3 * hidden + 16
    depth = -(-nf * blk // LANE) * LANE
    return pl.pallas_call(
        forward_kernel,
        grid=(rows // blk,),
        in_specs=[
            pl.BlockSpec((nf, blk, cols), lambda i: (0, i, 0)),
            whole(weight_in.shape),
            whole(weight_mid.shape),
            whole(weight_top.shape),
            whole(weight_out.shape),
            whole(biases.shape),
        ],
        out_specs=[
            pl.BlockSpec((blk, high, cols), lambda i: (i, 0, 0)),
            pl.BlockSpec((blk, cols), lambda i: (i, 0)),
        ],
        out_shape=[
            jax.ShapeDtypeStruct((rows, high, cols), BF16),
            jax.ShapeDtypeStruct((rows, cols), F32),
        ],
        scratch_shapes=[
            pltpu.VMEM((blk * (hidden + 16), depth), BF16),
            pltpu.VMEM((depth, cols), BF16),
            pltpu.VMEM((hidden, hidden), BF16),
            pltpu.VMEM((hidden, hidden), BF16),
            pltpu.VMEM((4, hidden, LANE), F32),
        ],
        compiler_params=params(),
        cost_estimate=pl.CostEstimate(
            flops=2 * rows * cols * (nf + 2 * hidden) * hidden,
            bytes_accessed=2 * rows * cols * (high + nf),
            transcendentals=3 * rows * cols * hidden,
        ),
        name="network_forward",
    )(features, weight_in, weight_mid, weight_top, weight_out, biases)


def tile_at(ref, lead, t, k):
    return ref[lead + (slice(t * SUB, (t + 1) * SUB), slice(k * LANE, (k + 1) * LANE))]


class Shifts:
    def __init__(self, tiles, lanes):
        self.tiles, self.lanes = tiles, lanes
        sub = lax.broadcasted_iota(jnp.int32, (SUB, LANE), 0)
        lane = lax.broadcasted_iota(jnp.int32, (SUB, LANE), 1)
        self.first_sub, self.last_sub = sub == 0, sub == SUB - 1
        self.first_lane, self.last_lane = lane == 0, lane == LANE - 1

    def above(self, ref, lead, t, k):
        here, other = tile_at(ref, lead, t, k), tile_at(ref, lead, max(t - 1, 0), k)
        return pltpu.roll(jnp.where(self.last_sub, other, here), 1, 0)

    def below(self, ref, lead, t, k):
        here, other = tile_at(ref, lead, t, k), tile_at(ref, lead, min(t + 1, self.tiles - 1), k)
        return pltpu.roll(jnp.where(self.first_sub, other, here), SUB - 1, 0)

    def left(self, ref, lead, t, k):
        here, other = tile_at(ref, lead, t, k), tile_at(ref, lead, t, (k - 1) % self.lanes)
        return pltpu.roll(jnp.where(self.last_lane, other, here), 1, 1)

    def right(self, ref, lead, t, k):
        here, other = tile_at(ref, lead, t, k), tile_at(ref, lead, t, (k + 1) % self.lanes)
        return pltpu.roll(jnp.where(self.first_lane, other, here), LANE - 1, 1)


def sweep_all(src, cpl, dia, bc, north, south, west, east, mix, adj_out, raw, src_x, cpl_x, adj_a, adj_b):
    nv, rows, cols = src.shape
    nc = cpl.shape[0]
    tall = rows + 2 * EDGE
    tiles, lanes = tall // SUB, cols // LANE + 1
    shifts = Shifts(tiles, lanes)
    inner = slice(EDGE, EDGE + rows)
    lane = lax.broadcasted_iota(jnp.int32, (tall, LANE), 1)
    from_east, from_west = lane < EDGE, lane >= LANE - EDGE
    for f in range(nv + nc + 1):
        if f < nv:
            raw[f, inner, 0:cols] = src[f].astype(F32)
        elif f < nv + nc:
            raw[f, inner, 0:cols] = cpl[f - nv].astype(F32)
        else:
            raw[f, inner, 0:cols] = inverse_diag(dia[...], bc[...])
        raw[f, 0:EDGE, 0:cols] = north[f]
        raw[f, EDGE + rows :, 0:cols] = south[f]
        e = pltpu.roll(east[...], (LANE - EDGE * f) % LANE, 1)
        w = pltpu.roll(west[...], (LANE - EDGE - EDGE * f) % LANE, 1)
        raw[f, :, cols:] = jnp.where(from_east, e, jnp.where(from_west, w, 0.0))

    moves = (shifts.above, shifts.below, shifts.left, shifts.right)
    for t in range(tiles):
        for k in range(lanes):
            at = (slice(t * SUB, (t + 1) * SUB), slice(k * LANE, (k + 1) * LANE))
            inv = tile_at(raw, (nv + nc,), t, k)
            for v in range(nv):
                src_x[(v,) + at] = inv * tile_at(raw, (v,), t, k)
            for d in range(nc):
                cpl_x[(d,) + at] = inv * moves[d](raw, (nv + d,), t, k)

    def sweep(old, new, last):
        for t in range(1, tiles - 1) if last else range(tiles):
            for k in range(lanes - 1) if last else range(lanes):
                at = (slice(t * SUB, (t + 1) * SUB), slice(k * LANE, (k + 1) * LANE))
                couple = [cpl_x[(d,) + at] for d in range(nc)]
                total = [src_x[(a,) + at] for a in range(nv)]
                for b in range(nv):
                    inc = couple[0] * moves[0](old, (b,), t, k)
                    for d in range(1, nc):
                        inc = inc + couple[d] * moves[d](old, (b,), t, k)
                    total = [total[a] + mix[b, a] * inc for a in range(nv)]
                if last:
                    at = (slice((t - 1) * SUB, t * SUB), at[1])
                for a in range(nv):
                    new[(a,) + at] = total[a]

    sweep(src_x, adj_a, False)

    @pl.loop(0, (SWEEPS - 2) // 2)
    def _(i):
        sweep(adj_a, adj_b, False)
        sweep(adj_b, adj_a, False)

    sweep(adj_a, adj_out, True)


def backward_kernel(
    src, cpl, dia, bc, prod, beta, north, south, west, east, mix, wmid, wtop, wout, acts,
    adj_out, packed,
    raw, src_x, cpl_x, adj_a, adj_b, sens, sums, g_mid, g_top, g_in,
):
    step = pl.program_id(0)
    nv = src.shape[0]
    blk, _, cols = acts.shape
    hidden = wmid.shape[0]

    @pl.when(step == 0)
    def _():
        sweep_all(
            src, cpl, dia, bc, north, south, west, east, mix, adj_out, raw, src_x, cpl_x, adj_a, adj_b
        )
        sens[...] = adj_out[nv - 1] * prod[...] + REG_WEIGHT * (beta[...] - 1.0)
        sums[...] = jnp.zeros(sums.shape, F32)
        sums[4] = column_of(wout[...])
        g_mid[...] = jnp.zeros(g_mid.shape, F32)
        g_top[...] = jnp.zeros(g_top.shape, F32)
        g_in[...] = jnp.zeros(g_in.shape, F32)

    rows_sens = sens[pl.ds(pl.multiple_of(step * blk, blk), blk), :]
    wo = across(sums[4], cols)

    def fold(x):
        parts = [x[:, k * LANE : (k + 1) * LANE] for k in range(cols // LANE)]
        return functools.reduce(jnp.add, parts)

    ones, twos, feats, d1s, d2s, d3s = [], [], [], [], [], []
    acc = [jnp.zeros((hidden, LANE), F32) for _ in range(4)]
    for q in range(blk):
        one, two = acts[q, 0:hidden], acts[q, hidden : 2 * hidden]
        three_f = acts[q, 2 * hidden : 3 * hidden].astype(F32)
        sen = jnp.broadcast_to(rows_sens[q : q + 1], (hidden, cols))
        acc[0] = acc[0] + fold(three_f * sen)
        d3 = sen * wo * (1.0 - three_f * three_f)
        acc[3] = acc[3] + fold(d3)
        d3 = d3.astype(BF16)
        two_f = two.astype(F32)
        d2 = jnp.dot(wtop[...], d3, preferred_element_type=F32) * (1.0 - two_f * two_f)
        acc[2] = acc[2] + fold(d2)
        d2 = d2.astype(BF16)
        one_f = one.astype(F32)
        d1 = jnp.dot(wmid[...], d2, preferred_element_type=F32) * (1.0 - one_f * one_f)
        acc[1] = acc[1] + fold(d1)
        d1 = d1.astype(BF16)
        ones.append(one)
        twos.append(two)
        feats.append(acts[q, 3 * hidden :])
        d1s.append(d1)
        d2s.append(d2)
        d3s.append(d3)

    def outer(xs, ds):
        return lax.dot_general(
            jnp.concatenate(xs, axis=1), jnp.concatenate(ds, axis=1), NT, preferred_element_type=F32
        )

    g_mid[...] += outer(ones, d2s)
    g_top[...] += outer(twos, d3s)
    g_in[...] += outer(feats, d1s)
    for k in range(4):
        sums[k] += acc[k]

    @pl.when(step == pl.num_programs(0) - 1)
    def _():
        packed[0:hidden, :] = jnp.concatenate([g_mid[...], g_top[...]], axis=1)
        tail = g_in[SUB : 2 * SUB]
        row = lax.broadcasted_iota(jnp.int32, (SUB, hidden), 0)
        for k in range(4):
            line = jnp.sum(jnp.transpose(sums[k]), axis=0, keepdims=True)
            tail = tail + jnp.where(row == k + 2, jnp.broadcast_to(line, (SUB, hidden)), 0.0)
        packed[hidden : hidden + SUB, :] = jnp.concatenate([g_in[0:SUB], tail], axis=1)


def sweeps_and_backward(source, coupling, diagonal, bc_code, production, beta, halos, mixing, weights, acts):
    nv, rows, cols = source.shape
    nc = coupling.shape[0]
    weight_mid, weight_top, weight_out = weights
    hidden = weight_mid.shape[0]
    blk = 8
    tall, wide = rows + 2 * EDGE, cols + LANE
    operands = [source, coupling, diagonal, bc_code, production, beta, *halos]
    return pl.pallas_call(
        backward_kernel,
        grid=(rows // blk,),
        in_specs=[whole(x.shape) for x in operands]
        + [pl.BlockSpec(memory_space=pltpu.SMEM)]
        + [whole(x.shape) for x in weights]
        + [pl.BlockSpec((blk,) + acts.shape[1:], lambda i: (i, 0, 0))],
        out_specs=[whole((nv, rows, cols)), whole((hidden + SUB, LANE))],
        out_shape=[
            jax.ShapeDtypeStruct((nv, rows, cols), F32),
            jax.ShapeDtypeStruct((hidden + SUB, LANE), F32),
        ],
        scratch_shapes=[
            pltpu.VMEM((nv + nc + 1, tall, wide), F32),
            pltpu.VMEM((nv, tall, wide), F32),
            pltpu.VMEM((nc, tall, wide), F32),
            pltpu.VMEM((nv, tall, wide), F32),
            pltpu.VMEM((nv, tall, wide), F32),
            pltpu.VMEM((rows, cols), F32),
            pltpu.VMEM((5, hidden, LANE), F32),
            pltpu.VMEM((hidden, hidden), F32),
            pltpu.VMEM((hidden, hidden), F32),
            pltpu.VMEM((16, hidden), F32),
        ],
        compiler_params=params(),
        name="sweeps_backward",
    )(*operands, mixing, *weights, acts)


def clip_kernel(parts, gin, gmid, gtop, gout, gbias):
    hidden = gmid.shape[0]
    total = parts[0]
    for k in range(1, parts.shape[0]):
        total = total + parts[k]
    squares = jnp.sum(jnp.sum(total * total, axis=0, keepdims=True), axis=1, keepdims=True)
    total = total * (CLIP_NORM / jnp.maximum(jnp.sqrt(squares), CLIP_NORM))
    gmid[...] = total[:hidden, :hidden]
    gtop[...] = total[:hidden, hidden:]
    low, high = total[hidden:, :hidden], total[hidden:, hidden:]
    gin[0:SUB] = low
    gin[SUB:] = high[: gin.shape[0] - SUB]
    gout[...] = high[2:3]
    gbias[...] = high[3:6]


def clip_all(parts, num_feat, hidden):
    shapes = [(num_feat, hidden), (hidden, hidden), (hidden, hidden), (1, hidden), (3, hidden)]
    return pl.pallas_call(
        clip_kernel,
        grid=(1,),
        in_specs=[whole(parts.shape)],
        out_specs=[whole(s) for s in shapes],
        out_shape=[jax.ShapeDtypeStruct(s, F32) for s in shapes],
        compiler_params=params(),
        name="clip",
    )(parts)


def sum_parts(packed):
    for axis in ("gy", "gx"):
        count = lax.axis_size(axis)
        step = 1
        while step < count:
            packed = packed + lax.ppermute(packed, axis, [(i, i ^ step) for i in range(count)])
            step *= 2
    return packed[None]


def shift_pair(low_edge, high_edge, axis):
    count = lax.axis_size(axis)
    up = [(i, i + 1) for i in range(count - 1)]
    down = [(b, a) for a, b in up]
    return lax.ppermute(high_edge, axis, up), lax.ppermute(low_edge, axis, down)


def shards(
    features, source, coupling, diagonal, production, bc_code, mixing,
    weight_in, weight_mid, weight_top, weight_out, biases,
):
    num_feat = features.shape[0]
    hidden = weight_mid.shape[0]
    wout = weight_out.reshape(1, hidden)
    top, bottom = row_slabs(source, coupling, diagonal, bc_code)
    north, south = shift_pair(top, bottom, "gx")
    first, last = col_slabs(source, coupling, diagonal, bc_code, north, south)
    west, east = shift_pair(first, last, "gy")
    acts, beta = forward(features, weight_in, weight_mid, weight_top, wout, biases)
    adjoint, packed = sweeps_and_backward(
        source, coupling, diagonal, bc_code, production, beta, (north, south, west, east), mixing,
        (weight_mid, weight_top, wout), acts,
    )
    grad_in, grad_mid, grad_top, grad_out, grad_bias = clip_all(sum_parts(packed), num_feat, hidden)
    return (adjoint, beta, grad_in, grad_mid, grad_top, grad_out.reshape(hidden), grad_bias)


def solution(mesh):
    cells3 = P(None, ("case", "gx"), "gy")
    cells2 = P(("case", "gx"), "gy")
    return jax.shard_map(
        shards,
        mesh=mesh,
        in_specs=(cells3,) * 3 + (cells2,) * 3 + (P(),) * 6,
        out_specs=(cells3, cells2, P("case"), P("case"), P("case"), P("case"), P("case")),
        check_vma=False,
    )
```

profile of v0, /device:TPU:0, one launch (start us, length us, event | category | flops | bytes accessed | tf_op | source)
XLA Modules:
  0.0 63.5 jit_solution(8980875441136338127)
XLA Ops:
  0.6 0.0 copy-start
  0.6 0.9 %copy-done = bf16[5,64,256]{2,1,0:T(8,128)(2,1)S(1)} copy-done((bf16[5,64,256]{2,1,0:T(8,128)(2,1)S(1)}, bf16[5,64,256]{2,1,0:T(8,128)(2,1)}, u32[]{:S(2)}) %copy-start) | copy-done | bytes 163864
  1.6 0.0 copy-start.2
  1.6 0.9 %copy-done.2 = bf16[4,64,256]{2,1,0:T(8,128)(2,1)S(1)} copy-done((bf16[4,64,256]{2,1,0:T(8,128)(2,1)S(1)}, bf16[4,64,256]{2,1,0:T(8,128)(2,1)}, u32[]{:S(2)}) %copy-start.2) | copy-done | bytes 131096
  2.5 0.0 copy-start.4
  2.5 0.8 %copy-done.4 = f32[64,256]{1,0:T(8,128)S(1)} copy-done((f32[64,256]{1,0:T(8,128)S(1)}, f32[64,256]{1,0:T(8,128)}, u32[]{:S(2)}) %copy-start.4) | copy-done | bytes 65560
  3.3 0.0 copy-start.6
  3.3 0.8 %copy-done.6 = s32[64,256]{1,0:T(8,128)S(1)} copy-done((s32[64,256]{1,0:T(8,128)S(1)}, s32[64,256]{1,0:T(8,128)}, u32[]{:S(2)}) %copy-start.6) | copy-done | bytes 65560
  4.1 0.0 copy-start.1
  4.1 0.0 copy-start.3
  4.1 0.0 copy-start.5
  4.1 0.0 copy-start.7
  4.1 0.0 copy-start.8
  4.2 0.0 copy-start.12
  4.2 5.1 %collective-permute-start = (f32[10,8,256]{2,1,0:T(8,128)S(1)}, f32[10,8,256]{2,1,0:T(8,128)S(1)}, u32[]{:S(2)}, u32[]{:S(2)}) collective-permute-start(f32[10,8,256]{2,1,0:T(8,128)S(1)} %get-tuple-element.21), channel_id=1, source_target_pairs={{0,4},{4,8},{8,12},{1,5},{5,9},{9,13},{2,6},{6,10},{10,14},{3,7},{... | collective-permute-start | bytes 245768 | tf_op jit(solution)/shard_map/ppermute | solution.py:485
  9.3 1.3 %collective-permute-start.1 = (f32[10,8,256]{2,1,0:T(8,128)S(1)}, f32[10,8,256]{2,1,0:T(8,128)S(1)}, u32[]{:S(2)}, u32[]{:S(2)}) collective-permute-start(f32[10,8,256]{2,1,0:T(8,128)S(1)} %get-tuple-element.22), channel_id=1, source_target_pairs={{4,0},{8,4},{12,8},{5,1},{9,5},{13,9},{6,2},{10,6},{14,10},{7,3},{... | collective-permute-start | bytes 245768 | tf_op jit(solution)/shard_map/ppermute | solution.py:485
  10.6 0.7 %collective-permute-done.north = f32[10,8,256]{2,1,0:T(8,128)S(1)} collective-permute-done((f32[10,8,256]{2,1,0:T(8,128)S(1)}, f32[10,8,256]{2,1,0:T(8,128)S(1)}, u32[]{:S(2)}, u32[]{:S(2)}) %collective-permute-start) | collective-permute-done | bytes 81952 | tf_op jit(solution)/shard_map/ppermute | solution.py:485
  11.3 4.3 %collective-permute-done.1.south = f32[10,8,256]{2,1,0:T(8,128)S(1)} collective-permute-done((f32[10,8,256]{2,1,0:T(8,128)S(1)}, f32[10,8,256]{2,1,0:T(8,128)S(1)}, u32[]{:S(2)}, u32[]{:S(2)}) %collective-permute-start.1) | collective-permute-done | bytes 81952 | tf_op jit(solution)/shard_map/ppermute | solution.py:485
  15.6 0.2 col_slabs.1
  15.8 1.3 %collective-permute-start.2 = (f32[80,128]{1,0:T(8,128)S(1)}, f32[80,128]{1,0:T(8,128)S(1)}, u32[]{:S(2)}, u32[]{:S(2)}) collective-permute-start(f32[80,128]{1,0:T(8,128)S(1)} %get-tuple-element.23), channel_id=1, source_target_pairs={{0,1},{1,2},{2,3},{4,5},{5,6},{6,7},{8,9},{9,10},{10,11},{12,13},{... | collective-permute-start | bytes 122888 | tf_op jit(solution)/shard_map/ppermute | solution.py:485
  17.1 1.3 %collective-permute-start.3 = (f32[80,128]{1,0:T(8,128)S(1)}, f32[80,128]{1,0:T(8,128)S(1)}, u32[]{:S(2)}, u32[]{:S(2)}) collective-permute-start(f32[80,128]{1,0:T(8,128)S(1)} %get-tuple-element.24), channel_id=1, source_target_pairs={{1,0},{2,1},{3,2},{5,4},{6,5},{7,6},{9,8},{10,9},{11,10},{13,12},{... | collective-permute-start | bytes 122888 | tf_op jit(solution)/shard_map/ppermute | solution.py:485
  18.4 0.0 copy-start.10
  18.4 0.7 %copy-done.10 = bf16[64,64]{1,0:T(8,128)(2,1)S(1)} copy-done((bf16[64,64]{1,0:T(8,128)(2,1)S(1)}, bf16[64,64]{1,0:T(8,128)(2,1)}, u32[]{:S(2)}) %copy-start.10) | copy-done | bytes 8216
  19.1 0.0 copy-start.11
  19.1 0.7 %copy-done.11 = bf16[64,64]{1,0:T(8,128)(2,1)S(1)} copy-done((bf16[64,64]{1,0:T(8,128)(2,1)S(1)}, bf16[64,64]{1,0:T(8,128)(2,1)}, u32[]{:S(2)}) %copy-start.11) | copy-done | bytes 8216
  19.9 0.0 copy-start.13
  19.9 0.7 %copy-done.13 = f32[64]{0:T(128)S(1)} copy-done((f32[64]{0:T(128)S(1)}, f32[64]{0:T(128)}, u32[]{:S(2)}) %copy-start.13) | copy-done | bytes 280
  20.5 0.0 copy-start.14
  20.5 1.0 %copy-done.14 = bf16[10,64,256]{2,1,0:T(8,128)(2,1)S(1)} copy-done((bf16[10,64,256]{2,1,0:T(8,128)(2,1)S(1)}, bf16[10,64,256]{2,1,0:T(8,128)(2,1)}, u32[]{:S(2)}) %copy-start.14) | copy-done | bytes 327704
  21.5 0.0 copy-start.15
  21.5 0.7 %copy-done.15 = bf16[10,64]{1,0:T(8,128)(2,1)S(1)} copy-done((bf16[10,64]{1,0:T(8,128)(2,1)S(1)}, bf16[10,64]{1,0:T(8,128)(2,1)}, u32[]{:S(2)}) %copy-start.15) | copy-done | bytes 1304
  22.2 0.0 copy-start.16
  22.2 0.7 %copy-done.16 = f32[3,64]{1,0:T(4,128)S(1)} copy-done((f32[3,64]{1,0:T(4,128)S(1)}, f32[3,64]{1,0:T(4,128)}, u32[]{:S(2)}) %copy-start.16) | copy-done | bytes 792
  22.9 10.2 %network_forward.1 = (bf16[64,208,256]{2,1,0:T(8,128)(2,1)}, f32[64,256]{1,0:T(8,128)}) custom-call(bf16[10,64,256]{2,1,0:T(8,128)(2,1)S(1)} %copy-done.14, bf16[10,64]{1,0:T(8,128)(2,1)S(1)} %copy-done.15, bf16[64,64]{1,0:T(8,128)(2,1)S(1)} %copy-done.10, bf16[64,64]{1,0:T(8,128)(2,1)S(1)} %copy-done.11, f32[1,64]{1,0:T(1,128)S(1)} %bitcast.4, ...), custom_call_target="tpu_custom_call" | custom-call | flops 289406976 | bytes 7143424 | tf_op jit(solution)/shard_map/network_forward/pallas_call | solution.py:206
  33.1 0.0 collective-permute-done.2.west
  33.1 0.0 collective-permute-done.3.east
  33.1 0.0 copy-done.1
  33.1 0.0 copy-done.3
  33.1 0.0 copy-done.5
  33.1 0.0 copy-done.7
  33.1 0.0 copy-done.8
  33.1 0.0 copy-done.12
  33.1 0.0 copy-start.9
  33.2 0.8 %copy-done.9 = f32[64,256]{1,0:T(8,128)S(1)} copy-done((f32[64,256]{1,0:T(8,128)S(1)}, f32[64,256]{1,0:T(8,128)}, u32[]{:S(2)}) %copy-start.9) | copy-done | bytes 65560
  34.0 12.1 %sweeps_backward.1 = (f32[5,64,256]{2,1,0:T(8,128)}, f32[72,128]{1,0:T(8,128)S(1)}) custom-call(bf16[5,64,256]{2,1,0:T(8,128)(2,1)S(1)} %copy-done.1, bf16[4,64,256]{2,1,0:T(8,128)(2,1)S(1)} %copy-done.3, f32[64,256]{1,0:T(8,128)S(1)} %copy-done.5, s32[64,256]{1,0:T(8,128)S(1)} %copy-done.7, f32[64,256]{1,0:T(8,128)S(1)} %copy-done.8, ...), custom_call_target="tpu_custom_call" | custom-call | tf_op jit(solution)/shard_map/sweeps_backward/pallas_call | solution.py:413
  46.1 2.9 %collective-permute-start.4 = (f32[72,128]{1,0:T(8,128)S(1)}, f32[72,128]{1,0:T(8,128)S(1)}, u32[]{:S(2)}, u32[]{:S(2)}) collective-permute-start(f32[72,128]{1,0:T(8,128)S(1)} %get-tuple-element.27), channel_id=1, source_target_pairs={{0,1},{1,0},{2,3},{3,2},{4,5},{5,4},{6,7},{7,6},{8,9},{9,8},{10,11... | collective-permute-start | bytes 110600 | tf_op jit(solution)/shard_map/ppermute | solution.py:476
  49.0 0.9 %collective-permute-done.4 = f32[72,128]{1,0:T(8,128)S(1)} collective-permute-done((f32[72,128]{1,0:T(8,128)S(1)}, f32[72,128]{1,0:T(8,128)S(1)}, u32[]{:S(2)}, u32[]{:S(2)}) %collective-permute-start.4) | collective-permute-done | bytes 36896 | tf_op jit(solution)/shard_map/ppermute | solution.py:476
  49.8 2.0 %collective-permute-start.5 = (f32[72,128]{1,0:T(8,128)S(1)}, f32[72,128]{1,0:T(8,128)S(1)}, u32[]{:S(2)}, u32[]{:S(2)}) collective-permute-start(f32[72,128]{1,0:T(8,128)S(1)} %add.12), channel_id=1, source_target_pairs={{0,2},{1,3},{2,0},{3,1},{4,6},{5,7},{6,4},{7,5},{8,10},{9,11},{10,... | collective-permute-start | bytes 110600 | tf_op jit(solution)/shard_map/ppermute | solution.py:476
  51.8 2.0 %collective-permute-done.5 = f32[72,128]{1,0:T(8,128)S(1)} collective-permute-done((f32[72,128]{1,0:T(8,128)S(1)}, f32[72,128]{1,0:T(8,128)S(1)}, u32[]{:S(2)}, u32[]{:S(2)}) %collective-permute-start.5) | collective-permute-done | bytes 36896 | tf_op jit(solution)/shard_map/ppermute | solution.py:476
  53.8 1.6 %collective-permute-start.6 = (f32[72,128]{1,0:T(8,128)S(1)}, f32[72,128]{1,0:T(8,128)S(1)}, u32[]{:S(2)}, u32[]{:S(2)}) collective-permute-start(f32[72,128]{1,0:T(8,128)S(1)} %add.13), channel_id=1, source_target_pairs={{0,4},{4,0},{8,12},{12,8},{1,5},{5,1},{9,13},{13,9},{2,6},{6,2},{1... | collective-permute-start | bytes 110600 | tf_op jit(solution)/shard_map/ppermute | solution.py:476
  55.4 2.4 %collective-permute-done.6 = f32[72,128]{1,0:T(8,128)S(1)} collective-permute-done((f32[72,128]{1,0:T(8,128)S(1)}, f32[72,128]{1,0:T(8,128)S(1)}, u32[]{:S(2)}, u32[]{:S(2)}) %collective-permute-start.6) | collective-permute-done | bytes 36896 | tf_op jit(solution)/shard_map/ppermute | solution.py:476
  57.8 2.6 %collective-permute-start.7 = (f32[72,128]{1,0:T(8,128)S(1)}, f32[72,128]{1,0:T(8,128)S(1)}, u32[]{:S(2)}, u32[]{:S(2)}) collective-permute-start(f32[72,128]{1,0:T(8,128)S(1)} %add.14), channel_id=1, source_target_pairs={{0,8},{4,12},{8,0},{12,4},{1,9},{5,13},{9,1},{13,5},{2,10},{6,14},... | collective-permute-start | bytes 110600 | tf_op jit(solution)/shard_map/ppermute | solution.py:476
  60.4 2.3 %collective-permute-done.7 = f32[72,128]{1,0:T(8,128)S(1)} collective-permute-done((f32[72,128]{1,0:T(8,128)S(1)}, f32[72,128]{1,0:T(8,128)S(1)}, u32[]{:S(2)}, u32[]{:S(2)}) %collective-permute-start.7) | collective-permute-done | bytes 36896 | tf_op jit(solution)/shard_map/ppermute | solution.py:476
  62.6 0.8 %clip.1 = (f32[10,64]{1,0:T(8,128)}, f32[64,64]{1,0:T(8,128)}, f32[64,64]{1,0:T(8,128)}, f32[1,64]{1,0:T(1,128)}, f32[3,64]{1,0:T(4,128)}) custom-call(f32[1,72,128]{2,1,0:T(8,128)S(1)} %add_bitcast_fusion.parts), custom_call_target="tpu_custom_call" | custom-call | tf_op jit(solution)/shard_map/clip/pallas_call | solution.py:460
  (5 shorter events, 0.0 us)
Async XLA Ops:
  0.6 0.9 %copy-start = (bf16[5,64,256]{2,1,0:T(8,128)(2,1)S(1)}, bf16[5,64,256]{2,1,0:T(8,128)(2,1)}, u32[]{:S(2)}) copy-start(bf16[5,64,256]{2,1,0:T(8,128)(2,1)} %src.1) | copy-start | bytes 491524
  1.6 0.9 %copy-start.2 = (bf16[4,64,256]{2,1,0:T(8,128)(2,1)S(1)}, bf16[4,64,256]{2,1,0:T(8,128)(2,1)}, u32[]{:S(2)}) copy-start(bf16[4,64,256]{2,1,0:T(8,128)(2,1)} %cpl.1) | copy-start | bytes 393220
  2.5 0.8 %copy-start.4 = (f32[64,256]{1,0:T(8,128)S(1)}, f32[64,256]{1,0:T(8,128)}, u32[]{:S(2)}) copy-start(f32[64,256]{1,0:T(8,128)} %dia.1) | copy-start | bytes 196612
  3.3 0.8 %copy-start.6 = (s32[64,256]{1,0:T(8,128)S(1)}, s32[64,256]{1,0:T(8,128)}, u32[]{:S(2)}) copy-start(s32[64,256]{1,0:T(8,128)} %bc.1) | copy-start | bytes 196612
  4.1 29.0 %copy-start.1 = (bf16[5,64,256]{2,1,0:T(8,128)(2,1)S(1)}, bf16[5,64,256]{2,1,0:T(8,128)(2,1)}, u32[]{:S(2)}) copy-start(bf16[5,64,256]{2,1,0:T(8,128)(2,1)} %src.1) | copy-start | bytes 491524
  4.1 29.0 %copy-start.3 = (bf16[4,64,256]{2,1,0:T(8,128)(2,1)S(1)}, bf16[4,64,256]{2,1,0:T(8,128)(2,1)}, u32[]{:S(2)}) copy-start(bf16[4,64,256]{2,1,0:T(8,128)(2,1)} %cpl.1) | copy-start | bytes 393220
  4.1 29.0 %copy-start.5 = (f32[64,256]{1,0:T(8,128)S(1)}, f32[64,256]{1,0:T(8,128)}, u32[]{:S(2)}) copy-start(f32[64,256]{1,0:T(8,128)} %dia.1) | copy-start | bytes 196612
  4.1 29.0 %copy-start.7 = (s32[64,256]{1,0:T(8,128)S(1)}, s32[64,256]{1,0:T(8,128)}, u32[]{:S(2)}) copy-start(s32[64,256]{1,0:T(8,128)} %bc.1) | copy-start | bytes 196612
  4.1 29.0 %copy-start.8 = (f32[64,256]{1,0:T(8,128)S(1)}, f32[64,256]{1,0:T(8,128)}, u32[]{:S(2)}) copy-start(f32[64,256]{1,0:T(8,128)} %prod.1) | copy-start | bytes 196612
  4.2 29.0 %copy-start.12 = (f32[5,5]{1,0:T(8,128)S(1)}, f32[5,5]{1,0:T(8,128)}, u32[]{:S(2)}) copy-start(f32[5,5]{1,0:T(8,128)} %mix.1) | copy-start | bytes 304
  4.2 7.1 %collective-permute-start = (f32[10,8,256]{2,1,0:T(8,128)S(1)}, f32[10,8,256]{2,1,0:T(8,128)S(1)}, u32[]{:S(2)}, u32[]{:S(2)}) collective-permute-start(f32[10,8,256]{2,1,0:T(8,128)S(1)} %get-tuple-element.21), channel_id=1, source_target_pairs={{0,4},{4,8},{8,12},{1,5},{5,9},{9,13},{2,6},{6,10},{10,14},{3,7},{... | collective-permute-start | bytes 245768 | tf_op jit(solution)/shard_map/ppermute | solution.py:485
  9.3 6.3 %collective-permute-start.1 = (f32[10,8,256]{2,1,0:T(8,128)S(1)}, f32[10,8,256]{2,1,0:T(8,128)S(1)}, u32[]{:S(2)}, u32[]{:S(2)}) collective-permute-start(f32[10,8,256]{2,1,0:T(8,128)S(1)} %get-tuple-element.22), channel_id=1, source_target_pairs={{4,0},{8,4},{12,8},{5,1},{9,5},{13,9},{6,2},{10,6},{14,10},{7,3},{... | collective-permute-start | bytes 245768 | tf_op jit(solution)/shard_map/ppermute | solution.py:485
  15.8 17.3 %collective-permute-start.2 = (f32[80,128]{1,0:T(8,128)S(1)}, f32[80,128]{1,0:T(8,128)S(1)}, u32[]{:S(2)}, u32[]{:S(2)}) collective-permute-start(f32[80,128]{1,0:T(8,128)S(1)} %get-tuple-element.23), channel_id=1, source_target_pairs={{0,1},{1,2},{2,3},{4,5},{5,6},{6,7},{8,9},{9,10},{10,11},{12,13},{... | collective-permute-start | bytes 122888 | tf_op jit(solution)/shard_map/ppermute | solution.py:485
  17.1 16.0 %collective-permute-start.3 = (f32[80,128]{1,0:T(8,128)S(1)}, f32[80,128]{1,0:T(8,128)S(1)}, u32[]{:S(2)}, u32[]{:S(2)}) collective-permute-start(f32[80,128]{1,0:T(8,128)S(1)} %get-tuple-element.24), channel_id=1, source_target_pairs={{1,0},{2,1},{3,2},{5,4},{6,5},{7,6},{9,8},{10,9},{11,10},{13,12},{... | collective-permute-start | bytes 122888 | tf_op jit(solution)/shard_map/ppermute | solution.py:485
  18.4 0.7 %copy-start.10 = (bf16[64,64]{1,0:T(8,128)(2,1)S(1)}, bf16[64,64]{1,0:T(8,128)(2,1)}, u32[]{:S(2)}) copy-start(bf16[64,64]{1,0:T(8,128)(2,1)} %wmid.1) | copy-start | bytes 24580
  19.1 0.7 %copy-start.11 = (bf16[64,64]{1,0:T(8,128)(2,1)S(1)}, bf16[64,64]{1,0:T(8,128)(2,1)}, u32[]{:S(2)}) copy-start(bf16[64,64]{1,0:T(8,128)(2,1)} %wtop.1) | copy-start | bytes 24580
  19.9 0.7 %copy-start.13 = (f32[64]{0:T(128)S(1)}, f32[64]{0:T(128)}, u32[]{:S(2)}) copy-start(f32[64]{0:T(128)} %param.22) | copy-start | bytes 772
  20.5 1.0 %copy-start.14 = (bf16[10,64,256]{2,1,0:T(8,128)(2,1)S(1)}, bf16[10,64,256]{2,1,0:T(8,128)(2,1)}, u32[]{:S(2)}) copy-start(bf16[10,64,256]{2,1,0:T(8,128)(2,1)} %feat_ref.1) | copy-start | bytes 983044
  21.5 0.7 %copy-start.15 = (bf16[10,64]{1,0:T(8,128)(2,1)S(1)}, bf16[10,64]{1,0:T(8,128)(2,1)}, u32[]{:S(2)}) copy-start(bf16[10,64]{1,0:T(8,128)(2,1)} %win_ref.1) | copy-start | bytes 3844
  22.2 0.7 %copy-start.16 = (f32[3,64]{1,0:T(4,128)S(1)}, f32[3,64]{1,0:T(4,128)}, u32[]{:S(2)}) copy-start(f32[3,64]{1,0:T(4,128)} %bias_ref.1) | copy-start | bytes 2308
  33.1 0.8 %copy-start.9 = (f32[64,256]{1,0:T(8,128)S(1)}, f32[64,256]{1,0:T(8,128)}, u32[]{:S(2)}) copy-start(f32[64,256]{1,0:T(8,128)} %get-tuple-element.14.beta) | copy-start | bytes 196612
  46.1 3.7 %collective-permute-start.4 = (f32[72,128]{1,0:T(8,128)S(1)}, f32[72,128]{1,0:T(8,128)S(1)}, u32[]{:S(2)}, u32[]{:S(2)}) collective-permute-start(f32[72,128]{1,0:T(8,128)S(1)} %get-tuple-element.27), channel_id=1, source_target_pairs={{0,1},{1,0},{2,3},{3,2},{4,5},{5,4},{6,7},{7,6},{8,9},{9,8},{10,11... | collective-permute-start | bytes 110600 | tf_op jit(solution)/shard_map/ppermute | solution.py:476
  49.8 4.0 %collective-permute-start.5 = (f32[72,128]{1,0:T(8,128)S(1)}, f32[72,128]{1,0:T(8,128)S(1)}, u32[]{:S(2)}, u32[]{:S(2)}) collective-permute-start(f32[72,128]{1,0:T(8,128)S(1)} %add.12), channel_id=1, source_target_pairs={{0,2},{1,3},{2,0},{3,1},{4,6},{5,7},{6,4},{7,5},{8,10},{9,11},{10,... | collective-permute-start | bytes 110600 | tf_op jit(solution)/shard_map/ppermute | solution.py:476
  53.8 4.0 %collective-permute-start.6 = (f32[72,128]{1,0:T(8,128)S(1)}, f32[72,128]{1,0:T(8,128)S(1)}, u32[]{:S(2)}, u32[]{:S(2)}) collective-permute-start(f32[72,128]{1,0:T(8,128)S(1)} %add.13), channel_id=1, source_target_pairs={{0,4},{4,0},{8,12},{12,8},{1,5},{5,1},{9,13},{13,9},{2,6},{6,2},{1... | collective-permute-start | bytes 110600 | tf_op jit(solution)/shard_map/ppermute | solution.py:476
  57.8 4.9 %collective-permute-start.7 = (f32[72,128]{1,0:T(8,128)S(1)}, f32[72,128]{1,0:T(8,128)S(1)}, u32[]{:S(2)}, u32[]{:S(2)}) collective-permute-start(f32[72,128]{1,0:T(8,128)S(1)} %add.14), channel_id=1, source_target_pairs={{0,8},{4,12},{8,0},{12,4},{1,9},{5,13},{9,1},{13,5},{2,10},{6,14},... | collective-permute-start | bytes 110600 | tf_op jit(solution)/shard_map/ppermute | solution.py:476
where the time goes:
time: 64.2 us; the launch traced here: 63.5 us
  Pallas kernels  23.4 us (36%)
  starting transfers between devices  17.9 us (28%)
  waiting for transfers between devices  12.5 us (19%)
  local copies, waits for them, and re-layouts  8.77 us (14%)
  between operations  0.79 us (1%)
    pallas_call x1, Pallas kernels, sweeps_and_backward(): pl.pallas_call(backward_kernel, grid=(rows // blk,), in_specs=[whole(x.sh...  12.1 us
    pallas_call x1, Pallas kernels, forward(): pl.pallas_call(forward_kernel, grid=(rows // blk,), in_specs=[pl.BlockSpe...  10.2 us
    ppermute x4, starting transfers between devices, sum_parts(): lax.ppermute(packed, axis, [(i, i ^ step) for i in range(count)])  8.99 us
    unnamed x34, local copies, waits for them, and re-layouts  8.77 us
    ppermute x4, waiting for transfers between devices, sum_parts(): lax.ppermute(packed, axis, [(i, i ^ step) for i in range(count)])  7.5 us
    ppermute x2, starting transfers between devices, shift_pair(): lax.ppermute(high_edge, axis, up)  6.36 us
    ppermute x2, waiting for transfers between devices, shift_pair(): lax.ppermute(low_edge, axis, down)  4.3 us
    ppermute x2, starting transfers between devices, shift_pair(): lax.ppermute(low_edge, axis, down)  2.58 us
  transfers between devices with their start and end apart: 8, of which 6 were waited for; matrix products, arithmetic and copies ran while one was open for 0% of the time, Pallas kernels for 16%

commit v1 on v0

v1 whole, which is shorter than its diff:
```python
import functools

import jax
import jax.numpy as jnp
from jax import lax
from jax.experimental import pallas as pl
from jax.experimental.pallas import tpu as pltpu
from jax.sharding import PartitionSpec as P

SWEEPS = 6
WALL_EXTRA = 0.2
FAR_EXTRA = 0.6
REG_WEIGHT = 0.5
CLIP_NORM = 64.0
EDGE = 8
SUB, LANE = 8, 128
F32, BF16 = jnp.float32, jnp.bfloat16
NT = (((1,), (1,)), ((), ()))
TN = (((0,), (0,)), ((), ()))
VMEM_BYTES = 16 * 1024 * 1024


def whole(shape):
    return pl.BlockSpec(shape, lambda *_: (0,) * len(shape))


def in_hbm(x):
    return pltpu.with_memory_space_constraint(x, pltpu.HBM)


def on_chip(kernel, operands, outs, scratch=(), far=(), far_outs=(), **kwargs):
    here, there = pl.BlockSpec(memory_space=pltpu.VMEM), pl.BlockSpec(memory_space=pltpu.HBM)
    return pl.pallas_call(
        kernel,
        in_specs=[here] * len(operands) + [there] * len(far),
        out_specs=[here] * len(outs) + [there] * len(far_outs),
        out_shape=[pltpu.VMEM(*o) for o in outs] + [pltpu.HBM(*o) for o in far_outs],
        scratch_shapes=list(scratch),
        compiler_params=params(),
        **kwargs,
    )(*operands, *[in_hbm(x) for x in far])


def like(x):
    return (x.shape, x.dtype)


def params():
    return pltpu.CompilerParams(vmem_limit_bytes=VMEM_BYTES)


def inverse_diag(diag, code):
    total = diag + jnp.where(code == 1, WALL_EXTRA, 0.0) + jnp.where(code == 2, FAR_EXTRA, 0.0)
    return 1.0 / total


def load_kernel(count, *refs):
    far, near = refs[:count], refs[count : 2 * count]
    inv, top, bottom, sems = refs[2 * count :]
    copies = [pltpu.make_async_copy(far[k], near[k], sems.at[k]) for k in range(count)]
    for copy in copies:
        copy.start()
    src, cpl, dia, bc = near[:4]
    for copy in copies[:4]:
        copy.wait()
    nv, rows, _ = src.shape
    nc = cpl.shape[0]
    inv[...] = inverse_diag(dia[...], bc[...])
    for v in range(nv):
        top[v] = src[v, 0:16].astype(F32)[:EDGE]
        bottom[v] = src[v, rows - 16 :].astype(F32)[16 - EDGE :]
    for d in range(nc):
        top[nv + d] = cpl[d, 0:16].astype(F32)[:EDGE]
        bottom[nv + d] = cpl[d, rows - 16 :].astype(F32)[16 - EDGE :]
    top[nv + nc] = inv[0:EDGE]
    bottom[nv + nc] = inv[rows - EDGE :]
    for copy in copies[4:]:
        copy.wait()


def load(arrays):
    source, coupling = arrays[:2]
    nv, rows, cols = source.shape
    slab = ((nv + coupling.shape[0] + 1, EDGE, cols), F32)
    return on_chip(
        functools.partial(load_kernel, len(arrays)),
        [],
        [like(x) for x in arrays] + [((rows, cols), F32), slab, slab],
        [pltpu.SemaphoreType.DMA((len(arrays),))],
        far=arrays,
        name="load",
    )


def cols_kernel(src, cpl, inv, north, south, west_ref, east_ref):
    nv, rows, cols = src.shape
    nc = cpl.shape[0]
    lane = lax.broadcasted_iota(jnp.int32, (rows, LANE), 1) // EDGE
    lane_h = lane[:EDGE]
    sides = ((west_ref, slice(0, LANE), 0), (east_ref, slice(cols - LANE, cols), EDGE))
    for out, window, extra in sides:
        mid = jnp.zeros((rows, LANE), F32)
        up = jnp.zeros((EDGE, LANE), F32)
        down = jnp.zeros((EDGE, LANE), F32)
        for f in range(nv + nc + 1):
            if f < nv:
                x = src[f, :, window].astype(F32)
            elif f < nv + nc:
                x = cpl[f - nv, :, window].astype(F32)
            else:
                x = inv[:, window]
            shift = (EDGE * f + extra) % LANE
            mid = jnp.where(lane == f, pltpu.roll(x, shift, 1), mid)
            up = jnp.where(lane_h == f, pltpu.roll(north[f, :, window], shift, 1), up)
            down = jnp.where(lane_h == f, pltpu.roll(south[f, :, window], shift, 1), down)
        out[0:EDGE] = up
        out[EDGE : EDGE + rows] = mid
        out[EDGE + rows :] = down


def col_slabs(source, coupling, inv, north, south):
    slab = ((source.shape[1] + 2 * EDGE, LANE), F32)
    return on_chip(cols_kernel, [source, coupling, inv, north, south], [slab, slab], name="col_slabs")


def column_of(row):
    hidden = row.shape[1]
    wide = jnp.concatenate([row, jnp.zeros((1, LANE - hidden), F32)], axis=1)
    return jnp.transpose(jnp.broadcast_to(wide, (LANE, LANE)))[:hidden]


def across(block, width):
    return jnp.concatenate([block] * (width // LANE), axis=1)


def weights_kernel(win, wmid, wtop, wout, bias, w1, w2, w3, cst):
    nf, hidden = win.shape
    step_rows, blk = hidden + 16, 16
    depth = w1.shape[1]
    feat_of = lax.broadcasted_iota(jnp.int32, (nf, depth), 1) // blk
    pick = (feat_of == lax.broadcasted_iota(jnp.int32, (nf, depth), 0)).astype(F32).astype(BF16)
    spread = lax.dot_general(win[...], pick, TN, preferred_element_type=F32)
    col = lax.broadcasted_iota(jnp.int32, (hidden, depth), 1)
    col_f = lax.broadcasted_iota(jnp.int32, (16, depth), 1)
    row_f = lax.broadcasted_iota(jnp.int32, (16, depth), 0)
    for r in range(blk):
        base = r * step_rows
        w1[base : base + hidden] = jnp.where(col % blk == r, spread, 0.0).astype(BF16)
        same = jnp.logical_and(col_f == row_f * blk + r, row_f < nf)
        w1[base + hidden : base + step_rows] = jnp.where(same, 1.0, 0.0).astype(BF16)
    w2[...] = jnp.transpose(wmid[...].astype(F32)).astype(BF16)
    w3[...] = jnp.transpose(wtop[...].astype(F32)).astype(BF16)
    for k in range(3):
        cst[k] = column_of(bias[k : k + 1, :])
    cst[3] = column_of(wout[...])


def prepare(weight_in, weight_mid, weight_top, weight_out, biases):
    nf, hidden = weight_in.shape
    depth = -(-nf * 16 // LANE) * LANE
    return on_chip(
        weights_kernel,
        [weight_in, weight_mid, weight_top, weight_out, biases],
        [
            ((16 * (hidden + 16), depth), BF16),
            ((hidden, hidden), BF16),
            ((hidden, hidden), BF16),
            ((4, hidden, LANE), F32),
        ],
        name="weights",
    )


def forward_kernel(first_row, feat, w1, w2, w3, cst, acts, beta, x1):
    nf, _, cols = feat.shape
    hidden = w2.shape[0]
    step_rows, blk, per = hidden + 16, 16, 4
    x1[...] = jnp.zeros(x1.shape, BF16)

    @pl.loop(0, acts.shape[0] // blk)
    def _(block):
        start = pl.multiple_of(block * blk, blk)
        x1[0 : nf * blk] = feat[:, pl.ds(first_row + start, blk), :].reshape(nf * blk, cols)
        b1, b2, b3, wo = (across(cst[k], cols) for k in range(4))
        lines = []
        for g in range(blk // per):
            lo = g * per * step_rows
            first = jnp.dot(w1[lo : lo + per * step_rows], x1[...], preferred_element_type=F32)
            ones = []
            for q in range(per):
                part = first[q * step_rows : (q + 1) * step_rows]
                one = jnp.tanh(part[:hidden] + b1).astype(BF16)
                acts[start + (g * per + q), 0:hidden] = one
                acts[start + (g * per + q), 3 * hidden :] = part[hidden:].astype(BF16)
                ones.append(one)
            second = jnp.dot(w2[...], jnp.concatenate(ones, axis=1), preferred_element_type=F32)
            twos = []
            for q in range(per):
                two = jnp.tanh(second[:, q * cols : (q + 1) * cols] + b2).astype(BF16)
                acts[start + (g * per + q), hidden : 2 * hidden] = two
                twos.append(two)
            third = jnp.dot(w3[...], jnp.concatenate(twos, axis=1), preferred_element_type=F32)
            for q in range(per):
                three = jnp.tanh(third[:, q * cols : (q + 1) * cols] + b3).astype(BF16)
                acts[start + (g * per + q), 2 * hidden : 3 * hidden] = three
                lines.append(1.0 + jnp.sum(three.astype(F32) * wo, axis=0, keepdims=True))
        beta[pl.ds(start, blk), :] = jnp.concatenate(lines, axis=0)


def forward(features, prepared, first_row, count):
    nf, _, cols = features.shape
    w1, w2 = prepared[:2]
    hidden = w2.shape[0]
    high = 3 * hidden + 16
    return on_chip(
        functools.partial(forward_kernel, first_row),
        [features, *prepared],
        [((count, high, cols), BF16), ((count, cols), F32)],
        [pltpu.VMEM((w1.shape[1], cols), BF16)],
        cost_estimate=pl.CostEstimate(
            flops=2 * count * cols * (nf + 2 * hidden) * hidden,
            bytes_accessed=2 * count * cols * (high + nf),
            transcendentals=3 * count * cols * hidden,
        ),
        name="network_forward",
    )


def tile_at(ref, lead, t, k):
    return ref[lead + (slice(t * SUB, (t + 1) * SUB), slice(k * LANE, (k + 1) * LANE))]


class Shifts:
    def __init__(self, tiles, lanes):
        self.tiles, self.lanes = tiles, lanes
        sub = lax.broadcasted_iota(jnp.int32, (SUB, LANE), 0)
        lane = lax.broadcasted_iota(jnp.int32, (SUB, LANE), 1)
        self.first_sub, self.last_sub = sub == 0, sub == SUB - 1
        self.first_lane, self.last_lane = lane == 0, lane == LANE - 1

    def above(self, ref, lead, t, k):
        here, other = tile_at(ref, lead, t, k), tile_at(ref, lead, max(t - 1, 0), k)
        return pltpu.roll(jnp.where(self.last_sub, other, here), 1, 0)

    def below(self, ref, lead, t, k):
        here, other = tile_at(ref, lead, t, k), tile_at(ref, lead, min(t + 1, self.tiles - 1), k)
        return pltpu.roll(jnp.where(self.first_sub, other, here), SUB - 1, 0)

    def left(self, ref, lead, t, k):
        here, other = tile_at(ref, lead, t, k), tile_at(ref, lead, t, (k - 1) % self.lanes)
        return pltpu.roll(jnp.where(self.last_lane, other, here), 1, 1)

    def right(self, ref, lead, t, k):
        here, other = tile_at(ref, lead, t, k), tile_at(ref, lead, t, (k + 1) % self.lanes)
        return pltpu.roll(jnp.where(self.first_lane, other, here), LANE - 1, 1)


def sweep_kernel(
    src, cpl, inverse, prod, beta_a, beta_b, north, south, west, east, mix,
    adj_out, sens, beta,
    raw, src_x, cpl_x, adj_a, adj_b,
):
    nv, rows, cols = src.shape
    nc = cpl.shape[0]
    tall = rows + 2 * EDGE
    tiles, lanes = tall // SUB, cols // LANE + 1
    shifts = Shifts(tiles, lanes)
    inner = slice(EDGE, EDGE + rows)
    lane = lax.broadcasted_iota(jnp.int32, (tall, LANE), 1)
    from_east, from_west = lane < EDGE, lane >= LANE - EDGE
    for f in range(nv + nc + 1):
        if f < nv:
            raw[f, inner, 0:cols] = src[f].astype(F32)
        elif f < nv + nc:
            raw[f, inner, 0:cols] = cpl[f - nv].astype(F32)
        else:
            raw[f, inner, 0:cols] = inverse[...]
        raw[f, 0:EDGE, 0:cols] = north[f]
        raw[f, EDGE + rows :, 0:cols] = south[f]
        e = pltpu.roll(east[...], (LANE - EDGE * f) % LANE, 1)
        w = pltpu.roll(west[...], (LANE - EDGE - EDGE * f) % LANE, 1)
        raw[f, :, cols:] = jnp.where(from_east, e, jnp.where(from_west, w, 0.0))

    moves = (shifts.above, shifts.below, shifts.left, shifts.right)
    for t in range(tiles):
        for k in range(lanes):
            at = (slice(t * SUB, (t + 1) * SUB), slice(k * LANE, (k + 1) * LANE))
            inv = tile_at(raw, (nv + nc,), t, k)
            for v in range(nv):
                src_x[(v,) + at] = inv * tile_at(raw, (v,), t, k)
            for d in range(nc):
                cpl_x[(d,) + at] = inv * moves[d](raw, (nv + d,), t, k)

    def sweep(old, new, last):
        for t in range(1, tiles - 1) if last else range(tiles):
            for k in range(lanes - 1) if last else range(lanes):
                at = (slice(t * SUB, (t + 1) * SUB), slice(k * LANE, (k + 1) * LANE))
                couple = [cpl_x[(d,) + at] for d in range(nc)]
                total = [src_x[(a,) + at] for a in range(nv)]
                for b in range(nv):
                    inc = couple[0] * moves[0](old, (b,), t, k)
                    for d in range(1, nc):
                        inc = inc + couple[d] * moves[d](old, (b,), t, k)
                    total = [total[a] + mix[b, a] * inc for a in range(nv)]
                if last:
                    at = (slice((t - 1) * SUB, t * SUB), at[1])
                for a in range(nv):
                    new[(a,) + at] = total[a]

    sweep(src_x, adj_a, False)

    @pl.loop(0, (SWEEPS - 2) // 2)
    def _(i):
        sweep(adj_a, adj_b, False)
        sweep(adj_b, adj_a, False)

    sweep(adj_a, adj_out, True)
    half = beta_a.shape[0]
    beta[0:half] = beta_a[...]
    beta[half:] = beta_b[...]
    sens[...] = adj_out[nv - 1] * prod[...] + REG_WEIGHT * (beta[...] - 1.0)


def sweeps(source, coupling, inverse, production, betas, halos, mixing):
    nv, rows, cols = source.shape
    nc = coupling.shape[0]
    tall, wide = rows + 2 * EDGE, cols + LANE
    near = pl.BlockSpec(memory_space=pltpu.VMEM)
    operands = [source, coupling, inverse, production, *betas, *halos]
    flat = ((rows, cols), F32)
    return pl.pallas_call(
        sweep_kernel,
        in_specs=[near] * len(operands) + [pl.BlockSpec(memory_space=pltpu.SMEM)],
        out_specs=[near] * 3,
        out_shape=[pltpu.VMEM((nv, rows, cols), F32), pltpu.VMEM(*flat), pltpu.VMEM(*flat)],
        scratch_shapes=[
            pltpu.VMEM((nv + nc + 1, tall, wide), F32),
            pltpu.VMEM((nv, tall, wide), F32),
            pltpu.VMEM((nc, tall, wide), F32),
            pltpu.VMEM((nv, tall, wide), F32),
            pltpu.VMEM((nv, tall, wide), F32),
        ],
        compiler_params=params(),
        name="sweeps",
    )(*operands, mixing)


def backward_kernel(
    adj, beta, sens, wmid, wtop, cst, acts_a, acts_b,
    packed, adj_out, beta_out,
    sums, g_mid, g_top, g_in, sems,
):
    out_copies = [
        pltpu.make_async_copy(adj, adj_out, sems.at[0]),
        pltpu.make_async_copy(beta, beta_out, sems.at[1]),
    ]
    for copy in out_copies:
        copy.start()
    blk, cols = 8, sens.shape[1]
    hidden = wmid.shape[0]
    sums[...] = jnp.zeros(sums.shape, F32)
    g_mid[...] = jnp.zeros(g_mid.shape, F32)
    g_top[...] = jnp.zeros(g_top.shape, F32)
    g_in[...] = jnp.zeros(g_in.shape, F32)

    def fold(x):
        parts = [x[:, k * LANE : (k + 1) * LANE] for k in range(cols // LANE)]
        return functools.reduce(jnp.add, parts)

    def outer(xs, ds):
        return lax.dot_general(
            jnp.concatenate(xs, axis=1), jnp.concatenate(ds, axis=1), NT, preferred_element_type=F32
        )

    def block(acts, start, first_row):
        rows_sens = sens[pl.ds(pl.multiple_of(first_row + start, blk), blk), :]
        wo = across(cst[3], cols)
        ones, twos, feats, d1s, d2s, d3s = [], [], [], [], [], []
        acc = [jnp.zeros((hidden, LANE), F32) for _ in range(4)]
        for q in range(blk):
            one, two = acts[start + q, 0:hidden], acts[start + q, hidden : 2 * hidden]
            three_f = acts[start + q, 2 * hidden : 3 * hidden].astype(F32)
            sen = jnp.broadcast_to(rows_sens[q : q + 1], (hidden, cols))
            acc[0] = acc[0] + fold(three_f * sen)
            d3 = sen * wo * (1.0 - three_f * three_f)
            acc[3] = acc[3] + fold(d3)
            d3 = d3.astype(BF16)
            two_f = two.astype(F32)
            d2 = jnp.dot(wtop[...], d3, preferred_element_type=F32) * (1.0 - two_f * two_f)
            acc[2] = acc[2] + fold(d2)
            d2 = d2.astype(BF16)
            one_f = one.astype(F32)
            d1 = jnp.dot(wmid[...], d2, preferred_element_type=F32) * (1.0 - one_f * one_f)
            acc[1] = acc[1] + fold(d1)
            d1 = d1.astype(BF16)
            ones.append(one)
            twos.append(two)
            feats.append(acts[start + q, 3 * hidden :])
            d1s.append(d1)
            d2s.append(d2)
            d3s.append(d3)
        g_mid[...] += outer(ones, d2s)
        g_top[...] += outer(twos, d3s)
        g_in[...] += outer(feats, d1s)
        for k in range(4):
            sums[k] += acc[k]

    half = acts_a.shape[0]
    for acts, first_row in ((acts_a, 0), (acts_b, half)):

        @pl.loop(0, acts.shape[0] // blk)
        def _(i, acts=acts, first_row=first_row):
            block(acts, pl.multiple_of(i * blk, blk), first_row)

    packed[0:hidden, :] = jnp.concatenate([g_mid[...], g_top[...]], axis=1)
    tail = g_in[SUB : 2 * SUB]
    row = lax.broadcasted_iota(jnp.int32, (SUB, hidden), 0)
    for k in range(4):
        line = jnp.sum(jnp.transpose(sums[k]), axis=0, keepdims=True)
        tail = tail + jnp.where(row == k + 2, jnp.broadcast_to(line, (SUB, hidden)), 0.0)
    packed[hidden : hidden + SUB, :] = jnp.concatenate([g_in[0:SUB], tail], axis=1)
    for copy in out_copies:
        copy.wait()


def backward(adj, beta, sens, weight_mid, weight_top, cst, acts):
    hidden = weight_mid.shape[0]
    return on_chip(
        backward_kernel,
        [adj, beta, sens, weight_mid, weight_top, cst, *acts],
        [((hidden + SUB, LANE), F32)],
        [
            pltpu.VMEM((4, hidden, LANE), F32),
            pltpu.VMEM((hidden, hidden), F32),
            pltpu.VMEM((hidden, hidden), F32),
            pltpu.VMEM((16, hidden), F32),
            pltpu.SemaphoreType.DMA((2,)),
        ],
        far_outs=[like(adj), like(beta)],
        name="backward",
    )


def clip_kernel(parts, gin, gmid, gtop, gout, gbias):
    hidden = gmid.shape[0]
    total = parts[0]
    for k in range(1, parts.shape[0]):
        total = total + parts[k]
    squares = jnp.sum(jnp.sum(total * total, axis=0, keepdims=True), axis=1, keepdims=True)
    total = total * (CLIP_NORM / jnp.maximum(jnp.sqrt(squares), CLIP_NORM))
    gmid[...] = total[:hidden, :hidden]
    gtop[...] = total[:hidden, hidden:]
    low, high = total[hidden:, :hidden], total[hidden:, hidden:]
    gin[0:SUB] = low
    gin[SUB:] = high[: gin.shape[0] - SUB]
    gout[...] = high[2:3]
    gbias[...] = high[3:6]


def clip_all(parts, num_feat, hidden):
    shapes = [(num_feat, hidden), (hidden, hidden), (hidden, hidden), (1, hidden), (3, hidden)]
    return pl.pallas_call(
        clip_kernel,
        grid=(1,),
        in_specs=[whole(parts.shape)],
        out_specs=[whole(s) for s in shapes],
        out_shape=[jax.ShapeDtypeStruct(s, F32) for s in shapes],
        compiler_params=params(),
        name="clip",
    )(parts)


def sum_parts(packed):
    return lax.all_gather(packed, ("gx", "gy"))


def shift_pair(low_edge, high_edge, axis):
    count = lax.axis_size(axis)
    up = [(i, i + 1) for i in range(count - 1)]
    down = [(b, a) for a, b in up]
    return lax.ppermute(high_edge, axis, up), lax.ppermute(low_edge, axis, down)


def shards(
    features, source, coupling, diagonal, production, bc_code, mixing,
    weight_in, weight_mid, weight_top, weight_out, biases,
):
    num_feat, rows, _ = features.shape
    hidden = weight_mid.shape[0]
    loaded = load([
        source, coupling, diagonal, bc_code, production, features,
        weight_in, weight_mid, weight_top, weight_out.reshape(1, hidden), biases,
    ])
    source, coupling, _, _, production, features, weight_in, weight_mid, weight_top, wout, biases = loaded[:11]
    inverse, top, bottom = loaded[11:]
    north, south = shift_pair(top, bottom, "gx")
    prepared = prepare(weight_in, weight_mid, weight_top, wout, biases)
    half = rows // 32 * 16
    acts_a, beta_a = forward(features, prepared, 0, half)
    north, south, beta_a = lax.optimization_barrier((north, south, beta_a))
    first, last = col_slabs(source, coupling, inverse, north, south)
    west, east = shift_pair(first, last, "gy")
    acts_b, beta_b = forward(features, prepared, half, rows - half)
    adj, sens, beta = sweeps(
        source, coupling, inverse, production, (beta_a, beta_b), (north, south, west, east), mixing
    )
    packed, adjoint, beta = backward(adj, beta, sens, weight_mid, weight_top, prepared[3], (acts_a, acts_b))
    grad_in, grad_mid, grad_top, grad_out, grad_bias = clip_all(sum_parts(packed), num_feat, hidden)
    return (adjoint, beta, grad_in, grad_mid, grad_top, grad_out.reshape(hidden), grad_bias)


def solution(mesh):
    cells3 = P(None, ("case", "gx"), "gy")
    cells2 = P(("case", "gx"), "gy")
    return jax.shard_map(
        shards,
        mesh=mesh,
        in_specs=(cells3,) * 3 + (cells2,) * 3 + (P(),) * 6,
        out_specs=(cells3, cells2, P("case"), P("case"), P("case"), P("case"), P("case")),
        check_vma=False,
    )
```

time: 64.2 us -> 56 us (0.87)
  blocking collectives: 0 us -> 25.6 us
  waiting for transfers between devices: 12.5 us -> 1.84 us
  starting transfers between devices: 17.9 us -> 8.81 us
  local copies, waits for them, and re-layouts: 8.77 us -> 0.01 us
  Pallas kernels: 23.4 us -> 18.7 us
    all_gather x0 -> x1, blocking collectives: none -> 25.6 us  [sum_parts(): return lax.all_gather(packed, ('gx', 'gy'))]
    ppermute x4 -> x0, starting transfers between devices: 8.99 us -> none  [sum_parts(): lax.ppermute(packed, axis, [(i, i ^ step) for i in range(count)])]
    unnamed x34 -> x2, local copies, waits for them, and re-layouts: 8.77 us -> 0.01 us
    ppermute x4 -> x0, waiting for transfers between devices: 7.5 us -> none  [sum_parts(): lax.ppermute(packed, axis, [(i, i ^ step) for i in range(count)])]
    pallas_call x4 -> x7, Pallas kernels: 22.6 us -> 17.9 us  [the longest x6 14.1 us: on_chip(): pl.pallas_call(kernel, in_specs=[here] * len(operands) + [there] * len(fa...]
    ppermute x2, waiting for transfers between devices: 4.3 us -> 1.83 us  [shift_pair(): lax.ppermute(low_edge, axis, down)]
    ppermute x2, waiting for transfers between devices: 0.74 us -> 0.01 us  [shift_pair(): lax.ppermute(high_edge, axis, up)]
  transfers between devices with their start and end apart: 8 -> 4, of which waited for: 6 -> 2; matrix products, arithmetic and copies ran while one was open for 0% -> 0% of each run, Pallas kernels for 16% -> 12%
where the time goes in v1:
time: 56 us; the launch traced here: 55.7 us
  blocking collectives  25.6 us (46%)
  Pallas kernels  18.7 us (33%)
  starting transfers between devices  8.81 us (16%)
  waiting for transfers between devices  1.84 us (3%)
  between operations  0.75 us (1%)
    all_gather x1, blocking collectives, sum_parts(): return lax.all_gather(packed, ('gx', 'gy'))  25.6 us
    pallas_call x6, Pallas kernels, on_chip(): pl.pallas_call(kernel, in_specs=[here] * len(operands) + [there] * len(fa...  14.1 us
    ppermute x2, starting transfers between devices, shift_pair(): lax.ppermute(high_edge, axis, up)  6.22 us
    pallas_call x1, Pallas kernels, sweeps(): pl.pallas_call(sweep_kernel, in_specs=[near] * len(operands) + [pl.BlockS...  3.79 us
    ppermute x2, starting transfers between devices, shift_pair(): lax.ppermute(low_edge, axis, down)  2.58 us
    ppermute x2, waiting for transfers between devices, shift_pair(): lax.ppermute(low_edge, axis, down)  1.83 us
  transfers between devices with their start and end apart: 4, of which 2 were waited for; matrix products, arithmetic and copies ran while one was open for 0% of the time, Pallas kernels for 12%

profile of v1, /device:TPU:0, one launch (start us, length us, event | category | flops | bytes accessed | tf_op | source)
XLA Modules:
  0.0 55.7 jit_solution(4363658187116927585)
XLA Ops:
  0.6 2.0 %load.1 = (bf16[5,64,256]{2,1,0:T(8,128)(2,1)S(1)}, bf16[4,64,256]{2,1,0:T(8,128)(2,1)S(1)}, f32[64,256]{1,0:T(8,128)}, s32[64,256]{1,0:T(8,128)}, f32[64,256]{1...) custom-call(bf16[5,64,256]{2,1,0:T(8,128)(2,1)} %refs_0_.1, ...), custom_call_target="tpu_custom_call" | custom-call | tf_op jit(solution)/shard_map/load/pallas_call | solution.py:33
  2.6 0.0 copy-start
  2.6 4.9 %collective-permute-start = (f32[10,8,256]{2,1,0:T(8,128)S(1)}, f32[10,8,256]{2,1,0:T(8,128)S(1)}, u32[]{:S(2)}, u32[]{:S(2)}) collective-permute-start(f32[10,8,256]{2,1,0:T(8,128)S(1)} %get-tuple-element.47), channel_id=1, source_target_pairs={{0,4},{4,8},{8,12},{1,5},{5,9},{9,13},{2,6},{6,10},{10,14},{3,7},{... | collective-permute-start | bytes 245768 | tf_op jit(solution)/shard_map/ppermute | solution.py:481
  7.6 1.3 %collective-permute-start.1 = (f32[10,8,256]{2,1,0:T(8,128)S(1)}, f32[10,8,256]{2,1,0:T(8,128)S(1)}, u32[]{:S(2)}, u32[]{:S(2)}) collective-permute-start(f32[10,8,256]{2,1,0:T(8,128)S(1)} %get-tuple-element.48), channel_id=1, source_target_pairs={{4,0},{8,4},{12,8},{5,1},{9,5},{13,9},{6,2},{10,6},{14,10},{7,3},{... | collective-permute-start | bytes 245768 | tf_op jit(solution)/shard_map/ppermute | solution.py:481
  8.9 0.2 weights.1
  9.1 3.2 %network_forward.2 = (bf16[32,208,256]{2,1,0:T(8,128)(2,1)S(1)}, f32[32,256]{1,0:T(8,128)S(1)}) custom-call(bf16[10,64,256]{2,1,0:T(8,128)(2,1)S(1)} %get-tuple-element.49.feat, bf16[1280,256]{1,0:T(8,128)(2,1)S(1)} %get-tuple-element.55.w1, bf16[64,64]{1,0:T(8,128)(2,1)S(1)} %get-tuple-element.56.w2, bf16[64,64]{1,0:T(8,128)(2,1)S(1)} %get-tuple-element.57.w3, ...), custom_call_target="tpu_custom_call" | custom-call | flops 144703488 | bytes 3571712 | tf_op jit(solution)/shard_map/network_forward/pallas_call | solution.py:33
  12.4 0.0 collective-permute-done.north
  12.4 1.5 %collective-permute-done.1.south = f32[10,8,256]{2,1,0:T(8,128)S(1)} collective-permute-done((f32[10,8,256]{2,1,0:T(8,128)S(1)}, f32[10,8,256]{2,1,0:T(8,128)S(1)}, u32[]{:S(2)}, u32[]{:S(2)}) %collective-permute-start.1) | collective-permute-done | bytes 81952 | tf_op jit(solution)/shard_map/ppermute | solution.py:481
  13.9 0.2 col_slabs.1
  14.1 1.3 %collective-permute-start.2 = (f32[80,128]{1,0:T(8,128)S(1)}, f32[80,128]{1,0:T(8,128)S(1)}, u32[]{:S(2)}, u32[]{:S(2)}) collective-permute-start(f32[80,128]{1,0:T(8,128)S(1)} %get-tuple-element.64), channel_id=1, source_target_pairs={{0,1},{1,2},{2,3},{4,5},{5,6},{6,7},{8,9},{9,10},{10,11},{12,13},{... | collective-permute-start | bytes 122888 | tf_op jit(solution)/shard_map/ppermute | solution.py:481
  15.4 1.3 %collective-permute-start.3 = (f32[80,128]{1,0:T(8,128)S(1)}, f32[80,128]{1,0:T(8,128)S(1)}, u32[]{:S(2)}, u32[]{:S(2)}) collective-permute-start(f32[80,128]{1,0:T(8,128)S(1)} %get-tuple-element.65), channel_id=1, source_target_pairs={{1,0},{2,1},{3,2},{5,4},{6,5},{7,6},{9,8},{10,9},{11,10},{13,12},{... | collective-permute-start | bytes 122888 | tf_op jit(solution)/shard_map/ppermute | solution.py:481
  16.7 3.2 %network_forward.3 = (bf16[32,208,256]{2,1,0:T(8,128)(2,1)S(1)}, f32[32,256]{1,0:T(8,128)S(1)}) custom-call(bf16[10,64,256]{2,1,0:T(8,128)(2,1)S(1)} %get-tuple-element.49.feat, bf16[1280,256]{1,0:T(8,128)(2,1)S(1)} %get-tuple-element.55.w1, bf16[64,64]{1,0:T(8,128)(2,1)S(1)} %get-tuple-element.56.w2, bf16[64,64]{1,0:T(8,128)(2,1)S(1)} %get-tuple-element.57.w3, ...), custom_call_target="tpu_custom_call" | custom-call | flops 144703488 | bytes 3571712 | tf_op jit(solution)/shard_map/network_forward/pallas_call | solution.py:33
  20.0 0.0 collective-permute-done.2.west
  20.0 0.3 collective-permute-done.3.east
  20.3 0.0 copy-done
  20.3 3.8 %sweeps.1 = (f32[5,64,256]{2,1,0:T(8,128)S(1)}, f32[64,256]{1,0:T(8,128)S(1)}, f32[64,256]{1,0:T(8,128)S(1)}) custom-call(bf16[5,64,256]{2,1,0:T(8,128)(2,1)S(1)} %get-tuple-element.43.src, bf16[4,64,256]{2,1,0:T(8,128)(2,1)S(1)} %get-tuple-element.44.cpl, f32[64,256]{1,0:T(8,128)S(1)} %get-tuple-element.45.inv.inverse, ...), custom_call_target="tpu_custom_call" | custom-call | tf_op jit(solution)/shard_map/sweeps/pallas_call | solution.py:331
  24.1 5.2 %backward.1 = (f32[72,128]{1,0:T(8,128)S(1)}, f32[5,64,256]{2,1,0:T(8,128)}, f32[64,256]{1,0:T(8,128)}) custom-call(f32[5,64,256]{2,1,0:T(8,128)S(1)} %get-tuple-element.66.adj, f32[64,256]{1,0:T(8,128)S(1)} %get-tuple-element.67.beta, f32[64,256]{1,0:T(8,128)S(1)} %get-tuple-element.68.sens, bf16[64,64]{1,0:T(8,128)(2,1)S(1)} %get-tuple-element.51.wmid, ...), custom_call_target="tpu_custom_call" | custom-call | tf_op jit(solution)/shard_map/backward/pallas_call | solution.py:33
  29.3 25.6 %all-gather = f32[1152,128]{1,0:T(8,128)S(1)} all-gather(f32[72,128]{1,0:T(8,128)S(1)} %get-tuple-element.73), channel_id=2, replica_groups=mesh['case'=2,'gx'=4,'gy'=4] {'gx','gy'}, dimensions={0}, use_global_device_ids=true | all-gather | bytes 626688 | tf_op jit(solution)/shard_map/all_gather | solution.py:474
  54.9 0.8 %clip.1 = (f32[10,64]{1,0:T(8,128)}, f32[64,64]{1,0:T(8,128)}, f32[64,64]{1,0:T(8,128)}, f32[1,64]{1,0:T(1,128)}, f32[3,64]{1,0:T(4,128)}) custom-call(f32[16,72,128]{2,1,0:T(8,128)S(1)} %bitcast.3), custom_call_target="tpu_custom_call" | custom-call | tf_op jit(solution)/shard_map/clip/pallas_call | solution.py:462
Async XLA Ops:
  2.6 17.6 %copy-start = (f32[5,5]{1,0:T(8,128)S(1)}, f32[5,5]{1,0:T(8,128)}, u32[]{:S(2)}) copy-start(f32[5,5]{1,0:T(8,128)} %mix.1) | copy-start | bytes 304
  2.6 9.7 %collective-permute-start = (f32[10,8,256]{2,1,0:T(8,128)S(1)}, f32[10,8,256]{2,1,0:T(8,128)S(1)}, u32[]{:S(2)}, u32[]{:S(2)}) collective-permute-start(f32[10,8,256]{2,1,0:T(8,128)S(1)} %get-tuple-element.47), channel_id=1, source_target_pairs={{0,4},{4,8},{8,12},{1,5},{5,9},{9,13},{2,6},{6,10},{10,14},{3,7},{... | collective-permute-start | bytes 245768 | tf_op jit(solution)/shard_map/ppermute | solution.py:481
  7.6 6.3 %collective-permute-start.1 = (f32[10,8,256]{2,1,0:T(8,128)S(1)}, f32[10,8,256]{2,1,0:T(8,128)S(1)}, u32[]{:S(2)}, u32[]{:S(2)}) collective-permute-start(f32[10,8,256]{2,1,0:T(8,128)S(1)} %get-tuple-element.48), channel_id=1, source_target_pairs={{4,0},{8,4},{12,8},{5,1},{9,5},{13,9},{6,2},{10,6},{14,10},{7,3},{... | collective-permute-start | bytes 245768 | tf_op jit(solution)/shard_map/ppermute | solution.py:481
  14.1 5.8 %collective-permute-start.2 = (f32[80,128]{1,0:T(8,128)S(1)}, f32[80,128]{1,0:T(8,128)S(1)}, u32[]{:S(2)}, u32[]{:S(2)}) collective-permute-start(f32[80,128]{1,0:T(8,128)S(1)} %get-tuple-element.64), channel_id=1, source_target_pairs={{0,1},{1,2},{2,3},{4,5},{5,6},{6,7},{8,9},{9,10},{10,11},{12,13},{... | collective-permute-start | bytes 122888 | tf_op jit(solution)/shard_map/ppermute | solution.py:481
  15.4 4.8 %collective-permute-start.3 = (f32[80,128]{1,0:T(8,128)S(1)}, f32[80,128]{1,0:T(8,128)S(1)}, u32[]{:S(2)}, u32[]{:S(2)}) collective-permute-start(f32[80,128]{1,0:T(8,128)S(1)} %get-tuple-element.65), channel_id=1, source_target_pairs={{1,0},{2,1},{3,2},{5,4},{6,5},{7,6},{9,8},{10,9},{11,10},{13,12},{... | collective-permute-start | bytes 122888 | tf_op jit(solution)/shard_map/ppermute | solution.py:481

commit v2 on v1

--- a/solution.py
+++ b/solution.py
@@ -54,9 +54,13 @@
     return 1.0 / total
 
 
+def is_odd(axis):
+    return lax.axis_index(axis) % 2 == 1
+
+
 def load_kernel(count, *refs):
     far, near = refs[:count], refs[count : 2 * count]
-    inv, top, bottom, sems = refs[2 * count :]
+    inv, first, second, sems = refs[2 * count :]
     copies = [pltpu.make_async_copy(far[k], near[k], sems.at[k]) for k in range(count)]
     for copy in copies:
         copy.start()
@@ -66,14 +70,15 @@
     nv, rows, _ = src.shape
     nc = cpl.shape[0]
     inv[...] = inverse_diag(dia[...], bc[...])
-    for v in range(nv):
-        top[v] = src[v, 0:16].astype(F32)[:EDGE]
-        bottom[v] = src[v, rows - 16 :].astype(F32)[16 - EDGE :]
-    for d in range(nc):
-        top[nv + d] = cpl[d, 0:16].astype(F32)[:EDGE]
-        bottom[nv + d] = cpl[d, rows - 16 :].astype(F32)[16 - EDGE :]
-    top[nv + nc] = inv[0:EDGE]
-    bottom[nv + nc] = inv[rows - EDGE :]
+    odd = is_odd("gx")
+    for f in range(nv + nc + 1):
+        if f < nv + nc:
+            ref, k = (src, f) if f < nv else (cpl, f - nv)
+            top, bottom = ref[k, 0:16].astype(F32)[:EDGE], ref[k, rows - 16 :].astype(F32)[16 - EDGE :]
+        else:
+            top, bottom = inv[0:EDGE], inv[rows - EDGE :]
+        first[f] = jnp.where(odd, top, bottom)
+        second[f] = jnp.where(odd, bottom, top)
     for copy in copies[4:]:
         copy.wait()
 
@@ -92,13 +97,18 @@
     )
 
 
-def cols_kernel(src, cpl, inv, north, south, west_ref, east_ref):
+def ordered(axis, first, second):
+    odd = is_odd(axis)
+    return jnp.where(odd, first, second), jnp.where(odd, second, first)
+
+
+def cols_kernel(src, cpl, inv, row_first, row_second, col_first, col_second):
     nv, rows, cols = src.shape
     nc = cpl.shape[0]
     lane = lax.broadcasted_iota(jnp.int32, (rows, LANE), 1) // EDGE
     lane_h = lane[:EDGE]
-    sides = ((west_ref, slice(0, LANE), 0), (east_ref, slice(cols - LANE, cols), EDGE))
-    for out, window, extra in sides:
+    slabs = []
+    for window, extra in ((slice(0, LANE), 0), (slice(cols - LANE, cols), EDGE)):
         mid = jnp.zeros((rows, LANE), F32)
         up = jnp.zeros((EDGE, LANE), F32)
         down = jnp.zeros((EDGE, LANE), F32)
@@ -111,16 +121,18 @@
                 x = inv[:, window]
             shift = (EDGE * f + extra) % LANE
             mid = jnp.where(lane == f, pltpu.roll(x, shift, 1), mid)
-            up = jnp.where(lane_h == f, pltpu.roll(north[f, :, window], shift, 1), up)
-            down = jnp.where(lane_h == f, pltpu.roll(south[f, :, window], shift, 1), down)
-        out[0:EDGE] = up
-        out[EDGE : EDGE + rows] = mid
-        out[EDGE + rows :] = down
-
-
-def col_slabs(source, coupling, inv, north, south):
+            north, south = ordered("gx", row_first[f, :, window], row_second[f, :, window])
+            up = jnp.where(lane_h == f, pltpu.roll(north, shift, 1), up)
+            down = jnp.where(lane_h == f, pltpu.roll(south, shift, 1), down)
+        slabs.append(jnp.concatenate([up, mid, down], axis=0))
+    odd = is_odd("gy")
+    col_first[...] = jnp.where(odd, slabs[0], slabs[1])
+    col_second[...] = jnp.where(odd, slabs[1], slabs[0])
+
+
+def col_slabs(source, coupling, inv, row_halos):
     slab = ((source.shape[1] + 2 * EDGE, LANE), F32)
-    return on_chip(cols_kernel, [source, coupling, inv, north, south], [slab, slab], name="col_slabs")
+    return on_chip(cols_kernel, [source, coupling, inv, *row_halos], [slab, slab], name="col_slabs")
 
 
 def column_of(row):
@@ -256,7 +268,7 @@
 
 
 def sweep_kernel(
-    src, cpl, inverse, prod, beta_a, beta_b, north, south, west, east, mix,
+    src, cpl, inverse, prod, beta_a, beta_b, row_first, row_second, col_first, col_second, mix,
     adj_out, sens, beta,
     raw, src_x, cpl_x, adj_a, adj_b,
 ):
@@ -268,6 +280,7 @@
     inner = slice(EDGE, EDGE + rows)
     lane = lax.broadcasted_iota(jnp.int32, (tall, LANE), 1)
     from_east, from_west = lane < EDGE, lane >= LANE - EDGE
+    west, east = ordered("gy", col_first[...], col_second[...])
     for f in range(nv + nc + 1):
         if f < nv:
             raw[f, inner, 0:cols] = src[f].astype(F32)
@@ -275,10 +288,11 @@
             raw[f, inner, 0:cols] = cpl[f - nv].astype(F32)
         else:
             raw[f, inner, 0:cols] = inverse[...]
-        raw[f, 0:EDGE, 0:cols] = north[f]
-        raw[f, EDGE + rows :, 0:cols] = south[f]
-        e = pltpu.roll(east[...], (LANE - EDGE * f) % LANE, 1)
-        w = pltpu.roll(west[...], (LANE - EDGE - EDGE * f) % LANE, 1)
+        north, south = ordered("gx", row_first[f], row_second[f])
+        raw[f, 0:EDGE, 0:cols] = north
+        raw[f, EDGE + rows :, 0:cols] = south
+        e = pltpu.roll(east, (LANE - EDGE * f) % LANE, 1)
+        w = pltpu.roll(west, (LANE - EDGE - EDGE * f) % LANE, 1)
         raw[f, :, cols:] = jnp.where(from_east, e, jnp.where(from_west, w, 0.0))
 
     moves = (shifts.above, shifts.below, shifts.left, shifts.right)
@@ -441,11 +455,9 @@
     )
 
 
-def clip_kernel(parts, gin, gmid, gtop, gout, gbias):
+def clip_kernel(summed, gin, gmid, gtop, gout, gbias):
     hidden = gmid.shape[0]
-    total = parts[0]
-    for k in range(1, parts.shape[0]):
-        total = total + parts[k]
+    total = summed[0 : hidden + SUB]
     squares = jnp.sum(jnp.sum(total * total, axis=0, keepdims=True), axis=1, keepdims=True)
     total = total * (CLIP_NORM / jnp.maximum(jnp.sqrt(squares), CLIP_NORM))
     gmid[...] = total[:hidden, :hidden]
@@ -457,28 +469,37 @@
     gbias[...] = high[3:6]
 
 
-def clip_all(parts, num_feat, hidden):
+def clip_all(summed, num_feat, hidden):
     shapes = [(num_feat, hidden), (hidden, hidden), (hidden, hidden), (1, hidden), (3, hidden)]
     return pl.pallas_call(
         clip_kernel,
         grid=(1,),
-        in_specs=[whole(parts.shape)],
+        in_specs=[whole(summed.shape)],
         out_specs=[whole(s) for s in shapes],
         out_shape=[jax.ShapeDtypeStruct(s, F32) for s in shapes],
         compiler_params=params(),
         name="clip",
-    )(parts)
-
-
-def sum_parts(packed):
-    return lax.all_gather(packed, ("gx", "gy"))
-
-
-def shift_pair(low_edge, high_edge, axis):
+    )(summed)
+
+
+def sum_over_case(packed):
+    axes = ("gx", "gy")
+    count = lax.axis_size(axes)
+    piece = -(-packed.shape[0] // (count * SUB)) * SUB
+    padded = jnp.pad(packed, ((0, count * piece - packed.shape[0]), (0, 0))).reshape(count, piece, LANE)
+    mine = jnp.sum(lax.all_to_all(padded, axes, 0, 0), axis=0, keepdims=True)
+    pieces = lax.all_to_all(jnp.broadcast_to(mine, padded.shape), axes, 0, 0)
+    return pieces.reshape(count * piece, LANE)
+
+
+def swaps(first, second, axis):
     count = lax.axis_size(axis)
-    up = [(i, i + 1) for i in range(count - 1)]
-    down = [(b, a) for a, b in up]
-    return lax.ppermute(high_edge, axis, up), lax.ppermute(low_edge, axis, down)
+
+    def pairs(start):
+        low = range(start, count - 1, 2)
+        return [(i, i + 1) for i in low] + [(i + 1, i) for i in low]
+
+    return lax.ppermute(first, axis, pairs(0)), lax.ppermute(second, axis, pairs(1))
 
 
 def shards(
@@ -492,20 +513,19 @@
         weight_in, weight_mid, weight_top, weight_out.reshape(1, hidden), biases,
     ])
     source, coupling, _, _, production, features, weight_in, weight_mid, weight_top, wout, biases = loaded[:11]
-    inverse, top, bottom = loaded[11:]
-    north, south = shift_pair(top, bottom, "gx")
+    inverse, *row_slabs = loaded[11:]
+    row_halos = swaps(*row_slabs, "gx")
     prepared = prepare(weight_in, weight_mid, weight_top, wout, biases)
     half = rows // 32 * 16
     acts_a, beta_a = forward(features, prepared, 0, half)
-    north, south, beta_a = lax.optimization_barrier((north, south, beta_a))
-    first, last = col_slabs(source, coupling, inverse, north, south)
-    west, east = shift_pair(first, last, "gy")
+    *row_halos, beta_a = lax.optimization_barrier((*row_halos, beta_a))
+    col_halos = swaps(*col_slabs(source, coupling, inverse, row_halos), "gy")
     acts_b, beta_b = forward(features, prepared, half, rows - half)
     adj, sens, beta = sweeps(
-        source, coupling, inverse, production, (beta_a, beta_b), (north, south, west, east), mixing
+        source, coupling, inverse, production, (beta_a, beta_b), (*row_halos, *col_halos), mixing
     )
     packed, adjoint, beta = backward(adj, beta, sens, weight_mid, weight_top, prepared[3], (acts_a, acts_b))
-    grad_in, grad_mid, grad_top, grad_out, grad_bias = clip_all(sum_parts(packed), num_feat, hidden)
+    grad_in, grad_mid, grad_top, grad_out, grad_bias = clip_all(sum_over_case(packed), num_feat, hidden)
     return (adjoint, beta, grad_in, grad_mid, grad_top, grad_out.reshape(hidden), grad_bias)
 
 

time: 56 us -> 49.4 us (0.88)
  starting transfers between devices: 8.81 us -> 4.48 us
  waiting for transfers between devices: 1.84 us -> 0.01 us
    all_gather x1 -> x0, blocking collectives: 25.6 us -> none  [sum_parts(): return lax.all_gather(packed, ('gx', 'gy'))]
    all_to_all x0 -> x2, blocking collectives: none -> 25.1 us  [the longest x1 15.6 us: sum_over_case(): mine = jnp.sum(lax.all_to_all(padded, axes, 0, 0), axis=0, keepdims=True)]
    ppermute x4, starting transfers between devices: 8.81 us -> 4.48 us  [the longest x2 3.16 us: swaps(): lax.ppermute(first, axis, pairs(0))]
    ppermute x4, waiting for transfers between devices: 1.84 us -> 0.01 us  [the longest x2 0.01 us: swaps(): lax.ppermute(first, axis, pairs(0))]
  transfers between devices with their start and end apart: 4 -> 4, of which waited for: 2 -> 0; matrix products, arithmetic and copies ran while one was open for 0% -> 0% of each run, Pallas kernels for 12% -> 14%
where the time goes in v2:
time: 49.4 us; the launch traced here: 49.1 us
  blocking collectives  25.1 us (51%)
  Pallas kernels  18.7 us (38%)
  starting transfers between devices  4.48 us (9%)
  between operations  0.77 us (2%)
    all_to_all x1, blocking collectives, sum_over_case(): mine = jnp.sum(lax.all_to_all(padded, axes, 0, 0), axis=0, keepdims=True)  15.6 us
    pallas_call x6, Pallas kernels, on_chip(): pl.pallas_call(kernel, in_specs=[here] * len(operands) + [there] * len(fa...  14.1 us
    all_to_all x1, blocking collectives, sum_over_case(): pieces = lax.all_to_all(jnp.broadcast_to(mine, padded.shape), axes, 0, 0)  9.48 us
    pallas_call x1, Pallas kernels, sweeps(): pl.pallas_call(sweep_kernel, in_specs=[near] * len(operands) + [pl.BlockS...  3.82 us
    ppermute x2, starting transfers between devices, swaps(): lax.ppermute(first, axis, pairs(0))  3.16 us
    ppermute x2, starting transfers between devices, swaps(): lax.ppermute(second, axis, pairs(1))  1.32 us
  transfers between devices with their start and end apart: 4, of which 0 were waited for; matrix products, arithmetic and copies ran while one was open for 0% of the time, Pallas kernels for 14%

profile of v2, /device:TPU:0, one launch (start us, length us, event | category | flops | bytes accessed | tf_op | source)
XLA Modules:
  0.0 49.1 jit_solution(10049369818871959959)
XLA Ops:
  0.6 2.0 %load.1 = (bf16[5,64,256]{2,1,0:T(8,128)(2,1)S(1)}, bf16[4,64,256]{2,1,0:T(8,128)(2,1)S(1)}, f32[64,256]{1,0:T(8,128)}, s32[64,256]{1,0:T(8,128)}, f32[64,256]{1...) custom-call(bf16[5,64,256]{2,1,0:T(8,128)(2,1)} %refs_0_.1, ...), custom_call_target="tpu_custom_call" | custom-call | tf_op jit(solution)/shard_map/load/pallas_call | solution.py:33
  2.6 0.0 copy-start
  2.6 3.1 %collective-permute-start = (f32[10,8,256]{2,1,0:T(8,128)S(1)}, f32[10,8,256]{2,1,0:T(8,128)S(1)}, u32[]{:S(2)}, u32[]{:S(2)}) collective-permute-start(f32[10,8,256]{2,1,0:T(8,128)S(1)} %get-tuple-element.47), channel_id=1, source_target_pairs={{0,4},{8,12},{4,0},{12,8},{1,5},{9,13},{5,1},{13,9},{2,6},{10,14},... | collective-permute-start | bytes 245768 | tf_op jit(solution)/shard_map/ppermute | solution.py:502
  5.7 0.7 %collective-permute-start.1 = (f32[10,8,256]{2,1,0:T(8,128)S(1)}, f32[10,8,256]{2,1,0:T(8,128)S(1)}, u32[]{:S(2)}, u32[]{:S(2)}) collective-permute-start(f32[10,8,256]{2,1,0:T(8,128)S(1)} %get-tuple-element.48), channel_id=1, source_target_pairs={{4,8},{8,4},{5,9},{9,5},{6,10},{10,6},{7,11},{11,7},{20,24},{24,20... | collective-permute-start | bytes 245768 | tf_op jit(solution)/shard_map/ppermute | solution.py:502
  6.4 0.2 weights.1
  6.6 3.2 %network_forward.2 = (bf16[32,208,256]{2,1,0:T(8,128)(2,1)S(1)}, f32[32,256]{1,0:T(8,128)S(1)}) custom-call(bf16[10,64,256]{2,1,0:T(8,128)(2,1)S(1)} %get-tuple-element.49.feat, bf16[1280,256]{1,0:T(8,128)(2,1)S(1)} %get-tuple-element.55.w1, bf16[64,64]{1,0:T(8,128)(2,1)S(1)} %get-tuple-element.56.w2, bf16[64,64]{1,0:T(8,128)(2,1)S(1)} %get-tuple-element.57.w3, ...), custom_call_target="tpu_custom_call" | custom-call | flops 144703488 | bytes 3571712 | tf_op jit(solution)/shard_map/network_forward/pallas_call | solution.py:33
  9.9 0.0 collective-permute-done.row_first
  9.9 0.0 collective-permute-done.1.row_second
  9.9 0.2 col_slabs.1
  10.1 0.1 collective-permute-start.2
  10.2 0.7 %collective-permute-start.3 = (f32[80,128]{1,0:T(8,128)S(1)}, f32[80,128]{1,0:T(8,128)S(1)}, u32[]{:S(2)}, u32[]{:S(2)}) collective-permute-start(f32[80,128]{1,0:T(8,128)S(1)} %get-tuple-element.65), channel_id=1, source_target_pairs={{1,2},{2,1},{5,6},{6,5},{9,10},{10,9},{13,14},{14,13},{17,18},{18,... | collective-permute-start | bytes 122888 | tf_op jit(solution)/shard_map/ppermute | solution.py:502
  10.9 3.2 %network_forward.3 = (bf16[32,208,256]{2,1,0:T(8,128)(2,1)S(1)}, f32[32,256]{1,0:T(8,128)S(1)}) custom-call(bf16[10,64,256]{2,1,0:T(8,128)(2,1)S(1)} %get-tuple-element.49.feat, bf16[1280,256]{1,0:T(8,128)(2,1)S(1)} %get-tuple-element.55.w1, bf16[64,64]{1,0:T(8,128)(2,1)S(1)} %get-tuple-element.56.w2, bf16[64,64]{1,0:T(8,128)(2,1)S(1)} %get-tuple-element.57.w3, ...), custom_call_target="tpu_custom_call" | custom-call | flops 144703488 | bytes 3571712 | tf_op jit(solution)/shard_map/network_forward/pallas_call | solution.py:33
  14.1 0.0 collective-permute-done.2.col_first
  14.1 0.0 collective-permute-done.3.col_second
  14.1 0.0 copy-done
  14.1 3.8 %sweeps.1 = (f32[5,64,256]{2,1,0:T(8,128)S(1)}, f32[64,256]{1,0:T(8,128)S(1)}, f32[64,256]{1,0:T(8,128)S(1)}) custom-call(bf16[5,64,256]{2,1,0:T(8,128)(2,1)S(1)} %get-tuple-element.43.src, bf16[4,64,256]{2,1,0:T(8,128)(2,1)S(1)} %get-tuple-element.44.cpl, f32[64,256]{1,0:T(8,128)S(1)} %get-tuple-element.45.inv.inverse, ...), custom_call_target="tpu_custom_call" | custom-call | tf_op jit(solution)/shard_map/sweeps/pallas_call | solution.py:345
  17.9 5.2 %backward.1 = (f32[72,128]{1,0:T(8,128)S(1)}, f32[5,64,256]{2,1,0:T(8,128)}, f32[64,256]{1,0:T(8,128)}) custom-call(f32[5,64,256]{2,1,0:T(8,128)S(1)} %get-tuple-element.66.adj, f32[64,256]{1,0:T(8,128)S(1)} %get-tuple-element.67.beta, f32[64,256]{1,0:T(8,128)S(1)} %get-tuple-element.68.sens, bf16[64,64]{1,0:T(8,128)(2,1)S(1)} %get-tuple-element.51.wmid, ...), custom_call_target="tpu_custom_call" | custom-call | tf_op jit(solution)/shard_map/backward/pallas_call | solution.py:33
  23.2 15.6 %all_to_all.10 = f32[16,8,128]{2,1,0:T(8,128)S(1)} all-to-all(f32[16,8,128]{2,1,0:T(8,128)S(1)} %pad_bitcast_fusion), channel_id=1, replica_groups=mesh['case'=2,'gx'=4,'gy'=4] {'gx','gy'}, dimensions={0} | all-to-all | bytes 131072 | tf_op jit(solution)/shard_map/all_to_all | solution.py:490
  38.8 9.5 %all_to_all.11 = f32[16,8,128]{2,1,0:T(8,128)S(1)} all-to-all(f32[16,8,128]{2,1,0:T(8,128)S(1)} %broadcast_in_dim.2), channel_id=1, replica_groups=mesh['case'=2,'gx'=4,'gy'=4] {'gx','gy'}, dimensions={0} | all-to-all | bytes 131072 | tf_op jit(solution)/shard_map/all_to_all | solution.py:491
  48.3 0.8 %clip.1 = (f32[10,64]{1,0:T(8,128)}, f32[64,64]{1,0:T(8,128)}, f32[64,64]{1,0:T(8,128)}, f32[1,64]{1,0:T(1,128)}, f32[3,64]{1,0:T(4,128)}) custom-call(f32[128,128]{1,0:T(8,128)S(1)} %bitcast.5), custom_call_target="tpu_custom_call" | custom-call | tf_op jit(solution)/shard_map/clip/pallas_call | solution.py:474
  (3 shorter events, 0.0 us)
Async XLA Ops:
  2.6 11.5 %copy-start = (f32[5,5]{1,0:T(8,128)S(1)}, f32[5,5]{1,0:T(8,128)}, u32[]{:S(2)}) copy-start(f32[5,5]{1,0:T(8,128)} %mix.1) | copy-start | bytes 304
  2.6 7.2 %collective-permute-start = (f32[10,8,256]{2,1,0:T(8,128)S(1)}, f32[10,8,256]{2,1,0:T(8,128)S(1)}, u32[]{:S(2)}, u32[]{:S(2)}) collective-permute-start(f32[10,8,256]{2,1,0:T(8,128)S(1)} %get-tuple-element.47), channel_id=1, source_target_pairs={{0,4},{8,12},{4,0},{12,8},{1,5},{9,13},{5,1},{13,9},{2,6},{10,14},... | collective-permute-start | bytes 245768 | tf_op jit(solution)/shard_map/ppermute | solution.py:502
  5.7 4.2 %collective-permute-start.1 = (f32[10,8,256]{2,1,0:T(8,128)S(1)}, f32[10,8,256]{2,1,0:T(8,128)S(1)}, u32[]{:S(2)}, u32[]{:S(2)}) collective-permute-start(f32[10,8,256]{2,1,0:T(8,128)S(1)} %get-tuple-element.48), channel_id=1, source_target_pairs={{4,8},{8,4},{5,9},{9,5},{6,10},{10,6},{7,11},{11,7},{20,24},{24,20... | collective-permute-start | bytes 245768 | tf_op jit(solution)/shard_map/ppermute | solution.py:502
  10.1 4.0 %collective-permute-start.2 = (f32[80,128]{1,0:T(8,128)S(1)}, f32[80,128]{1,0:T(8,128)S(1)}, u32[]{:S(2)}, u32[]{:S(2)}) collective-permute-start(f32[80,128]{1,0:T(8,128)S(1)} %get-tuple-element.64), channel_id=1, source_target_pairs={{0,1},{2,3},{1,0},{3,2},{4,5},{6,7},{5,4},{7,6},{8,9},{10,11},{9,8... | collective-permute-start | bytes 122888 | tf_op jit(solution)/shard_map/ppermute | solution.py:502
  10.2 3.9 %collective-permute-start.3 = (f32[80,128]{1,0:T(8,128)S(1)}, f32[80,128]{1,0:T(8,128)S(1)}, u32[]{:S(2)}, u32[]{:S(2)}) collective-permute-start(f32[80,128]{1,0:T(8,128)S(1)} %get-tuple-element.65), channel_id=1, source_target_pairs={{1,2},{2,1},{5,6},{6,5},{9,10},{10,9},{13,14},{14,13},{17,18},{18,... | collective-permute-start | bytes 122888 | tf_op jit(solution)/shard_map/ppermute | solution.py:502

commit v3 on v2

--- a/solution.py
+++ b/solution.py
@@ -195,15 +195,14 @@
         x1[0 : nf * blk] = feat[:, pl.ds(first_row + start, blk), :].reshape(nf * blk, cols)
         b1, b2, b3, wo = (across(cst[k], cols) for k in range(4))
         lines = []
+        first = jnp.dot(w1[...], x1[...], preferred_element_type=F32)
         for g in range(blk // per):
-            lo = g * per * step_rows
-            first = jnp.dot(w1[lo : lo + per * step_rows], x1[...], preferred_element_type=F32)
             ones = []
-            for q in range(per):
+            for q in range(g * per, (g + 1) * per):
                 part = first[q * step_rows : (q + 1) * step_rows]
                 one = jnp.tanh(part[:hidden] + b1).astype(BF16)
-                acts[start + (g * per + q), 0:hidden] = one
-                acts[start + (g * per + q), 3 * hidden :] = part[hidden:].astype(BF16)
+                acts[start + q, 0:hidden] = one
+                acts[start + q, 2 * hidden : 2 * hidden + 16] = part[hidden:].astype(BF16)
                 ones.append(one)
             second = jnp.dot(w2[...], jnp.concatenate(ones, axis=1), preferred_element_type=F32)
             twos = []
@@ -214,7 +213,7 @@
             third = jnp.dot(w3[...], jnp.concatenate(twos, axis=1), preferred_element_type=F32)
             for q in range(per):
                 three = jnp.tanh(third[:, q * cols : (q + 1) * cols] + b3).astype(BF16)
-                acts[start + (g * per + q), 2 * hidden : 3 * hidden] = three
+                acts[start + (g * per + q), 2 * hidden + 16 :] = three
                 lines.append(1.0 + jnp.sum(three.astype(F32) * wo, axis=0, keepdims=True))
         beta[pl.ds(start, blk), :] = jnp.concatenate(lines, axis=0)
 
@@ -360,9 +359,9 @@
 
 
 def backward_kernel(
-    adj, beta, sens, wmid, wtop, cst, acts_a, acts_b,
+    num_feat, adj, beta, sens, wmid, wtop, cst, acts_a, acts_b,
     packed, adj_out, beta_out,
-    sums, g_mid, g_top, g_in, sems,
+    sums, grads, sems,
 ):
     out_copies = [
         pltpu.make_async_copy(adj, adj_out, sems.at[0]),
@@ -373,50 +372,49 @@
     blk, cols = 8, sens.shape[1]
     hidden = wmid.shape[0]
     sums[...] = jnp.zeros(sums.shape, F32)
-    g_mid[...] = jnp.zeros(g_mid.shape, F32)
-    g_top[...] = jnp.zeros(g_top.shape, F32)
-    g_in[...] = jnp.zeros(g_in.shape, F32)
+    grads[...] = jnp.zeros(grads.shape, F32)
+    feat_row = lax.broadcasted_iota(jnp.int32, (16, cols), 0)
 
     def fold(x):
         parts = [x[:, k * LANE : (k + 1) * LANE] for k in range(cols // LANE)]
         return functools.reduce(jnp.add, parts)
 
-    def outer(xs, ds):
-        return lax.dot_general(
-            jnp.concatenate(xs, axis=1), jnp.concatenate(ds, axis=1), NT, preferred_element_type=F32
-        )
+    def with_sens(feats, line):
+        out, rest = feats.astype(F32), line
+        for k in range(3):
+            part = rest.astype(BF16).astype(F32)
+            out = jnp.where(feat_row == num_feat + k, jnp.broadcast_to(part, out.shape), out)
+            rest = rest - part
+        return out.astype(BF16)
 
     def block(acts, start, first_row):
         rows_sens = sens[pl.ds(pl.multiple_of(first_row + start, blk), blk), :]
         wo = across(cst[3], cols)
-        ones, twos, feats, d1s, d2s, d3s = [], [], [], [], [], []
-        acc = [jnp.zeros((hidden, LANE), F32) for _ in range(4)]
+        lefts, rights = [], []
+        acc = [jnp.zeros((hidden, LANE), F32) for _ in range(3)]
         for q in range(blk):
             one, two = acts[start + q, 0:hidden], acts[start + q, hidden : 2 * hidden]
-            three_f = acts[start + q, 2 * hidden : 3 * hidden].astype(F32)
-            sen = jnp.broadcast_to(rows_sens[q : q + 1], (hidden, cols))
-            acc[0] = acc[0] + fold(three_f * sen)
-            d3 = sen * wo * (1.0 - three_f * three_f)
-            acc[3] = acc[3] + fold(d3)
+            three = acts[start + q, 2 * hidden + 16 :]
+            three_f = three.astype(F32)
+            line = rows_sens[q : q + 1]
+            d3 = jnp.broadcast_to(line, (hidden, cols)) * wo * (1.0 - three_f * three_f)
+            acc[2] = acc[2] + fold(d3)
             d3 = d3.astype(BF16)
             two_f = two.astype(F32)
             d2 = jnp.dot(wtop[...], d3, preferred_element_type=F32) * (1.0 - two_f * two_f)
-            acc[2] = acc[2] + fold(d2)
+            acc[1] = acc[1] + fold(d2)
             d2 = d2.astype(BF16)
             one_f = one.astype(F32)
             d1 = jnp.dot(wmid[...], d2, preferred_element_type=F32) * (1.0 - one_f * one_f)
-            acc[1] = acc[1] + fold(d1)
+            acc[0] = acc[0] + fold(d1)
             d1 = d1.astype(BF16)
-            ones.append(one)
-            twos.append(two)
-            feats.append(acts[start + q, 3 * hidden :])
-            d1s.append(d1)
-            d2s.append(d2)
-            d3s.append(d3)
-        g_mid[...] += outer(ones, d2s)
-        g_top[...] += outer(twos, d3s)
-        g_in[...] += outer(feats, d1s)
-        for k in range(4):
+            feats = with_sens(acts[start + q, 2 * hidden : 2 * hidden + 16], line)
+            lefts.append(jnp.concatenate([one, two, feats], axis=0))
+            rights.append(jnp.concatenate([d2, d3, d1, three], axis=0))
+        grads[...] += lax.dot_general(
+            jnp.concatenate(lefts, axis=1), jnp.concatenate(rights, axis=1), NT, preferred_element_type=F32
+        )
+        for k in range(3):
             sums[k] += acc[k]
 
     half = acts_a.shape[0]
@@ -426,28 +424,34 @@
         def _(i, acts=acts, first_row=first_row):
             block(acts, pl.multiple_of(i * blk, blk), first_row)
 
-    packed[0:hidden, :] = jnp.concatenate([g_mid[...], g_top[...]], axis=1)
-    tail = g_in[SUB : 2 * SUB]
+    lane = lax.broadcasted_iota(jnp.int32, (hidden, LANE), 1)
+    packed[0:hidden, :] = jnp.where(
+        lane < hidden, grads[0:hidden, 0:LANE], grads[hidden : 2 * hidden, 0:LANE]
+    )
+    low = grads[2 * hidden : 2 * hidden + SUB, 2 * hidden : 3 * hidden]
+    high = grads[2 * hidden + SUB :, 2 * hidden : 3 * hidden]
+    outs = grads[2 * hidden + SUB :, 3 * hidden :]
     row = lax.broadcasted_iota(jnp.int32, (SUB, hidden), 0)
-    for k in range(4):
-        line = jnp.sum(jnp.transpose(sums[k]), axis=0, keepdims=True)
-        tail = tail + jnp.where(row == k + 2, jnp.broadcast_to(line, (SUB, hidden)), 0.0)
-    packed[hidden : hidden + SUB, :] = jnp.concatenate([g_in[0:SUB], tail], axis=1)
+    at = num_feat - SUB
+    tail = jnp.where(row < at, high, 0.0)
+    lines = [jnp.sum(jnp.where((row >= at) & (row < at + 3), outs, 0.0), axis=0, keepdims=True)]
+    lines += [jnp.sum(jnp.transpose(sums[k]), axis=0, keepdims=True) for k in range(3)]
+    for k, line in enumerate(lines):
+        tail = tail + jnp.where(row == k + at, jnp.broadcast_to(line, (SUB, hidden)), 0.0)
+    packed[hidden : hidden + SUB, :] = jnp.concatenate([low, tail], axis=1)
     for copy in out_copies:
         copy.wait()
 
 
-def backward(adj, beta, sens, weight_mid, weight_top, cst, acts):
+def backward(num_feat, adj, beta, sens, weight_mid, weight_top, cst, acts):
     hidden = weight_mid.shape[0]
     return on_chip(
-        backward_kernel,
+        functools.partial(backward_kernel, num_feat),
         [adj, beta, sens, weight_mid, weight_top, cst, *acts],
         [((hidden + SUB, LANE), F32)],
         [
-            pltpu.VMEM((4, hidden, LANE), F32),
-            pltpu.VMEM((hidden, hidden), F32),
-            pltpu.VMEM((hidden, hidden), F32),
-            pltpu.VMEM((16, hidden), F32),
+            pltpu.VMEM((3, hidden, LANE), F32),
+            pltpu.VMEM((2 * hidden + 16, 4 * hidden), F32),
             pltpu.SemaphoreType.DMA((2,)),
         ],
         far_outs=[like(adj), like(beta)],
@@ -455,9 +459,9 @@
     )
 
 
-def clip_kernel(summed, gin, gmid, gtop, gout, gbias):
+def clip_kernel(own, other, gin, gmid, gtop, gout, gbias):
     hidden = gmid.shape[0]
-    total = summed[0 : hidden + SUB]
+    total = jnp.where(is_odd("gy"), own[...], other[...])
     squares = jnp.sum(jnp.sum(total * total, axis=0, keepdims=True), axis=1, keepdims=True)
     total = total * (CLIP_NORM / jnp.maximum(jnp.sqrt(squares), CLIP_NORM))
     gmid[...] = total[:hidden, :hidden]
@@ -465,31 +469,39 @@
     low, high = total[hidden:, :hidden], total[hidden:, hidden:]
     gin[0:SUB] = low
     gin[SUB:] = high[: gin.shape[0] - SUB]
-    gout[...] = high[2:3]
-    gbias[...] = high[3:6]
-
-
-def clip_all(summed, num_feat, hidden):
+    at = gin.shape[0] - SUB
+    gout[...] = high[at : at + 1]
+    gbias[...] = high[at + 1 : at + 4]
+
+
+def clip_all(own, other, num_feat, hidden):
     shapes = [(num_feat, hidden), (hidden, hidden), (hidden, hidden), (1, hidden), (3, hidden)]
     return pl.pallas_call(
         clip_kernel,
         grid=(1,),
-        in_specs=[whole(summed.shape)],
+        in_specs=[whole(own.shape)] * 2,
         out_specs=[whole(s) for s in shapes],
         out_shape=[jax.ShapeDtypeStruct(s, F32) for s in shapes],
         compiler_params=params(),
         name="clip",
-    )(summed)
+    )(own, other)
 
 
 def sum_over_case(packed):
-    axes = ("gx", "gy")
-    count = lax.axis_size(axes)
-    piece = -(-packed.shape[0] // (count * SUB)) * SUB
-    padded = jnp.pad(packed, ((0, count * piece - packed.shape[0]), (0, 0))).reshape(count, piece, LANE)
-    mine = jnp.sum(lax.all_to_all(padded, axes, 0, 0), axis=0, keepdims=True)
-    pieces = lax.all_to_all(jnp.broadcast_to(mine, padded.shape), axes, 0, 0)
-    return pieces.reshape(count * piece, LANE)
+    num_x, num_y = lax.axis_size("gx"), lax.axis_size("gy")
+    to_odd = [(i, i + 1) for i in range(0, num_y, 2)]
+    total = packed + lax.ppermute(packed, "gy", to_odd)
+    step = 2
+    while step < num_y:
+        pairs = [(i, i ^ step) for i in range(1, num_y, 2)]
+        total = total + lax.ppermute(total, "gy", pairs)
+        step *= 2
+    step = 1
+    while step < num_x:
+        pairs = [(i * num_y + j, (i ^ step) * num_y + j) for i in range(num_x) for j in range(1, num_y, 2)]
+        total = total + lax.ppermute(total, ("gx", "gy"), pairs)
+        step *= 2
+    return total, lax.ppermute(total, "gy", [(b, a) for a, b in to_odd])
 
 
 def swaps(first, second, axis):
@@ -524,8 +536,8 @@
     adj, sens, beta = sweeps(
         source, coupling, inverse, production, (beta_a, beta_b), (*row_halos, *col_halos), mixing
     )
-    packed, adjoint, beta = backward(adj, beta, sens, weight_mid, weight_top, prepared[3], (acts_a, acts_b))
-    grad_in, grad_mid, grad_top, grad_out, grad_bias = clip_all(sum_over_case(packed), num_feat, hidden)
+    packed, adjoint, beta = backward(num_feat, adj, beta, sens, weight_mid, weight_top, prepared[3], (acts_a, acts_b))
+    grad_in, grad_mid, grad_top, grad_out, grad_bias = clip_all(*sum_over_case(packed), num_feat, hidden)
     return (adjoint, beta, grad_in, grad_mid, grad_top, grad_out.reshape(hidden), grad_bias)
 
 

time: 49.4 us -> 49.4 us (level)
  blocking collectives: 25.1 us -> 0 us
  waiting for transfers between devices: 0.01 us -> 17.8 us
  starting transfers between devices: 4.48 us -> 12.5 us
  Pallas kernels: 18.7 us -> 17.9 us
    all_to_all x2 -> x0, blocking collectives: 25.1 us -> none  [the longest x1 15.6 us: sum_over_case(): mine = jnp.sum(lax.all_to_all(padded, axes, 0, 0), axis=0, keepdims=True)]
    ppermute x0 -> x5, waiting for transfers between devices: none -> 17.8 us  [the longest x1 16.9 us: sum_over_case(): return (total, lax.ppermute(total, 'gy', [(b, a) for a, b in to_odd]))]
    ppermute x0 -> x5, starting transfers between devices: none -> 8.03 us  [the longest x1 4.76 us: sum_over_case(): total = packed + lax.ppermute(packed, 'gy', to_odd)]
    pallas_call x6, Pallas kernels: 14.1 us -> 13.3 us  [on_chip(): pl.pallas_call(kernel, in_specs=[here] * len(operands) + [there] * len(fa...]
  transfers between devices with their start and end apart: 4 -> 9, of which waited for: 0 -> 2; matrix products, arithmetic and copies ran while one was open for 0% -> 0% of each run, Pallas kernels for 14% -> 10%
where the time goes in v3:
time: 49.4 us; the launch traced here: 49.1 us
  Pallas kernels  17.9 us (36%)
  waiting for transfers between devices  17.8 us (36%)
  starting transfers between devices  12.5 us (25%)
  between operations  0.85 us (2%)
    ppermute x1, waiting for transfers between devices, sum_over_case(): return (total, lax.ppermute(total, 'gy', [(b, a) for a, b in to_odd]))  16.9 us
    pallas_call x6, Pallas kernels, on_chip(): pl.pallas_call(kernel, in_specs=[here] * len(operands) + [there] * len(fa...  13.3 us
    ppermute x1, starting transfers between devices, sum_over_case(): total = packed + lax.ppermute(packed, 'gy', to_odd)  4.76 us
    pallas_call x1, Pallas kernels, sweeps(): pl.pallas_call(sweep_kernel, in_specs=[near] * len(operands) + [pl.BlockS...  3.82 us
    ppermute x2, starting transfers between devices, swaps(): lax.ppermute(first, axis, pairs(0))  3.16 us
    ppermute x2, starting transfers between devices, sum_over_case(): total = total + lax.ppermute(total, ('gx', 'gy'), pairs)  1.33 us
    ppermute x2, starting transfers between devices, swaps(): lax.ppermute(second, axis, pairs(1))  1.32 us
    ppermute x1, starting transfers between devices, sum_over_case(): return (total, lax.ppermute(total, 'gy', [(b, a) for a, b in to_odd]))  1.29 us
  transfers between devices with their start and end apart: 9, of which 2 were waited for; matrix products, arithmetic and copies ran while one was open for 0% of the time, Pallas kernels for 10%

profile of v3, /device:TPU:0, one launch (start us, length us, event | category | flops | bytes accessed | tf_op | source)
XLA Modules:
  0.0 49.1 jit_solution(3787152486718327875)
XLA Ops:
  0.6 2.0 %load.1 = (bf16[5,64,256]{2,1,0:T(8,128)(2,1)S(1)}, bf16[4,64,256]{2,1,0:T(8,128)(2,1)S(1)}, f32[64,256]{1,0:T(8,128)}, s32[64,256]{1,0:T(8,128)}, f32[64,256]{1...) custom-call(bf16[5,64,256]{2,1,0:T(8,128)(2,1)} %refs_0_.1, ...), custom_call_target="tpu_custom_call" | custom-call | tf_op jit(solution)/shard_map/load/pallas_call | solution.py:33
  2.6 0.0 copy-start
  2.6 3.1 %collective-permute-start = (f32[10,8,256]{2,1,0:T(8,128)S(1)}, f32[10,8,256]{2,1,0:T(8,128)S(1)}, u32[]{:S(2)}, u32[]{:S(2)}) collective-permute-start(f32[10,8,256]{2,1,0:T(8,128)S(1)} %get-tuple-element.47), channel_id=1, source_target_pairs={{0,4},{8,12},{4,0},{12,8},{1,5},{9,13},{5,1},{13,9},{2,6},{10,14},... | collective-permute-start | bytes 245768 | tf_op jit(solution)/shard_map/ppermute | solution.py:514
  5.7 0.7 %collective-permute-start.1 = (f32[10,8,256]{2,1,0:T(8,128)S(1)}, f32[10,8,256]{2,1,0:T(8,128)S(1)}, u32[]{:S(2)}, u32[]{:S(2)}) collective-permute-start(f32[10,8,256]{2,1,0:T(8,128)S(1)} %get-tuple-element.48), channel_id=1, source_target_pairs={{4,8},{8,4},{5,9},{9,5},{6,10},{10,6},{7,11},{11,7},{20,24},{24,20... | collective-permute-start | bytes 245768 | tf_op jit(solution)/shard_map/ppermute | solution.py:514
  6.4 0.2 weights.1
  6.6 2.4 %network_forward.2 = (bf16[32,208,256]{2,1,0:T(8,128)(2,1)S(1)}, f32[32,256]{1,0:T(8,128)S(1)}) custom-call(bf16[10,64,256]{2,1,0:T(8,128)(2,1)S(1)} %get-tuple-element.49.feat, bf16[1280,256]{1,0:T(8,128)(2,1)S(1)} %get-tuple-element.55.w1, bf16[64,64]{1,0:T(8,128)(2,1)S(1)} %get-tuple-element.56.w2, bf16[64,64]{1,0:T(8,128)(2,1)S(1)} %get-tuple-element.57.w3, ...), custom_call_target="tpu_custom_call" | custom-call | flops 144703488 | bytes 3571712 | tf_op jit(solution)/shard_map/network_forward/pallas_call | solution.py:33
  9.0 0.0 collective-permute-done.row_first
  9.0 0.0 collective-permute-done.1.row_second
  9.0 0.2 col_slabs.1
  9.2 0.1 collective-permute-start.2
  9.3 0.7 %collective-permute-start.3 = (f32[80,128]{1,0:T(8,128)S(1)}, f32[80,128]{1,0:T(8,128)S(1)}, u32[]{:S(2)}, u32[]{:S(2)}) collective-permute-start(f32[80,128]{1,0:T(8,128)S(1)} %get-tuple-element.65), channel_id=1, source_target_pairs={{1,2},{2,1},{5,6},{6,5},{9,10},{10,9},{13,14},{14,13},{17,18},{18,... | collective-permute-start | bytes 122888 | tf_op jit(solution)/shard_map/ppermute | solution.py:514
  10.0 2.4 %network_forward.3 = (bf16[32,208,256]{2,1,0:T(8,128)(2,1)S(1)}, f32[32,256]{1,0:T(8,128)S(1)}) custom-call(bf16[10,64,256]{2,1,0:T(8,128)(2,1)S(1)} %get-tuple-element.49.feat, bf16[1280,256]{1,0:T(8,128)(2,1)S(1)} %get-tuple-element.55.w1, bf16[64,64]{1,0:T(8,128)(2,1)S(1)} %get-tuple-element.56.w2, bf16[64,64]{1,0:T(8,128)(2,1)S(1)} %get-tuple-element.57.w3, ...), custom_call_target="tpu_custom_call" | custom-call | flops 144703488 | bytes 3571712 | tf_op jit(solution)/shard_map/network_forward/pallas_call | solution.py:33
  12.4 0.0 collective-permute-done.2.col_first
  12.4 0.0 collective-permute-done.3.col_second
  12.4 0.0 copy-done
  12.4 3.8 %sweeps.1 = (f32[5,64,256]{2,1,0:T(8,128)S(1)}, f32[64,256]{1,0:T(8,128)S(1)}, f32[64,256]{1,0:T(8,128)S(1)}) custom-call(bf16[5,64,256]{2,1,0:T(8,128)(2,1)S(1)} %get-tuple-element.43.src, bf16[4,64,256]{2,1,0:T(8,128)(2,1)S(1)} %get-tuple-element.44.cpl, f32[64,256]{1,0:T(8,128)S(1)} %get-tuple-element.45.inv.inverse, ...), custom_call_target="tpu_custom_call" | custom-call | tf_op jit(solution)/shard_map/sweeps/pallas_call | solution.py:344
  16.2 6.2 %backward.1 = (f32[72,128]{1,0:T(8,128)S(1)}, f32[5,64,256]{2,1,0:T(8,128)}, f32[64,256]{1,0:T(8,128)}) custom-call(f32[5,64,256]{2,1,0:T(8,128)S(1)} %get-tuple-element.66.adj, f32[64,256]{1,0:T(8,128)S(1)} %get-tuple-element.67.beta, f32[64,256]{1,0:T(8,128)S(1)} %get-tuple-element.68.sens, bf16[64,64]{1,0:T(8,128)(2,1)S(1)} %get-tuple-element.51.wmid, ...), custom_call_target="tpu_custom_call" | custom-call | tf_op jit(solution)/shard_map/backward/pallas_call | solution.py:33
  22.4 4.8 %collective-permute-start.4 = (f32[72,128]{1,0:T(8,128)S(1)}, f32[72,128]{1,0:T(8,128)S(1)}, u32[]{:S(2)}, u32[]{:S(2)}) collective-permute-start(f32[72,128]{1,0:T(8,128)S(1)} %get-tuple-element.73), channel_id=1, source_target_pairs={{0,1},{2,3},{4,5},{6,7},{8,9},{10,11},{12,13},{14,15},{16,17},{18,... | collective-permute-start | bytes 110600 | tf_op jit(solution)/shard_map/ppermute | solution.py:493
  27.1 0.8 %collective-permute-done.4 = f32[72,128]{1,0:T(8,128)S(1)} collective-permute-done((f32[72,128]{1,0:T(8,128)S(1)}, f32[72,128]{1,0:T(8,128)S(1)}, u32[]{:S(2)}, u32[]{:S(2)}) %collective-permute-start.4) | collective-permute-done | bytes 36896 | tf_op jit(solution)/shard_map/ppermute | solution.py:493
  28.0 0.7 %collective-permute-start.5 = (f32[72,128]{1,0:T(8,128)S(1)}, f32[72,128]{1,0:T(8,128)S(1)}, u32[]{:S(2)}, u32[]{:S(2)}) collective-permute-start(f32[72,128]{1,0:T(8,128)S(1)} %add.12), channel_id=1, source_target_pairs={{1,3},{3,1},{5,7},{7,5},{9,11},{11,9},{13,15},{15,13},{17,19},{19,... | collective-permute-start | bytes 110600 | tf_op jit(solution)/shard_map/ppermute | solution.py:497
  28.7 0.0 collective-permute-done.5
  28.7 0.7 %collective-permute-start.6 = (f32[72,128]{1,0:T(8,128)S(1)}, f32[72,128]{1,0:T(8,128)S(1)}, u32[]{:S(2)}, u32[]{:S(2)}) collective-permute-start(f32[72,128]{1,0:T(8,128)S(1)} %add.13), channel_id=1, source_target_pairs={{1,5},{3,7},{5,1},{7,3},{9,13},{11,15},{13,9},{15,11},{17,21},{19,... | collective-permute-start | bytes 110600 | tf_op jit(solution)/shard_map/ppermute | solution.py:502
  29.3 0.0 collective-permute-done.6
  29.4 0.7 %collective-permute-start.7 = (f32[72,128]{1,0:T(8,128)S(1)}, f32[72,128]{1,0:T(8,128)S(1)}, u32[]{:S(2)}, u32[]{:S(2)}) collective-permute-start(f32[72,128]{1,0:T(8,128)S(1)} %add.14), channel_id=1, source_target_pairs={{1,9},{3,11},{5,13},{7,15},{9,1},{11,3},{13,5},{15,7},{17,25},{19,... | collective-permute-start | bytes 110600 | tf_op jit(solution)/shard_map/ppermute | solution.py:502
  30.0 0.0 collective-permute-done.7
  30.1 1.3 %collective-permute-start.8 = (f32[72,128]{1,0:T(8,128)S(1)}, f32[72,128]{1,0:T(8,128)S(1)}, u32[]{:S(2)}, u32[]{:S(2)}) collective-permute-start(f32[72,128]{1,0:T(8,128)S(1)} %add.15.own), channel_id=1, source_target_pairs={{1,0},{3,2},{5,4},{7,6},{9,8},{11,10},{13,12},{15,14},{17,16},{19,... | collective-permute-start | bytes 110600 | tf_op jit(solution)/shard_map/ppermute | solution.py:504
  31.4 16.9 %collective-permute-done.8.other = f32[72,128]{1,0:T(8,128)S(1)} collective-permute-done((f32[72,128]{1,0:T(8,128)S(1)}, f32[72,128]{1,0:T(8,128)S(1)}, u32[]{:S(2)}, u32[]{:S(2)}) %collective-permute-start.8) | collective-permute-done | bytes 36896 | tf_op jit(solution)/shard_map/ppermute | solution.py:504
  48.3 0.8 %clip.1 = (f32[10,64]{1,0:T(8,128)}, f32[64,64]{1,0:T(8,128)}, f32[64,64]{1,0:T(8,128)}, f32[1,64]{1,0:T(1,128)}, f32[3,64]{1,0:T(4,128)}) custom-call(f32[72,128]{1,0:T(8,128)S(1)} %add.15.own, f32[72,128]{1,0:T(8,128)S(1)} %collective-permute-done.8.other), custom_call_target="tpu_custom_call" | custom-call | tf_op jit(solution)/shard_map/clip/pallas_call | solution.py:479
  (4 shorter events, 0.0 us)
Async XLA Ops:
  2.6 9.7 %copy-start = (f32[5,5]{1,0:T(8,128)S(1)}, f32[5,5]{1,0:T(8,128)}, u32[]{:S(2)}) copy-start(f32[5,5]{1,0:T(8,128)} %mix.1) | copy-start | bytes 304
  2.6 6.4 %collective-permute-start = (f32[10,8,256]{2,1,0:T(8,128)S(1)}, f32[10,8,256]{2,1,0:T(8,128)S(1)}, u32[]{:S(2)}, u32[]{:S(2)}) collective-permute-start(f32[10,8,256]{2,1,0:T(8,128)S(1)} %get-tuple-element.47), channel_id=1, source_target_pairs={{0,4},{8,12},{4,0},{12,8},{1,5},{9,13},{5,1},{13,9},{2,6},{10,14},... | collective-permute-start | bytes 245768 | tf_op jit(solution)/shard_map/ppermute | solution.py:514
  5.7 3.3 %collective-permute-start.1 = (f32[10,8,256]{2,1,0:T(8,128)S(1)}, f32[10,8,256]{2,1,0:T(8,128)S(1)}, u32[]{:S(2)}, u32[]{:S(2)}) collective-permute-start(f32[10,8,256]{2,1,0:T(8,128)S(1)} %get-tuple-element.48), channel_id=1, source_target_pairs={{4,8},{8,4},{5,9},{9,5},{6,10},{10,6},{7,11},{11,7},{20,24},{24,20... | collective-permute-start | bytes 245768 | tf_op jit(solution)/shard_map/ppermute | solution.py:514
  9.2 3.1 %collective-permute-start.2 = (f32[80,128]{1,0:T(8,128)S(1)}, f32[80,128]{1,0:T(8,128)S(1)}, u32[]{:S(2)}, u32[]{:S(2)}) collective-permute-start(f32[80,128]{1,0:T(8,128)S(1)} %get-tuple-element.64), channel_id=1, source_target_pairs={{0,1},{2,3},{1,0},{3,2},{4,5},{6,7},{5,4},{7,6},{8,9},{10,11},{9,8... | collective-permute-start | bytes 122888 | tf_op jit(solution)/shard_map/ppermute | solution.py:514
  9.3 3.1 %collective-permute-start.3 = (f32[80,128]{1,0:T(8,128)S(1)}, f32[80,128]{1,0:T(8,128)S(1)}, u32[]{:S(2)}, u32[]{:S(2)}) collective-permute-start(f32[80,128]{1,0:T(8,128)S(1)} %get-tuple-element.65), channel_id=1, source_target_pairs={{1,2},{2,1},{5,6},{6,5},{9,10},{10,9},{13,14},{14,13},{17,18},{18,... | collective-permute-start | bytes 122888 | tf_op jit(solution)/shard_map/ppermute | solution.py:514
  22.4 5.6 %collective-permute-start.4 = (f32[72,128]{1,0:T(8,128)S(1)}, f32[72,128]{1,0:T(8,128)S(1)}, u32[]{:S(2)}, u32[]{:S(2)}) collective-permute-start(f32[72,128]{1,0:T(8,128)S(1)} %get-tuple-element.73), channel_id=1, source_target_pairs={{0,1},{2,3},{4,5},{6,7},{8,9},{10,11},{12,13},{14,15},{16,17},{18,... | collective-permute-start | bytes 110600 | tf_op jit(solution)/shard_map/ppermute | solution.py:493
  28.0 0.7 %collective-permute-start.5 = (f32[72,128]{1,0:T(8,128)S(1)}, f32[72,128]{1,0:T(8,128)S(1)}, u32[]{:S(2)}, u32[]{:S(2)}) collective-permute-start(f32[72,128]{1,0:T(8,128)S(1)} %add.12), channel_id=1, source_target_pairs={{1,3},{3,1},{5,7},{7,5},{9,11},{11,9},{13,15},{15,13},{17,19},{19,... | collective-permute-start | bytes 110600 | tf_op jit(solution)/shard_map/ppermute | solution.py:497
  28.7 0.7 %collective-permute-start.6 = (f32[72,128]{1,0:T(8,128)S(1)}, f32[72,128]{1,0:T(8,128)S(1)}, u32[]{:S(2)}, u32[]{:S(2)}) collective-permute-start(f32[72,128]{1,0:T(8,128)S(1)} %add.13), channel_id=1, source_target_pairs={{1,5},{3,7},{5,1},{7,3},{9,13},{11,15},{13,9},{15,11},{17,21},{19,... | collective-permute-start | bytes 110600 | tf_op jit(solution)/shard_map/ppermute | solution.py:502
  29.4 0.7 %collective-permute-start.7 = (f32[72,128]{1,0:T(8,128)S(1)}, f32[72,128]{1,0:T(8,128)S(1)}, u32[]{:S(2)}, u32[]{:S(2)}) collective-permute-start(f32[72,128]{1,0:T(8,128)S(1)} %add.14), channel_id=1, source_target_pairs={{1,9},{3,11},{5,13},{7,15},{9,1},{11,3},{13,5},{15,7},{17,25},{19,... | collective-permute-start | bytes 110600 | tf_op jit(solution)/shard_map/ppermute | solution.py:502
  30.1 18.2 %collective-permute-start.8 = (f32[72,128]{1,0:T(8,128)S(1)}, f32[72,128]{1,0:T(8,128)S(1)}, u32[]{:S(2)}, u32[]{:S(2)}) collective-permute-start(f32[72,128]{1,0:T(8,128)S(1)} %add.15.own), channel_id=1, source_target_pairs={{1,0},{3,2},{5,4},{7,6},{9,8},{11,10},{13,12},{15,14},{17,16},{19,... | collective-permute-start | bytes 110600 | tf_op jit(solution)/shard_map/ppermute | solution.py:504

commit v4 on v2

--- a/solution.py
+++ b/solution.py
@@ -98,8 +98,9 @@
 
 
 def ordered(axis, first, second):
-    odd = is_odd(axis)
-    return jnp.where(odd, first, second), jnp.where(odd, second, first)
+    odd, at = is_odd(axis), lax.axis_index(axis)
+    before, after = jnp.where(odd, first, second), jnp.where(odd, second, first)
+    return jnp.where(at == 0, 0.0, before), jnp.where(at == lax.axis_size(axis) - 1, 0.0, after)
 
 
 def cols_kernel(src, cpl, inv, row_first, row_second, col_first, col_second):
@@ -195,15 +196,14 @@
         x1[0 : nf * blk] = feat[:, pl.ds(first_row + start, blk), :].reshape(nf * blk, cols)
         b1, b2, b3, wo = (across(cst[k], cols) for k in range(4))
         lines = []
+        first = jnp.dot(w1[...], x1[...], preferred_element_type=F32)
         for g in range(blk // per):
-            lo = g * per * step_rows
-            first = jnp.dot(w1[lo : lo + per * step_rows], x1[...], preferred_element_type=F32)
             ones = []
-            for q in range(per):
+            for q in range(g * per, (g + 1) * per):
                 part = first[q * step_rows : (q + 1) * step_rows]
                 one = jnp.tanh(part[:hidden] + b1).astype(BF16)
-                acts[start + (g * per + q), 0:hidden] = one
-                acts[start + (g * per + q), 3 * hidden :] = part[hidden:].astype(BF16)
+                acts[start + q, 0:hidden] = one
+                acts[start + q, 2 * hidden : 2 * hidden + 16] = part[hidden:].astype(BF16)
                 ones.append(one)
             second = jnp.dot(w2[...], jnp.concatenate(ones, axis=1), preferred_element_type=F32)
             twos = []
@@ -214,7 +214,7 @@
             third = jnp.dot(w3[...], jnp.concatenate(twos, axis=1), preferred_element_type=F32)
             for q in range(per):
                 three = jnp.tanh(third[:, q * cols : (q + 1) * cols] + b3).astype(BF16)
-                acts[start + (g * per + q), 2 * hidden : 3 * hidden] = three
+                acts[start + (g * per + q), 2 * hidden + 16 :] = three
                 lines.append(1.0 + jnp.sum(three.astype(F32) * wo, axis=0, keepdims=True))
         beta[pl.ds(start, blk), :] = jnp.concatenate(lines, axis=0)
 
@@ -360,7 +360,7 @@
 
 
 def backward_kernel(
-    adj, beta, sens, wmid, wtop, cst, acts_a, acts_b,
+    num_feat, adj, beta, sens, wmid, wtop, cst, acts_a, acts_b,
     packed, adj_out, beta_out,
     sums, g_mid, g_top, g_in, sems,
 ):
@@ -381,43 +381,45 @@
         parts = [x[:, k * LANE : (k + 1) * LANE] for k in range(cols // LANE)]
         return functools.reduce(jnp.add, parts)
 
-    def outer(xs, ds):
-        return lax.dot_general(
-            jnp.concatenate(xs, axis=1), jnp.concatenate(ds, axis=1), NT, preferred_element_type=F32
-        )
+    def joined(xs):
+        return jnp.concatenate(xs, axis=1)
+
+    def outer(x, d):
+        return lax.dot_general(x, d, NT, preferred_element_type=F32)
 
     def block(acts, start, first_row):
         rows_sens = sens[pl.ds(pl.multiple_of(first_row + start, blk), blk), :]
         wo = across(cst[3], cols)
-        ones, twos, feats, d1s, d2s, d3s = [], [], [], [], [], []
-        acc = [jnp.zeros((hidden, LANE), F32) for _ in range(4)]
+
+        def layer(lo, high):
+            return joined([acts[start + q, lo:high] for q in range(blk)])
+
+        def behind(weight, delta, lo):
+            raw = jnp.dot(weight, delta, preferred_element_type=F32)
+            total, out = jnp.zeros((hidden, LANE), F32), []
+            for q in range(blk):
+                act = acts[start + q, lo : lo + hidden].astype(F32)
+                d = raw[:, q * cols : (q + 1) * cols] * (1.0 - act * act)
+                total = total + fold(d)
+                out.append(d.astype(BF16))
+            return joined(out), total
+
+        out_sum, top_sum, d3 = jnp.zeros((hidden, LANE), F32), jnp.zeros((hidden, LANE), F32), []
         for q in range(blk):
-            one, two = acts[start + q, 0:hidden], acts[start + q, hidden : 2 * hidden]
-            three_f = acts[start + q, 2 * hidden : 3 * hidden].astype(F32)
+            act = acts[start + q, 2 * hidden + 16 :].astype(F32)
             sen = jnp.broadcast_to(rows_sens[q : q + 1], (hidden, cols))
-            acc[0] = acc[0] + fold(three_f * sen)
-            d3 = sen * wo * (1.0 - three_f * three_f)
-            acc[3] = acc[3] + fold(d3)
-            d3 = d3.astype(BF16)
-            two_f = two.astype(F32)
-            d2 = jnp.dot(wtop[...], d3, preferred_element_type=F32) * (1.0 - two_f * two_f)
-            acc[2] = acc[2] + fold(d2)
-            d2 = d2.astype(BF16)
-            one_f = one.astype(F32)
-            d1 = jnp.dot(wmid[...], d2, preferred_element_type=F32) * (1.0 - one_f * one_f)
-            acc[1] = acc[1] + fold(d1)
-            d1 = d1.astype(BF16)
-            ones.append(one)
-            twos.append(two)
-            feats.append(acts[start + q, 3 * hidden :])
-            d1s.append(d1)
-            d2s.append(d2)
-            d3s.append(d3)
-        g_mid[...] += outer(ones, d2s)
-        g_top[...] += outer(twos, d3s)
-        g_in[...] += outer(feats, d1s)
-        for k in range(4):
-            sums[k] += acc[k]
+            out_sum = out_sum + fold(act * sen)
+            d = sen * wo * (1.0 - act * act)
+            top_sum = top_sum + fold(d)
+            d3.append(d.astype(BF16))
+        d3 = joined(d3)
+        d2, mid_sum = behind(wtop[...], d3, hidden)
+        g_top[...] += outer(layer(hidden, 2 * hidden), d3)
+        d1, in_sum = behind(wmid[...], d2, 0)
+        g_mid[...] += outer(layer(0, hidden), d2)
+        g_in[...] += outer(d1, layer(2 * hidden, 2 * hidden + 16))
+        for k, part in enumerate((out_sum, in_sum, mid_sum, top_sum)):
+            sums[k] += part
 
     half = acts_a.shape[0]
     for acts, first_row in ((acts_a, 0), (acts_b, half)):
@@ -426,28 +428,29 @@
         def _(i, acts=acts, first_row=first_row):
             block(acts, pl.multiple_of(i * blk, blk), first_row)
 
-    packed[0:hidden, :] = jnp.concatenate([g_mid[...], g_top[...]], axis=1)
-    tail = g_in[SUB : 2 * SUB]
+    packed[0:hidden, :] = joined([g_mid[...], g_top[...]])
+    turned = jnp.transpose(joined([g_in[...], jnp.zeros((hidden, LANE - 16), F32)]))
+    tail = turned[SUB : 2 * SUB]
     row = lax.broadcasted_iota(jnp.int32, (SUB, hidden), 0)
     for k in range(4):
         line = jnp.sum(jnp.transpose(sums[k]), axis=0, keepdims=True)
-        tail = tail + jnp.where(row == k + 2, jnp.broadcast_to(line, (SUB, hidden)), 0.0)
-    packed[hidden : hidden + SUB, :] = jnp.concatenate([g_in[0:SUB], tail], axis=1)
+        tail = tail + jnp.where(row == k + num_feat - SUB, jnp.broadcast_to(line, (SUB, hidden)), 0.0)
+    packed[hidden : hidden + SUB, :] = joined([turned[0:SUB], tail])
     for copy in out_copies:
         copy.wait()
 
 
-def backward(adj, beta, sens, weight_mid, weight_top, cst, acts):
+def backward(num_feat, adj, beta, sens, weight_mid, weight_top, cst, acts):
     hidden = weight_mid.shape[0]
     return on_chip(
-        backward_kernel,
+        functools.partial(backward_kernel, num_feat),
         [adj, beta, sens, weight_mid, weight_top, cst, *acts],
         [((hidden + SUB, LANE), F32)],
         [
             pltpu.VMEM((4, hidden, LANE), F32),
             pltpu.VMEM((hidden, hidden), F32),
             pltpu.VMEM((hidden, hidden), F32),
-            pltpu.VMEM((16, hidden), F32),
+            pltpu.VMEM((hidden, 16), F32),
             pltpu.SemaphoreType.DMA((2,)),
         ],
         far_outs=[like(adj), like(beta)],
@@ -455,9 +458,11 @@
     )
 
 
-def clip_kernel(summed, gin, gmid, gtop, gout, gbias):
+def clip_kernel(parts, gin, gmid, gtop, gout, gbias):
     hidden = gmid.shape[0]
-    total = summed[0 : hidden + SUB]
+    total = parts[0]
+    for k in range(1, parts.shape[0]):
+        total = total + parts[k]
     squares = jnp.sum(jnp.sum(total * total, axis=0, keepdims=True), axis=1, keepdims=True)
     total = total * (CLIP_NORM / jnp.maximum(jnp.sqrt(squares), CLIP_NORM))
     gmid[...] = total[:hidden, :hidden]
@@ -465,31 +470,31 @@
     low, high = total[hidden:, :hidden], total[hidden:, hidden:]
     gin[0:SUB] = low
     gin[SUB:] = high[: gin.shape[0] - SUB]
-    gout[...] = high[2:3]
-    gbias[...] = high[3:6]
-
-
-def clip_all(summed, num_feat, hidden):
+    at = gin.shape[0] - SUB
+    gout[...] = high[at : at + 1]
+    gbias[...] = high[at + 1 : at + 4]
+
+
+def clip_all(parts, num_feat, hidden):
     shapes = [(num_feat, hidden), (hidden, hidden), (hidden, hidden), (1, hidden), (3, hidden)]
     return pl.pallas_call(
         clip_kernel,
         grid=(1,),
-        in_specs=[whole(summed.shape)],
+        in_specs=[whole(parts.shape)],
         out_specs=[whole(s) for s in shapes],
         out_shape=[jax.ShapeDtypeStruct(s, F32) for s in shapes],
         compiler_params=params(),
         name="clip",
-    )(summed)
-
-
-def sum_over_case(packed):
-    axes = ("gx", "gy")
-    count = lax.axis_size(axes)
-    piece = -(-packed.shape[0] // (count * SUB)) * SUB
-    padded = jnp.pad(packed, ((0, count * piece - packed.shape[0]), (0, 0))).reshape(count, piece, LANE)
-    mine = jnp.sum(lax.all_to_all(padded, axes, 0, 0), axis=0, keepdims=True)
-    pieces = lax.all_to_all(jnp.broadcast_to(mine, padded.shape), axes, 0, 0)
-    return pieces.reshape(count * piece, LANE)
+    )(parts)
+
+
+def parts_of_sum(packed):
+    count = lax.axis_size("gy")
+    step = 1
+    while step < count:
+        packed = packed + lax.ppermute(packed, "gy", [(i, i ^ step) for i in range(count)])
+        step *= 2
+    return lax.all_gather(packed, "gx")
 
 
 def swaps(first, second, axis):
@@ -497,7 +502,9 @@
 
     def pairs(start):
         low = range(start, count - 1, 2)
-        return [(i, i + 1) for i in low] + [(i + 1, i) for i in low]
+        paired = [(i, i + 1) for i in low] + [(i + 1, i) for i in low]
+        alone = set(range(count)) - {i for i, _ in paired}
+        return paired + [(i, i) for i in sorted(alone)]
 
     return lax.ppermute(first, axis, pairs(0)), lax.ppermute(second, axis, pairs(1))
 
@@ -524,8 +531,8 @@
     adj, sens, beta = sweeps(
         source, coupling, inverse, production, (beta_a, beta_b), (*row_halos, *col_halos), mixing
     )
-    packed, adjoint, beta = backward(adj, beta, sens, weight_mid, weight_top, prepared[3], (acts_a, acts_b))
-    grad_in, grad_mid, grad_top, grad_out, grad_bias = clip_all(sum_over_case(packed), num_feat, hidden)
+    packed, adjoint, beta = backward(num_feat, adj, beta, sens, weight_mid, weight_top, prepared[3], (acts_a, acts_b))
+    grad_in, grad_mid, grad_top, grad_out, grad_bias = clip_all(parts_of_sum(packed), num_feat, hidden)
     return (adjoint, beta, grad_in, grad_mid, grad_top, grad_out.reshape(hidden), grad_bias)
 
 

time: 49.4 us -> 47.2 us (0.955)
  blocking collectives: 25.1 us -> 16.8 us
  starting transfers between devices: 4.48 us -> 8.63 us
  waiting for transfers between devices: 0.01 us -> 3.59 us
  Pallas kernels: 18.7 us -> 17.1 us
    all_to_all x2 -> x0, blocking collectives: 25.1 us -> none  [the longest x1 15.6 us: sum_over_case(): mine = jnp.sum(lax.all_to_all(padded, axes, 0, 0), axis=0, keepdims=True)]
    all_gather x0 -> x1, blocking collectives: none -> 16.8 us  [parts_of_sum(): return lax.all_gather(packed, 'gx')]
    ppermute x0 -> x2, starting transfers between devices: none -> 4.15 us  [parts_of_sum(): lax.ppermute(packed, 'gy', [(i, i ^ step) for i in range(count)])]
    ppermute x0 -> x2, waiting for transfers between devices: none -> 3.58 us  [parts_of_sum(): lax.ppermute(packed, 'gy', [(i, i ^ step) for i in range(count)])]
    pallas_call x6, Pallas kernels: 14.1 us -> 12.5 us  [on_chip(): pl.pallas_call(kernel, in_specs=[here] * len(operands) + [there] * len(fa...]
  transfers between devices with their start and end apart: 4 -> 6, of which waited for: 0 -> 2; matrix products, arithmetic and copies ran while one was open for 0% -> 0% of each run, Pallas kernels for 14% -> 11%
where the time goes in v4:
time: 47.2 us; the launch traced here: 47 us
  Pallas kernels  17.1 us (36%)
  blocking collectives  16.8 us (36%)
  starting transfers between devices  8.63 us (18%)
  waiting for transfers between devices  3.59 us (8%)
  between operations  0.77 us (2%)
    all_gather x1, blocking collectives, parts_of_sum(): return lax.all_gather(packed, 'gx')  16.8 us
    pallas_call x6, Pallas kernels, on_chip(): pl.pallas_call(kernel, in_specs=[here] * len(operands) + [there] * len(fa...  12.5 us
    ppermute x2, starting transfers between devices, parts_of_sum(): lax.ppermute(packed, 'gy', [(i, i ^ step) for i in range(count)])  4.15 us
    pallas_call x1, Pallas kernels, sweeps(): pl.pallas_call(sweep_kernel, in_specs=[near] * len(operands) + [pl.BlockS...  3.82 us
    ppermute x2, waiting for transfers between devices, parts_of_sum(): lax.ppermute(packed, 'gy', [(i, i ^ step) for i in range(count)])  3.58 us
    ppermute x2, starting transfers between devices, swaps(): lax.ppermute(first, axis, pairs(0))  3.16 us
    ppermute x2, starting transfers between devices, swaps(): lax.ppermute(second, axis, pairs(1))  1.32 us
  transfers between devices with their start and end apart: 6, of which 2 were waited for; matrix products, arithmetic and copies ran while one was open for 0% of the time, Pallas kernels for 11%

profile of v4, /device:TPU:0, one launch (start us, length us, event | category | flops | bytes accessed | tf_op | source)
XLA Modules:
  0.0 47.0 jit_solution(11421387501908643879)
XLA Ops:
  0.6 2.0 %load.1 = (bf16[5,64,256]{2,1,0:T(8,128)(2,1)S(1)}, bf16[4,64,256]{2,1,0:T(8,128)(2,1)S(1)}, f32[64,256]{1,0:T(8,128)}, s32[64,256]{1,0:T(8,128)}, f32[64,256]{1...) custom-call(bf16[5,64,256]{2,1,0:T(8,128)(2,1)} %refs_0_.1, ...), custom_call_target="tpu_custom_call" | custom-call | tf_op jit(solution)/shard_map/load/pallas_call | solution.py:33
  2.6 0.0 copy-start
  2.6 3.1 %collective-permute-start = (f32[10,8,256]{2,1,0:T(8,128)S(1)}, f32[10,8,256]{2,1,0:T(8,128)S(1)}, u32[]{:S(2)}, u32[]{:S(2)}) collective-permute-start(f32[10,8,256]{2,1,0:T(8,128)S(1)} %get-tuple-element.47), channel_id=1, source_target_pairs={{0,4},{8,12},{4,0},{12,8},{1,5},{9,13},{5,1},{13,9},{2,6},{10,14},... | collective-permute-start | bytes 245768 | tf_op jit(solution)/shard_map/ppermute | solution.py:509
  5.7 0.7 %collective-permute-start.1 = (f32[10,8,256]{2,1,0:T(8,128)S(1)}, f32[10,8,256]{2,1,0:T(8,128)S(1)}, u32[]{:S(2)}, u32[]{:S(2)}) collective-permute-start(f32[10,8,256]{2,1,0:T(8,128)S(1)} %get-tuple-element.48), channel_id=1, source_target_pairs={{4,8},{8,4},{0,0},{12,12},{5,9},{9,5},{1,1},{13,13},{6,10},{10,6},... | collective-permute-start | bytes 245768 | tf_op jit(solution)/shard_map/ppermute | solution.py:509
  6.4 0.2 weights.1
  6.6 2.4 %network_forward.2 = (bf16[32,208,256]{2,1,0:T(8,128)(2,1)S(1)}, f32[32,256]{1,0:T(8,128)S(1)}) custom-call(bf16[10,64,256]{2,1,0:T(8,128)(2,1)S(1)} %get-tuple-element.49.feat, bf16[1280,256]{1,0:T(8,128)(2,1)S(1)} %get-tuple-element.55.w1, bf16[64,64]{1,0:T(8,128)(2,1)S(1)} %get-tuple-element.56.w2, bf16[64,64]{1,0:T(8,128)(2,1)S(1)} %get-tuple-element.57.w3, ...), custom_call_target="tpu_custom_call" | custom-call | flops 144703488 | bytes 3571712 | tf_op jit(solution)/shard_map/network_forward/pallas_call | solution.py:33
  9.0 0.0 collective-permute-done.row_first
  9.0 0.0 collective-permute-done.1.row_second
  9.0 0.2 col_slabs.1
  9.2 0.1 collective-permute-start.2
  9.3 0.7 %collective-permute-start.3 = (f32[80,128]{1,0:T(8,128)S(1)}, f32[80,128]{1,0:T(8,128)S(1)}, u32[]{:S(2)}, u32[]{:S(2)}) collective-permute-start(f32[80,128]{1,0:T(8,128)S(1)} %get-tuple-element.65), channel_id=1, source_target_pairs={{1,2},{2,1},{0,0},{3,3},{5,6},{6,5},{4,4},{7,7},{9,10},{10,9},{8,8... | collective-permute-start | bytes 122888 | tf_op jit(solution)/shard_map/ppermute | solution.py:509
  10.0 2.4 %network_forward.3 = (bf16[32,208,256]{2,1,0:T(8,128)(2,1)S(1)}, f32[32,256]{1,0:T(8,128)S(1)}) custom-call(bf16[10,64,256]{2,1,0:T(8,128)(2,1)S(1)} %get-tuple-element.49.feat, bf16[1280,256]{1,0:T(8,128)(2,1)S(1)} %get-tuple-element.55.w1, bf16[64,64]{1,0:T(8,128)(2,1)S(1)} %get-tuple-element.56.w2, bf16[64,64]{1,0:T(8,128)(2,1)S(1)} %get-tuple-element.57.w3, ...), custom_call_target="tpu_custom_call" | custom-call | flops 144703488 | bytes 3571712 | tf_op jit(solution)/shard_map/network_forward/pallas_call | solution.py:33
  12.4 0.0 collective-permute-done.2.col_first
  12.4 0.0 collective-permute-done.3.col_second
  12.4 0.0 copy-done
  12.4 3.8 %sweeps.1 = (f32[5,64,256]{2,1,0:T(8,128)S(1)}, f32[64,256]{1,0:T(8,128)S(1)}, f32[64,256]{1,0:T(8,128)S(1)}) custom-call(bf16[5,64,256]{2,1,0:T(8,128)(2,1)S(1)} %get-tuple-element.43.src, bf16[4,64,256]{2,1,0:T(8,128)(2,1)S(1)} %get-tuple-element.44.cpl, f32[64,256]{1,0:T(8,128)S(1)} %get-tuple-element.45.inv.inverse, ...), custom_call_target="tpu_custom_call" | custom-call | tf_op jit(solution)/shard_map/sweeps/pallas_call | solution.py:345
  16.2 5.4 %backward.1 = (f32[72,128]{1,0:T(8,128)S(1)}, f32[5,64,256]{2,1,0:T(8,128)}, f32[64,256]{1,0:T(8,128)}) custom-call(f32[5,64,256]{2,1,0:T(8,128)S(1)} %get-tuple-element.66.adj, f32[64,256]{1,0:T(8,128)S(1)} %get-tuple-element.67.beta, f32[64,256]{1,0:T(8,128)S(1)} %get-tuple-element.68.sens, bf16[64,64]{1,0:T(8,128)(2,1)S(1)} %get-tuple-element.51.wmid, ...), custom_call_target="tpu_custom_call" | custom-call | tf_op jit(solution)/shard_map/backward/pallas_call | solution.py:33
  21.6 2.9 %collective-permute-start.4 = (f32[72,128]{1,0:T(8,128)S(1)}, f32[72,128]{1,0:T(8,128)S(1)}, u32[]{:S(2)}, u32[]{:S(2)}) collective-permute-start(f32[72,128]{1,0:T(8,128)S(1)} %get-tuple-element.73), channel_id=1, source_target_pairs={{0,1},{1,0},{2,3},{3,2},{4,5},{5,4},{6,7},{7,6},{8,9},{9,8},{10,11... | collective-permute-start | bytes 110600 | tf_op jit(solution)/shard_map/ppermute | solution.py:495
  24.5 0.9 %collective-permute-done.4 = f32[72,128]{1,0:T(8,128)S(1)} collective-permute-done((f32[72,128]{1,0:T(8,128)S(1)}, f32[72,128]{1,0:T(8,128)S(1)}, u32[]{:S(2)}, u32[]{:S(2)}) %collective-permute-start.4) | collective-permute-done | bytes 36896 | tf_op jit(solution)/shard_map/ppermute | solution.py:495
  25.4 1.2 %collective-permute-start.5 = (f32[72,128]{1,0:T(8,128)S(1)}, f32[72,128]{1,0:T(8,128)S(1)}, u32[]{:S(2)}, u32[]{:S(2)}) collective-permute-start(f32[72,128]{1,0:T(8,128)S(1)} %add.6), channel_id=1, source_target_pairs={{0,2},{1,3},{2,0},{3,1},{4,6},{5,7},{6,4},{7,5},{8,10},{9,11},{10,... | collective-permute-start | bytes 110600 | tf_op jit(solution)/shard_map/ppermute | solution.py:495
  26.6 2.7 %collective-permute-done.5 = f32[72,128]{1,0:T(8,128)S(1)} collective-permute-done((f32[72,128]{1,0:T(8,128)S(1)}, f32[72,128]{1,0:T(8,128)S(1)}, u32[]{:S(2)}, u32[]{:S(2)}) %collective-permute-start.5) | collective-permute-done | bytes 36896 | tf_op jit(solution)/shard_map/ppermute | solution.py:495
  29.3 16.8 %all-gather = f32[288,128]{1,0:T(8,128)S(1)} all-gather(f32[72,128]{1,0:T(8,128)S(1)} %add.7), channel_id=2, replica_groups=mesh['case'=2,'gx'=4,'gy'=4] {'gx'}, dimensions={0}, use_global_device_ids=true | all-gather | bytes 184320 | tf_op jit(solution)/shard_map/all_gather | solution.py:497
  46.2 0.8 %clip.1 = (f32[10,64]{1,0:T(8,128)}, f32[64,64]{1,0:T(8,128)}, f32[64,64]{1,0:T(8,128)}, f32[1,64]{1,0:T(1,128)}, f32[3,64]{1,0:T(4,128)}) custom-call(f32[4,72,128]{2,1,0:T(8,128)S(1)} %bitcast.3), custom_call_target="tpu_custom_call" | custom-call | tf_op jit(solution)/shard_map/clip/pallas_call | solution.py:480
  (2 shorter events, 0.0 us)
Async XLA Ops:
  2.6 9.7 %copy-start = (f32[5,5]{1,0:T(8,128)S(1)}, f32[5,5]{1,0:T(8,128)}, u32[]{:S(2)}) copy-start(f32[5,5]{1,0:T(8,128)} %mix.1) | copy-start | bytes 304
  2.6 6.4 %collective-permute-start = (f32[10,8,256]{2,1,0:T(8,128)S(1)}, f32[10,8,256]{2,1,0:T(8,128)S(1)}, u32[]{:S(2)}, u32[]{:S(2)}) collective-permute-start(f32[10,8,256]{2,1,0:T(8,128)S(1)} %get-tuple-element.47), channel_id=1, source_target_pairs={{0,4},{8,12},{4,0},{12,8},{1,5},{9,13},{5,1},{13,9},{2,6},{10,14},... | collective-permute-start | bytes 245768 | tf_op jit(solution)/shard_map/ppermute | solution.py:509
  5.7 3.3 %collective-permute-start.1 = (f32[10,8,256]{2,1,0:T(8,128)S(1)}, f32[10,8,256]{2,1,0:T(8,128)S(1)}, u32[]{:S(2)}, u32[]{:S(2)}) collective-permute-start(f32[10,8,256]{2,1,0:T(8,128)S(1)} %get-tuple-element.48), channel_id=1, source_target_pairs={{4,8},{8,4},{0,0},{12,12},{5,9},{9,5},{1,1},{13,13},{6,10},{10,6},... | collective-permute-start | bytes 245768 | tf_op jit(solution)/shard_map/ppermute | solution.py:509
  9.2 3.1 %collective-permute-start.2 = (f32[80,128]{1,0:T(8,128)S(1)}, f32[80,128]{1,0:T(8,128)S(1)}, u32[]{:S(2)}, u32[]{:S(2)}) collective-permute-start(f32[80,128]{1,0:T(8,128)S(1)} %get-tuple-element.64), channel_id=1, source_target_pairs={{0,1},{2,3},{1,0},{3,2},{4,5},{6,7},{5,4},{7,6},{8,9},{10,11},{9,8... | collective-permute-start | bytes 122888 | tf_op jit(solution)/shard_map/ppermute | solution.py:509
  9.3 3.0 %collective-permute-start.3 = (f32[80,128]{1,0:T(8,128)S(1)}, f32[80,128]{1,0:T(8,128)S(1)}, u32[]{:S(2)}, u32[]{:S(2)}) collective-permute-start(f32[80,128]{1,0:T(8,128)S(1)} %get-tuple-element.65), channel_id=1, source_target_pairs={{1,2},{2,1},{0,0},{3,3},{5,6},{6,5},{4,4},{7,7},{9,10},{10,9},{8,8... | collective-permute-start | bytes 122888 | tf_op jit(solution)/shard_map/ppermute | solution.py:509
  21.6 3.8 %collective-permute-start.4 = (f32[72,128]{1,0:T(8,128)S(1)}, f32[72,128]{1,0:T(8,128)S(1)}, u32[]{:S(2)}, u32[]{:S(2)}) collective-permute-start(f32[72,128]{1,0:T(8,128)S(1)} %get-tuple-element.73), channel_id=1, source_target_pairs={{0,1},{1,0},{2,3},{3,2},{4,5},{5,4},{6,7},{7,6},{8,9},{9,8},{10,11... | collective-permute-start | bytes 110600 | tf_op jit(solution)/shard_map/ppermute | solution.py:495
  25.4 4.0 %collective-permute-start.5 = (f32[72,128]{1,0:T(8,128)S(1)}, f32[72,128]{1,0:T(8,128)S(1)}, u32[]{:S(2)}, u32[]{:S(2)}) collective-permute-start(f32[72,128]{1,0:T(8,128)S(1)} %add.6), channel_id=1, source_target_pairs={{0,2},{1,3},{2,0},{3,1},{4,6},{5,7},{6,4},{7,5},{8,10},{9,11},{10,... | collective-permute-start | bytes 110600 | tf_op jit(solution)/shard_map/ppermute | solution.py:495

commit v5 on v4

--- a/solution.py
+++ b/solution.py
@@ -184,7 +184,11 @@
     )
 
 
-def forward_kernel(first_row, feat, w1, w2, w3, cst, acts, beta, x1):
+def slope(act):
+    return 1.0 - act * act
+
+
+def forward_kernel(first_row, feat, w1, w2, w3, cst, acts, slopes, beta, x1):
     nf, _, cols = feat.shape
     hidden = w2.shape[0]
     step_rows, blk, per = hidden + 16, 16, 4
@@ -202,6 +206,7 @@
             for q in range(g * per, (g + 1) * per):
                 part = first[q * step_rows : (q + 1) * step_rows]
                 one = jnp.tanh(part[:hidden] + b1).astype(BF16)
+                slopes[start + q, 0:hidden] = slope(one.astype(F32))
                 acts[start + q, 0:hidden] = one
                 acts[start + q, 2 * hidden : 2 * hidden + 16] = part[hidden:].astype(BF16)
                 ones.append(one)
@@ -209,13 +214,16 @@
             twos = []
             for q in range(per):
                 two = jnp.tanh(second[:, q * cols : (q + 1) * cols] + b2).astype(BF16)
+                slopes[start + (g * per + q), hidden : 2 * hidden] = slope(two.astype(F32))
                 acts[start + (g * per + q), hidden : 2 * hidden] = two
                 twos.append(two)
             third = jnp.dot(w3[...], jnp.concatenate(twos, axis=1), preferred_element_type=F32)
             for q in range(per):
                 three = jnp.tanh(third[:, q * cols : (q + 1) * cols] + b3).astype(BF16)
                 acts[start + (g * per + q), 2 * hidden + 16 :] = three
-                lines.append(1.0 + jnp.sum(three.astype(F32) * wo, axis=0, keepdims=True))
+                three = three.astype(F32)
+                slopes[start + (g * per + q), 2 * hidden :] = wo * slope(three)
+                lines.append(1.0 + jnp.sum(three * wo, axis=0, keepdims=True))
         beta[pl.ds(start, blk), :] = jnp.concatenate(lines, axis=0)
 
 
@@ -227,7 +235,7 @@
     return on_chip(
         functools.partial(forward_kernel, first_row),
         [features, *prepared],
-        [((count, high, cols), BF16), ((count, cols), F32)],
+        [((count, high, cols), BF16), ((count, 3 * hidden, cols), F32), ((count, cols), F32)],
         [pltpu.VMEM((w1.shape[1], cols), BF16)],
         cost_estimate=pl.CostEstimate(
             flops=2 * count * cols * (nf + 2 * hidden) * hidden,
@@ -360,7 +368,7 @@
 
 
 def backward_kernel(
-    num_feat, adj, beta, sens, wmid, wtop, cst, acts_a, acts_b,
+    num_feat, adj, beta, sens, wmid, wtop, acts_a, slopes_a, acts_b, slopes_b,
     packed, adj_out, beta_out,
     sums, g_mid, g_top, g_in, sems,
 ):
@@ -387,9 +395,8 @@
     def outer(x, d):
         return lax.dot_general(x, d, NT, preferred_element_type=F32)
 
-    def block(acts, start, first_row):
+    def block(acts, slopes, start, first_row):
         rows_sens = sens[pl.ds(pl.multiple_of(first_row + start, blk), blk), :]
-        wo = across(cst[3], cols)
 
         def layer(lo, high):
             return joined([acts[start + q, lo:high] for q in range(blk)])
@@ -398,8 +405,7 @@
             raw = jnp.dot(weight, delta, preferred_element_type=F32)
             total, out = jnp.zeros((hidden, LANE), F32), []
             for q in range(blk):
-                act = acts[start + q, lo : lo + hidden].astype(F32)
-                d = raw[:, q * cols : (q + 1) * cols] * (1.0 - act * act)
+                d = raw[:, q * cols : (q + 1) * cols] * slopes[start + q, lo : lo + hidden]
                 total = total + fold(d)
                 out.append(d.astype(BF16))
             return joined(out), total
@@ -409,7 +415,7 @@
             act = acts[start + q, 2 * hidden + 16 :].astype(F32)
             sen = jnp.broadcast_to(rows_sens[q : q + 1], (hidden, cols))
             out_sum = out_sum + fold(act * sen)
-            d = sen * wo * (1.0 - act * act)
+            d = sen * slopes[start + q, 2 * hidden :]
             top_sum = top_sum + fold(d)
             d3.append(d.astype(BF16))
         d3 = joined(d3)
@@ -422,11 +428,11 @@
             sums[k] += part
 
     half = acts_a.shape[0]
-    for acts, first_row in ((acts_a, 0), (acts_b, half)):
+    for acts, slopes, first_row in ((acts_a, slopes_a, 0), (acts_b, slopes_b, half)):
 
         @pl.loop(0, acts.shape[0] // blk)
-        def _(i, acts=acts, first_row=first_row):
-            block(acts, pl.multiple_of(i * blk, blk), first_row)
+        def _(i, acts=acts, slopes=slopes, first_row=first_row):
+            block(acts, slopes, pl.multiple_of(i * blk, blk), first_row)
 
     packed[0:hidden, :] = joined([g_mid[...], g_top[...]])
     turned = jnp.transpose(joined([g_in[...], jnp.zeros((hidden, LANE - 16), F32)]))
@@ -440,11 +446,11 @@
         copy.wait()
 
 
-def backward(num_feat, adj, beta, sens, weight_mid, weight_top, cst, acts):
+def backward(num_feat, adj, beta, sens, weight_mid, weight_top, nets):
     hidden = weight_mid.shape[0]
     return on_chip(
         functools.partial(backward_kernel, num_feat),
-        [adj, beta, sens, weight_mid, weight_top, cst, *acts],
+        [adj, beta, sens, weight_mid, weight_top, *nets],
         [((hidden + SUB, LANE), F32)],
         [
             pltpu.VMEM((4, hidden, LANE), F32),
@@ -458,11 +464,9 @@
     )
 
 
-def clip_kernel(parts, gin, gmid, gtop, gout, gbias):
+def clip_kernel(summed, gin, gmid, gtop, gout, gbias):
     hidden = gmid.shape[0]
-    total = parts[0]
-    for k in range(1, parts.shape[0]):
-        total = total + parts[k]
+    total = summed[...]
     squares = jnp.sum(jnp.sum(total * total, axis=0, keepdims=True), axis=1, keepdims=True)
     total = total * (CLIP_NORM / jnp.maximum(jnp.sqrt(squares), CLIP_NORM))
     gmid[...] = total[:hidden, :hidden]
@@ -475,36 +479,42 @@
     gbias[...] = high[at + 1 : at + 4]
 
 
-def clip_all(parts, num_feat, hidden):
+def clip_all(summed, num_feat, hidden):
     shapes = [(num_feat, hidden), (hidden, hidden), (hidden, hidden), (1, hidden), (3, hidden)]
     return pl.pallas_call(
         clip_kernel,
         grid=(1,),
-        in_specs=[whole(parts.shape)],
+        in_specs=[whole(summed.shape)],
         out_specs=[whole(s) for s in shapes],
         out_shape=[jax.ShapeDtypeStruct(s, F32) for s in shapes],
         compiler_params=params(),
         name="clip",
-    )(parts)
-
-
-def parts_of_sum(packed):
-    count = lax.axis_size("gy")
-    step = 1
-    while step < count:
-        packed = packed + lax.ppermute(packed, "gy", [(i, i ^ step) for i in range(count)])
-        step *= 2
-    return lax.all_gather(packed, "gx")
+    )(summed)
+
+
+def sum_over_case(packed):
+    for axis, radix in (("gy", 2), ("gx", 4)):
+        count = lax.axis_size(axis)
+        step = 1
+        while step < count:
+            parts = [packed]
+            for k in range(1, min(radix, count // step)):
+                parts.append(lax.ppermute(packed, axis, [(i, i ^ (k * step)) for i in range(count)]))
+            while len(parts) > 1:
+                parts = [a + b for a, b in zip(parts[::2], parts[1::2])]
+            packed = parts[0]
+            step *= radix
+    return packed
 
 
 def swaps(first, second, axis):
     count = lax.axis_size(axis)
 
     def pairs(start):
-        low = range(start, count - 1, 2)
-        paired = [(i, i + 1) for i in low] + [(i + 1, i) for i in low]
-        alone = set(range(count)) - {i for i, _ in paired}
-        return paired + [(i, i) for i in sorted(alone)]
+        low = [(i, i + 1) for i in range(start, count - 1, 2)]
+        if count % 2 == 0 and start == 1:
+            low.append((0, count - 1))
+        return low + [(b, a) for a, b in low]
 
     return lax.ppermute(first, axis, pairs(0)), lax.ppermute(second, axis, pairs(1))
 
@@ -524,15 +534,15 @@
     row_halos = swaps(*row_slabs, "gx")
     prepared = prepare(weight_in, weight_mid, weight_top, wout, biases)
     half = rows // 32 * 16
-    acts_a, beta_a = forward(features, prepared, 0, half)
+    *net_a, beta_a = forward(features, prepared, 0, half)
     *row_halos, beta_a = lax.optimization_barrier((*row_halos, beta_a))
     col_halos = swaps(*col_slabs(source, coupling, inverse, row_halos), "gy")
-    acts_b, beta_b = forward(features, prepared, half, rows - half)
+    *net_b, beta_b = forward(features, prepared, half, rows - half)
     adj, sens, beta = sweeps(
         source, coupling, inverse, production, (beta_a, beta_b), (*row_halos, *col_halos), mixing
     )
-    packed, adjoint, beta = backward(num_feat, adj, beta, sens, weight_mid, weight_top, prepared[3], (acts_a, acts_b))
-    grad_in, grad_mid, grad_top, grad_out, grad_bias = clip_all(parts_of_sum(packed), num_feat, hidden)
+    packed, adjoint, beta = backward(num_feat, adj, beta, sens, weight_mid, weight_top, (*net_a, *net_b))
+    grad_in, grad_mid, grad_top, grad_out, grad_bias = clip_all(sum_over_case(packed), num_feat, hidden)
     return (adjoint, beta, grad_in, grad_mid, grad_top, grad_out.reshape(hidden), grad_bias)
 
 

time: 47.2 us -> 38.7 us (0.82)
  blocking collectives: 16.8 us -> 0 us
  waiting for transfers between devices: 3.59 us -> 8.19 us
  starting transfers between devices: 8.63 us -> 12.7 us
    all_gather x1 -> x0, blocking collectives: 16.8 us -> none  [parts_of_sum(): return lax.all_gather(packed, 'gx')]
    ppermute x2 -> x5, waiting for transfers between devices: 3.58 us -> 6.79 us  [sum_over_case(): lax.ppermute(packed, axis, [(i, i ^ k * step) for i in range(count)])]
    ppermute x2, starting transfers between devices: 1.32 us -> 4.08 us  [swaps(): lax.ppermute(second, axis, pairs(1))]
    ppermute x2, waiting for transfers between devices: 0.01 us -> 1.39 us  [swaps(): lax.ppermute(second, axis, pairs(1))]
    ppermute x2 -> x5, starting transfers between devices: 4.15 us -> 5.43 us  [sum_over_case(): lax.ppermute(packed, axis, [(i, i ^ k * step) for i in range(count)])]
  transfers between devices with their start and end apart: 6 -> 9, of which waited for: 2 -> 5; matrix products, arithmetic and copies ran while one was open for 0% -> 0% of each run, Pallas kernels for 11% -> 14%
where the time goes in v5:
time: 38.7 us; the launch traced here: 38.5 us
  Pallas kernels  16.9 us (44%)
  starting transfers between devices  12.7 us (33%)
  waiting for transfers between devices  8.19 us (21%)
  between operations  0.75 us (2%)
    pallas_call x6, Pallas kernels, on_chip(): pl.pallas_call(kernel, in_specs=[here] * len(operands) + [there] * len(fa...  12.3 us
    ppermute x5, waiting for transfers between devices, sum_over_case(): lax.ppermute(packed, axis, [(i, i ^ k * step) for i in range(count)])  6.79 us
    ppermute x5, starting transfers between devices, sum_over_case(): lax.ppermute(packed, axis, [(i, i ^ k * step) for i in range(count)])  5.43 us
    ppermute x2, starting transfers between devices, swaps(): lax.ppermute(second, axis, pairs(1))  4.08 us
    pallas_call x1, Pallas kernels, sweeps(): pl.pallas_call(sweep_kernel, in_specs=[near] * len(operands) + [pl.BlockS...  3.82 us
    ppermute x2, starting transfers between devices, swaps(): lax.ppermute(first, axis, pairs(0))  3.16 us
    ppermute x2, waiting for transfers between devices, swaps(): lax.ppermute(second, axis, pairs(1))  1.39 us
    pallas_call x1, Pallas kernels, clip_all(): pl.pallas_call(clip_kernel, grid=(1,), in_specs=[whole(summed.shape)], ou...  0.81 us
  transfers between devices with their start and end apart: 9, of which 5 were waited for; matrix products, arithmetic and copies ran while one was open for 0% of the time, Pallas kernels for 14%

profile of v5, /device:TPU:0, one launch (start us, length us, event | category | flops | bytes accessed | tf_op | source)
XLA Modules:
  0.0 38.5 jit_solution(3588537145456558208)
XLA Ops:
  0.6 0.0 copy-start
  0.6 2.0 %load.1 = (bf16[5,64,256]{2,1,0:T(8,128)(2,1)S(1)}, bf16[4,64,256]{2,1,0:T(8,128)(2,1)S(1)}, f32[64,256]{1,0:T(8,128)}, s32[64,256]{1,0:T(8,128)}, f32[64,256]{1...) custom-call(bf16[5,64,256]{2,1,0:T(8,128)(2,1)} %refs_0_.1, ...), custom_call_target="tpu_custom_call" | custom-call | tf_op jit(solution)/shard_map/load/pallas_call | solution.py:33
  2.6 3.1 %collective-permute-start = (f32[10,8,256]{2,1,0:T(8,128)S(1)}, f32[10,8,256]{2,1,0:T(8,128)S(1)}, u32[]{:S(2)}, u32[]{:S(2)}) collective-permute-start(f32[10,8,256]{2,1,0:T(8,128)S(1)} %get-tuple-element.49), channel_id=1, source_target_pairs={{0,4},{8,12},{4,0},{12,8},{1,5},{9,13},{5,1},{13,9},{2,6},{10,14},... | collective-permute-start | bytes 245768 | tf_op jit(solution)/shard_map/ppermute | solution.py:519
  5.7 2.5 %collective-permute-start.1 = (f32[10,8,256]{2,1,0:T(8,128)S(1)}, f32[10,8,256]{2,1,0:T(8,128)S(1)}, u32[]{:S(2)}, u32[]{:S(2)}) collective-permute-start(f32[10,8,256]{2,1,0:T(8,128)S(1)} %get-tuple-element.50), channel_id=1, source_target_pairs={{4,8},{0,12},{8,4},{12,0},{5,9},{1,13},{9,5},{13,1},{6,10},{2,14},... | collective-permute-start | bytes 245768 | tf_op jit(solution)/shard_map/ppermute | solution.py:519
  8.2 0.2 weights.1
  8.5 2.5 %network_forward.2 = (bf16[32,208,256]{2,1,0:T(8,128)(2,1)S(1)}, f32[32,192,256]{2,1,0:T(8,128)S(1)}, f32[32,256]{1,0:T(8,128)S(1)}) custom-call(bf16[10,64,256]{2,1,0:T(8,128)(2,1)S(1)} %get-tuple-element.51.feat, bf16[1280,256]{1,0:T(8,128)(2,1)S(1)} %get-tuple-element.57.w1, bf16[64,64]{1,0:T(8,128)(2,1)S(1)} %get-tuple-element.58.w2, ...), custom_call_target="tpu_custom_call" | custom-call | flops 144703488 | bytes 3571712 | tf_op jit(solution)/shard_map/network_forward/pallas_call | solution.py:33
  11.0 0.0 collective-permute-done.row_first
  11.0 1.4 %collective-permute-done.1.row_second = f32[10,8,256]{2,1,0:T(8,128)S(1)} collective-permute-done((f32[10,8,256]{2,1,0:T(8,128)S(1)}, f32[10,8,256]{2,1,0:T(8,128)S(1)}, u32[]{:S(2)}, u32[]{:S(2)}) %collective-permute-start.1) | collective-permute-done | bytes 81952 | tf_op jit(solution)/shard_map/ppermute | solution.py:519
  12.4 0.2 col_slabs.1
  12.6 0.1 collective-permute-start.2
  12.7 1.6 %collective-permute-start.3 = (f32[80,128]{1,0:T(8,128)S(1)}, f32[80,128]{1,0:T(8,128)S(1)}, u32[]{:S(2)}, u32[]{:S(2)}) collective-permute-start(f32[80,128]{1,0:T(8,128)S(1)} %get-tuple-element.67), channel_id=1, source_target_pairs={{1,2},{0,3},{2,1},{3,0},{5,6},{4,7},{6,5},{7,4},{9,10},{8,11},{10,... | collective-permute-start | bytes 122888 | tf_op jit(solution)/shard_map/ppermute | solution.py:519
  14.3 2.5 %network_forward.3 = (bf16[32,208,256]{2,1,0:T(8,128)(2,1)S(1)}, f32[32,192,256]{2,1,0:T(8,128)S(1)}, f32[32,256]{1,0:T(8,128)S(1)}) custom-call(bf16[10,64,256]{2,1,0:T(8,128)(2,1)S(1)} %get-tuple-element.51.feat, bf16[1280,256]{1,0:T(8,128)(2,1)S(1)} %get-tuple-element.57.w1, bf16[64,64]{1,0:T(8,128)(2,1)S(1)} %get-tuple-element.58.w2, ...), custom_call_target="tpu_custom_call" | custom-call | flops 144703488 | bytes 3571712 | tf_op jit(solution)/shard_map/network_forward/pallas_call | solution.py:33
  16.8 0.0 collective-permute-done.2.col_first
  16.8 0.0 collective-permute-done.3.col_second
  16.8 0.0 copy-done
  16.8 3.8 %sweeps.1 = (f32[5,64,256]{2,1,0:T(8,128)S(1)}, f32[64,256]{1,0:T(8,128)S(1)}, f32[64,256]{1,0:T(8,128)S(1)}) custom-call(bf16[5,64,256]{2,1,0:T(8,128)(2,1)S(1)} %get-tuple-element.45.src, bf16[4,64,256]{2,1,0:T(8,128)(2,1)S(1)} %get-tuple-element.46.cpl, f32[64,256]{1,0:T(8,128)S(1)} %get-tuple-element.47.inv.inverse, ...), custom_call_target="tpu_custom_call" | custom-call | tf_op jit(solution)/shard_map/sweeps/pallas_call | solution.py:353
  20.6 4.8 %backward.1 = (f32[72,128]{1,0:T(8,128)S(1)}, f32[5,64,256]{2,1,0:T(8,128)}, f32[64,256]{1,0:T(8,128)}) custom-call(f32[5,64,256]{2,1,0:T(8,128)S(1)} %get-tuple-element.68.adj, f32[64,256]{1,0:T(8,128)S(1)} %get-tuple-element.69.beta, f32[64,256]{1,0:T(8,128)S(1)} %get-tuple-element.70.sens, bf16[64,64]{1,0:T(8,128)(2,1)S(1)} %get-tuple-element.53.wmid, ...), custom_call_target="tpu_custom_call" | custom-call | tf_op jit(solution)/shard_map/backward/pallas_call | solution.py:33
  25.5 0.1 collective-permute-start.4
  25.6 1.1 %collective-permute-done.4 = f32[72,128]{1,0:T(8,128)S(1)} collective-permute-done((f32[72,128]{1,0:T(8,128)S(1)}, f32[72,128]{1,0:T(8,128)S(1)}, u32[]{:S(2)}, u32[]{:S(2)}) %collective-permute-start.4) | collective-permute-done | bytes 36896 | tf_op jit(solution)/shard_map/ppermute | solution.py:502
  26.8 0.9 %collective-permute-start.5 = (f32[72,128]{1,0:T(8,128)S(1)}, f32[72,128]{1,0:T(8,128)S(1)}, u32[]{:S(2)}, u32[]{:S(2)}) collective-permute-start(f32[72,128]{1,0:T(8,128)S(1)} %add.15), channel_id=1, source_target_pairs={{0,2},{1,3},{2,0},{3,1},{4,6},{5,7},{6,4},{7,5},{8,10},{9,11},{10,... | collective-permute-start | bytes 110600 | tf_op jit(solution)/shard_map/ppermute | solution.py:502
  27.7 3.0 %collective-permute-done.5 = f32[72,128]{1,0:T(8,128)S(1)} collective-permute-done((f32[72,128]{1,0:T(8,128)S(1)}, f32[72,128]{1,0:T(8,128)S(1)}, u32[]{:S(2)}, u32[]{:S(2)}) %collective-permute-start.5) | collective-permute-done | bytes 36896 | tf_op jit(solution)/shard_map/ppermute | solution.py:502
  30.7 2.1 %collective-permute-start.8 = (f32[72,128]{1,0:T(8,128)S(1)}, f32[72,128]{1,0:T(8,128)S(1)}, u32[]{:S(2)}, u32[]{:S(2)}) collective-permute-start(f32[72,128]{1,0:T(8,128)S(1)} %add.16), channel_id=1, source_target_pairs={{0,12},{4,8},{8,4},{12,0},{1,13},{5,9},{9,5},{13,1},{2,14},{6,10},... | collective-permute-start | bytes 110600 | tf_op jit(solution)/shard_map/ppermute | solution.py:502
  32.9 0.0 collective-permute-start.7
  32.9 2.3 %collective-permute-start.6 = (f32[72,128]{1,0:T(8,128)S(1)}, f32[72,128]{1,0:T(8,128)S(1)}, u32[]{:S(2)}, u32[]{:S(2)}) collective-permute-start(f32[72,128]{1,0:T(8,128)S(1)} %add.16), channel_id=1, source_target_pairs={{0,4},{4,0},{8,12},{12,8},{1,5},{5,1},{9,13},{13,9},{2,6},{6,2},{1... | collective-permute-start | bytes 110600 | tf_op jit(solution)/shard_map/ppermute | solution.py:502
  35.1 1.6 %collective-permute-done.8 = f32[72,128]{1,0:T(8,128)S(1)} collective-permute-done((f32[72,128]{1,0:T(8,128)S(1)}, f32[72,128]{1,0:T(8,128)S(1)}, u32[]{:S(2)}, u32[]{:S(2)}) %collective-permute-start.8) | collective-permute-done | bytes 36896 | tf_op jit(solution)/shard_map/ppermute | solution.py:502
  36.7 1.0 %collective-permute-done.7 = f32[72,128]{1,0:T(8,128)S(1)} collective-permute-done((f32[72,128]{1,0:T(8,128)S(1)}, f32[72,128]{1,0:T(8,128)S(1)}, u32[]{:S(2)}, u32[]{:S(2)}) %collective-permute-start.7) | collective-permute-done | bytes 36896 | tf_op jit(solution)/shard_map/ppermute | solution.py:502
  37.7 0.0 collective-permute-done.6
  37.7 0.8 %clip.1 = (f32[10,64]{1,0:T(8,128)}, f32[64,64]{1,0:T(8,128)}, f32[64,64]{1,0:T(8,128)}, f32[1,64]{1,0:T(1,128)}, f32[3,64]{1,0:T(4,128)}) custom-call(f32[72,128]{1,0:T(8,128)S(1)} %add_add_fusion.summed), custom_call_target="tpu_custom_call" | custom-call | tf_op jit(solution)/shard_map/clip/pallas_call | solution.py:484
  (3 shorter events, 0.0 us)
Async XLA Ops:
  0.6 16.2 %copy-start = (f32[5,5]{1,0:T(8,128)S(1)}, f32[5,5]{1,0:T(8,128)}, u32[]{:S(2)}) copy-start(f32[5,5]{1,0:T(8,128)} %mix.1) | copy-start | bytes 304
  2.6 8.3 %collective-permute-start = (f32[10,8,256]{2,1,0:T(8,128)S(1)}, f32[10,8,256]{2,1,0:T(8,128)S(1)}, u32[]{:S(2)}, u32[]{:S(2)}) collective-permute-start(f32[10,8,256]{2,1,0:T(8,128)S(1)} %get-tuple-element.49), channel_id=1, source_target_pairs={{0,4},{8,12},{4,0},{12,8},{1,5},{9,13},{5,1},{13,9},{2,6},{10,14},... | collective-permute-start | bytes 245768 | tf_op jit(solution)/shard_map/ppermute | solution.py:519
  5.7 6.6 %collective-permute-start.1 = (f32[10,8,256]{2,1,0:T(8,128)S(1)}, f32[10,8,256]{2,1,0:T(8,128)S(1)}, u32[]{:S(2)}, u32[]{:S(2)}) collective-permute-start(f32[10,8,256]{2,1,0:T(8,128)S(1)} %get-tuple-element.50), channel_id=1, source_target_pairs={{4,8},{0,12},{8,4},{12,0},{5,9},{1,13},{9,5},{13,1},{6,10},{2,14},... | collective-permute-start | bytes 245768 | tf_op jit(solution)/shard_map/ppermute | solution.py:519
  12.6 4.2 %collective-permute-start.2 = (f32[80,128]{1,0:T(8,128)S(1)}, f32[80,128]{1,0:T(8,128)S(1)}, u32[]{:S(2)}, u32[]{:S(2)}) collective-permute-start(f32[80,128]{1,0:T(8,128)S(1)} %get-tuple-element.66), channel_id=1, source_target_pairs={{0,1},{2,3},{1,0},{3,2},{4,5},{6,7},{5,4},{7,6},{8,9},{10,11},{9,8... | collective-permute-start | bytes 122888 | tf_op jit(solution)/shard_map/ppermute | solution.py:519
  12.7 4.1 %collective-permute-start.3 = (f32[80,128]{1,0:T(8,128)S(1)}, f32[80,128]{1,0:T(8,128)S(1)}, u32[]{:S(2)}, u32[]{:S(2)}) collective-permute-start(f32[80,128]{1,0:T(8,128)S(1)} %get-tuple-element.67), channel_id=1, source_target_pairs={{1,2},{0,3},{2,1},{3,0},{5,6},{4,7},{6,5},{7,4},{9,10},{8,11},{10,... | collective-permute-start | bytes 122888 | tf_op jit(solution)/shard_map/ppermute | solution.py:519
  25.5 1.3 %collective-permute-start.4 = (f32[72,128]{1,0:T(8,128)S(1)}, f32[72,128]{1,0:T(8,128)S(1)}, u32[]{:S(2)}, u32[]{:S(2)}) collective-permute-start(f32[72,128]{1,0:T(8,128)S(1)} %get-tuple-element.77), channel_id=1, source_target_pairs={{0,1},{1,0},{2,3},{3,2},{4,5},{5,4},{6,7},{7,6},{8,9},{9,8},{10,11... | collective-permute-start | bytes 110600 | tf_op jit(solution)/shard_map/ppermute | solution.py:502
  26.8 4.0 %collective-permute-start.5 = (f32[72,128]{1,0:T(8,128)S(1)}, f32[72,128]{1,0:T(8,128)S(1)}, u32[]{:S(2)}, u32[]{:S(2)}) collective-permute-start(f32[72,128]{1,0:T(8,128)S(1)} %add.15), channel_id=1, source_target_pairs={{0,2},{1,3},{2,0},{3,1},{4,6},{5,7},{6,4},{7,5},{8,10},{9,11},{10,... | collective-permute-start | bytes 110600 | tf_op jit(solution)/shard_map/ppermute | solution.py:502
  30.7 6.0 %collective-permute-start.8 = (f32[72,128]{1,0:T(8,128)S(1)}, f32[72,128]{1,0:T(8,128)S(1)}, u32[]{:S(2)}, u32[]{:S(2)}) collective-permute-start(f32[72,128]{1,0:T(8,128)S(1)} %add.16), channel_id=1, source_target_pairs={{0,12},{4,8},{8,4},{12,0},{1,13},{5,9},{9,5},{13,1},{2,14},{6,10},... | collective-permute-start | bytes 110600 | tf_op jit(solution)/shard_map/ppermute | solution.py:502
  32.9 4.9 %collective-permute-start.7 = (f32[72,128]{1,0:T(8,128)S(1)}, f32[72,128]{1,0:T(8,128)S(1)}, u32[]{:S(2)}, u32[]{:S(2)}) collective-permute-start(f32[72,128]{1,0:T(8,128)S(1)} %add.16), channel_id=1, source_target_pairs={{0,8},{4,12},{8,0},{12,4},{1,9},{5,13},{9,1},{13,5},{2,10},{6,14},... | collective-permute-start | bytes 110600 | tf_op jit(solution)/shard_map/ppermute | solution.py:502
  32.9 4.9 %collective-permute-start.6 = (f32[72,128]{1,0:T(8,128)S(1)}, f32[72,128]{1,0:T(8,128)S(1)}, u32[]{:S(2)}, u32[]{:S(2)}) collective-permute-start(f32[72,128]{1,0:T(8,128)S(1)} %add.16), channel_id=1, source_target_pairs={{0,4},{4,0},{8,12},{12,8},{1,5},{5,1},{9,13},{13,9},{2,6},{6,2},{1... | collective-permute-start | bytes 110600 | tf_op jit(solution)/shard_map/ppermute | solution.py:502

commit v6 on v5

--- a/solution.py
+++ b/solution.py
@@ -246,8 +246,8 @@
     )
 
 
-def tile_at(ref, lead, t, k):
-    return ref[lead + (slice(t * SUB, (t + 1) * SUB), slice(k * LANE, (k + 1) * LANE))]
+def span(t, k):
+    return (slice(t * SUB, (t + 1) * SUB), slice(k * LANE, (k + 1) * LANE))
 
 
 class Shifts:
@@ -257,38 +257,33 @@
         lane = lax.broadcasted_iota(jnp.int32, (SUB, LANE), 1)
         self.first_sub, self.last_sub = sub == 0, sub == SUB - 1
         self.first_lane, self.last_lane = lane == 0, lane == LANE - 1
+        self.all = (self.above, self.below, self.left, self.right)
 
     def above(self, ref, lead, t, k):
-        here, other = tile_at(ref, lead, t, k), tile_at(ref, lead, max(t - 1, 0), k)
+        here, other = ref[lead + span(t, k)], ref[lead + span(max(t - 1, 0), k)]
         return pltpu.roll(jnp.where(self.last_sub, other, here), 1, 0)
 
     def below(self, ref, lead, t, k):
-        here, other = tile_at(ref, lead, t, k), tile_at(ref, lead, min(t + 1, self.tiles - 1), k)
+        here, other = ref[lead + span(t, k)], ref[lead + span(min(t + 1, self.tiles - 1), k)]
         return pltpu.roll(jnp.where(self.first_sub, other, here), SUB - 1, 0)
 
     def left(self, ref, lead, t, k):
-        here, other = tile_at(ref, lead, t, k), tile_at(ref, lead, t, (k - 1) % self.lanes)
+        here, other = ref[lead + span(t, k)], ref[lead + span(t, (k - 1) % self.lanes)]
         return pltpu.roll(jnp.where(self.last_lane, other, here), 1, 1)
 
     def right(self, ref, lead, t, k):
-        here, other = tile_at(ref, lead, t, k), tile_at(ref, lead, t, (k + 1) % self.lanes)
+        here, other = ref[lead + span(t, k)], ref[lead + span(t, (k + 1) % self.lanes)]
         return pltpu.roll(jnp.where(self.first_lane, other, here), LANE - 1, 1)
 
 
-def sweep_kernel(
-    src, cpl, inverse, prod, beta_a, beta_b, row_first, row_second, col_first, col_second, mix,
-    adj_out, sens, beta,
-    raw, src_x, cpl_x, adj_a, adj_b,
-):
+def extend(src, cpl, inverse, row_halos, col_halos, shifts, raw, src_x, cpl_x):
     nv, rows, cols = src.shape
     nc = cpl.shape[0]
     tall = rows + 2 * EDGE
-    tiles, lanes = tall // SUB, cols // LANE + 1
-    shifts = Shifts(tiles, lanes)
     inner = slice(EDGE, EDGE + rows)
     lane = lax.broadcasted_iota(jnp.int32, (tall, LANE), 1)
     from_east, from_west = lane < EDGE, lane >= LANE - EDGE
-    west, east = ordered("gy", col_first[...], col_second[...])
+    west, east = ordered("gy", *(x[...] for x in col_halos))
     for f in range(nv + nc + 1):
         if f < nv:
             raw[f, inner, 0:cols] = src[f].astype(F32)
@@ -296,94 +291,60 @@
             raw[f, inner, 0:cols] = cpl[f - nv].astype(F32)
         else:
             raw[f, inner, 0:cols] = inverse[...]
-        north, south = ordered("gx", row_first[f], row_second[f])
+        north, south = ordered("gx", *(x[f] for x in row_halos))
         raw[f, 0:EDGE, 0:cols] = north
         raw[f, EDGE + rows :, 0:cols] = south
         e = pltpu.roll(east, (LANE - EDGE * f) % LANE, 1)
         w = pltpu.roll(west, (LANE - EDGE - EDGE * f) % LANE, 1)
         raw[f, :, cols:] = jnp.where(from_east, e, jnp.where(from_west, w, 0.0))
-
-    moves = (shifts.above, shifts.below, shifts.left, shifts.right)
-    for t in range(tiles):
-        for k in range(lanes):
-            at = (slice(t * SUB, (t + 1) * SUB), slice(k * LANE, (k + 1) * LANE))
-            inv = tile_at(raw, (nv + nc,), t, k)
+    for t in range(shifts.tiles):
+        for k in range(shifts.lanes):
+            inv = raw[(nv + nc,) + span(t, k)]
             for v in range(nv):
-                src_x[(v,) + at] = inv * tile_at(raw, (v,), t, k)
+                src_x[(v,) + span(t, k)] = inv * raw[(v,) + span(t, k)]
             for d in range(nc):
-                cpl_x[(d,) + at] = inv * moves[d](raw, (nv + d,), t, k)
-
-    def sweep(old, new, last):
-        for t in range(1, tiles - 1) if last else range(tiles):
-            for k in range(lanes - 1) if last else range(lanes):
-                at = (slice(t * SUB, (t + 1) * SUB), slice(k * LANE, (k + 1) * LANE))
-                couple = [cpl_x[(d,) + at] for d in range(nc)]
-                total = [src_x[(a,) + at] for a in range(nv)]
-                for b in range(nv):
-                    inc = couple[0] * moves[0](old, (b,), t, k)
-                    for d in range(1, nc):
-                        inc = inc + couple[d] * moves[d](old, (b,), t, k)
-                    total = [total[a] + mix[b, a] * inc for a in range(nv)]
+                cpl_x[(d,) + span(t, k)] = inv * shifts.all[d](raw, (nv + d,), t, k)
+
+
+def adjoint_kernel(
+    num_feat, src, cpl, inverse, prod, beta_a, beta_b, row_first, row_second, col_first, col_second,
+    wmid, wtop, acts_a, slopes_a, acts_b, slopes_b, mix,
+    packed, adj_out, beta_out,
+    raw, src_x, cpl_x, adj, done, sums, g_mid, g_top, g_in, sems,
+):
+    nv, rows, cols = src.shape
+    nc = cpl.shape[0]
+    hidden, blk = wmid.shape[0], SUB
+    half = beta_a.shape[0]
+    tiles, lanes = (rows + 2 * EDGE) // SUB, cols // LANE + 1
+    copies = [
+        pltpu.make_async_copy(beta_a, beta_out.at[0:half], sems.at[0]),
+        pltpu.make_async_copy(beta_b, beta_out.at[half:rows], sems.at[1]),
+        pltpu.make_async_copy(done, adj_out, sems.at[2]),
+    ]
+    copies[0].start()
+    copies[1].start()
+    shifts = Shifts(tiles, lanes)
+    extend(
+        src, cpl, inverse, (row_first, row_second), (col_first, col_second), shifts, raw, src_x, cpl_x
+    )
+
+    def sweep(number, t):
+        last = number == SWEEPS
+        for k in range(lanes - 1 if last else lanes):
+            couple = [cpl_x[(d,) + span(t, k)] for d in range(nc)]
+            total = [src_x[(a,) + span(t, k)] for a in range(nv)]
+            for b in range(nv):
+                old, lead = (src_x, (b,)) if number == 1 else (adj, (number - 2, b))
+                inc = couple[0] * shifts.all[0](old, lead, t, k)
+                for d in range(1, nc):
+                    inc = inc + couple[d] * shifts.all[d](old, lead, t, k)
+                total = [total[a] + mix[b, a] * inc for a in range(nv)]
+            for a in range(nv):
                 if last:
-                    at = (slice((t - 1) * SUB, t * SUB), at[1])
-                for a in range(nv):
-                    new[(a,) + at] = total[a]
-
-    sweep(src_x, adj_a, False)
-
-    @pl.loop(0, (SWEEPS - 2) // 2)
-    def _(i):
-        sweep(adj_a, adj_b, False)
-        sweep(adj_b, adj_a, False)
-
-    sweep(adj_a, adj_out, True)
-    half = beta_a.shape[0]
-    beta[0:half] = beta_a[...]
-    beta[half:] = beta_b[...]
-    sens[...] = adj_out[nv - 1] * prod[...] + REG_WEIGHT * (beta[...] - 1.0)
-
-
-def sweeps(source, coupling, inverse, production, betas, halos, mixing):
-    nv, rows, cols = source.shape
-    nc = coupling.shape[0]
-    tall, wide = rows + 2 * EDGE, cols + LANE
-    near = pl.BlockSpec(memory_space=pltpu.VMEM)
-    operands = [source, coupling, inverse, production, *betas, *halos]
-    flat = ((rows, cols), F32)
-    return pl.pallas_call(
-        sweep_kernel,
-        in_specs=[near] * len(operands) + [pl.BlockSpec(memory_space=pltpu.SMEM)],
-        out_specs=[near] * 3,
-        out_shape=[pltpu.VMEM((nv, rows, cols), F32), pltpu.VMEM(*flat), pltpu.VMEM(*flat)],
-        scratch_shapes=[
-            pltpu.VMEM((nv + nc + 1, tall, wide), F32),
-            pltpu.VMEM((nv, tall, wide), F32),
-            pltpu.VMEM((nc, tall, wide), F32),
-            pltpu.VMEM((nv, tall, wide), F32),
-            pltpu.VMEM((nv, tall, wide), F32),
-        ],
-        compiler_params=params(),
-        name="sweeps",
-    )(*operands, mixing)
-
-
-def backward_kernel(
-    num_feat, adj, beta, sens, wmid, wtop, acts_a, slopes_a, acts_b, slopes_b,
-    packed, adj_out, beta_out,
-    sums, g_mid, g_top, g_in, sems,
-):
-    out_copies = [
-        pltpu.make_async_copy(adj, adj_out, sems.at[0]),
-        pltpu.make_async_copy(beta, beta_out, sems.at[1]),
-    ]
-    for copy in out_copies:
-        copy.start()
-    blk, cols = 8, sens.shape[1]
-    hidden = wmid.shape[0]
-    sums[...] = jnp.zeros(sums.shape, F32)
-    g_mid[...] = jnp.zeros(g_mid.shape, F32)
-    g_top[...] = jnp.zeros(g_top.shape, F32)
-    g_in[...] = jnp.zeros(g_in.shape, F32)
+                    done[(a,) + span(t - EDGE // SUB, k)] = total[a]
+                else:
+                    adj[(number - 1, a) + span(t, k)] = total[a]
 
     def fold(x):
         parts = [x[:, k * LANE : (k + 1) * LANE] for k in range(cols // LANE)]
@@ -395,17 +356,22 @@
     def outer(x, d):
         return lax.dot_general(x, d, NT, preferred_element_type=F32)
 
-    def block(acts, slopes, start, first_row):
-        rows_sens = sens[pl.ds(pl.multiple_of(first_row + start, blk), blk), :]
+    def backward(first):
+        if first < half:
+            acts, slopes, beta, start = acts_a, slopes_a, beta_a, first
+        else:
+            acts, slopes, beta, start = acts_b, slopes_b, beta_b, first - half
+        here = slice(first, first + blk)
+        sens = done[nv - 1, here] * prod[here] + REG_WEIGHT * (beta[start : start + blk] - 1.0)
 
         def layer(lo, high):
             return joined([acts[start + q, lo:high] for q in range(blk)])
 
         def behind(weight, delta, lo):
-            raw = jnp.dot(weight, delta, preferred_element_type=F32)
+            product = jnp.dot(weight, delta, preferred_element_type=F32)
             total, out = jnp.zeros((hidden, LANE), F32), []
             for q in range(blk):
-                d = raw[:, q * cols : (q + 1) * cols] * slopes[start + q, lo : lo + hidden]
+                d = product[:, q * cols : (q + 1) * cols] * slopes[start + q, lo : lo + hidden]
                 total = total + fold(d)
                 out.append(d.astype(BF16))
             return joined(out), total
@@ -413,26 +379,34 @@
         out_sum, top_sum, d3 = jnp.zeros((hidden, LANE), F32), jnp.zeros((hidden, LANE), F32), []
         for q in range(blk):
             act = acts[start + q, 2 * hidden + 16 :].astype(F32)
-            sen = jnp.broadcast_to(rows_sens[q : q + 1], (hidden, cols))
+            sen = jnp.broadcast_to(sens[q : q + 1], (hidden, cols))
             out_sum = out_sum + fold(act * sen)
             d = sen * slopes[start + q, 2 * hidden :]
             top_sum = top_sum + fold(d)
             d3.append(d.astype(BF16))
         d3 = joined(d3)
         d2, mid_sum = behind(wtop[...], d3, hidden)
-        g_top[...] += outer(layer(hidden, 2 * hidden), d3)
         d1, in_sum = behind(wmid[...], d2, 0)
-        g_mid[...] += outer(layer(0, hidden), d2)
-        g_in[...] += outer(d1, layer(2 * hidden, 2 * hidden + 16))
-        for k, part in enumerate((out_sum, in_sum, mid_sum, top_sum)):
-            sums[k] += part
-
-    half = acts_a.shape[0]
-    for acts, slopes, first_row in ((acts_a, slopes_a, 0), (acts_b, slopes_b, half)):
-
-        @pl.loop(0, acts.shape[0] // blk)
-        def _(i, acts=acts, slopes=slopes, first_row=first_row):
-            block(acts, slopes, pl.multiple_of(i * blk, blk), first_row)
+        new = (
+            (g_top, outer(layer(hidden, 2 * hidden), d3)),
+            (g_mid, outer(layer(0, hidden), d2)),
+            (g_in, outer(d1, layer(2 * hidden, 2 * hidden + 16))),
+            *((sums.at[k], part) for k, part in enumerate((out_sum, in_sum, mid_sum, top_sum))),
+        )
+        for ref, part in new:
+            ref[...] = part if first == 0 else ref[...] + part
+
+    for number in range(1, SWEEPS):
+        for t in range(SWEEPS + 1 - number):
+            sweep(number, t)
+    for t in range(1, tiles - 1):
+        for number in range(1, SWEEPS + 1):
+            if t + SWEEPS - number < tiles:
+                sweep(number, t + SWEEPS - number)
+        if t > 1:
+            backward((t - 2) * blk)
+    copies[2].start()
+    backward(rows - blk)
 
     packed[0:hidden, :] = joined([g_mid[...], g_top[...]])
     turned = jnp.transpose(joined([g_in[...], jnp.zeros((hidden, LANE - 16), F32)]))
@@ -442,26 +416,41 @@
         line = jnp.sum(jnp.transpose(sums[k]), axis=0, keepdims=True)
         tail = tail + jnp.where(row == k + num_feat - SUB, jnp.broadcast_to(line, (SUB, hidden)), 0.0)
     packed[hidden : hidden + SUB, :] = joined([turned[0:SUB], tail])
-    for copy in out_copies:
+    for copy in copies:
         copy.wait()
 
 
-def backward(num_feat, adj, beta, sens, weight_mid, weight_top, nets):
-    hidden = weight_mid.shape[0]
-    return on_chip(
-        functools.partial(backward_kernel, num_feat),
-        [adj, beta, sens, weight_mid, weight_top, *nets],
-        [((hidden + SUB, LANE), F32)],
-        [
+def sweeps_and_backward(num_feat, source, coupling, inverse, production, betas, halos, weights, nets, mixing):
+    nv, rows, cols = source.shape
+    nc = coupling.shape[0]
+    hidden = weights[0].shape[0]
+    tall, wide = rows + 2 * EDGE, cols + LANE
+    near, far = pl.BlockSpec(memory_space=pltpu.VMEM), pl.BlockSpec(memory_space=pltpu.HBM)
+    operands = [source, coupling, inverse, production, *betas, *halos, *weights, *nets]
+    return pl.pallas_call(
+        functools.partial(adjoint_kernel, num_feat),
+        in_specs=[near] * len(operands) + [pl.BlockSpec(memory_space=pltpu.SMEM)],
+        out_specs=[near, far, far],
+        out_shape=[
+            pltpu.VMEM((hidden + SUB, LANE), F32),
+            pltpu.HBM((nv, rows, cols), F32),
+            pltpu.HBM((rows, cols), F32),
+        ],
+        scratch_shapes=[
+            pltpu.VMEM((nv + nc + 1, tall, wide), F32),
+            pltpu.VMEM((nv, tall, wide), F32),
+            pltpu.VMEM((nc, tall, wide), F32),
+            pltpu.VMEM((SWEEPS - 1, nv, tall, wide), F32),
+            pltpu.VMEM((nv, rows, cols), F32),
             pltpu.VMEM((4, hidden, LANE), F32),
             pltpu.VMEM((hidden, hidden), F32),
             pltpu.VMEM((hidden, hidden), F32),
             pltpu.VMEM((hidden, 16), F32),
-            pltpu.SemaphoreType.DMA((2,)),
+            pltpu.SemaphoreType.DMA((3,)),
         ],
-        far_outs=[like(adj), like(beta)],
-        name="backward",
-    )
+        compiler_params=params(),
+        name="sweeps_backward",
+    )(*operands, mixing)
 
 
 def clip_kernel(summed, gin, gmid, gtop, gout, gbias):
@@ -507,16 +496,31 @@
     return packed
 
 
-def swaps(first, second, axis):
-    count = lax.axis_size(axis)
-
-    def pairs(start):
+def row_swaps(first, second):
+    num_x, num_y = lax.axis_size("gx"), lax.axis_size("gy")
+    out = []
+    for start, slab in ((0, first), (1, second)):
+        partner = {}
+        for i in range(num_x):
+            j = i + 1 if i % 2 == start else i - 1
+            for y in range(num_y):
+                if 0 <= j < num_x:
+                    partner[i * num_y + y] = j * num_y + y
+                elif num_y % 2 == 0:
+                    partner[i * num_y + y] = i * num_y + (y ^ 1)
+        out.append(lax.ppermute(slab, ("gx", "gy"), sorted(partner.items())))
+    return out
+
+
+def col_swaps(first, second):
+    count = lax.axis_size("gy")
+    out = []
+    for start, slab in ((0, first), (1, second)):
         low = [(i, i + 1) for i in range(start, count - 1, 2)]
         if count % 2 == 0 and start == 1:
             low.append((0, count - 1))
-        return low + [(b, a) for a, b in low]
-
-    return lax.ppermute(first, axis, pairs(0)), lax.ppermute(second, axis, pairs(1))
+        out.append(lax.ppermute(slab, "gy", low + [(b, a) for a, b in low]))
+    return out
 
 
 def shards(
@@ -531,17 +535,17 @@
     ])
     source, coupling, _, _, production, features, weight_in, weight_mid, weight_top, wout, biases = loaded[:11]
     inverse, *row_slabs = loaded[11:]
-    row_halos = swaps(*row_slabs, "gx")
+    row_halos = row_swaps(*row_slabs)
     prepared = prepare(weight_in, weight_mid, weight_top, wout, biases)
-    half = rows // 32 * 16
+    half = rows - 32
     *net_a, beta_a = forward(features, prepared, 0, half)
     *row_halos, beta_a = lax.optimization_barrier((*row_halos, beta_a))
-    col_halos = swaps(*col_slabs(source, coupling, inverse, row_halos), "gy")
+    col_halos = col_swaps(*col_slabs(source, coupling, inverse, row_halos))
     *net_b, beta_b = forward(features, prepared, half, rows - half)
-    adj, sens, beta = sweeps(
-        source, coupling, inverse, production, (beta_a, beta_b), (*row_halos, *col_halos), mixing
+    packed, adjoint, beta = sweeps_and_backward(
+        num_feat, source, coupling, inverse, production, (beta_a, beta_b), (*row_halos, *col_halos),
+        (weight_mid, weight_top), (*net_a, *net_b), mixing,
     )
-    packed, adjoint, beta = backward(num_feat, adj, beta, sens, weight_mid, weight_top, (*net_a, *net_b))
     grad_in, grad_mid, grad_top, grad_out, grad_bias = clip_all(sum_over_case(packed), num_feat, hidden)
     return (adjoint, beta, grad_in, grad_mid, grad_top, grad_out.reshape(hidden), grad_bias)
 

time: 38.7 us -> 36.2 us (0.935)
  starting transfers between devices: 12.7 us -> 11.3 us
  waiting for transfers between devices: 8.19 us -> 7.67 us
  Pallas kernels: 16.9 us -> 16.4 us
    pallas_call x6 -> x5, Pallas kernels: 12.3 us -> 7.45 us  [on_chip(): pl.pallas_call(kernel, in_specs=[here] * len(operands) + [there] * len(fa...]
    pallas_call x1, Pallas kernels: 3.82 us -> 8.12 us  [sweeps_and_backward(): pl.pallas_call(functools.partial(adjoint_kernel, num_feat), in_specs=[nea...]
    ppermute x4, starting transfers between devices: 7.24 us -> 4.84 us  [the longest x2 3.09 us: row_swaps(): out.append(lax.ppermute(slab, ('gx', 'gy'), sorted(partner.items())))]
    ppermute x4, waiting for transfers between devices: 1.4 us -> 0.01 us  [the longest x2 0.01 us: row_swaps(): out.append(lax.ppermute(slab, ('gx', 'gy'), sorted(partner.items())))]
    ppermute x5, starting transfers between devices: 5.43 us -> 6.44 us  [sum_over_case(): lax.ppermute(packed, axis, [(i, i ^ k * step) for i in range(count)])]
    ppermute x5, waiting for transfers between devices: 6.79 us -> 7.66 us  [sum_over_case(): lax.ppermute(packed, axis, [(i, i ^ k * step) for i in range(count)])]
  transfers between devices with their start and end apart: 9 -> 9, of which waited for: 5 -> 5; matrix products, arithmetic and copies ran while one was open for 0% -> 0% of each run, Pallas kernels for 14% -> 15%
where the time goes in v6:
time: 36.2 us; the launch traced here: 36.1 us
  Pallas kernels  16.4 us (45%)
  starting transfers between devices  11.3 us (31%)
  waiting for transfers between devices  7.67 us (21%)
  between operations  0.74 us (2%)
    pallas_call x1, Pallas kernels, sweeps_and_backward(): pl.pallas_call(functools.partial(adjoint_kernel, num_feat), in_specs=[nea...  8.12 us
    ppermute x5, waiting for transfers between devices, sum_over_case(): lax.ppermute(packed, axis, [(i, i ^ k * step) for i in range(count)])  7.66 us
    pallas_call x5, Pallas kernels, on_chip(): pl.pallas_call(kernel, in_specs=[here] * len(operands) + [there] * len(fa...  7.45 us
    ppermute x5, starting transfers between devices, sum_over_case(): lax.ppermute(packed, axis, [(i, i ^ k * step) for i in range(count)])  6.44 us
    ppermute x2, starting transfers between devices, row_swaps(): out.append(lax.ppermute(slab, ('gx', 'gy'), sorted(partner.items())))  3.09 us
    ppermute x2, starting transfers between devices, col_swaps(): out.append(lax.ppermute(slab, 'gy', low + [(b, a) for a, b in low]))  1.75 us
    pallas_call x1, Pallas kernels, clip_all(): pl.pallas_call(clip_kernel, grid=(1,), in_specs=[whole(summed.shape)], ou...  0.81 us
  transfers between devices with their start and end apart: 9, of which 5 were waited for; matrix products, arithmetic and copies ran while one was open for 0% of the time, Pallas kernels for 15%

profile of v6, /device:TPU:0, one launch (start us, length us, event | category | flops | bytes accessed | tf_op | source)
XLA Modules:
  0.0 36.1 jit_solution(15547560835382282547)
XLA Ops:
  0.6 0.0 copy-start
  0.6 2.0 %load.1 = (bf16[5,64,256]{2,1,0:T(8,128)(2,1)S(1)}, bf16[4,64,256]{2,1,0:T(8,128)(2,1)S(1)}, f32[64,256]{1,0:T(8,128)}, s32[64,256]{1,0:T(8,128)}, f32[64,256]{1...) custom-call(bf16[5,64,256]{2,1,0:T(8,128)(2,1)} %refs_0_.1, ...), custom_call_target="tpu_custom_call" | custom-call | tf_op jit(solution)/shard_map/load/pallas_call | solution.py:33
  2.6 3.1 %collective-permute-start = (f32[10,8,256]{2,1,0:T(8,128)S(1)}, f32[10,8,256]{2,1,0:T(8,128)S(1)}, u32[]{:S(2)}, u32[]{:S(2)}) collective-permute-start(f32[10,8,256]{2,1,0:T(8,128)S(1)} %get-tuple-element.46), channel_id=1, source_target_pairs={{0,4},{1,5},{2,6},{3,7},{4,0},{5,1},{6,2},{7,3},{8,12},{9,13},{10,... | collective-permute-start | bytes 245768 | tf_op jit(solution)/shard_map/ppermute | solution.py:511
  5.7 0.0 collective-permute-start.1
  5.7 0.2 weights.1
  6.0 2.5 %network_forward.2 = (bf16[32,208,256]{2,1,0:T(8,128)(2,1)S(1)}, f32[32,192,256]{2,1,0:T(8,128)S(1)}, f32[32,256]{1,0:T(8,128)S(1)}) custom-call(bf16[10,64,256]{2,1,0:T(8,128)(2,1)S(1)} %get-tuple-element.48.feat, bf16[1280,256]{1,0:T(8,128)(2,1)S(1)} %get-tuple-element.54.w1, bf16[64,64]{1,0:T(8,128)(2,1)S(1)} %get-tuple-element.55.w2, ...), custom_call_target="tpu_custom_call" | custom-call | flops 144703488 | bytes 3571712 | tf_op jit(solution)/shard_map/network_forward/pallas_call | solution.py:33
  8.5 0.0 collective-permute-done.row_first
  8.5 0.0 collective-permute-done.1.row_second
  8.5 0.2 col_slabs.1
  8.7 0.6 %collective-permute-start.2 = (f32[80,128]{1,0:T(8,128)S(1)}, f32[80,128]{1,0:T(8,128)S(1)}, u32[]{:S(2)}, u32[]{:S(2)}) collective-permute-start(f32[80,128]{1,0:T(8,128)S(1)} %get-tuple-element.63), channel_id=1, source_target_pairs={{0,1},{2,3},{1,0},{3,2},{4,5},{6,7},{5,4},{7,6},{8,9},{10,11},{9,8... | collective-permute-start | bytes 122888 | tf_op jit(solution)/shard_map/ppermute | solution.py:522
  9.3 1.2 %collective-permute-start.3 = (f32[80,128]{1,0:T(8,128)S(1)}, f32[80,128]{1,0:T(8,128)S(1)}, u32[]{:S(2)}, u32[]{:S(2)}) collective-permute-start(f32[80,128]{1,0:T(8,128)S(1)} %get-tuple-element.64), channel_id=1, source_target_pairs={{1,2},{0,3},{2,1},{3,0},{5,6},{4,7},{6,5},{7,4},{9,10},{8,11},{10,... | collective-permute-start | bytes 122888 | tf_op jit(solution)/shard_map/ppermute | solution.py:522
  10.5 2.5 %network_forward.3 = (bf16[32,208,256]{2,1,0:T(8,128)(2,1)S(1)}, f32[32,192,256]{2,1,0:T(8,128)S(1)}, f32[32,256]{1,0:T(8,128)S(1)}) custom-call(bf16[10,64,256]{2,1,0:T(8,128)(2,1)S(1)} %get-tuple-element.48.feat, bf16[1280,256]{1,0:T(8,128)(2,1)S(1)} %get-tuple-element.54.w1, bf16[64,64]{1,0:T(8,128)(2,1)S(1)} %get-tuple-element.55.w2, ...), custom_call_target="tpu_custom_call" | custom-call | flops 144703488 | bytes 3571712 | tf_op jit(solution)/shard_map/network_forward/pallas_call | solution.py:33
  13.0 0.0 collective-permute-done.2.col_first
  13.0 0.0 collective-permute-done.3.col_second
  13.0 0.0 copy-done
  13.0 8.1 %sweeps_backward.1 = (f32[72,128]{1,0:T(8,128)S(1)}, f32[5,64,256]{2,1,0:T(8,128)}, f32[64,256]{1,0:T(8,128)}) custom-call(bf16[5,64,256]{2,1,0:T(8,128)(2,1)S(1)} %get-tuple-element.42.src, bf16[4,64,256]{2,1,0:T(8,128)(2,1)S(1)} %get-tuple-element.43.cpl, f32[64,256]{1,0:T(8,128)S(1)} %get-tuple-element.44.inv.inverse, ...), custom_call_target="tpu_custom_call" | custom-call | tf_op jit(solution)/shard_map/sweeps_backward/pallas_call | solution.py:430
  21.2 0.5 %collective-permute-start.4 = (f32[72,128]{1,0:T(8,128)S(1)}, f32[72,128]{1,0:T(8,128)S(1)}, u32[]{:S(2)}, u32[]{:S(2)}) collective-permute-start(f32[72,128]{1,0:T(8,128)S(1)} %get-tuple-element.71), channel_id=1, source_target_pairs={{0,1},{1,0},{2,3},{3,2},{4,5},{5,4},{6,7},{7,6},{8,9},{9,8},{10,11... | collective-permute-start | bytes 110600 | tf_op jit(solution)/shard_map/ppermute | solution.py:491
  21.6 0.9 %collective-permute-done.4 = f32[72,128]{1,0:T(8,128)S(1)} collective-permute-done((f32[72,128]{1,0:T(8,128)S(1)}, f32[72,128]{1,0:T(8,128)S(1)}, u32[]{:S(2)}, u32[]{:S(2)}) %collective-permute-start.4) | collective-permute-done | bytes 36896 | tf_op jit(solution)/shard_map/ppermute | solution.py:491
  22.5 1.3 %collective-permute-start.5 = (f32[72,128]{1,0:T(8,128)S(1)}, f32[72,128]{1,0:T(8,128)S(1)}, u32[]{:S(2)}, u32[]{:S(2)}) collective-permute-start(f32[72,128]{1,0:T(8,128)S(1)} %add.15), channel_id=1, source_target_pairs={{0,2},{1,3},{2,0},{3,1},{4,6},{5,7},{6,4},{7,5},{8,10},{9,11},{10,... | collective-permute-start | bytes 110600 | tf_op jit(solution)/shard_map/ppermute | solution.py:491
  23.8 2.7 %collective-permute-done.5 = f32[72,128]{1,0:T(8,128)S(1)} collective-permute-done((f32[72,128]{1,0:T(8,128)S(1)}, f32[72,128]{1,0:T(8,128)S(1)}, u32[]{:S(2)}, u32[]{:S(2)}) %collective-permute-start.5) | collective-permute-done | bytes 36896 | tf_op jit(solution)/shard_map/ppermute | solution.py:491
  26.5 3.5 %collective-permute-start.8 = (f32[72,128]{1,0:T(8,128)S(1)}, f32[72,128]{1,0:T(8,128)S(1)}, u32[]{:S(2)}, u32[]{:S(2)}) collective-permute-start(f32[72,128]{1,0:T(8,128)S(1)} %add.16), channel_id=1, source_target_pairs={{0,12},{4,8},{8,4},{12,0},{1,13},{5,9},{9,5},{13,1},{2,14},{6,10},... | collective-permute-start | bytes 110600 | tf_op jit(solution)/shard_map/ppermute | solution.py:491
  30.0 0.9 %collective-permute-start.7 = (f32[72,128]{1,0:T(8,128)S(1)}, f32[72,128]{1,0:T(8,128)S(1)}, u32[]{:S(2)}, u32[]{:S(2)}) collective-permute-start(f32[72,128]{1,0:T(8,128)S(1)} %add.16), channel_id=1, source_target_pairs={{0,8},{4,12},{8,0},{12,4},{1,9},{5,13},{9,1},{13,5},{2,10},{6,14},... | collective-permute-start | bytes 110600 | tf_op jit(solution)/shard_map/ppermute | solution.py:491
  31.0 0.2 collective-permute-start.6
  31.1 1.1 %collective-permute-done.8 = f32[72,128]{1,0:T(8,128)S(1)} collective-permute-done((f32[72,128]{1,0:T(8,128)S(1)}, f32[72,128]{1,0:T(8,128)S(1)}, u32[]{:S(2)}, u32[]{:S(2)}) %collective-permute-start.8) | collective-permute-done | bytes 36896 | tf_op jit(solution)/shard_map/ppermute | solution.py:491
  32.3 2.6 %collective-permute-done.7 = f32[72,128]{1,0:T(8,128)S(1)} collective-permute-done((f32[72,128]{1,0:T(8,128)S(1)}, f32[72,128]{1,0:T(8,128)S(1)}, u32[]{:S(2)}, u32[]{:S(2)}) %collective-permute-start.7) | collective-permute-done | bytes 36896 | tf_op jit(solution)/shard_map/ppermute | solution.py:491
  34.9 0.4 %collective-permute-done.6 = f32[72,128]{1,0:T(8,128)S(1)} collective-permute-done((f32[72,128]{1,0:T(8,128)S(1)}, f32[72,128]{1,0:T(8,128)S(1)}, u32[]{:S(2)}, u32[]{:S(2)}) %collective-permute-start.6) | collective-permute-done | bytes 36896 | tf_op jit(solution)/shard_map/ppermute | solution.py:491
  35.3 0.8 %clip.1 = (f32[10,64]{1,0:T(8,128)}, f32[64,64]{1,0:T(8,128)}, f32[64,64]{1,0:T(8,128)}, f32[1,64]{1,0:T(1,128)}, f32[3,64]{1,0:T(4,128)}) custom-call(f32[72,128]{1,0:T(8,128)S(1)} %add_add_fusion.summed), custom_call_target="tpu_custom_call" | custom-call | tf_op jit(solution)/shard_map/clip/pallas_call | solution.py:473
  (3 shorter events, 0.0 us)
Async XLA Ops:
  0.6 12.4 %copy-start = (f32[5,5]{1,0:T(8,128)S(1)}, f32[5,5]{1,0:T(8,128)}, u32[]{:S(2)}) copy-start(f32[5,5]{1,0:T(8,128)} %mix.1) | copy-start | bytes 304
  2.6 5.9 %collective-permute-start = (f32[10,8,256]{2,1,0:T(8,128)S(1)}, f32[10,8,256]{2,1,0:T(8,128)S(1)}, u32[]{:S(2)}, u32[]{:S(2)}) collective-permute-start(f32[10,8,256]{2,1,0:T(8,128)S(1)} %get-tuple-element.46), channel_id=1, source_target_pairs={{0,4},{1,5},{2,6},{3,7},{4,0},{5,1},{6,2},{7,3},{8,12},{9,13},{10,... | collective-permute-start | bytes 245768 | tf_op jit(solution)/shard_map/ppermute | solution.py:511
  5.7 2.8 %collective-permute-start.1 = (f32[10,8,256]{2,1,0:T(8,128)S(1)}, f32[10,8,256]{2,1,0:T(8,128)S(1)}, u32[]{:S(2)}, u32[]{:S(2)}) collective-permute-start(f32[10,8,256]{2,1,0:T(8,128)S(1)} %get-tuple-element.47), channel_id=1, source_target_pairs={{0,1},{1,0},{2,3},{3,2},{4,8},{5,9},{6,10},{7,11},{8,4},{9,5},{10,... | collective-permute-start | bytes 245768 | tf_op jit(solution)/shard_map/ppermute | solution.py:511
  8.7 4.3 %collective-permute-start.2 = (f32[80,128]{1,0:T(8,128)S(1)}, f32[80,128]{1,0:T(8,128)S(1)}, u32[]{:S(2)}, u32[]{:S(2)}) collective-permute-start(f32[80,128]{1,0:T(8,128)S(1)} %get-tuple-element.63), channel_id=1, source_target_pairs={{0,1},{2,3},{1,0},{3,2},{4,5},{6,7},{5,4},{7,6},{8,9},{10,11},{9,8... | collective-permute-start | bytes 122888 | tf_op jit(solution)/shard_map/ppermute | solution.py:522
  9.3 3.7 %collective-permute-start.3 = (f32[80,128]{1,0:T(8,128)S(1)}, f32[80,128]{1,0:T(8,128)S(1)}, u32[]{:S(2)}, u32[]{:S(2)}) collective-permute-start(f32[80,128]{1,0:T(8,128)S(1)} %get-tuple-element.64), channel_id=1, source_target_pairs={{1,2},{0,3},{2,1},{3,0},{5,6},{4,7},{6,5},{7,4},{9,10},{8,11},{10,... | collective-permute-start | bytes 122888 | tf_op jit(solution)/shard_map/ppermute | solution.py:522
  21.2 1.4 %collective-permute-start.4 = (f32[72,128]{1,0:T(8,128)S(1)}, f32[72,128]{1,0:T(8,128)S(1)}, u32[]{:S(2)}, u32[]{:S(2)}) collective-permute-start(f32[72,128]{1,0:T(8,128)S(1)} %get-tuple-element.71), channel_id=1, source_target_pairs={{0,1},{1,0},{2,3},{3,2},{4,5},{5,4},{6,7},{7,6},{8,9},{9,8},{10,11... | collective-permute-start | bytes 110600 | tf_op jit(solution)/shard_map/ppermute | solution.py:491
  22.5 4.0 %collective-permute-start.5 = (f32[72,128]{1,0:T(8,128)S(1)}, f32[72,128]{1,0:T(8,128)S(1)}, u32[]{:S(2)}, u32[]{:S(2)}) collective-permute-start(f32[72,128]{1,0:T(8,128)S(1)} %add.15), channel_id=1, source_target_pairs={{0,2},{1,3},{2,0},{3,1},{4,6},{5,7},{6,4},{7,5},{8,10},{9,11},{10,... | collective-permute-start | bytes 110600 | tf_op jit(solution)/shard_map/ppermute | solution.py:491
  26.5 5.8 %collective-permute-start.8 = (f32[72,128]{1,0:T(8,128)S(1)}, f32[72,128]{1,0:T(8,128)S(1)}, u32[]{:S(2)}, u32[]{:S(2)}) collective-permute-start(f32[72,128]{1,0:T(8,128)S(1)} %add.16), channel_id=1, source_target_pairs={{0,12},{4,8},{8,4},{12,0},{1,13},{5,9},{9,5},{13,1},{2,14},{6,10},... | collective-permute-start | bytes 110600 | tf_op jit(solution)/shard_map/ppermute | solution.py:491
  30.0 4.9 %collective-permute-start.7 = (f32[72,128]{1,0:T(8,128)S(1)}, f32[72,128]{1,0:T(8,128)S(1)}, u32[]{:S(2)}, u32[]{:S(2)}) collective-permute-start(f32[72,128]{1,0:T(8,128)S(1)} %add.16), channel_id=1, source_target_pairs={{0,8},{4,12},{8,0},{12,4},{1,9},{5,13},{9,1},{13,5},{2,10},{6,14},... | collective-permute-start | bytes 110600 | tf_op jit(solution)/shard_map/ppermute | solution.py:491
  31.0 4.3 %collective-permute-start.6 = (f32[72,128]{1,0:T(8,128)S(1)}, f32[72,128]{1,0:T(8,128)S(1)}, u32[]{:S(2)}, u32[]{:S(2)}) collective-permute-start(f32[72,128]{1,0:T(8,128)S(1)} %add.16), channel_id=1, source_target_pairs={{0,4},{4,0},{8,12},{12,8},{1,5},{5,1},{9,13},{13,9},{2,6},{6,2},{1... | collective-permute-start | bytes 110600 | tf_op jit(solution)/shard_map/ppermute | solution.py:491

commit v7 on v6

--- a/solution.py
+++ b/solution.py
@@ -12,6 +12,7 @@
 FAR_EXTRA = 0.6
 REG_WEIGHT = 0.5
 CLIP_NORM = 64.0
+DEPTH = SWEEPS
 EDGE = 8
 SUB, LANE = 8, 128
 F32, BF16 = jnp.float32, jnp.bfloat16
@@ -74,11 +75,11 @@
     for f in range(nv + nc + 1):
         if f < nv + nc:
             ref, k = (src, f) if f < nv else (cpl, f - nv)
-            top, bottom = ref[k, 0:16].astype(F32)[:EDGE], ref[k, rows - 16 :].astype(F32)[16 - EDGE :]
+            top, bottom = ref[k, 0:16].astype(F32)[:DEPTH], ref[k, rows - 16 :].astype(F32)[16 - DEPTH :]
         else:
-            top, bottom = inv[0:EDGE], inv[rows - EDGE :]
-        first[f] = jnp.where(odd, top, bottom)
-        second[f] = jnp.where(odd, bottom, top)
+            top, bottom = inv[0:DEPTH], inv[rows - DEPTH :]
+        first[f * DEPTH : (f + 1) * DEPTH] = jnp.where(odd, top, bottom)
+        second[f * DEPTH : (f + 1) * DEPTH] = jnp.where(odd, bottom, top)
     for copy in copies[4:]:
         copy.wait()
 
@@ -86,7 +87,7 @@
 def load(arrays):
     source, coupling = arrays[:2]
     nv, rows, cols = source.shape
-    slab = ((nv + coupling.shape[0] + 1, EDGE, cols), F32)
+    slab = (((nv + coupling.shape[0] + 1) * DEPTH, cols), F32)
     return on_chip(
         functools.partial(load_kernel, len(arrays)),
         [],
@@ -103,16 +104,21 @@
     return jnp.where(at == 0, 0.0, before), jnp.where(at == lax.axis_size(axis) - 1, 0.0, after)
 
 
-def cols_kernel(src, cpl, inv, row_first, row_second, col_first, col_second):
+def cols_kernel(src, cpl, inv, row_first, row_second, col_first, col_second, north, south):
     nv, rows, cols = src.shape
     nc = cpl.shape[0]
-    lane = lax.broadcasted_iota(jnp.int32, (rows, LANE), 1) // EDGE
-    lane_h = lane[:EDGE]
+    half = col_first.shape[0]
+    north[...] = jnp.zeros(north.shape, F32)
+    south[...] = jnp.zeros(south.shape, F32)
+    for f in range(nv + nc + 1):
+        here = slice(f * DEPTH, (f + 1) * DEPTH)
+        before, after = ordered("gx", row_first[here], row_second[here])
+        north[f, EDGE - DEPTH :] = before
+        south[f, 0:DEPTH] = after
+    lane = lax.broadcasted_iota(jnp.int32, (half, LANE), 1)
     slabs = []
-    for window, extra in ((slice(0, LANE), 0), (slice(cols - LANE, cols), EDGE)):
-        mid = jnp.zeros((rows, LANE), F32)
-        up = jnp.zeros((EDGE, LANE), F32)
-        down = jnp.zeros((EDGE, LANE), F32)
+    for window, extra in ((slice(0, LANE), 0), (slice(cols - LANE, cols), DEPTH)):
+        slab = jnp.zeros((half, LANE), F32)
         for f in range(nv + nc + 1):
             if f < nv:
                 x = src[f, :, window].astype(F32)
@@ -120,20 +126,23 @@
                 x = cpl[f - nv, :, window].astype(F32)
             else:
                 x = inv[:, window]
-            shift = (EDGE * f + extra) % LANE
-            mid = jnp.where(lane == f, pltpu.roll(x, shift, 1), mid)
-            north, south = ordered("gx", row_first[f, :, window], row_second[f, :, window])
-            up = jnp.where(lane_h == f, pltpu.roll(north, shift, 1), up)
-            down = jnp.where(lane_h == f, pltpu.roll(south, shift, 1), down)
-        slabs.append(jnp.concatenate([up, mid, down], axis=0))
+            x = jnp.concatenate([north[f, :, window], x, south[f, :, window]], axis=0)
+            for part, at in ((x[:half], DEPTH * f), (x[half:], DEPTH * f + LANE // 2)):
+                own = jnp.logical_and(lane >= at, lane < at + DEPTH)
+                slab = jnp.where(own, pltpu.roll(part, (at + extra) % LANE, 1), slab)
+        slabs.append(slab)
     odd = is_odd("gy")
     col_first[...] = jnp.where(odd, slabs[0], slabs[1])
     col_second[...] = jnp.where(odd, slabs[1], slabs[0])
 
 
 def col_slabs(source, coupling, inv, row_halos):
-    slab = ((source.shape[1] + 2 * EDGE, LANE), F32)
-    return on_chip(cols_kernel, [source, coupling, inv, *row_halos], [slab, slab], name="col_slabs")
+    nv, rows, cols = source.shape
+    slab = (((rows + 2 * EDGE) // 2, LANE), F32)
+    halo = ((nv + coupling.shape[0] + 1, EDGE, cols), F32)
+    return on_chip(
+        cols_kernel, [source, coupling, inv, *row_halos], [slab, slab, halo, halo], name="col_slabs"
+    )
 
 
 def column_of(row):
@@ -257,32 +266,37 @@
         lane = lax.broadcasted_iota(jnp.int32, (SUB, LANE), 1)
         self.first_sub, self.last_sub = sub == 0, sub == SUB - 1
         self.first_lane, self.last_lane = lane == 0, lane == LANE - 1
-        self.all = (self.above, self.below, self.left, self.right)
-
-    def above(self, ref, lead, t, k):
-        here, other = ref[lead + span(t, k)], ref[lead + span(max(t - 1, 0), k)]
-        return pltpu.roll(jnp.where(self.last_sub, other, here), 1, 0)
-
-    def below(self, ref, lead, t, k):
-        here, other = ref[lead + span(t, k)], ref[lead + span(min(t + 1, self.tiles - 1), k)]
-        return pltpu.roll(jnp.where(self.first_sub, other, here), SUB - 1, 0)
-
-    def left(self, ref, lead, t, k):
-        here, other = ref[lead + span(t, k)], ref[lead + span(t, (k - 1) % self.lanes)]
-        return pltpu.roll(jnp.where(self.last_lane, other, here), 1, 1)
-
-    def right(self, ref, lead, t, k):
-        here, other = ref[lead + span(t, k)], ref[lead + span(t, (k + 1) % self.lanes)]
-        return pltpu.roll(jnp.where(self.first_lane, other, here), LANE - 1, 1)
-
-
-def extend(src, cpl, inverse, row_halos, col_halos, shifts, raw, src_x, cpl_x):
+
+    def row(self, ref, lead, t):
+        t = min(max(t, 0), self.tiles - 1)
+        return [ref[lead + span(t, k)] for k in range(self.lanes)]
+
+    def above(self, rows, k):
+        return pltpu.roll(jnp.where(self.last_sub, rows[0][k], rows[1][k]), 1, 0)
+
+    def below(self, rows, k):
+        return pltpu.roll(jnp.where(self.first_sub, rows[2][k], rows[1][k]), SUB - 1, 0)
+
+    def left(self, rows, k):
+        return pltpu.roll(jnp.where(self.last_lane, rows[1][(k - 1) % self.lanes], rows[1][k]), 1, 1)
+
+    def right(self, rows, k):
+        other = rows[1][(k + 1) % self.lanes]
+        return pltpu.roll(jnp.where(self.first_lane, other, rows[1][k]), LANE - 1, 1)
+
+    def around(self, ref, lead, t, k_count):
+        rows = [self.row(ref, lead, t + o) for o in (-1, 0, 1)]
+        moves = (self.above, self.below, self.left, self.right)
+        return [[move(rows, k) for move in moves] for k in range(k_count)]
+
+
+def extend(src, cpl, inverse, north, south, col_halos, shifts, raw, src_x, cpl_x):
     nv, rows, cols = src.shape
     nc = cpl.shape[0]
     tall = rows + 2 * EDGE
     inner = slice(EDGE, EDGE + rows)
     lane = lax.broadcasted_iota(jnp.int32, (tall, LANE), 1)
-    from_east, from_west = lane < EDGE, lane >= LANE - EDGE
+    from_east, from_west = lane < DEPTH, lane >= LANE - DEPTH
     west, east = ordered("gy", *(x[...] for x in col_halos))
     for f in range(nv + nc + 1):
         if f < nv:
@@ -291,25 +305,27 @@
             raw[f, inner, 0:cols] = cpl[f - nv].astype(F32)
         else:
             raw[f, inner, 0:cols] = inverse[...]
-        north, south = ordered("gx", *(x[f] for x in row_halos))
-        raw[f, 0:EDGE, 0:cols] = north
-        raw[f, EDGE + rows :, 0:cols] = south
-        e = pltpu.roll(east, (LANE - EDGE * f) % LANE, 1)
-        w = pltpu.roll(west, (LANE - EDGE - EDGE * f) % LANE, 1)
+        raw[f, 0:EDGE, 0:cols] = north[f]
+        raw[f, EDGE + rows :, 0:cols] = south[f]
+        low, high = (-DEPTH * f) % LANE, (LANE // 2 - DEPTH * f) % LANE
+        e = jnp.concatenate([pltpu.roll(east, at, 1) for at in (low, high)], axis=0)
+        w = jnp.concatenate([pltpu.roll(west, (at - DEPTH) % LANE, 1) for at in (low, high)], axis=0)
         raw[f, :, cols:] = jnp.where(from_east, e, jnp.where(from_west, w, 0.0))
     for t in range(shifts.tiles):
+        inv = shifts.row(raw, (nv + nc,), t)
         for k in range(shifts.lanes):
-            inv = raw[(nv + nc,) + span(t, k)]
             for v in range(nv):
-                src_x[(v,) + span(t, k)] = inv * raw[(v,) + span(t, k)]
-            for d in range(nc):
-                cpl_x[(d,) + span(t, k)] = inv * shifts.all[d](raw, (nv + d,), t, k)
+                src_x[(v,) + span(t, k)] = inv[k] * raw[(v,) + span(t, k)]
+        for d, move in enumerate((shifts.above, shifts.below, shifts.left, shifts.right)):
+            rows_d = [shifts.row(raw, (nv + d,), t + o) for o in (-1, 0, 1)]
+            for k in range(shifts.lanes):
+                cpl_x[(d,) + span(t, k)] = inv[k] * move(rows_d, k)
 
 
 def adjoint_kernel(
-    num_feat, src, cpl, inverse, prod, beta_a, beta_b, row_first, row_second, col_first, col_second,
+    num_feat, src, cpl, inverse, prod, beta_a, beta_b, north, south, col_first, col_second,
     wmid, wtop, acts_a, slopes_a, acts_b, slopes_b, mix,
-    packed, adj_out, beta_out,
+    keep, give, adj_out, beta_out,
     raw, src_x, cpl_x, adj, done, sums, g_mid, g_top, g_in, sems,
 ):
     nv, rows, cols = src.shape
@@ -325,26 +341,27 @@
     copies[0].start()
     copies[1].start()
     shifts = Shifts(tiles, lanes)
-    extend(
-        src, cpl, inverse, (row_first, row_second), (col_first, col_second), shifts, raw, src_x, cpl_x
-    )
+    extend(src, cpl, inverse, north, south, (col_first, col_second), shifts, raw, src_x, cpl_x)
+    weights = [[mix[b, a] for a in range(nv)] for b in range(nv)]
 
     def sweep(number, t):
         last = number == SWEEPS
-        for k in range(lanes - 1 if last else lanes):
-            couple = [cpl_x[(d,) + span(t, k)] for d in range(nc)]
-            total = [src_x[(a,) + span(t, k)] for a in range(nv)]
-            for b in range(nv):
-                old, lead = (src_x, (b,)) if number == 1 else (adj, (number - 2, b))
-                inc = couple[0] * shifts.all[0](old, lead, t, k)
-                for d in range(1, nc):
-                    inc = inc + couple[d] * shifts.all[d](old, lead, t, k)
-                total = [total[a] + mix[b, a] * inc for a in range(nv)]
+        count = lanes - 1 if last else lanes
+        couple = [[cpl_x[(d,) + span(t, k)] for d in range(nc)] for k in range(count)]
+        total = [[src_x[(a,) + span(t, k)] for a in range(nv)] for k in range(count)]
+        for b in range(nv):
+            old, lead = (src_x, (b,)) if number == 1 else (adj, (number - 2, b))
+            around = shifts.around(old, lead, t, count)
+            for k in range(count):
+                terms = [couple[k][d] * around[k][d] for d in range(nc)]
+                inc = (terms[0] + terms[1]) + (terms[2] + terms[3])
+                total[k] = [total[k][a] + weights[b][a] * inc for a in range(nv)]
+        for k in range(count):
             for a in range(nv):
                 if last:
-                    done[(a,) + span(t - EDGE // SUB, k)] = total[a]
+                    done[(a,) + span(t - EDGE // SUB, k)] = total[k][a]
                 else:
-                    adj[(number - 1, a) + span(t, k)] = total[a]
+                    adj[(number - 1, a) + span(t, k)] = total[k][a]
 
     def fold(x):
         parts = [x[:, k * LANE : (k + 1) * LANE] for k in range(cols // LANE)]
@@ -408,14 +425,19 @@
     copies[2].start()
     backward(rows - blk)
 
-    packed[0:hidden, :] = joined([g_mid[...], g_top[...]])
     turned = jnp.transpose(joined([g_in[...], jnp.zeros((hidden, LANE - 16), F32)]))
     tail = turned[SUB : 2 * SUB]
     row = lax.broadcasted_iota(jnp.int32, (SUB, hidden), 0)
     for k in range(4):
         line = jnp.sum(jnp.transpose(sums[k]), axis=0, keepdims=True)
         tail = tail + jnp.where(row == k + num_feat - SUB, jnp.broadcast_to(line, (SUB, hidden)), 0.0)
-    packed[hidden : hidden + SUB, :] = joined([turned[0:SUB], tail])
+    whole_sum = jnp.concatenate([joined([g_mid[...], g_top[...]]), joined([turned[0:SUB], tail])], axis=0)
+    size = keep.shape[0]
+    missing = jnp.zeros((2 * size - hidden - SUB, LANE), F32)
+    upper, lower = whole_sum[:size], jnp.concatenate([whole_sum[size:], missing], axis=0)
+    odd = is_odd("gy")
+    keep[...] = jnp.where(odd, lower, upper)
+    give[...] = jnp.where(odd, upper, lower)
     for copy in copies:
         copy.wait()
 
@@ -424,15 +446,17 @@
     nv, rows, cols = source.shape
     nc = coupling.shape[0]
     hidden = weights[0].shape[0]
+    size = -(-(hidden + SUB) // (2 * SUB)) * SUB
     tall, wide = rows + 2 * EDGE, cols + LANE
     near, far = pl.BlockSpec(memory_space=pltpu.VMEM), pl.BlockSpec(memory_space=pltpu.HBM)
     operands = [source, coupling, inverse, production, *betas, *halos, *weights, *nets]
     return pl.pallas_call(
         functools.partial(adjoint_kernel, num_feat),
         in_specs=[near] * len(operands) + [pl.BlockSpec(memory_space=pltpu.SMEM)],
-        out_specs=[near, far, far],
+        out_specs=[near, near, far, far],
         out_shape=[
-            pltpu.VMEM((hidden + SUB, LANE), F32),
+            pltpu.VMEM((size, LANE), F32),
+            pltpu.VMEM((size, LANE), F32),
             pltpu.HBM((nv, rows, cols), F32),
             pltpu.HBM((rows, cols), F32),
         ],
@@ -453,9 +477,11 @@
     )(*operands, mixing)
 
 
-def clip_kernel(summed, gin, gmid, gtop, gout, gbias):
+def clip_kernel(mine, other, gin, gmid, gtop, gout, gbias):
     hidden = gmid.shape[0]
-    total = summed[...]
+    odd = is_odd("gy")
+    own, sent = mine[...], other[...]
+    total = jnp.concatenate([jnp.where(odd, sent, own), jnp.where(odd, own, sent)], axis=0)[: hidden + SUB]
     squares = jnp.sum(jnp.sum(total * total, axis=0, keepdims=True), axis=1, keepdims=True)
     total = total * (CLIP_NORM / jnp.maximum(jnp.sqrt(squares), CLIP_NORM))
     gmid[...] = total[:hidden, :hidden]
@@ -468,32 +494,33 @@
     gbias[...] = high[at + 1 : at + 4]
 
 
-def clip_all(summed, num_feat, hidden):
+def clip_all(mine, other, num_feat, hidden):
     shapes = [(num_feat, hidden), (hidden, hidden), (hidden, hidden), (1, hidden), (3, hidden)]
     return pl.pallas_call(
         clip_kernel,
         grid=(1,),
-        in_specs=[whole(summed.shape)],
+        in_specs=[whole(mine.shape)] * 2,
         out_specs=[whole(s) for s in shapes],
         out_shape=[jax.ShapeDtypeStruct(s, F32) for s in shapes],
         compiler_params=params(),
         name="clip",
-    )(summed)
-
-
-def sum_over_case(packed):
-    for axis, radix in (("gy", 2), ("gx", 4)):
+    )(mine, other)
+
+
+def sum_over_case(keep, give):
+    def swapped(x, axis, k):
+        return lax.ppermute(x, axis, [(i, i ^ k) for i in range(lax.axis_size(axis))])
+
+    mine = keep + swapped(give, "gy", 1)
+    for axis, step, radix in (("gy", 2, 2), ("gx", 1, 4)):
         count = lax.axis_size(axis)
-        step = 1
         while step < count:
-            parts = [packed]
-            for k in range(1, min(radix, count // step)):
-                parts.append(lax.ppermute(packed, axis, [(i, i ^ (k * step)) for i in range(count)]))
+            parts = [mine] + [swapped(mine, axis, k * step) for k in range(1, min(radix, count // step))]
             while len(parts) > 1:
                 parts = [a + b for a, b in zip(parts[::2], parts[1::2])]
-            packed = parts[0]
+            mine = parts[0]
             step *= radix
-    return packed
+    return mine, swapped(mine, "gy", 1)
 
 
 def row_swaps(first, second):
@@ -540,13 +567,14 @@
     half = rows - 32
     *net_a, beta_a = forward(features, prepared, 0, half)
     *row_halos, beta_a = lax.optimization_barrier((*row_halos, beta_a))
-    col_halos = col_swaps(*col_slabs(source, coupling, inverse, row_halos))
+    first, second, *row_halos = col_slabs(source, coupling, inverse, row_halos)
+    col_halos = col_swaps(first, second)
     *net_b, beta_b = forward(features, prepared, half, rows - half)
-    packed, adjoint, beta = sweeps_and_backward(
+    keep, give, adjoint, beta = sweeps_and_backward(
         num_feat, source, coupling, inverse, production, (beta_a, beta_b), (*row_halos, *col_halos),
         (weight_mid, weight_top), (*net_a, *net_b), mixing,
     )
-    grad_in, grad_mid, grad_top, grad_out, grad_bias = clip_all(sum_over_case(packed), num_feat, hidden)
+    grad_in, grad_mid, grad_top, grad_out, grad_bias = clip_all(*sum_over_case(keep, give), num_feat, hidden)
     return (adjoint, beta, grad_in, grad_mid, grad_top, grad_out.reshape(hidden), grad_bias)
 
 

time: 36.2 us -> 36.6 us (1.011)
  waiting for transfers between devices: 7.67 us -> 8.74 us
  starting transfers between devices: 11.3 us -> 10.7 us
    ppermute x5 -> x6, waiting for transfers between devices: 7.66 us -> 8.73 us  [swapped(): lax.ppermute(x, axis, [(i, i ^ k) for i in range(lax.axis_size(axis))])]
    ppermute x5 -> x6, starting transfers between devices: 6.44 us -> 5.9 us  [swapped(): lax.ppermute(x, axis, [(i, i ^ k) for i in range(lax.axis_size(axis))])]
  transfers between devices with their start and end apart: 9 -> 10, of which waited for: 5 -> 6; matrix products, arithmetic and copies ran while one was open for 0% -> 0% of each run, Pallas kernels for 15% -> 14%
where the time goes in v7:
time: 36.6 us; the launch traced here: 36.5 us
  Pallas kernels  16.3 us (45%)
  starting transfers between devices  10.7 us (29%)
  waiting for transfers between devices  8.74 us (24%)
  between operations  0.75 us (2%)
    ppermute x6, waiting for transfers between devices, swapped(): lax.ppermute(x, axis, [(i, i ^ k) for i in range(lax.axis_size(axis))])  8.73 us
    pallas_call x1, Pallas kernels, sweeps_and_backward(): pl.pallas_call(functools.partial(adjoint_kernel, num_feat), in_specs=[nea...  7.97 us
    pallas_call x5, Pallas kernels, on_chip(): pl.pallas_call(kernel, in_specs=[here] * len(operands) + [there] * len(fa...  7.47 us
    ppermute x6, starting transfers between devices, swapped(): lax.ppermute(x, axis, [(i, i ^ k) for i in range(lax.axis_size(axis))])  5.9 us
    ppermute x2, starting transfers between devices, row_swaps(): out.append(lax.ppermute(slab, ('gx', 'gy'), sorted(partner.items())))  3.09 us
    ppermute x2, starting transfers between devices, col_swaps(): out.append(lax.ppermute(slab, 'gy', low + [(b, a) for a, b in low]))  1.74 us
    pallas_call x1, Pallas kernels, clip_all(): pl.pallas_call(clip_kernel, grid=(1,), in_specs=[whole(mine.shape)] * 2,...  0.81 us
  transfers between devices with their start and end apart: 10, of which 6 were waited for; matrix products, arithmetic and copies ran while one was open for 0% of the time, Pallas kernels for 14%

profile of v7, /device:TPU:0, one launch (start us, length us, event | category | flops | bytes accessed | tf_op | source)
XLA Modules:
  0.0 36.5 jit_solution(671760290744929110)
XLA Ops:
  0.6 0.0 copy-start
  0.6 2.0 %load.1 = (bf16[5,64,256]{2,1,0:T(8,128)(2,1)S(1)}, bf16[4,64,256]{2,1,0:T(8,128)(2,1)S(1)}, f32[64,256]{1,0:T(8,128)}, s32[64,256]{1,0:T(8,128)}, f32[64,256]{1...) custom-call(bf16[5,64,256]{2,1,0:T(8,128)(2,1)} %refs_0_.1, ...), custom_call_target="tpu_custom_call" | custom-call | tf_op jit(solution)/shard_map/load/pallas_call | solution.py:34
  2.6 3.1 %collective-permute-start = (f32[60,256]{1,0:T(8,128)S(1)}, f32[60,256]{1,0:T(8,128)S(1)}, u32[]{:S(2)}, u32[]{:S(2)}) collective-permute-start(f32[60,256]{1,0:T(8,128)S(1)} %get-tuple-element.49), channel_id=1, source_target_pairs={{0,4},{1,5},{2,6},{3,7},{4,0},{5,1},{6,2},{7,3},{8,12},{9,13},{10,... | collective-permute-start | bytes 184328 | tf_op jit(solution)/shard_map/ppermute | solution.py:538
  5.7 0.0 collective-permute-start.1
  5.7 0.2 weights.1
  6.0 2.5 %network_forward.2 = (bf16[32,208,256]{2,1,0:T(8,128)(2,1)S(1)}, f32[32,192,256]{2,1,0:T(8,128)S(1)}, f32[32,256]{1,0:T(8,128)S(1)}) custom-call(bf16[10,64,256]{2,1,0:T(8,128)(2,1)S(1)} %get-tuple-element.51.feat, bf16[1280,256]{1,0:T(8,128)(2,1)S(1)} %get-tuple-element.57.w1, bf16[64,64]{1,0:T(8,128)(2,1)S(1)} %get-tuple-element.58.w2, ...), custom_call_target="tpu_custom_call" | custom-call | flops 144703488 | bytes 3571712 | tf_op jit(solution)/shard_map/network_forward/pallas_call | solution.py:34
  8.5 0.0 collective-permute-done.row_first
  8.5 0.0 collective-permute-done.1.row_second
  8.5 0.2 col_slabs.1
  8.7 0.6 %collective-permute-start.2 = (f32[40,128]{1,0:T(8,128)S(1)}, f32[40,128]{1,0:T(8,128)S(1)}, u32[]{:S(2)}, u32[]{:S(2)}) collective-permute-start(f32[40,128]{1,0:T(8,128)S(1)} %get-tuple-element.68), channel_id=1, source_target_pairs={{0,1},{2,3},{1,0},{3,2},{4,5},{6,7},{5,4},{7,6},{8,9},{10,11},{9,8... | collective-permute-start | bytes 61448 | tf_op jit(solution)/shard_map/ppermute | solution.py:549
  9.3 1.2 %collective-permute-start.3 = (f32[40,128]{1,0:T(8,128)S(1)}, f32[40,128]{1,0:T(8,128)S(1)}, u32[]{:S(2)}, u32[]{:S(2)}) collective-permute-start(f32[40,128]{1,0:T(8,128)S(1)} %get-tuple-element.69), channel_id=1, source_target_pairs={{1,2},{0,3},{2,1},{3,0},{5,6},{4,7},{6,5},{7,4},{9,10},{8,11},{10,... | collective-permute-start | bytes 61448 | tf_op jit(solution)/shard_map/ppermute | solution.py:549
  10.5 2.5 %network_forward.3 = (bf16[32,208,256]{2,1,0:T(8,128)(2,1)S(1)}, f32[32,192,256]{2,1,0:T(8,128)S(1)}, f32[32,256]{1,0:T(8,128)S(1)}) custom-call(bf16[10,64,256]{2,1,0:T(8,128)(2,1)S(1)} %get-tuple-element.51.feat, bf16[1280,256]{1,0:T(8,128)(2,1)S(1)} %get-tuple-element.57.w1, bf16[64,64]{1,0:T(8,128)(2,1)S(1)} %get-tuple-element.58.w2, ...), custom_call_target="tpu_custom_call" | custom-call | flops 144703488 | bytes 3571712 | tf_op jit(solution)/shard_map/network_forward/pallas_call | solution.py:34
  13.0 0.0 collective-permute-done.2.col_first
  13.0 0.0 collective-permute-done.3.col_second
  13.0 0.0 copy-done
  13.0 8.0 %sweeps_backward.1 = (f32[40,128]{1,0:T(8,128)S(1)}, f32[40,128]{1,0:T(8,128)S(1)}, f32[5,64,256]{2,1,0:T(8,128)}, f32[64,256]{1,0:T(8,128)}) custom-call(bf16[5,64,256]{2,1,0:T(8,128)(2,1)S(1)} %get-tuple-element.45.src, bf16[4,64,256]{2,1,0:T(8,128)(2,1)S(1)} %get-tuple-element.46.cpl, f32[64,256]{1,0:T(8,128)S(1)} %get-tuple-element.47.inv.inverse, ...), custom_call_target="tpu_custom_call" | custom-call | tf_op jit(solution)/shard_map/sweeps_backward/pallas_call | solution.py:453
  21.0 0.5 %collective-permute-start.4 = (f32[40,128]{1,0:T(8,128)S(1)}, f32[40,128]{1,0:T(8,128)S(1)}, u32[]{:S(2)}, u32[]{:S(2)}) collective-permute-start(f32[40,128]{1,0:T(8,128)S(1)} %get-tuple-element.77), channel_id=1, source_target_pairs={{0,1},{1,0},{2,3},{3,2},{4,5},{5,4},{6,7},{7,6},{8,9},{9,8},{10,11... | collective-permute-start | bytes 61448 | tf_op jit(solution)/shard_map/ppermute | solution.py:512
  21.5 0.8 %collective-permute-done.4 = f32[40,128]{1,0:T(8,128)S(1)} collective-permute-done((f32[40,128]{1,0:T(8,128)S(1)}, f32[40,128]{1,0:T(8,128)S(1)}, u32[]{:S(2)}, u32[]{:S(2)}) %collective-permute-start.4) | collective-permute-done | bytes 20512 | tf_op jit(solution)/shard_map/ppermute | solution.py:512
  22.4 0.9 %collective-permute-start.5 = (f32[40,128]{1,0:T(8,128)S(1)}, f32[40,128]{1,0:T(8,128)S(1)}, u32[]{:S(2)}, u32[]{:S(2)}) collective-permute-start(f32[40,128]{1,0:T(8,128)S(1)} %add.15), channel_id=1, source_target_pairs={{0,2},{1,3},{2,0},{3,1},{4,6},{5,7},{6,4},{7,5},{8,10},{9,11},{10,... | collective-permute-start | bytes 61448 | tf_op jit(solution)/shard_map/ppermute | solution.py:512
  23.2 2.9 %collective-permute-done.5 = f32[40,128]{1,0:T(8,128)S(1)} collective-permute-done((f32[40,128]{1,0:T(8,128)S(1)}, f32[40,128]{1,0:T(8,128)S(1)}, u32[]{:S(2)}, u32[]{:S(2)}) %collective-permute-start.5) | collective-permute-done | bytes 20512 | tf_op jit(solution)/shard_map/ppermute | solution.py:512
  26.2 3.3 %collective-permute-start.8 = (f32[40,128]{1,0:T(8,128)S(1)}, f32[40,128]{1,0:T(8,128)S(1)}, u32[]{:S(2)}, u32[]{:S(2)}) collective-permute-start(f32[40,128]{1,0:T(8,128)S(1)} %add.16), channel_id=1, source_target_pairs={{0,12},{4,8},{8,4},{12,0},{1,13},{5,9},{9,5},{13,1},{2,14},{6,10},... | collective-permute-start | bytes 61448 | tf_op jit(solution)/shard_map/ppermute | solution.py:512
  29.5 1.1 %collective-permute-start.7 = (f32[40,128]{1,0:T(8,128)S(1)}, f32[40,128]{1,0:T(8,128)S(1)}, u32[]{:S(2)}, u32[]{:S(2)}) collective-permute-start(f32[40,128]{1,0:T(8,128)S(1)} %add.16), channel_id=1, source_target_pairs={{0,8},{4,12},{8,0},{12,4},{1,9},{5,13},{9,1},{13,5},{2,10},{6,14},... | collective-permute-start | bytes 61448 | tf_op jit(solution)/shard_map/ppermute | solution.py:512
  30.6 0.0 collective-permute-start.6
  30.6 1.1 %collective-permute-done.8 = f32[40,128]{1,0:T(8,128)S(1)} collective-permute-done((f32[40,128]{1,0:T(8,128)S(1)}, f32[40,128]{1,0:T(8,128)S(1)}, u32[]{:S(2)}, u32[]{:S(2)}) %collective-permute-start.8) | collective-permute-done | bytes 20512 | tf_op jit(solution)/shard_map/ppermute | solution.py:512
  31.8 2.4 %collective-permute-done.7 = f32[40,128]{1,0:T(8,128)S(1)} collective-permute-done((f32[40,128]{1,0:T(8,128)S(1)}, f32[40,128]{1,0:T(8,128)S(1)}, u32[]{:S(2)}, u32[]{:S(2)}) %collective-permute-start.7) | collective-permute-done | bytes 20512 | tf_op jit(solution)/shard_map/ppermute | solution.py:512
  34.2 0.2 collective-permute-done.6
  34.4 0.1 collective-permute-start.9
  34.5 1.2 %collective-permute-done.9.other = f32[40,128]{1,0:T(8,128)S(1)} collective-permute-done((f32[40,128]{1,0:T(8,128)S(1)}, f32[40,128]{1,0:T(8,128)S(1)}, u32[]{:S(2)}, u32[]{:S(2)}) %collective-permute-start.9) | collective-permute-done | bytes 20512 | tf_op jit(solution)/shard_map/ppermute | solution.py:512
  35.7 0.8 %clip.1 = (f32[10,64]{1,0:T(8,128)}, f32[64,64]{1,0:T(8,128)}, f32[64,64]{1,0:T(8,128)}, f32[1,64]{1,0:T(1,128)}, f32[3,64]{1,0:T(4,128)}) custom-call(f32[40,128]{1,0:T(8,128)S(1)} %add_add_fusion.mine, f32[40,128]{1,0:T(8,128)S(1)} %collective-permute-done.9.other), custom_call_target="tpu_custom_call" | custom-call | tf_op jit(solution)/shard_map/clip/pallas_call | solution.py:499
  (3 shorter events, 0.0 us)
Async XLA Ops:
  0.6 12.4 %copy-start = (f32[5,5]{1,0:T(8,128)S(1)}, f32[5,5]{1,0:T(8,128)}, u32[]{:S(2)}) copy-start(f32[5,5]{1,0:T(8,128)} %mix.1) | copy-start | bytes 304
  2.6 5.9 %collective-permute-start = (f32[60,256]{1,0:T(8,128)S(1)}, f32[60,256]{1,0:T(8,128)S(1)}, u32[]{:S(2)}, u32[]{:S(2)}) collective-permute-start(f32[60,256]{1,0:T(8,128)S(1)} %get-tuple-element.49), channel_id=1, source_target_pairs={{0,4},{1,5},{2,6},{3,7},{4,0},{5,1},{6,2},{7,3},{8,12},{9,13},{10,... | collective-permute-start | bytes 184328 | tf_op jit(solution)/shard_map/ppermute | solution.py:538
  5.7 2.8 %collective-permute-start.1 = (f32[60,256]{1,0:T(8,128)S(1)}, f32[60,256]{1,0:T(8,128)S(1)}, u32[]{:S(2)}, u32[]{:S(2)}) collective-permute-start(f32[60,256]{1,0:T(8,128)S(1)} %get-tuple-element.50), channel_id=1, source_target_pairs={{0,1},{1,0},{2,3},{3,2},{4,8},{5,9},{6,10},{7,11},{8,4},{9,5},{10,... | collective-permute-start | bytes 184328 | tf_op jit(solution)/shard_map/ppermute | solution.py:538
  8.7 4.3 %collective-permute-start.2 = (f32[40,128]{1,0:T(8,128)S(1)}, f32[40,128]{1,0:T(8,128)S(1)}, u32[]{:S(2)}, u32[]{:S(2)}) collective-permute-start(f32[40,128]{1,0:T(8,128)S(1)} %get-tuple-element.68), channel_id=1, source_target_pairs={{0,1},{2,3},{1,0},{3,2},{4,5},{6,7},{5,4},{7,6},{8,9},{10,11},{9,8... | collective-permute-start | bytes 61448 | tf_op jit(solution)/shard_map/ppermute | solution.py:549
  9.3 3.7 %collective-permute-start.3 = (f32[40,128]{1,0:T(8,128)S(1)}, f32[40,128]{1,0:T(8,128)S(1)}, u32[]{:S(2)}, u32[]{:S(2)}) collective-permute-start(f32[40,128]{1,0:T(8,128)S(1)} %get-tuple-element.69), channel_id=1, source_target_pairs={{1,2},{0,3},{2,1},{3,0},{5,6},{4,7},{6,5},{7,4},{9,10},{8,11},{10,... | collective-permute-start | bytes 61448 | tf_op jit(solution)/shard_map/ppermute | solution.py:549
  21.0 1.4 %collective-permute-start.4 = (f32[40,128]{1,0:T(8,128)S(1)}, f32[40,128]{1,0:T(8,128)S(1)}, u32[]{:S(2)}, u32[]{:S(2)}) collective-permute-start(f32[40,128]{1,0:T(8,128)S(1)} %get-tuple-element.77), channel_id=1, source_target_pairs={{0,1},{1,0},{2,3},{3,2},{4,5},{5,4},{6,7},{7,6},{8,9},{9,8},{10,11... | collective-permute-start | bytes 61448 | tf_op jit(solution)/shard_map/ppermute | solution.py:512
  22.4 3.8 %collective-permute-start.5 = (f32[40,128]{1,0:T(8,128)S(1)}, f32[40,128]{1,0:T(8,128)S(1)}, u32[]{:S(2)}, u32[]{:S(2)}) collective-permute-start(f32[40,128]{1,0:T(8,128)S(1)} %add.15), channel_id=1, source_target_pairs={{0,2},{1,3},{2,0},{3,1},{4,6},{5,7},{6,4},{7,5},{8,10},{9,11},{10,... | collective-permute-start | bytes 61448 | tf_op jit(solution)/shard_map/ppermute | solution.py:512
  26.2 5.6 %collective-permute-start.8 = (f32[40,128]{1,0:T(8,128)S(1)}, f32[40,128]{1,0:T(8,128)S(1)}, u32[]{:S(2)}, u32[]{:S(2)}) collective-permute-start(f32[40,128]{1,0:T(8,128)S(1)} %add.16), channel_id=1, source_target_pairs={{0,12},{4,8},{8,4},{12,0},{1,13},{5,9},{9,5},{13,1},{2,14},{6,10},... | collective-permute-start | bytes 61448 | tf_op jit(solution)/shard_map/ppermute | solution.py:512
  29.5 4.7 %collective-permute-start.7 = (f32[40,128]{1,0:T(8,128)S(1)}, f32[40,128]{1,0:T(8,128)S(1)}, u32[]{:S(2)}, u32[]{:S(2)}) collective-permute-start(f32[40,128]{1,0:T(8,128)S(1)} %add.16), channel_id=1, source_target_pairs={{0,8},{4,12},{8,0},{12,4},{1,9},{5,13},{9,1},{13,5},{2,10},{6,14},... | collective-permute-start | bytes 61448 | tf_op jit(solution)/shard_map/ppermute | solution.py:512
  30.6 3.8 %collective-permute-start.6 = (f32[40,128]{1,0:T(8,128)S(1)}, f32[40,128]{1,0:T(8,128)S(1)}, u32[]{:S(2)}, u32[]{:S(2)}) collective-permute-start(f32[40,128]{1,0:T(8,128)S(1)} %add.16), channel_id=1, source_target_pairs={{0,4},{4,0},{8,12},{12,8},{1,5},{5,1},{9,13},{13,9},{2,6},{6,2},{1... | collective-permute-start | bytes 61448 | tf_op jit(solution)/shard_map/ppermute | solution.py:512
  34.4 1.2 %collective-permute-start.9 = (f32[40,128]{1,0:T(8,128)S(1)}, f32[40,128]{1,0:T(8,128)S(1)}, u32[]{:S(2)}, u32[]{:S(2)}) collective-permute-start(f32[40,128]{1,0:T(8,128)S(1)} %add_add_fusion.mine), channel_id=1, source_target_pairs={{0,1},{1,0},{2,3},{3,2},{4,5},{5,4},{6,7},{7,6},{8,9},{9,8},{10,11... | collective-permute-start | bytes 61448 | tf_op jit(solution)/shard_map/ppermute | solution.py:512

commit v8 on v7

--- a/solution.py
+++ b/solution.py
@@ -325,7 +325,7 @@
 def adjoint_kernel(
     num_feat, src, cpl, inverse, prod, beta_a, beta_b, north, south, col_first, col_second,
     wmid, wtop, acts_a, slopes_a, acts_b, slopes_b, mix,
-    keep, give, adj_out, beta_out,
+    packed, adj_out, beta_out,
     raw, src_x, cpl_x, adj, done, sums, g_mid, g_top, g_in, sems,
 ):
     nv, rows, cols = src.shape
@@ -384,46 +384,51 @@
         def layer(lo, high):
             return joined([acts[start + q, lo:high] for q in range(blk)])
 
-        def behind(weight, delta, lo):
-            product = jnp.dot(weight, delta, preferred_element_type=F32)
+        def add(ref, part):
+            ref[...] = part if first == 0 else ref[...] + part
+
+        def slanted(number, product, lo):
             total, out = jnp.zeros((hidden, LANE), F32), []
             for q in range(blk):
                 d = product[:, q * cols : (q + 1) * cols] * slopes[start + q, lo : lo + hidden]
                 total = total + fold(d)
                 out.append(d.astype(BF16))
-            return joined(out), total
-
-        out_sum, top_sum, d3 = jnp.zeros((hidden, LANE), F32), jnp.zeros((hidden, LANE), F32), []
+            add(sums.at[number], total)
+            return joined(out)
+
+        out_sum, sens_rows = jnp.zeros((hidden, LANE), F32), []
         for q in range(blk):
-            act = acts[start + q, 2 * hidden + 16 :].astype(F32)
             sen = jnp.broadcast_to(sens[q : q + 1], (hidden, cols))
-            out_sum = out_sum + fold(act * sen)
-            d = sen * slopes[start + q, 2 * hidden :]
-            top_sum = top_sum + fold(d)
-            d3.append(d.astype(BF16))
-        d3 = joined(d3)
-        d2, mid_sum = behind(wtop[...], d3, hidden)
-        d1, in_sum = behind(wmid[...], d2, 0)
-        new = (
-            (g_top, outer(layer(hidden, 2 * hidden), d3)),
-            (g_mid, outer(layer(0, hidden), d2)),
-            (g_in, outer(d1, layer(2 * hidden, 2 * hidden + 16))),
-            *((sums.at[k], part) for k, part in enumerate((out_sum, in_sum, mid_sum, top_sum))),
-        )
-        for ref, part in new:
-            ref[...] = part if first == 0 else ref[...] + part
+            out_sum = out_sum + fold(acts[start + q, 2 * hidden + 16 :].astype(F32) * sen)
+            sens_rows.append(sen)
+        add(sums.at[0], out_sum)
+        d3 = slanted(3, joined(sens_rows), 2 * hidden)
+        yield
+        product = jnp.dot(wtop[...], d3, preferred_element_type=F32)
+        yield
+        d2 = slanted(2, product, hidden)
+        add(g_top, outer(layer(hidden, 2 * hidden), d3))
+        yield
+        product = jnp.dot(wmid[...], d2, preferred_element_type=F32)
+        yield
+        d1 = slanted(1, product, 0)
+        add(g_mid, outer(layer(0, hidden), d2))
+        yield
+        add(g_in, outer(d1, layer(2 * hidden, 2 * hidden + 16)))
 
     for number in range(1, SWEEPS):
         for t in range(SWEEPS + 1 - number):
             sweep(number, t)
+    stages = iter(())
     for t in range(1, tiles - 1):
         for number in range(1, SWEEPS + 1):
             if t + SWEEPS - number < tiles:
                 sweep(number, t + SWEEPS - number)
-        if t > 1:
-            backward((t - 2) * blk)
+            next(stages, None)
+        stages = backward((t - 1) * blk)
     copies[2].start()
-    backward(rows - blk)
+    for _ in stages:
+        pass
 
     turned = jnp.transpose(joined([g_in[...], jnp.zeros((hidden, LANE - 16), F32)]))
     tail = turned[SUB : 2 * SUB]
@@ -431,13 +436,8 @@
     for k in range(4):
         line = jnp.sum(jnp.transpose(sums[k]), axis=0, keepdims=True)
         tail = tail + jnp.where(row == k + num_feat - SUB, jnp.broadcast_to(line, (SUB, hidden)), 0.0)
-    whole_sum = jnp.concatenate([joined([g_mid[...], g_top[...]]), joined([turned[0:SUB], tail])], axis=0)
-    size = keep.shape[0]
-    missing = jnp.zeros((2 * size - hidden - SUB, LANE), F32)
-    upper, lower = whole_sum[:size], jnp.concatenate([whole_sum[size:], missing], axis=0)
-    odd = is_odd("gy")
-    keep[...] = jnp.where(odd, lower, upper)
-    give[...] = jnp.where(odd, upper, lower)
+    packed[0:hidden, :] = joined([g_mid[...], g_top[...]])
+    packed[hidden : hidden + SUB, :] = joined([turned[0:SUB], tail])
     for copy in copies:
         copy.wait()
 
@@ -446,17 +446,15 @@
     nv, rows, cols = source.shape
     nc = coupling.shape[0]
     hidden = weights[0].shape[0]
-    size = -(-(hidden + SUB) // (2 * SUB)) * SUB
     tall, wide = rows + 2 * EDGE, cols + LANE
     near, far = pl.BlockSpec(memory_space=pltpu.VMEM), pl.BlockSpec(memory_space=pltpu.HBM)
     operands = [source, coupling, inverse, production, *betas, *halos, *weights, *nets]
     return pl.pallas_call(
         functools.partial(adjoint_kernel, num_feat),
         in_specs=[near] * len(operands) + [pl.BlockSpec(memory_space=pltpu.SMEM)],
-        out_specs=[near, near, far, far],
+        out_specs=[near, far, far],
         out_shape=[
-            pltpu.VMEM((size, LANE), F32),
-            pltpu.VMEM((size, LANE), F32),
+            pltpu.VMEM((hidden + SUB, LANE), F32),
             pltpu.HBM((nv, rows, cols), F32),
             pltpu.HBM((rows, cols), F32),
         ],
@@ -477,11 +475,9 @@
     )(*operands, mixing)
 
 
-def clip_kernel(mine, other, gin, gmid, gtop, gout, gbias):
+def clip_kernel(summed, gin, gmid, gtop, gout, gbias):
     hidden = gmid.shape[0]
-    odd = is_odd("gy")
-    own, sent = mine[...], other[...]
-    total = jnp.concatenate([jnp.where(odd, sent, own), jnp.where(odd, own, sent)], axis=0)[: hidden + SUB]
+    total = summed[...]
     squares = jnp.sum(jnp.sum(total * total, axis=0, keepdims=True), axis=1, keepdims=True)
     total = total * (CLIP_NORM / jnp.maximum(jnp.sqrt(squares), CLIP_NORM))
     gmid[...] = total[:hidden, :hidden]
@@ -494,39 +490,38 @@
     gbias[...] = high[at + 1 : at + 4]
 
 
-def clip_all(mine, other, num_feat, hidden):
+def clip_all(summed, num_feat, hidden):
     shapes = [(num_feat, hidden), (hidden, hidden), (hidden, hidden), (1, hidden), (3, hidden)]
     return pl.pallas_call(
         clip_kernel,
         grid=(1,),
-        in_specs=[whole(mine.shape)] * 2,
+        in_specs=[whole(summed.shape)],
         out_specs=[whole(s) for s in shapes],
         out_shape=[jax.ShapeDtypeStruct(s, F32) for s in shapes],
         compiler_params=params(),
         name="clip",
-    )(mine, other)
-
-
-def sum_over_case(keep, give):
-    def swapped(x, axis, k):
-        return lax.ppermute(x, axis, [(i, i ^ k) for i in range(lax.axis_size(axis))])
-
-    mine = keep + swapped(give, "gy", 1)
-    for axis, step, radix in (("gy", 2, 2), ("gx", 1, 4)):
+    )(summed)
+
+
+def sum_over_case(packed):
+    for axis, radix in (("gy", 2), ("gx", 4)):
         count = lax.axis_size(axis)
+        step = 1
         while step < count:
-            parts = [mine] + [swapped(mine, axis, k * step) for k in range(1, min(radix, count // step))]
+            parts = [packed]
+            for k in range(1, min(radix, count // step)):
+                parts.append(lax.ppermute(packed, axis, [(i, i ^ (k * step)) for i in range(count)]))
             while len(parts) > 1:
                 parts = [a + b for a, b in zip(parts[::2], parts[1::2])]
-            mine = parts[0]
+            packed = parts[0]
             step *= radix
-    return mine, swapped(mine, "gy", 1)
+    return packed
 
 
 def row_swaps(first, second):
     num_x, num_y = lax.axis_size("gx"), lax.axis_size("gy")
     out = []
-    for start, slab in ((0, first), (1, second)):
+    for start, slab in ((1, second), (0, first)):
         partner = {}
         for i in range(num_x):
             j = i + 1 if i % 2 == start else i - 1
@@ -536,7 +531,7 @@
                 elif num_y % 2 == 0:
                     partner[i * num_y + y] = i * num_y + (y ^ 1)
         out.append(lax.ppermute(slab, ("gx", "gy"), sorted(partner.items())))
-    return out
+    return out[::-1]
 
 
 def col_swaps(first, second):
@@ -570,11 +565,11 @@
     first, second, *row_halos = col_slabs(source, coupling, inverse, row_halos)
     col_halos = col_swaps(first, second)
     *net_b, beta_b = forward(features, prepared, half, rows - half)
-    keep, give, adjoint, beta = sweeps_and_backward(
+    packed, adjoint, beta = sweeps_and_backward(
         num_feat, source, coupling, inverse, production, (beta_a, beta_b), (*row_halos, *col_halos),
         (weight_mid, weight_top), (*net_a, *net_b), mixing,
     )
-    grad_in, grad_mid, grad_top, grad_out, grad_bias = clip_all(*sum_over_case(keep, give), num_feat, hidden)
+    grad_in, grad_mid, grad_top, grad_out, grad_bias = clip_all(sum_over_case(packed), num_feat, hidden)
     return (adjoint, beta, grad_in, grad_mid, grad_top, grad_out.reshape(hidden), grad_bias)
 
 

time: 36.6 us -> 35.2 us (0.962)
  Pallas kernels: 16.3 us -> 15.5 us
  waiting for transfers between devices: 8.74 us -> 8.08 us
    pallas_call x1, Pallas kernels: 7.97 us -> 7.23 us  [sweeps_and_backward(): pl.pallas_call(functools.partial(adjoint_kernel, num_feat), in_specs=[nea...]
    ppermute x6 -> x5, waiting for transfers between devices: 8.73 us -> 8.07 us  [sum_over_case(): lax.ppermute(packed, axis, [(i, i ^ k * step) for i in range(count)])]
    ppermute x6 -> x5, starting transfers between devices: 5.9 us -> 5.87 us  [sum_over_case(): lax.ppermute(packed, axis, [(i, i ^ k * step) for i in range(count)])]
  transfers between devices with their start and end apart: 10 -> 9, of which waited for: 6 -> 5; matrix products, arithmetic and copies ran while one was open for 0% -> 0% of each run, Pallas kernels for 14% -> 15%
where the time goes in v8:
time: 35.2 us; the launch traced here: 35 us
  Pallas kernels  15.5 us (44%)
  starting transfers between devices  10.7 us (30%)
  waiting for transfers between devices  8.08 us (23%)
  between operations  0.74 us (2%)
    ppermute x5, waiting for transfers between devices, sum_over_case(): lax.ppermute(packed, axis, [(i, i ^ k * step) for i in range(count)])  8.07 us
    pallas_call x5, Pallas kernels, on_chip(): pl.pallas_call(kernel, in_specs=[here] * len(operands) + [there] * len(fa...  7.45 us
    pallas_call x1, Pallas kernels, sweeps_and_backward(): pl.pallas_call(functools.partial(adjoint_kernel, num_feat), in_specs=[nea...  7.23 us
    ppermute x5, starting transfers between devices, sum_over_case(): lax.ppermute(packed, axis, [(i, i ^ k * step) for i in range(count)])  5.87 us
    ppermute x2, starting transfers between devices, row_swaps(): out.append(lax.ppermute(slab, ('gx', 'gy'), sorted(partner.items())))  3.09 us
    ppermute x2, starting transfers between devices, col_swaps(): out.append(lax.ppermute(slab, 'gy', low + [(b, a) for a, b in low]))  1.75 us
    pallas_call x1, Pallas kernels, clip_all(): pl.pallas_call(clip_kernel, grid=(1,), in_specs=[whole(summed.shape)], ou...  0.81 us
  transfers between devices with their start and end apart: 9, of which 5 were waited for; matrix products, arithmetic and copies ran while one was open for 0% of the time, Pallas kernels for 15%

profile of v8, /device:TPU:0, one launch (start us, length us, event | category | flops | bytes accessed | tf_op | source)
XLA Modules:
  0.0 35.0 jit_solution(6864728749083494131)
XLA Ops:
  0.6 0.0 copy-start
  0.6 2.0 %load.1 = (bf16[5,64,256]{2,1,0:T(8,128)(2,1)S(1)}, bf16[4,64,256]{2,1,0:T(8,128)(2,1)S(1)}, f32[64,256]{1,0:T(8,128)}, s32[64,256]{1,0:T(8,128)}, f32[64,256]{1...) custom-call(bf16[5,64,256]{2,1,0:T(8,128)(2,1)} %refs_0_.1, ...), custom_call_target="tpu_custom_call" | custom-call | tf_op jit(solution)/shard_map/load/pallas_call | solution.py:34
  2.6 3.1 %collective-permute-start = (f32[60,256]{1,0:T(8,128)S(1)}, f32[60,256]{1,0:T(8,128)S(1)}, u32[]{:S(2)}, u32[]{:S(2)}) collective-permute-start(f32[60,256]{1,0:T(8,128)S(1)} %get-tuple-element.48), channel_id=1, source_target_pairs={{0,4},{1,5},{2,6},{3,7},{4,0},{5,1},{6,2},{7,3},{8,12},{9,13},{10,... | collective-permute-start | bytes 184328 | tf_op jit(solution)/shard_map/ppermute | solution.py:533
  5.7 0.0 collective-permute-start.1
  5.7 0.2 weights.1
  6.0 2.5 %network_forward.2 = (bf16[32,208,256]{2,1,0:T(8,128)(2,1)S(1)}, f32[32,192,256]{2,1,0:T(8,128)S(1)}, f32[32,256]{1,0:T(8,128)S(1)}) custom-call(bf16[10,64,256]{2,1,0:T(8,128)(2,1)S(1)} %get-tuple-element.50.feat, bf16[1280,256]{1,0:T(8,128)(2,1)S(1)} %get-tuple-element.56.w1, bf16[64,64]{1,0:T(8,128)(2,1)S(1)} %get-tuple-element.57.w2, ...), custom_call_target="tpu_custom_call" | custom-call | flops 144703488 | bytes 3571712 | tf_op jit(solution)/shard_map/network_forward/pallas_call | solution.py:34
  8.5 0.0 collective-permute-done.row_first
  8.5 0.0 collective-permute-done.1.row_second
  8.5 0.2 col_slabs.1
  8.7 0.6 %collective-permute-start.2 = (f32[40,128]{1,0:T(8,128)S(1)}, f32[40,128]{1,0:T(8,128)S(1)}, u32[]{:S(2)}, u32[]{:S(2)}) collective-permute-start(f32[40,128]{1,0:T(8,128)S(1)} %get-tuple-element.67), channel_id=1, source_target_pairs={{0,1},{2,3},{1,0},{3,2},{4,5},{6,7},{5,4},{7,6},{8,9},{10,11},{9,8... | collective-permute-start | bytes 61448 | tf_op jit(solution)/shard_map/ppermute | solution.py:544
  9.3 1.2 %collective-permute-start.3 = (f32[40,128]{1,0:T(8,128)S(1)}, f32[40,128]{1,0:T(8,128)S(1)}, u32[]{:S(2)}, u32[]{:S(2)}) collective-permute-start(f32[40,128]{1,0:T(8,128)S(1)} %get-tuple-element.68), channel_id=1, source_target_pairs={{1,2},{0,3},{2,1},{3,0},{5,6},{4,7},{6,5},{7,4},{9,10},{8,11},{10,... | collective-permute-start | bytes 61448 | tf_op jit(solution)/shard_map/ppermute | solution.py:544
  10.5 2.5 %network_forward.3 = (bf16[32,208,256]{2,1,0:T(8,128)(2,1)S(1)}, f32[32,192,256]{2,1,0:T(8,128)S(1)}, f32[32,256]{1,0:T(8,128)S(1)}) custom-call(bf16[10,64,256]{2,1,0:T(8,128)(2,1)S(1)} %get-tuple-element.50.feat, bf16[1280,256]{1,0:T(8,128)(2,1)S(1)} %get-tuple-element.56.w1, bf16[64,64]{1,0:T(8,128)(2,1)S(1)} %get-tuple-element.57.w2, ...), custom_call_target="tpu_custom_call" | custom-call | flops 144703488 | bytes 3571712 | tf_op jit(solution)/shard_map/network_forward/pallas_call | solution.py:34
  13.0 0.0 collective-permute-done.2.col_first
  13.0 0.0 collective-permute-done.3.col_second
  13.0 0.0 copy-done
  13.0 7.2 %sweeps_backward.1 = (f32[72,128]{1,0:T(8,128)S(1)}, f32[5,64,256]{2,1,0:T(8,128)}, f32[64,256]{1,0:T(8,128)}) custom-call(bf16[5,64,256]{2,1,0:T(8,128)(2,1)S(1)} %get-tuple-element.44.src, bf16[4,64,256]{2,1,0:T(8,128)(2,1)S(1)} %get-tuple-element.45.cpl, f32[64,256]{1,0:T(8,128)S(1)} %get-tuple-element.46.inv.inverse, ...), custom_call_target="tpu_custom_call" | custom-call | tf_op jit(solution)/shard_map/sweeps_backward/pallas_call | solution.py:452
  20.3 0.5 %collective-permute-start.4 = (f32[72,128]{1,0:T(8,128)S(1)}, f32[72,128]{1,0:T(8,128)S(1)}, u32[]{:S(2)}, u32[]{:S(2)}) collective-permute-start(f32[72,128]{1,0:T(8,128)S(1)} %get-tuple-element.75), channel_id=1, source_target_pairs={{0,1},{1,0},{2,3},{3,2},{4,5},{5,4},{6,7},{7,6},{8,9},{9,8},{10,11... | collective-permute-start | bytes 110600 | tf_op jit(solution)/shard_map/ppermute | solution.py:513
  20.8 0.9 %collective-permute-done.4 = f32[72,128]{1,0:T(8,128)S(1)} collective-permute-done((f32[72,128]{1,0:T(8,128)S(1)}, f32[72,128]{1,0:T(8,128)S(1)}, u32[]{:S(2)}, u32[]{:S(2)}) %collective-permute-start.4) | collective-permute-done | bytes 36896 | tf_op jit(solution)/shard_map/ppermute | solution.py:513
  21.6 0.9 %collective-permute-start.5 = (f32[72,128]{1,0:T(8,128)S(1)}, f32[72,128]{1,0:T(8,128)S(1)}, u32[]{:S(2)}, u32[]{:S(2)}) collective-permute-start(f32[72,128]{1,0:T(8,128)S(1)} %add.15), channel_id=1, source_target_pairs={{0,2},{1,3},{2,0},{3,1},{4,6},{5,7},{6,4},{7,5},{8,10},{9,11},{10,... | collective-permute-start | bytes 110600 | tf_op jit(solution)/shard_map/ppermute | solution.py:513
  22.5 3.1 %collective-permute-done.5 = f32[72,128]{1,0:T(8,128)S(1)} collective-permute-done((f32[72,128]{1,0:T(8,128)S(1)}, f32[72,128]{1,0:T(8,128)S(1)}, u32[]{:S(2)}, u32[]{:S(2)}) %collective-permute-start.5) | collective-permute-done | bytes 36896 | tf_op jit(solution)/shard_map/ppermute | solution.py:513
  25.6 3.4 %collective-permute-start.8 = (f32[72,128]{1,0:T(8,128)S(1)}, f32[72,128]{1,0:T(8,128)S(1)}, u32[]{:S(2)}, u32[]{:S(2)}) collective-permute-start(f32[72,128]{1,0:T(8,128)S(1)} %add.16), channel_id=1, source_target_pairs={{0,12},{4,8},{8,4},{12,0},{1,13},{5,9},{9,5},{13,1},{2,14},{6,10},... | collective-permute-start | bytes 110600 | tf_op jit(solution)/shard_map/ppermute | solution.py:513
  29.0 1.1 %collective-permute-start.7 = (f32[72,128]{1,0:T(8,128)S(1)}, f32[72,128]{1,0:T(8,128)S(1)}, u32[]{:S(2)}, u32[]{:S(2)}) collective-permute-start(f32[72,128]{1,0:T(8,128)S(1)} %add.16), channel_id=1, source_target_pairs={{0,8},{4,12},{8,0},{12,4},{1,9},{5,13},{9,1},{13,5},{2,10},{6,14},... | collective-permute-start | bytes 110600 | tf_op jit(solution)/shard_map/ppermute | solution.py:513
  30.1 0.0 collective-permute-start.6
  30.1 1.3 %collective-permute-done.8 = f32[72,128]{1,0:T(8,128)S(1)} collective-permute-done((f32[72,128]{1,0:T(8,128)S(1)}, f32[72,128]{1,0:T(8,128)S(1)}, u32[]{:S(2)}, u32[]{:S(2)}) %collective-permute-start.8) | collective-permute-done | bytes 36896 | tf_op jit(solution)/shard_map/ppermute | solution.py:513
  31.4 2.4 %collective-permute-done.7 = f32[72,128]{1,0:T(8,128)S(1)} collective-permute-done((f32[72,128]{1,0:T(8,128)S(1)}, f32[72,128]{1,0:T(8,128)S(1)}, u32[]{:S(2)}, u32[]{:S(2)}) %collective-permute-start.7) | collective-permute-done | bytes 36896 | tf_op jit(solution)/shard_map/ppermute | solution.py:513
  33.8 0.4 %collective-permute-done.6 = f32[72,128]{1,0:T(8,128)S(1)} collective-permute-done((f32[72,128]{1,0:T(8,128)S(1)}, f32[72,128]{1,0:T(8,128)S(1)}, u32[]{:S(2)}, u32[]{:S(2)}) %collective-permute-start.6) | collective-permute-done | bytes 36896 | tf_op jit(solution)/shard_map/ppermute | solution.py:513
  34.2 0.8 %clip.1 = (f32[10,64]{1,0:T(8,128)}, f32[64,64]{1,0:T(8,128)}, f32[64,64]{1,0:T(8,128)}, f32[1,64]{1,0:T(1,128)}, f32[3,64]{1,0:T(4,128)}) custom-call(f32[72,128]{1,0:T(8,128)S(1)} %add_add_fusion.summed), custom_call_target="tpu_custom_call" | custom-call | tf_op jit(solution)/shard_map/clip/pallas_call | solution.py:495
  (3 shorter events, 0.0 us)
Async XLA Ops:
  0.6 12.4 %copy-start = (f32[5,5]{1,0:T(8,128)S(1)}, f32[5,5]{1,0:T(8,128)}, u32[]{:S(2)}) copy-start(f32[5,5]{1,0:T(8,128)} %mix.1) | copy-start | bytes 304
  2.6 5.9 %collective-permute-start = (f32[60,256]{1,0:T(8,128)S(1)}, f32[60,256]{1,0:T(8,128)S(1)}, u32[]{:S(2)}, u32[]{:S(2)}) collective-permute-start(f32[60,256]{1,0:T(8,128)S(1)} %get-tuple-element.48), channel_id=1, source_target_pairs={{0,4},{1,5},{2,6},{3,7},{4,0},{5,1},{6,2},{7,3},{8,12},{9,13},{10,... | collective-permute-start | bytes 184328 | tf_op jit(solution)/shard_map/ppermute | solution.py:533
  5.7 2.8 %collective-permute-start.1 = (f32[60,256]{1,0:T(8,128)S(1)}, f32[60,256]{1,0:T(8,128)S(1)}, u32[]{:S(2)}, u32[]{:S(2)}) collective-permute-start(f32[60,256]{1,0:T(8,128)S(1)} %get-tuple-element.49), channel_id=1, source_target_pairs={{0,1},{1,0},{2,3},{3,2},{4,8},{5,9},{6,10},{7,11},{8,4},{9,5},{10,... | collective-permute-start | bytes 184328 | tf_op jit(solution)/shard_map/ppermute | solution.py:533
  8.7 4.3 %collective-permute-start.2 = (f32[40,128]{1,0:T(8,128)S(1)}, f32[40,128]{1,0:T(8,128)S(1)}, u32[]{:S(2)}, u32[]{:S(2)}) collective-permute-start(f32[40,128]{1,0:T(8,128)S(1)} %get-tuple-element.67), channel_id=1, source_target_pairs={{0,1},{2,3},{1,0},{3,2},{4,5},{6,7},{5,4},{7,6},{8,9},{10,11},{9,8... | collective-permute-start | bytes 61448 | tf_op jit(solution)/shard_map/ppermute | solution.py:544
  9.3 3.7 %collective-permute-start.3 = (f32[40,128]{1,0:T(8,128)S(1)}, f32[40,128]{1,0:T(8,128)S(1)}, u32[]{:S(2)}, u32[]{:S(2)}) collective-permute-start(f32[40,128]{1,0:T(8,128)S(1)} %get-tuple-element.68), channel_id=1, source_target_pairs={{1,2},{0,3},{2,1},{3,0},{5,6},{4,7},{6,5},{7,4},{9,10},{8,11},{10,... | collective-permute-start | bytes 61448 | tf_op jit(solution)/shard_map/ppermute | solution.py:544
  20.3 1.4 %collective-permute-start.4 = (f32[72,128]{1,0:T(8,128)S(1)}, f32[72,128]{1,0:T(8,128)S(1)}, u32[]{:S(2)}, u32[]{:S(2)}) collective-permute-start(f32[72,128]{1,0:T(8,128)S(1)} %get-tuple-element.75), channel_id=1, source_target_pairs={{0,1},{1,0},{2,3},{3,2},{4,5},{5,4},{6,7},{7,6},{8,9},{9,8},{10,11... | collective-permute-start | bytes 110600 | tf_op jit(solution)/shard_map/ppermute | solution.py:513
  21.6 4.0 %collective-permute-start.5 = (f32[72,128]{1,0:T(8,128)S(1)}, f32[72,128]{1,0:T(8,128)S(1)}, u32[]{:S(2)}, u32[]{:S(2)}) collective-permute-start(f32[72,128]{1,0:T(8,128)S(1)} %add.15), channel_id=1, source_target_pairs={{0,2},{1,3},{2,0},{3,1},{4,6},{5,7},{6,4},{7,5},{8,10},{9,11},{10,... | collective-permute-start | bytes 110600 | tf_op jit(solution)/shard_map/ppermute | solution.py:513
  25.6 5.8 %collective-permute-start.8 = (f32[72,128]{1,0:T(8,128)S(1)}, f32[72,128]{1,0:T(8,128)S(1)}, u32[]{:S(2)}, u32[]{:S(2)}) collective-permute-start(f32[72,128]{1,0:T(8,128)S(1)} %add.16), channel_id=1, source_target_pairs={{0,12},{4,8},{8,4},{12,0},{1,13},{5,9},{9,5},{13,1},{2,14},{6,10},... | collective-permute-start | bytes 110600 | tf_op jit(solution)/shard_map/ppermute | solution.py:513
  29.0 4.9 %collective-permute-start.7 = (f32[72,128]{1,0:T(8,128)S(1)}, f32[72,128]{1,0:T(8,128)S(1)}, u32[]{:S(2)}, u32[]{:S(2)}) collective-permute-start(f32[72,128]{1,0:T(8,128)S(1)} %add.16), channel_id=1, source_target_pairs={{0,8},{4,12},{8,0},{12,4},{1,9},{5,13},{9,1},{13,5},{2,10},{6,14},... | collective-permute-start | bytes 110600 | tf_op jit(solution)/shard_map/ppermute | solution.py:513
  30.1 4.1 %collective-permute-start.6 = (f32[72,128]{1,0:T(8,128)S(1)}, f32[72,128]{1,0:T(8,128)S(1)}, u32[]{:S(2)}, u32[]{:S(2)}) collective-permute-start(f32[72,128]{1,0:T(8,128)S(1)} %add.16), channel_id=1, source_target_pairs={{0,4},{4,0},{8,12},{12,8},{1,5},{5,1},{9,13},{13,9},{2,6},{6,2},{1... | collective-permute-start | bytes 110600 | tf_op jit(solution)/shard_map/ppermute | solution.py:513

commit v9 on v8

--- a/solution.py
+++ b/solution.py
@@ -1,4 +1,5 @@
 import functools
+import itertools
 
 import jax
 import jax.numpy as jnp
@@ -61,7 +62,7 @@
 
 def load_kernel(count, *refs):
     far, near = refs[:count], refs[count : 2 * count]
-    inv, first, second, sems = refs[2 * count :]
+    inv, second, first, sems = refs[2 * count :]
     copies = [pltpu.make_async_copy(far[k], near[k], sems.at[k]) for k in range(count)]
     for copy in copies:
         copy.start()
@@ -356,6 +357,7 @@
                 terms = [couple[k][d] * around[k][d] for d in range(nc)]
                 inc = (terms[0] + terms[1]) + (terms[2] + terms[3])
                 total[k] = [total[k][a] + weights[b][a] * inc for a in range(nv)]
+            yield
         for k in range(count):
             for a in range(nv):
                 if last:
@@ -387,48 +389,57 @@
         def add(ref, part):
             ref[...] = part if first == 0 else ref[...] + part
 
-        def slanted(number, product, lo):
-            total, out = jnp.zeros((hidden, LANE), F32), []
+        def slanted(number, product, lo, out):
+            total = jnp.zeros((hidden, LANE), F32)
             for q in range(blk):
                 d = product[:, q * cols : (q + 1) * cols] * slopes[start + q, lo : lo + hidden]
                 total = total + fold(d)
                 out.append(d.astype(BF16))
+                yield
             add(sums.at[number], total)
-            return joined(out)
-
-        out_sum, sens_rows = jnp.zeros((hidden, LANE), F32), []
+
+        out_sum, sens_rows, d3, d2, d1 = jnp.zeros((hidden, LANE), F32), [], [], [], []
         for q in range(blk):
             sen = jnp.broadcast_to(sens[q : q + 1], (hidden, cols))
             out_sum = out_sum + fold(acts[start + q, 2 * hidden + 16 :].astype(F32) * sen)
             sens_rows.append(sen)
+            yield
         add(sums.at[0], out_sum)
-        d3 = slanted(3, joined(sens_rows), 2 * hidden)
-        yield
+        yield from slanted(3, joined(sens_rows), 2 * hidden, d3)
+        d3 = joined(d3)
         product = jnp.dot(wtop[...], d3, preferred_element_type=F32)
         yield
-        d2 = slanted(2, product, hidden)
         add(g_top, outer(layer(hidden, 2 * hidden), d3))
         yield
+        yield from slanted(2, product, hidden, d2)
+        d2 = joined(d2)
         product = jnp.dot(wmid[...], d2, preferred_element_type=F32)
         yield
-        d1 = slanted(1, product, 0)
         add(g_mid, outer(layer(0, hidden), d2))
         yield
-        add(g_in, outer(d1, layer(2 * hidden, 2 * hidden + 16)))
-
+        yield from slanted(1, product, 0, d1)
+        add(g_in, outer(joined(d1), layer(2 * hidden, 2 * hidden + 16)))
+
+    backward_turns = 4 * blk + 4
+
+    def together(sweeps, back):
+        turns = max(nv * len(sweeps), 1)
+        sweeps = itertools.chain(*(sweep(*x) for x in sweeps))
+        for turn in range(turns):
+            next(sweeps, None)
+            for _ in range(backward_turns * turn // turns, backward_turns * (turn + 1) // turns):
+                next(back, None)
+        for _ in itertools.chain(sweeps, back):
+            pass
+
+    ahead = [2 * (SWEEPS - number) for number in range(SWEEPS + 1)]
     for number in range(1, SWEEPS):
-        for t in range(SWEEPS + 1 - number):
-            sweep(number, t)
-    stages = iter(())
+        together([(number, t) for t in range(min(ahead[number] + 1, tiles))], iter(()))
     for t in range(1, tiles - 1):
-        for number in range(1, SWEEPS + 1):
-            if t + SWEEPS - number < tiles:
-                sweep(number, t + SWEEPS - number)
-            next(stages, None)
-        stages = backward((t - 1) * blk)
+        step = [(n, t + ahead[n]) for n in range(1, SWEEPS + 1) if t + ahead[n] < tiles]
+        together(step, backward((t - 2) * blk) if t > 1 else iter(()))
     copies[2].start()
-    for _ in stages:
-        pass
+    together([], backward(rows - blk))
 
     turned = jnp.transpose(joined([g_in[...], jnp.zeros((hidden, LANE - 16), F32)]))
     tail = turned[SUB : 2 * SUB]
@@ -556,8 +567,8 @@
         weight_in, weight_mid, weight_top, weight_out.reshape(1, hidden), biases,
     ])
     source, coupling, _, _, production, features, weight_in, weight_mid, weight_top, wout, biases = loaded[:11]
-    inverse, *row_slabs = loaded[11:]
-    row_halos = row_swaps(*row_slabs)
+    inverse, second, first = loaded[11:]
+    row_halos = row_swaps(first, second)
     prepared = prepare(weight_in, weight_mid, weight_top, wout, biases)
     half = rows - 32
     *net_a, beta_a = forward(features, prepared, 0, half)

time: 35.2 us -> 35.1 us (level)
  no operation moved by 1% of the time
where the time goes in v9:
time: 35.1 us; the launch traced here: 35 us
  Pallas kernels  15.4 us (44%)
  starting transfers between devices  10.7 us (30%)
  waiting for transfers between devices  8.08 us (23%)
  between operations  0.74 us (2%)
    ppermute x5, waiting for transfers between devices, sum_over_case(): lax.ppermute(packed, axis, [(i, i ^ k * step) for i in range(count)])  8.07 us
    pallas_call x5, Pallas kernels, on_chip(): pl.pallas_call(kernel, in_specs=[here] * len(operands) + [there] * len(fa...  7.45 us
    pallas_call x1, Pallas kernels, sweeps_and_backward(): pl.pallas_call(functools.partial(adjoint_kernel, num_feat), in_specs=[nea...  7.18 us
    ppermute x5, starting transfers between devices, sum_over_case(): lax.ppermute(packed, axis, [(i, i ^ k * step) for i in range(count)])  5.87 us
    ppermute x2, starting transfers between devices, row_swaps(): out.append(lax.ppermute(slab, ('gx', 'gy'), sorted(partner.items())))  3.09 us
    ppermute x2, starting transfers between devices, col_swaps(): out.append(lax.ppermute(slab, 'gy', low + [(b, a) for a, b in low]))  1.75 us
    pallas_call x1, Pallas kernels, clip_all(): pl.pallas_call(clip_kernel, grid=(1,), in_specs=[whole(summed.shape)], ou...  0.81 us
  transfers between devices with their start and end apart: 9, of which 5 were waited for; matrix products, arithmetic and copies ran while one was open for 0% of the time, Pallas kernels for 15%

profile of v9, /device:TPU:0, one launch (start us, length us, event | category | flops | bytes accessed | tf_op | source)
XLA Modules:
  0.0 35.0 jit_solution(12636896723073496976)
XLA Ops:
  0.6 0.0 copy-start
  0.6 2.0 %load.1 = (bf16[5,64,256]{2,1,0:T(8,128)(2,1)S(1)}, bf16[4,64,256]{2,1,0:T(8,128)(2,1)S(1)}, f32[64,256]{1,0:T(8,128)}, s32[64,256]{1,0:T(8,128)}, f32[64,256]{1...) custom-call(bf16[5,64,256]{2,1,0:T(8,128)(2,1)} %refs_0_.1, ...), custom_call_target="tpu_custom_call" | custom-call | tf_op jit(solution)/shard_map/load/pallas_call | solution.py:35
  2.6 3.1 %collective-permute-start = (f32[60,256]{1,0:T(8,128)S(1)}, f32[60,256]{1,0:T(8,128)S(1)}, u32[]{:S(2)}, u32[]{:S(2)}) collective-permute-start(f32[60,256]{1,0:T(8,128)S(1)} %get-tuple-element.48), channel_id=1, source_target_pairs={{0,4},{1,5},{2,6},{3,7},{4,0},{5,1},{6,2},{7,3},{8,12},{9,13},{10,... | collective-permute-start | bytes 184328 | tf_op jit(solution)/shard_map/ppermute | solution.py:544
  5.7 0.0 collective-permute-start.1
  5.7 0.2 weights.1
  6.0 2.5 %network_forward.2 = (bf16[32,208,256]{2,1,0:T(8,128)(2,1)S(1)}, f32[32,192,256]{2,1,0:T(8,128)S(1)}, f32[32,256]{1,0:T(8,128)S(1)}) custom-call(bf16[10,64,256]{2,1,0:T(8,128)(2,1)S(1)} %get-tuple-element.50.feat, bf16[1280,256]{1,0:T(8,128)(2,1)S(1)} %get-tuple-element.56.w1, bf16[64,64]{1,0:T(8,128)(2,1)S(1)} %get-tuple-element.57.w2, ...), custom_call_target="tpu_custom_call" | custom-call | flops 144703488 | bytes 3571712 | tf_op jit(solution)/shard_map/network_forward/pallas_call | solution.py:35
  8.5 0.0 collective-permute-done.row_first
  8.5 0.0 collective-permute-done.1.row_second
  8.5 0.2 col_slabs.1
  8.7 0.6 %collective-permute-start.2 = (f32[40,128]{1,0:T(8,128)S(1)}, f32[40,128]{1,0:T(8,128)S(1)}, u32[]{:S(2)}, u32[]{:S(2)}) collective-permute-start(f32[40,128]{1,0:T(8,128)S(1)} %get-tuple-element.67), channel_id=1, source_target_pairs={{0,1},{2,3},{1,0},{3,2},{4,5},{6,7},{5,4},{7,6},{8,9},{10,11},{9,8... | collective-permute-start | bytes 61448 | tf_op jit(solution)/shard_map/ppermute | solution.py:555
  9.3 1.2 %collective-permute-start.3 = (f32[40,128]{1,0:T(8,128)S(1)}, f32[40,128]{1,0:T(8,128)S(1)}, u32[]{:S(2)}, u32[]{:S(2)}) collective-permute-start(f32[40,128]{1,0:T(8,128)S(1)} %get-tuple-element.68), channel_id=1, source_target_pairs={{1,2},{0,3},{2,1},{3,0},{5,6},{4,7},{6,5},{7,4},{9,10},{8,11},{10,... | collective-permute-start | bytes 61448 | tf_op jit(solution)/shard_map/ppermute | solution.py:555
  10.5 2.5 %network_forward.3 = (bf16[32,208,256]{2,1,0:T(8,128)(2,1)S(1)}, f32[32,192,256]{2,1,0:T(8,128)S(1)}, f32[32,256]{1,0:T(8,128)S(1)}) custom-call(bf16[10,64,256]{2,1,0:T(8,128)(2,1)S(1)} %get-tuple-element.50.feat, bf16[1280,256]{1,0:T(8,128)(2,1)S(1)} %get-tuple-element.56.w1, bf16[64,64]{1,0:T(8,128)(2,1)S(1)} %get-tuple-element.57.w2, ...), custom_call_target="tpu_custom_call" | custom-call | flops 144703488 | bytes 3571712 | tf_op jit(solution)/shard_map/network_forward/pallas_call | solution.py:35
  13.0 0.0 collective-permute-done.2.col_first
  13.0 0.0 collective-permute-done.3.col_second
  13.0 0.0 copy-done
  13.0 7.2 %sweeps_backward.1 = (f32[72,128]{1,0:T(8,128)S(1)}, f32[5,64,256]{2,1,0:T(8,128)}, f32[64,256]{1,0:T(8,128)}) custom-call(bf16[5,64,256]{2,1,0:T(8,128)(2,1)S(1)} %get-tuple-element.44.src, bf16[4,64,256]{2,1,0:T(8,128)(2,1)S(1)} %get-tuple-element.45.cpl, f32[64,256]{1,0:T(8,128)S(1)} %get-tuple-element.46.inv.inverse, ...), custom_call_target="tpu_custom_call" | custom-call | tf_op jit(solution)/shard_map/sweeps_backward/pallas_call | solution.py:463
  20.2 0.5 %collective-permute-start.4 = (f32[72,128]{1,0:T(8,128)S(1)}, f32[72,128]{1,0:T(8,128)S(1)}, u32[]{:S(2)}, u32[]{:S(2)}) collective-permute-start(f32[72,128]{1,0:T(8,128)S(1)} %get-tuple-element.75), channel_id=1, source_target_pairs={{0,1},{1,0},{2,3},{3,2},{4,5},{5,4},{6,7},{7,6},{8,9},{9,8},{10,11... | collective-permute-start | bytes 110600 | tf_op jit(solution)/shard_map/ppermute | solution.py:524
  20.7 0.9 %collective-permute-done.4 = f32[72,128]{1,0:T(8,128)S(1)} collective-permute-done((f32[72,128]{1,0:T(8,128)S(1)}, f32[72,128]{1,0:T(8,128)S(1)}, u32[]{:S(2)}, u32[]{:S(2)}) %collective-permute-start.4) | collective-permute-done | bytes 36896 | tf_op jit(solution)/shard_map/ppermute | solution.py:524
  21.6 0.9 %collective-permute-start.5 = (f32[72,128]{1,0:T(8,128)S(1)}, f32[72,128]{1,0:T(8,128)S(1)}, u32[]{:S(2)}, u32[]{:S(2)}) collective-permute-start(f32[72,128]{1,0:T(8,128)S(1)} %add.15), channel_id=1, source_target_pairs={{0,2},{1,3},{2,0},{3,1},{4,6},{5,7},{6,4},{7,5},{8,10},{9,11},{10,... | collective-permute-start | bytes 110600 | tf_op jit(solution)/shard_map/ppermute | solution.py:524
  22.5 3.1 %collective-permute-done.5 = f32[72,128]{1,0:T(8,128)S(1)} collective-permute-done((f32[72,128]{1,0:T(8,128)S(1)}, f32[72,128]{1,0:T(8,128)S(1)}, u32[]{:S(2)}, u32[]{:S(2)}) %collective-permute-start.5) | collective-permute-done | bytes 36896 | tf_op jit(solution)/shard_map/ppermute | solution.py:524
  25.6 3.4 %collective-permute-start.8 = (f32[72,128]{1,0:T(8,128)S(1)}, f32[72,128]{1,0:T(8,128)S(1)}, u32[]{:S(2)}, u32[]{:S(2)}) collective-permute-start(f32[72,128]{1,0:T(8,128)S(1)} %add.16), channel_id=1, source_target_pairs={{0,12},{4,8},{8,4},{12,0},{1,13},{5,9},{9,5},{13,1},{2,14},{6,10},... | collective-permute-start | bytes 110600 | tf_op jit(solution)/shard_map/ppermute | solution.py:524
  28.9 1.1 %collective-permute-start.7 = (f32[72,128]{1,0:T(8,128)S(1)}, f32[72,128]{1,0:T(8,128)S(1)}, u32[]{:S(2)}, u32[]{:S(2)}) collective-permute-start(f32[72,128]{1,0:T(8,128)S(1)} %add.16), channel_id=1, source_target_pairs={{0,8},{4,12},{8,0},{12,4},{1,9},{5,13},{9,1},{13,5},{2,10},{6,14},... | collective-permute-start | bytes 110600 | tf_op jit(solution)/shard_map/ppermute | solution.py:524
  30.0 0.0 collective-permute-start.6
  30.0 1.3 %collective-permute-done.8 = f32[72,128]{1,0:T(8,128)S(1)} collective-permute-done((f32[72,128]{1,0:T(8,128)S(1)}, f32[72,128]{1,0:T(8,128)S(1)}, u32[]{:S(2)}, u32[]{:S(2)}) %collective-permute-start.8) | collective-permute-done | bytes 36896 | tf_op jit(solution)/shard_map/ppermute | solution.py:524
  31.4 2.4 %collective-permute-done.7 = f32[72,128]{1,0:T(8,128)S(1)} collective-permute-done((f32[72,128]{1,0:T(8,128)S(1)}, f32[72,128]{1,0:T(8,128)S(1)}, u32[]{:S(2)}, u32[]{:S(2)}) %collective-permute-start.7) | collective-permute-done | bytes 36896 | tf_op jit(solution)/shard_map/ppermute | solution.py:524
  33.8 0.4 %collective-permute-done.6 = f32[72,128]{1,0:T(8,128)S(1)} collective-permute-done((f32[72,128]{1,0:T(8,128)S(1)}, f32[72,128]{1,0:T(8,128)S(1)}, u32[]{:S(2)}, u32[]{:S(2)}) %collective-permute-start.6) | collective-permute-done | bytes 36896 | tf_op jit(solution)/shard_map/ppermute | solution.py:524
  34.2 0.8 %clip.1 = (f32[10,64]{1,0:T(8,128)}, f32[64,64]{1,0:T(8,128)}, f32[64,64]{1,0:T(8,128)}, f32[1,64]{1,0:T(1,128)}, f32[3,64]{1,0:T(4,128)}) custom-call(f32[72,128]{1,0:T(8,128)S(1)} %add_add_fusion.summed), custom_call_target="tpu_custom_call" | custom-call | tf_op jit(solution)/shard_map/clip/pallas_call | solution.py:506
  (3 shorter events, 0.0 us)
Async XLA Ops:
  0.6 12.4 %copy-start = (f32[5,5]{1,0:T(8,128)S(1)}, f32[5,5]{1,0:T(8,128)}, u32[]{:S(2)}) copy-start(f32[5,5]{1,0:T(8,128)} %mix.1) | copy-start | bytes 304
  2.6 5.9 %collective-permute-start = (f32[60,256]{1,0:T(8,128)S(1)}, f32[60,256]{1,0:T(8,128)S(1)}, u32[]{:S(2)}, u32[]{:S(2)}) collective-permute-start(f32[60,256]{1,0:T(8,128)S(1)} %get-tuple-element.48), channel_id=1, source_target_pairs={{0,4},{1,5},{2,6},{3,7},{4,0},{5,1},{6,2},{7,3},{8,12},{9,13},{10,... | collective-permute-start | bytes 184328 | tf_op jit(solution)/shard_map/ppermute | solution.py:544
  5.7 2.8 %collective-permute-start.1 = (f32[60,256]{1,0:T(8,128)S(1)}, f32[60,256]{1,0:T(8,128)S(1)}, u32[]{:S(2)}, u32[]{:S(2)}) collective-permute-start(f32[60,256]{1,0:T(8,128)S(1)} %get-tuple-element.49), channel_id=1, source_target_pairs={{0,1},{1,0},{2,3},{3,2},{4,8},{5,9},{6,10},{7,11},{8,4},{9,5},{10,... | collective-permute-start | bytes 184328 | tf_op jit(solution)/shard_map/ppermute | solution.py:544
  8.7 4.3 %collective-permute-start.2 = (f32[40,128]{1,0:T(8,128)S(1)}, f32[40,128]{1,0:T(8,128)S(1)}, u32[]{:S(2)}, u32[]{:S(2)}) collective-permute-start(f32[40,128]{1,0:T(8,128)S(1)} %get-tuple-element.67), channel_id=1, source_target_pairs={{0,1},{2,3},{1,0},{3,2},{4,5},{6,7},{5,4},{7,6},{8,9},{10,11},{9,8... | collective-permute-start | bytes 61448 | tf_op jit(solution)/shard_map/ppermute | solution.py:555
  9.3 3.7 %collective-permute-start.3 = (f32[40,128]{1,0:T(8,128)S(1)}, f32[40,128]{1,0:T(8,128)S(1)}, u32[]{:S(2)}, u32[]{:S(2)}) collective-permute-start(f32[40,128]{1,0:T(8,128)S(1)} %get-tuple-element.68), channel_id=1, source_target_pairs={{1,2},{0,3},{2,1},{3,0},{5,6},{4,7},{6,5},{7,4},{9,10},{8,11},{10,... | collective-permute-start | bytes 61448 | tf_op jit(solution)/shard_map/ppermute | solution.py:555
  20.2 1.4 %collective-permute-start.4 = (f32[72,128]{1,0:T(8,128)S(1)}, f32[72,128]{1,0:T(8,128)S(1)}, u32[]{:S(2)}, u32[]{:S(2)}) collective-permute-start(f32[72,128]{1,0:T(8,128)S(1)} %get-tuple-element.75), channel_id=1, source_target_pairs={{0,1},{1,0},{2,3},{3,2},{4,5},{5,4},{6,7},{7,6},{8,9},{9,8},{10,11... | collective-permute-start | bytes 110600 | tf_op jit(solution)/shard_map/ppermute | solution.py:524
  21.6 4.0 %collective-permute-start.5 = (f32[72,128]{1,0:T(8,128)S(1)}, f32[72,128]{1,0:T(8,128)S(1)}, u32[]{:S(2)}, u32[]{:S(2)}) collective-permute-start(f32[72,128]{1,0:T(8,128)S(1)} %add.15), channel_id=1, source_target_pairs={{0,2},{1,3},{2,0},{3,1},{4,6},{5,7},{6,4},{7,5},{8,10},{9,11},{10,... | collective-permute-start | bytes 110600 | tf_op jit(solution)/shard_map/ppermute | solution.py:524
  25.6 5.8 %collective-permute-start.8 = (f32[72,128]{1,0:T(8,128)S(1)}, f32[72,128]{1,0:T(8,128)S(1)}, u32[]{:S(2)}, u32[]{:S(2)}) collective-permute-start(f32[72,128]{1,0:T(8,128)S(1)} %add.16), channel_id=1, source_target_pairs={{0,12},{4,8},{8,4},{12,0},{1,13},{5,9},{9,5},{13,1},{2,14},{6,10},... | collective-permute-start | bytes 110600 | tf_op jit(solution)/shard_map/ppermute | solution.py:524
  28.9 4.9 %collective-permute-start.7 = (f32[72,128]{1,0:T(8,128)S(1)}, f32[72,128]{1,0:T(8,128)S(1)}, u32[]{:S(2)}, u32[]{:S(2)}) collective-permute-start(f32[72,128]{1,0:T(8,128)S(1)} %add.16), channel_id=1, source_target_pairs={{0,8},{4,12},{8,0},{12,4},{1,9},{5,13},{9,1},{13,5},{2,10},{6,14},... | collective-permute-start | bytes 110600 | tf_op jit(solution)/shard_map/ppermute | solution.py:524
  30.0 4.1 %collective-permute-start.6 = (f32[72,128]{1,0:T(8,128)S(1)}, f32[72,128]{1,0:T(8,128)S(1)}, u32[]{:S(2)}, u32[]{:S(2)}) collective-permute-start(f32[72,128]{1,0:T(8,128)S(1)} %add.16), channel_id=1, source_target_pairs={{0,4},{4,0},{8,12},{12,8},{1,5},{5,1},{9,13},{13,9},{2,6},{6,2},{1... | collective-permute-start | bytes 110600 | tf_op jit(solution)/shard_map/ppermute | solution.py:524

commit v10 on v9

--- a/solution.py
+++ b/solution.py
@@ -198,7 +198,7 @@
     return 1.0 - act * act
 
 
-def forward_kernel(first_row, feat, w1, w2, w3, cst, acts, slopes, beta, x1):
+def forward_kernel(first_row, feat, w1, w2, w3, cst, acts, turned, slopes, beta, x1):
     nf, _, cols = feat.shape
     hidden = w2.shape[0]
     step_rows, blk, per = hidden + 16, 16, 4
@@ -217,20 +217,19 @@
                 part = first[q * step_rows : (q + 1) * step_rows]
                 one = jnp.tanh(part[:hidden] + b1).astype(BF16)
                 slopes[start + q, 0:hidden] = slope(one.astype(F32))
-                acts[start + q, 0:hidden] = one
-                acts[start + q, 2 * hidden : 2 * hidden + 16] = part[hidden:].astype(BF16)
+                acts[start + q, 0:16] = part[hidden:].astype(BF16)
                 ones.append(one)
             second = jnp.dot(w2[...], jnp.concatenate(ones, axis=1), preferred_element_type=F32)
             twos = []
             for q in range(per):
                 two = jnp.tanh(second[:, q * cols : (q + 1) * cols] + b2).astype(BF16)
                 slopes[start + (g * per + q), hidden : 2 * hidden] = slope(two.astype(F32))
-                acts[start + (g * per + q), hidden : 2 * hidden] = two
+                turned[start + (g * per + q)] = jnp.transpose(jnp.concatenate([ones[q], two], axis=0))
                 twos.append(two)
             third = jnp.dot(w3[...], jnp.concatenate(twos, axis=1), preferred_element_type=F32)
             for q in range(per):
                 three = jnp.tanh(third[:, q * cols : (q + 1) * cols] + b3).astype(BF16)
-                acts[start + (g * per + q), 2 * hidden + 16 :] = three
+                acts[start + (g * per + q), 16:] = three
                 three = three.astype(F32)
                 slopes[start + (g * per + q), 2 * hidden :] = wo * slope(three)
                 lines.append(1.0 + jnp.sum(three * wo, axis=0, keepdims=True))
@@ -241,11 +240,16 @@
     nf, _, cols = features.shape
     w1, w2 = prepared[:2]
     hidden = w2.shape[0]
-    high = 3 * hidden + 16
+    high = hidden + 16
     return on_chip(
         functools.partial(forward_kernel, first_row),
         [features, *prepared],
-        [((count, high, cols), BF16), ((count, 3 * hidden, cols), F32), ((count, cols), F32)],
+        [
+            ((count, high, cols), BF16),
+            ((count, cols, 2 * hidden), BF16),
+            ((count, 3 * hidden, cols), F32),
+            ((count, cols), F32),
+        ],
         [pltpu.VMEM((w1.shape[1], cols), BF16)],
         cost_estimate=pl.CostEstimate(
             flops=2 * count * cols * (nf + 2 * hidden) * hidden,
@@ -325,9 +329,9 @@
 
 def adjoint_kernel(
     num_feat, src, cpl, inverse, prod, beta_a, beta_b, north, south, col_first, col_second,
-    wmid, wtop, acts_a, slopes_a, acts_b, slopes_b, mix,
+    wmid, wtop, acts_a, turned_a, slopes_a, acts_b, turned_b, slopes_b, mix,
     packed, adj_out, beta_out,
-    raw, src_x, cpl_x, adj, done, sums, g_mid, g_top, g_in, sems,
+    raw, src_x, cpl_x, adj, done, sums, g_two, g_in, sems,
 ):
     nv, rows, cols = src.shape
     nc = cpl.shape[0]
@@ -377,14 +381,11 @@
 
     def backward(first):
         if first < half:
-            acts, slopes, beta, start = acts_a, slopes_a, beta_a, first
+            acts, turned, slopes, beta, start = acts_a, turned_a, slopes_a, beta_a, first
         else:
-            acts, slopes, beta, start = acts_b, slopes_b, beta_b, first - half
+            acts, turned, slopes, beta, start = acts_b, turned_b, slopes_b, beta_b, first - half
         here = slice(first, first + blk)
         sens = done[nv - 1, here] * prod[here] + REG_WEIGHT * (beta[start : start + blk] - 1.0)
-
-        def layer(lo, high):
-            return joined([acts[start + q, lo:high] for q in range(blk)])
 
         def add(ref, part):
             ref[...] = part if first == 0 else ref[...] + part
@@ -401,7 +402,7 @@
         out_sum, sens_rows, d3, d2, d1 = jnp.zeros((hidden, LANE), F32), [], [], [], []
         for q in range(blk):
             sen = jnp.broadcast_to(sens[q : q + 1], (hidden, cols))
-            out_sum = out_sum + fold(acts[start + q, 2 * hidden + 16 :].astype(F32) * sen)
+            out_sum = out_sum + fold(acts[start + q, 16:].astype(F32) * sen)
             sens_rows.append(sen)
             yield
         add(sums.at[0], out_sum)
@@ -409,18 +410,23 @@
         d3 = joined(d3)
         product = jnp.dot(wtop[...], d3, preferred_element_type=F32)
         yield
-        add(g_top, outer(layer(hidden, 2 * hidden), d3))
-        yield
         yield from slanted(2, product, hidden, d2)
         d2 = joined(d2)
         product = jnp.dot(wmid[...], d2, preferred_element_type=F32)
         yield
-        add(g_mid, outer(layer(0, hidden), d2))
+        add(
+            g_two,
+            jnp.dot(
+                jnp.concatenate([d2, d3], axis=0),
+                turned[start : start + blk].reshape(blk * cols, 2 * hidden),
+                preferred_element_type=F32,
+            ),
+        )
         yield
         yield from slanted(1, product, 0, d1)
-        add(g_in, outer(joined(d1), layer(2 * hidden, 2 * hidden + 16)))
-
-    backward_turns = 4 * blk + 4
+        add(g_in, outer(joined(d1), joined([acts[start + q, 0:16] for q in range(blk)])))
+
+    backward_turns = 4 * blk + 3
 
     def together(sweeps, back):
         turns = max(nv * len(sweeps), 1)
@@ -441,14 +447,16 @@
     copies[2].start()
     together([], backward(rows - blk))
 
-    turned = jnp.transpose(joined([g_in[...], jnp.zeros((hidden, LANE - 16), F32)]))
-    tail = turned[SUB : 2 * SUB]
+    from_features = jnp.transpose(joined([g_in[...], jnp.zeros((hidden, LANE - 16), F32)]))
+    tail = from_features[SUB : 2 * SUB]
     row = lax.broadcasted_iota(jnp.int32, (SUB, hidden), 0)
     for k in range(4):
         line = jnp.sum(jnp.transpose(sums[k]), axis=0, keepdims=True)
         tail = tail + jnp.where(row == k + num_feat - SUB, jnp.broadcast_to(line, (SUB, hidden)), 0.0)
-    packed[0:hidden, :] = joined([g_mid[...], g_top[...]])
-    packed[hidden : hidden + SUB, :] = joined([turned[0:SUB], tail])
+    both = jnp.transpose(g_two[...])
+    lane = lax.broadcasted_iota(jnp.int32, (hidden, 2 * hidden), 1)
+    packed[0:hidden, :] = jnp.where(lane < hidden, both[:hidden], both[hidden:])
+    packed[hidden : hidden + SUB, :] = joined([from_features[0:SUB], tail])
     for copy in copies:
         copy.wait()
 
@@ -476,8 +484,7 @@
             pltpu.VMEM((SWEEPS - 1, nv, tall, wide), F32),
             pltpu.VMEM((nv, rows, cols), F32),
             pltpu.VMEM((4, hidden, LANE), F32),
-            pltpu.VMEM((hidden, hidden), F32),
-            pltpu.VMEM((hidden, hidden), F32),
+            pltpu.VMEM((2 * hidden, 2 * hidden), F32),
             pltpu.VMEM((hidden, 16), F32),
             pltpu.SemaphoreType.DMA((3,)),
         ],
@@ -515,17 +522,26 @@
 
 
 def sum_over_case(packed):
-    for axis, radix in (("gy", 2), ("gx", 4)):
-        count = lax.axis_size(axis)
-        step = 1
-        while step < count:
-            parts = [packed]
-            for k in range(1, min(radix, count // step)):
-                parts.append(lax.ppermute(packed, axis, [(i, i ^ (k * step)) for i in range(count)]))
-            while len(parts) > 1:
-                parts = [a + b for a, b in zip(parts[::2], parts[1::2])]
-            packed = parts[0]
-            step *= radix
+    num_x, num_y = lax.axis_size("gx"), lax.axis_size("gy")
+
+    def swapped(x, dx, dy):
+        pairs = [(i * num_y + j, (i ^ dx) * num_y + (j ^ dy)) for i in range(num_x) for j in range(num_y)]
+        return lax.ppermute(x, ("gx", "gy"), pairs)
+
+    cross = 1 if num_y > 1 else 0
+    if num_y > 1:
+        packed = packed + swapped(packed, 0, 1)
+    step = 2
+    while step < num_y:
+        packed = packed + swapped(packed, 0, step ^ cross)
+        step *= 2
+    step = 1
+    while step < num_x:
+        parts = [packed] + [swapped(packed, k * step, cross) for k in range(1, min(4, num_x // step))]
+        while len(parts) > 1:
+            parts = [a + b for a, b in zip(parts[::2], parts[1::2])]
+        packed = parts[0]
+        step *= 4
     return packed
 
 

time: 35.1 us -> 34.9 us (level)
  Pallas kernels: 15.4 us -> 16.1 us
  starting transfers between devices: 10.7 us -> 10.2 us
  waiting for transfers between devices: 8.08 us -> 7.65 us
    pallas_call x1, Pallas kernels: 7.18 us -> 7.81 us  [sweeps_and_backward(): pl.pallas_call(functools.partial(adjoint_kernel, num_feat), in_specs=[nea...]
    ppermute x5, starting transfers between devices: 5.87 us -> 5.39 us  [swapped(): return lax.ppermute(x, ('gx', 'gy'), pairs)]
    ppermute x5, waiting for transfers between devices: 8.07 us -> 7.64 us  [swapped(): return lax.ppermute(x, ('gx', 'gy'), pairs)]
where the time goes in v10:
time: 34.9 us; the launch traced here: 34.7 us
  Pallas kernels  16.1 us (46%)
  starting transfers between devices  10.2 us (29%)
  waiting for transfers between devices  7.65 us (22%)
  between operations  0.74 us (2%)
    pallas_call x1, Pallas kernels, sweeps_and_backward(): pl.pallas_call(functools.partial(adjoint_kernel, num_feat), in_specs=[nea...  7.81 us
    ppermute x5, waiting for transfers between devices, swapped(): return lax.ppermute(x, ('gx', 'gy'), pairs)  7.64 us
    pallas_call x5, Pallas kernels, on_chip(): pl.pallas_call(kernel, in_specs=[here] * len(operands) + [there] * len(fa...  7.45 us
    ppermute x5, starting transfers between devices, swapped(): return lax.ppermute(x, ('gx', 'gy'), pairs)  5.39 us
    ppermute x2, starting transfers between devices, row_swaps(): out.append(lax.ppermute(slab, ('gx', 'gy'), sorted(partner.items())))  3.09 us
    ppermute x2, starting transfers between devices, col_swaps(): out.append(lax.ppermute(slab, 'gy', low + [(b, a) for a, b in low]))  1.75 us
    pallas_call x1, Pallas kernels, clip_all(): pl.pallas_call(clip_kernel, grid=(1,), in_specs=[whole(summed.shape)], ou...  0.81 us
  transfers between devices with their start and end apart: 9, of which 5 were waited for; matrix products, arithmetic and copies ran while one was open for 0% of the time, Pallas kernels for 15%

profile of v10, /device:TPU:0, one launch (start us, length us, event | category | flops | bytes accessed | tf_op | source)
XLA Modules:
  0.0 34.7 jit_solution(14768305833867865764)
XLA Ops:
  0.6 2.0 %load.1 = (bf16[5,64,256]{2,1,0:T(8,128)(2,1)S(1)}, bf16[4,64,256]{2,1,0:T(8,128)(2,1)S(1)}, f32[64,256]{1,0:T(8,128)}, s32[64,256]{1,0:T(8,128)}, f32[64,256]{1...) custom-call(bf16[5,64,256]{2,1,0:T(8,128)(2,1)} %refs_0_.1, ...), custom_call_target="tpu_custom_call" | custom-call | tf_op jit(solution)/shard_map/load/pallas_call | solution.py:35
  2.6 3.1 %collective-permute-start = (f32[60,256]{1,0:T(8,128)S(1)}, f32[60,256]{1,0:T(8,128)S(1)}, u32[]{:S(2)}, u32[]{:S(2)}) collective-permute-start(f32[60,256]{1,0:T(8,128)S(1)} %get-tuple-element.50), channel_id=1, source_target_pairs={{0,4},{1,5},{2,6},{3,7},{4,0},{5,1},{6,2},{7,3},{8,12},{9,13},{10,... | collective-permute-start | bytes 184328 | tf_op jit(solution)/shard_map/ppermute | solution.py:560
  5.7 0.0 collective-permute-start.1
  5.7 0.2 weights.1
  6.0 2.5 %network_forward.2 = (bf16[32,80,256]{2,1,0:T(8,128)(2,1)S(1)}, bf16[32,256,128]{2,1,0:T(8,128)(2,1)S(1)}, f32[32,192,256]{2,1,0:T(8,128)S(1)}, f32[32,256]{1,0:T(8,128)S(1)}) custom-call(bf16[10,64,256]{2,1,0:T(8,128)(2,1)S(1)} %get-tuple-element.52.feat, bf16[1280,256]{1,0:T(8,128)(2,1)S(1)} %get-tuple-element.58.w1, ...), custom_call_target="tpu_custom_call" | custom-call | flops 144703488 | bytes 1474560 | tf_op jit(solution)/shard_map/network_forward/pallas_call | solution.py:35
  8.5 0.0 copy-start
  8.5 0.0 collective-permute-done.row_first
  8.5 0.0 collective-permute-done.1.row_second
  8.5 0.2 col_slabs.1
  8.7 0.6 %collective-permute-start.2 = (f32[40,128]{1,0:T(8,128)S(1)}, f32[40,128]{1,0:T(8,128)S(1)}, u32[]{:S(2)}, u32[]{:S(2)}) collective-permute-start(f32[40,128]{1,0:T(8,128)S(1)} %get-tuple-element.69), channel_id=1, source_target_pairs={{0,1},{2,3},{1,0},{3,2},{4,5},{6,7},{5,4},{7,6},{8,9},{10,11},{9,8... | collective-permute-start | bytes 61448 | tf_op jit(solution)/shard_map/ppermute | solution.py:571
  9.3 1.2 %collective-permute-start.3 = (f32[40,128]{1,0:T(8,128)S(1)}, f32[40,128]{1,0:T(8,128)S(1)}, u32[]{:S(2)}, u32[]{:S(2)}) collective-permute-start(f32[40,128]{1,0:T(8,128)S(1)} %get-tuple-element.70), channel_id=1, source_target_pairs={{1,2},{0,3},{2,1},{3,0},{5,6},{4,7},{6,5},{7,4},{9,10},{8,11},{10,... | collective-permute-start | bytes 61448 | tf_op jit(solution)/shard_map/ppermute | solution.py:571
  10.5 2.5 %network_forward.3 = (bf16[32,80,256]{2,1,0:T(8,128)(2,1)S(1)}, bf16[32,256,128]{2,1,0:T(8,128)(2,1)S(1)}, f32[32,192,256]{2,1,0:T(8,128)S(1)}, f32[32,256]{1,0:T(8,128)S(1)}) custom-call(bf16[10,64,256]{2,1,0:T(8,128)(2,1)S(1)} %get-tuple-element.52.feat, bf16[1280,256]{1,0:T(8,128)(2,1)S(1)} %get-tuple-element.58.w1, ...), custom_call_target="tpu_custom_call" | custom-call | flops 144703488 | bytes 1474560 | tf_op jit(solution)/shard_map/network_forward/pallas_call | solution.py:35
  13.0 0.0 collective-permute-done.2.col_first
  13.0 0.0 collective-permute-done.3.col_second
  13.0 0.0 copy-done
  13.0 7.8 %sweeps_backward.1 = (f32[72,128]{1,0:T(8,128)S(1)}, f32[5,64,256]{2,1,0:T(8,128)}, f32[64,256]{1,0:T(8,128)}) custom-call(bf16[5,64,256]{2,1,0:T(8,128)(2,1)S(1)} %get-tuple-element.46.src, bf16[4,64,256]{2,1,0:T(8,128)(2,1)S(1)} %get-tuple-element.47.cpl, f32[64,256]{1,0:T(8,128)S(1)} %get-tuple-element.48.inv.inverse, ...), custom_call_target="tpu_custom_call" | custom-call | tf_op jit(solution)/shard_map/sweeps_backward/pallas_call | solution.py:471
  20.8 0.5 %collective-permute-start.4 = (f32[72,128]{1,0:T(8,128)S(1)}, f32[72,128]{1,0:T(8,128)S(1)}, u32[]{:S(2)}, u32[]{:S(2)}) collective-permute-start(f32[72,128]{1,0:T(8,128)S(1)} %get-tuple-element.79), channel_id=1, source_target_pairs={{0,1},{1,0},{2,3},{3,2},{4,5},{5,4},{6,7},{7,6},{8,9},{9,8},{10,11... | collective-permute-start | bytes 110600 | tf_op jit(solution)/shard_map/ppermute | solution.py:529
  21.3 0.9 %collective-permute-done.4 = f32[72,128]{1,0:T(8,128)S(1)} collective-permute-done((f32[72,128]{1,0:T(8,128)S(1)}, f32[72,128]{1,0:T(8,128)S(1)}, u32[]{:S(2)}, u32[]{:S(2)}) %collective-permute-start.4) | collective-permute-done | bytes 36896 | tf_op jit(solution)/shard_map/ppermute | solution.py:529
  22.2 0.7 %collective-permute-start.5 = (f32[72,128]{1,0:T(8,128)S(1)}, f32[72,128]{1,0:T(8,128)S(1)}, u32[]{:S(2)}, u32[]{:S(2)}) collective-permute-start(f32[72,128]{1,0:T(8,128)S(1)} %add.15), channel_id=1, source_target_pairs={{0,3},{1,2},{2,1},{3,0},{4,7},{5,6},{6,5},{7,4},{8,11},{9,10},{10,... | collective-permute-start | bytes 110600 | tf_op jit(solution)/shard_map/ppermute | solution.py:529
  22.9 2.7 %collective-permute-done.5 = f32[72,128]{1,0:T(8,128)S(1)} collective-permute-done((f32[72,128]{1,0:T(8,128)S(1)}, f32[72,128]{1,0:T(8,128)S(1)}, u32[]{:S(2)}, u32[]{:S(2)}) %collective-permute-start.5) | collective-permute-done | bytes 36896 | tf_op jit(solution)/shard_map/ppermute | solution.py:529
  25.6 3.2 %collective-permute-start.8 = (f32[72,128]{1,0:T(8,128)S(1)}, f32[72,128]{1,0:T(8,128)S(1)}, u32[]{:S(2)}, u32[]{:S(2)}) collective-permute-start(f32[72,128]{1,0:T(8,128)S(1)} %add.16), channel_id=1, source_target_pairs={{0,13},{1,12},{2,15},{3,14},{4,9},{5,8},{6,11},{7,10},{8,5},{9,4},... | collective-permute-start | bytes 110600 | tf_op jit(solution)/shard_map/ppermute | solution.py:529
  28.8 1.1 %collective-permute-start.7 = (f32[72,128]{1,0:T(8,128)S(1)}, f32[72,128]{1,0:T(8,128)S(1)}, u32[]{:S(2)}, u32[]{:S(2)}) collective-permute-start(f32[72,128]{1,0:T(8,128)S(1)} %add.16), channel_id=1, source_target_pairs={{0,9},{1,8},{2,11},{3,10},{4,13},{5,12},{6,15},{7,14},{8,1},{9,0},... | collective-permute-start | bytes 110600 | tf_op jit(solution)/shard_map/ppermute | solution.py:529
  29.8 0.0 collective-permute-start.6
  29.9 0.9 %collective-permute-done.8 = f32[72,128]{1,0:T(8,128)S(1)} collective-permute-done((f32[72,128]{1,0:T(8,128)S(1)}, f32[72,128]{1,0:T(8,128)S(1)}, u32[]{:S(2)}, u32[]{:S(2)}) %collective-permute-start.8) | collective-permute-done | bytes 36896 | tf_op jit(solution)/shard_map/ppermute | solution.py:529
  30.8 2.3 %collective-permute-done.7 = f32[72,128]{1,0:T(8,128)S(1)} collective-permute-done((f32[72,128]{1,0:T(8,128)S(1)}, f32[72,128]{1,0:T(8,128)S(1)}, u32[]{:S(2)}, u32[]{:S(2)}) %collective-permute-start.7) | collective-permute-done | bytes 36896 | tf_op jit(solution)/shard_map/ppermute | solution.py:529
  33.1 0.8 %collective-permute-done.6 = f32[72,128]{1,0:T(8,128)S(1)} collective-permute-done((f32[72,128]{1,0:T(8,128)S(1)}, f32[72,128]{1,0:T(8,128)S(1)}, u32[]{:S(2)}, u32[]{:S(2)}) %collective-permute-start.6) | collective-permute-done | bytes 36896 | tf_op jit(solution)/shard_map/ppermute | solution.py:529
  33.9 0.8 %clip.1 = (f32[10,64]{1,0:T(8,128)}, f32[64,64]{1,0:T(8,128)}, f32[64,64]{1,0:T(8,128)}, f32[1,64]{1,0:T(1,128)}, f32[3,64]{1,0:T(4,128)}) custom-call(f32[72,128]{1,0:T(8,128)S(1)} %add_add_fusion.summed), custom_call_target="tpu_custom_call" | custom-call | tf_op jit(solution)/shard_map/clip/pallas_call | solution.py:513
  (3 shorter events, 0.0 us)
Async XLA Ops:
  2.6 5.9 %collective-permute-start = (f32[60,256]{1,0:T(8,128)S(1)}, f32[60,256]{1,0:T(8,128)S(1)}, u32[]{:S(2)}, u32[]{:S(2)}) collective-permute-start(f32[60,256]{1,0:T(8,128)S(1)} %get-tuple-element.50), channel_id=1, source_target_pairs={{0,4},{1,5},{2,6},{3,7},{4,0},{5,1},{6,2},{7,3},{8,12},{9,13},{10,... | collective-permute-start | bytes 184328 | tf_op jit(solution)/shard_map/ppermute | solution.py:560
  5.7 2.8 %collective-permute-start.1 = (f32[60,256]{1,0:T(8,128)S(1)}, f32[60,256]{1,0:T(8,128)S(1)}, u32[]{:S(2)}, u32[]{:S(2)}) collective-permute-start(f32[60,256]{1,0:T(8,128)S(1)} %get-tuple-element.51), channel_id=1, source_target_pairs={{0,1},{1,0},{2,3},{3,2},{4,8},{5,9},{6,10},{7,11},{8,4},{9,5},{10,... | collective-permute-start | bytes 184328 | tf_op jit(solution)/shard_map/ppermute | solution.py:560
  8.5 4.5 %copy-start = (f32[5,5]{1,0:T(8,128)S(1)}, f32[5,5]{1,0:T(8,128)}, u32[]{:S(2)}) copy-start(f32[5,5]{1,0:T(8,128)} %mix.1) | copy-start | bytes 304
  8.7 4.3 %collective-permute-start.2 = (f32[40,128]{1,0:T(8,128)S(1)}, f32[40,128]{1,0:T(8,128)S(1)}, u32[]{:S(2)}, u32[]{:S(2)}) collective-permute-start(f32[40,128]{1,0:T(8,128)S(1)} %get-tuple-element.69), channel_id=1, source_target_pairs={{0,1},{2,3},{1,0},{3,2},{4,5},{6,7},{5,4},{7,6},{8,9},{10,11},{9,8... | collective-permute-start | bytes 61448 | tf_op jit(solution)/shard_map/ppermute | solution.py:571
  9.3 3.7 %collective-permute-start.3 = (f32[40,128]{1,0:T(8,128)S(1)}, f32[40,128]{1,0:T(8,128)S(1)}, u32[]{:S(2)}, u32[]{:S(2)}) collective-permute-start(f32[40,128]{1,0:T(8,128)S(1)} %get-tuple-element.70), channel_id=1, source_target_pairs={{1,2},{0,3},{2,1},{3,0},{5,6},{4,7},{6,5},{7,4},{9,10},{8,11},{10,... | collective-permute-start | bytes 61448 | tf_op jit(solution)/shard_map/ppermute | solution.py:571
  20.8 1.4 %collective-permute-start.4 = (f32[72,128]{1,0:T(8,128)S(1)}, f32[72,128]{1,0:T(8,128)S(1)}, u32[]{:S(2)}, u32[]{:S(2)}) collective-permute-start(f32[72,128]{1,0:T(8,128)S(1)} %get-tuple-element.79), channel_id=1, source_target_pairs={{0,1},{1,0},{2,3},{3,2},{4,5},{5,4},{6,7},{7,6},{8,9},{9,8},{10,11... | collective-permute-start | bytes 110600 | tf_op jit(solution)/shard_map/ppermute | solution.py:529
  22.2 3.4 %collective-permute-start.5 = (f32[72,128]{1,0:T(8,128)S(1)}, f32[72,128]{1,0:T(8,128)S(1)}, u32[]{:S(2)}, u32[]{:S(2)}) collective-permute-start(f32[72,128]{1,0:T(8,128)S(1)} %add.15), channel_id=1, source_target_pairs={{0,3},{1,2},{2,1},{3,0},{4,7},{5,6},{6,5},{7,4},{8,11},{9,10},{10,... | collective-permute-start | bytes 110600 | tf_op jit(solution)/shard_map/ppermute | solution.py:529
  25.6 5.2 %collective-permute-start.8 = (f32[72,128]{1,0:T(8,128)S(1)}, f32[72,128]{1,0:T(8,128)S(1)}, u32[]{:S(2)}, u32[]{:S(2)}) collective-permute-start(f32[72,128]{1,0:T(8,128)S(1)} %add.16), channel_id=1, source_target_pairs={{0,13},{1,12},{2,15},{3,14},{4,9},{5,8},{6,11},{7,10},{8,5},{9,4},... | collective-permute-start | bytes 110600 | tf_op jit(solution)/shard_map/ppermute | solution.py:529
  28.8 4.3 %collective-permute-start.7 = (f32[72,128]{1,0:T(8,128)S(1)}, f32[72,128]{1,0:T(8,128)S(1)}, u32[]{:S(2)}, u32[]{:S(2)}) collective-permute-start(f32[72,128]{1,0:T(8,128)S(1)} %add.16), channel_id=1, source_target_pairs={{0,9},{1,8},{2,11},{3,10},{4,13},{5,12},{6,15},{7,14},{8,1},{9,0},... | collective-permute-start | bytes 110600 | tf_op jit(solution)/shard_map/ppermute | solution.py:529
  29.8 4.1 %collective-permute-start.6 = (f32[72,128]{1,0:T(8,128)S(1)}, f32[72,128]{1,0:T(8,128)S(1)}, u32[]{:S(2)}, u32[]{:S(2)}) collective-permute-start(f32[72,128]{1,0:T(8,128)S(1)} %add.16), channel_id=1, source_target_pairs={{0,5},{1,4},{2,7},{3,6},{4,1},{5,0},{6,3},{7,2},{8,13},{9,12},{10,... | collective-permute-start | bytes 110600 | tf_op jit(solution)/shard_map/ppermute | solution.py:529

commit v11 on v9

--- a/solution.py
+++ b/solution.py
@@ -61,12 +61,13 @@
 
 
 def load_kernel(count, *refs):
-    far, near = refs[:count], refs[count : 2 * count]
-    inv, second, first, sems = refs[2 * count :]
+    far, kept = refs[:count], refs[count : 2 * count - 2]
+    inv, second, first, dia, bc, sems = refs[2 * count - 2 :]
+    near = (*kept[:2], dia, bc, *kept[2:])
     copies = [pltpu.make_async_copy(far[k], near[k], sems.at[k]) for k in range(count)]
     for copy in copies:
         copy.start()
-    src, cpl, dia, bc = near[:4]
+    src, cpl = near[:2]
     for copy in copies[:4]:
         copy.wait()
     nv, rows, _ = src.shape
@@ -86,14 +87,14 @@
 
 
 def load(arrays):
-    source, coupling = arrays[:2]
+    source, coupling, diagonal, bc_code = arrays[:4]
     nv, rows, cols = source.shape
     slab = (((nv + coupling.shape[0] + 1) * DEPTH, cols), F32)
     return on_chip(
         functools.partial(load_kernel, len(arrays)),
         [],
-        [like(x) for x in arrays] + [((rows, cols), F32), slab, slab],
-        [pltpu.SemaphoreType.DMA((len(arrays),))],
+        [like(x) for x in (*arrays[:2], *arrays[4:])] + [((rows, cols), F32), slab, slab],
+        [pltpu.VMEM(*like(diagonal)), pltpu.VMEM(*like(bc_code)), pltpu.SemaphoreType.DMA((len(arrays),))],
         far=arrays,
         name="load",
     )
@@ -105,7 +106,7 @@
     return jnp.where(at == 0, 0.0, before), jnp.where(at == lax.axis_size(axis) - 1, 0.0, after)
 
 
-def cols_kernel(src, cpl, inv, row_first, row_second, col_first, col_second, north, south):
+def cols_kernel(src, cpl, inv, row_second, row_first, col_first, col_second, north, south):
     nv, rows, cols = src.shape
     nc = cpl.shape[0]
     half = col_first.shape[0]
@@ -515,17 +516,26 @@
 
 
 def sum_over_case(packed):
-    for axis, radix in (("gy", 2), ("gx", 4)):
-        count = lax.axis_size(axis)
-        step = 1
-        while step < count:
-            parts = [packed]
-            for k in range(1, min(radix, count // step)):
-                parts.append(lax.ppermute(packed, axis, [(i, i ^ (k * step)) for i in range(count)]))
-            while len(parts) > 1:
-                parts = [a + b for a, b in zip(parts[::2], parts[1::2])]
-            packed = parts[0]
-            step *= radix
+    num_x, num_y = lax.axis_size("gx"), lax.axis_size("gy")
+
+    def swapped(x, dx, dy):
+        pairs = [(i * num_y + j, (i ^ dx) * num_y + (j ^ dy)) for i in range(num_x) for j in range(num_y)]
+        return lax.ppermute(x, ("gx", "gy"), pairs)
+
+    cross = 1 if num_y > 1 else 0
+    if num_y > 1:
+        packed = packed + swapped(packed, 0, 1)
+    step = 2
+    while step < num_y:
+        packed = packed + swapped(packed, 0, step ^ cross)
+        step *= 2
+    step = 1
+    while step < num_x:
+        parts = [packed] + [swapped(packed, k * step, cross) for k in range(1, min(4, num_x // step))]
+        while len(parts) > 1:
+            parts = [a + b for a, b in zip(parts[::2], parts[1::2])]
+        packed = parts[0]
+        step *= 4
     return packed
 
 
@@ -542,7 +552,7 @@
                 elif num_y % 2 == 0:
                     partner[i * num_y + y] = i * num_y + (y ^ 1)
         out.append(lax.ppermute(slab, ("gx", "gy"), sorted(partner.items())))
-    return out[::-1]
+    return out
 
 
 def col_swaps(first, second):
@@ -566,8 +576,8 @@
         source, coupling, diagonal, bc_code, production, features,
         weight_in, weight_mid, weight_top, weight_out.reshape(1, hidden), biases,
     ])
-    source, coupling, _, _, production, features, weight_in, weight_mid, weight_top, wout, biases = loaded[:11]
-    inverse, second, first = loaded[11:]
+    source, coupling, production, features, weight_in, weight_mid, weight_top, wout, biases = loaded[:9]
+    inverse, second, first = loaded[9:]
     row_halos = row_swaps(first, second)
     prepared = prepare(weight_in, weight_mid, weight_top, wout, biases)
     half = rows - 32

time: 35.1 us -> 34 us (0.969)
  waiting for transfers between devices: 8.08 us -> 7.22 us
  Pallas kernels: 15.4 us -> 14.8 us
    ppermute x2, starting transfers between devices: 3.09 us -> 4.67 us  [row_swaps(): out.append(lax.ppermute(slab, ('gx', 'gy'), sorted(partner.items())))]
    ppermute x5, starting transfers between devices: 5.87 us -> 4.67 us  [swapped(): return lax.ppermute(x, ('gx', 'gy'), pairs)]
    ppermute x5, waiting for transfers between devices: 8.07 us -> 7.21 us  [swapped(): return lax.ppermute(x, ('gx', 'gy'), pairs)]
    pallas_call x5, Pallas kernels: 7.45 us -> 6.81 us  [on_chip(): pl.pallas_call(kernel, in_specs=[here] * len(operands) + [there] * len(fa...]
  transfers between devices with their start and end apart: 9 -> 9, of which waited for: 5 -> 4; matrix products, arithmetic and copies ran while one was open for 0% -> 0% of each run, Pallas kernels for 15% -> 16%
where the time goes in v11:
time: 34 us; the launch traced here: 33.8 us
  Pallas kernels  14.8 us (44%)
  starting transfers between devices  11 us (32%)
  waiting for transfers between devices  7.22 us (21%)
  between operations  0.75 us (2%)
    ppermute x5, waiting for transfers between devices, swapped(): return lax.ppermute(x, ('gx', 'gy'), pairs)  7.21 us
    pallas_call x1, Pallas kernels, sweeps_and_backward(): pl.pallas_call(functools.partial(adjoint_kernel, num_feat), in_specs=[nea...  7.18 us
    pallas_call x5, Pallas kernels, on_chip(): pl.pallas_call(kernel, in_specs=[here] * len(operands) + [there] * len(fa...  6.81 us
    ppermute x5, starting transfers between devices, swapped(): return lax.ppermute(x, ('gx', 'gy'), pairs)  4.67 us
    ppermute x2, starting transfers between devices, row_swaps(): out.append(lax.ppermute(slab, ('gx', 'gy'), sorted(partner.items())))  4.67 us
    ppermute x2, starting transfers between devices, col_swaps(): out.append(lax.ppermute(slab, 'gy', low + [(b, a) for a, b in low]))  1.68 us
    pallas_call x1, Pallas kernels, clip_all(): pl.pallas_call(clip_kernel, grid=(1,), in_specs=[whole(summed.shape)], ou...  0.81 us
  transfers between devices with their start and end apart: 9, of which 4 were waited for; matrix products, arithmetic and copies ran while one was open for 0% of the time, Pallas kernels for 16%

profile of v11, /device:TPU:0, one launch (start us, length us, event | category | flops | bytes accessed | tf_op | source)
XLA Modules:
  0.0 33.8 jit_solution(12957127251355845370)
XLA Ops:
  0.6 0.0 copy-start
  0.6 1.3 %load.1 = (bf16[5,64,256]{2,1,0:T(8,128)(2,1)S(1)}, bf16[4,64,256]{2,1,0:T(8,128)(2,1)S(1)}, f32[64,256]{1,0:T(8,128)S(1)}, bf16[10,64,256]{2,1,0:T(8,128)(2,1)S...) custom-call(bf16[5,64,256]{2,1,0:T(8,128)(2,1)} %refs_0_.1, ...), custom_call_target="tpu_custom_call" | custom-call | tf_op jit(solution)/shard_map/load/pallas_call | solution.py:35
  2.0 0.5 %collective-permute-start = (f32[60,256]{1,0:T(8,128)S(1)}, f32[60,256]{1,0:T(8,128)S(1)}, u32[]{:S(2)}, u32[]{:S(2)}) collective-permute-start(f32[60,256]{1,0:T(8,128)S(1)} %get-tuple-element.48), channel_id=1, source_target_pairs={{0,1},{1,0},{2,3},{3,2},{4,8},{5,9},{6,10},{7,11},{8,4},{9,5},{10,... | collective-permute-start | bytes 184328 | tf_op jit(solution)/shard_map/ppermute | solution.py:554
  2.5 4.1 %collective-permute-start.1 = (f32[60,256]{1,0:T(8,128)S(1)}, f32[60,256]{1,0:T(8,128)S(1)}, u32[]{:S(2)}, u32[]{:S(2)}) collective-permute-start(f32[60,256]{1,0:T(8,128)S(1)} %get-tuple-element.49), channel_id=1, source_target_pairs={{0,4},{1,5},{2,6},{3,7},{4,0},{5,1},{6,2},{7,3},{8,12},{9,13},{10,... | collective-permute-start | bytes 184328 | tf_op jit(solution)/shard_map/ppermute | solution.py:554
  6.7 0.2 weights.1
  6.9 2.5 %network_forward.2 = (bf16[32,208,256]{2,1,0:T(8,128)(2,1)S(1)}, f32[32,192,256]{2,1,0:T(8,128)S(1)}, f32[32,256]{1,0:T(8,128)S(1)}) custom-call(bf16[10,64,256]{2,1,0:T(8,128)(2,1)S(1)} %get-tuple-element.50.feat, bf16[1280,256]{1,0:T(8,128)(2,1)S(1)} %get-tuple-element.56.w1, bf16[64,64]{1,0:T(8,128)(2,1)S(1)} %get-tuple-element.57.w2, ...), custom_call_target="tpu_custom_call" | custom-call | flops 144703488 | bytes 3571712 | tf_op jit(solution)/shard_map/network_forward/pallas_call | solution.py:35
  9.4 0.0 collective-permute-done.row_second
  9.4 0.0 collective-permute-done.1.row_first
  9.4 0.2 col_slabs.1
  9.7 0.1 collective-permute-start.2
  9.7 1.6 %collective-permute-start.3 = (f32[40,128]{1,0:T(8,128)S(1)}, f32[40,128]{1,0:T(8,128)S(1)}, u32[]{:S(2)}, u32[]{:S(2)}) collective-permute-start(f32[40,128]{1,0:T(8,128)S(1)} %get-tuple-element.68), channel_id=1, source_target_pairs={{1,2},{0,3},{2,1},{3,0},{5,6},{4,7},{6,5},{7,4},{9,10},{8,11},{10,... | collective-permute-start | bytes 61448 | tf_op jit(solution)/shard_map/ppermute | solution.py:565
  11.3 2.5 %network_forward.3 = (bf16[32,208,256]{2,1,0:T(8,128)(2,1)S(1)}, f32[32,192,256]{2,1,0:T(8,128)S(1)}, f32[32,256]{1,0:T(8,128)S(1)}) custom-call(bf16[10,64,256]{2,1,0:T(8,128)(2,1)S(1)} %get-tuple-element.50.feat, bf16[1280,256]{1,0:T(8,128)(2,1)S(1)} %get-tuple-element.56.w1, bf16[64,64]{1,0:T(8,128)(2,1)S(1)} %get-tuple-element.57.w2, ...), custom_call_target="tpu_custom_call" | custom-call | flops 144703488 | bytes 3571712 | tf_op jit(solution)/shard_map/network_forward/pallas_call | solution.py:35
  13.9 0.0 collective-permute-done.2.col_first
  13.9 0.0 collective-permute-done.3.col_second
  13.9 0.0 copy-done
  13.9 7.2 %sweeps_backward.1 = (f32[72,128]{1,0:T(8,128)S(1)}, f32[5,64,256]{2,1,0:T(8,128)}, f32[64,256]{1,0:T(8,128)}) custom-call(bf16[5,64,256]{2,1,0:T(8,128)(2,1)S(1)} %get-tuple-element.44.src, bf16[4,64,256]{2,1,0:T(8,128)(2,1)S(1)} %get-tuple-element.45.cpl, f32[64,256]{1,0:T(8,128)S(1)} %get-tuple-element.46.inv.inverse, ...), custom_call_target="tpu_custom_call" | custom-call | tf_op jit(solution)/shard_map/sweeps_backward/pallas_call | solution.py:464
  21.1 0.1 collective-permute-start.4
  21.2 1.1 %collective-permute-done.4 = f32[72,128]{1,0:T(8,128)S(1)} collective-permute-done((f32[72,128]{1,0:T(8,128)S(1)}, f32[72,128]{1,0:T(8,128)S(1)}, u32[]{:S(2)}, u32[]{:S(2)}) %collective-permute-start.4) | collective-permute-done | bytes 36896 | tf_op jit(solution)/shard_map/ppermute | solution.py:523
  22.4 0.7 %collective-permute-start.5 = (f32[72,128]{1,0:T(8,128)S(1)}, f32[72,128]{1,0:T(8,128)S(1)}, u32[]{:S(2)}, u32[]{:S(2)}) collective-permute-start(f32[72,128]{1,0:T(8,128)S(1)} %add.15), channel_id=1, source_target_pairs={{0,3},{1,2},{2,1},{3,0},{4,7},{5,6},{6,5},{7,4},{8,11},{9,10},{10,... | collective-permute-start | bytes 110600 | tf_op jit(solution)/shard_map/ppermute | solution.py:523
  23.0 2.8 %collective-permute-done.5 = f32[72,128]{1,0:T(8,128)S(1)} collective-permute-done((f32[72,128]{1,0:T(8,128)S(1)}, f32[72,128]{1,0:T(8,128)S(1)}, u32[]{:S(2)}, u32[]{:S(2)}) %collective-permute-start.5) | collective-permute-done | bytes 36896 | tf_op jit(solution)/shard_map/ppermute | solution.py:523
  25.8 1.9 %collective-permute-start.8 = (f32[72,128]{1,0:T(8,128)S(1)}, f32[72,128]{1,0:T(8,128)S(1)}, u32[]{:S(2)}, u32[]{:S(2)}) collective-permute-start(f32[72,128]{1,0:T(8,128)S(1)} %add.16), channel_id=1, source_target_pairs={{0,13},{1,12},{2,15},{3,14},{4,9},{5,8},{6,11},{7,10},{8,5},{9,4},... | collective-permute-start | bytes 110600 | tf_op jit(solution)/shard_map/ppermute | solution.py:523
  27.8 0.7 %collective-permute-start.7 = (f32[72,128]{1,0:T(8,128)S(1)}, f32[72,128]{1,0:T(8,128)S(1)}, u32[]{:S(2)}, u32[]{:S(2)}) collective-permute-start(f32[72,128]{1,0:T(8,128)S(1)} %add.16), channel_id=1, source_target_pairs={{0,9},{1,8},{2,11},{3,10},{4,13},{5,12},{6,15},{7,14},{8,1},{9,0},... | collective-permute-start | bytes 110600 | tf_op jit(solution)/shard_map/ppermute | solution.py:523
  28.5 1.2 %collective-permute-start.6 = (f32[72,128]{1,0:T(8,128)S(1)}, f32[72,128]{1,0:T(8,128)S(1)}, u32[]{:S(2)}, u32[]{:S(2)}) collective-permute-start(f32[72,128]{1,0:T(8,128)S(1)} %add.16), channel_id=1, source_target_pairs={{0,5},{1,4},{2,7},{3,6},{4,1},{5,0},{6,3},{7,2},{8,13},{9,12},{10,... | collective-permute-start | bytes 110600 | tf_op jit(solution)/shard_map/ppermute | solution.py:523
  29.7 1.4 %collective-permute-done.8 = f32[72,128]{1,0:T(8,128)S(1)} collective-permute-done((f32[72,128]{1,0:T(8,128)S(1)}, f32[72,128]{1,0:T(8,128)S(1)}, u32[]{:S(2)}, u32[]{:S(2)}) %collective-permute-start.8) | collective-permute-done | bytes 36896 | tf_op jit(solution)/shard_map/ppermute | solution.py:523
  31.0 1.9 %collective-permute-done.7 = f32[72,128]{1,0:T(8,128)S(1)} collective-permute-done((f32[72,128]{1,0:T(8,128)S(1)}, f32[72,128]{1,0:T(8,128)S(1)}, u32[]{:S(2)}, u32[]{:S(2)}) %collective-permute-start.7) | collective-permute-done | bytes 36896 | tf_op jit(solution)/shard_map/ppermute | solution.py:523
  33.0 0.0 collective-permute-done.6
  33.0 0.8 %clip.1 = (f32[10,64]{1,0:T(8,128)}, f32[64,64]{1,0:T(8,128)}, f32[64,64]{1,0:T(8,128)}, f32[1,64]{1,0:T(1,128)}, f32[3,64]{1,0:T(4,128)}) custom-call(f32[72,128]{1,0:T(8,128)S(1)} %add_add_fusion.summed), custom_call_target="tpu_custom_call" | custom-call | tf_op jit(solution)/shard_map/clip/pallas_call | solution.py:507
  (3 shorter events, 0.0 us)
Async XLA Ops:
  0.6 13.3 %copy-start = (f32[5,5]{1,0:T(8,128)S(1)}, f32[5,5]{1,0:T(8,128)}, u32[]{:S(2)}) copy-start(f32[5,5]{1,0:T(8,128)} %mix.1) | copy-start | bytes 304
  2.0 7.4 %collective-permute-start = (f32[60,256]{1,0:T(8,128)S(1)}, f32[60,256]{1,0:T(8,128)S(1)}, u32[]{:S(2)}, u32[]{:S(2)}) collective-permute-start(f32[60,256]{1,0:T(8,128)S(1)} %get-tuple-element.48), channel_id=1, source_target_pairs={{0,1},{1,0},{2,3},{3,2},{4,8},{5,9},{6,10},{7,11},{8,4},{9,5},{10,... | collective-permute-start | bytes 184328 | tf_op jit(solution)/shard_map/ppermute | solution.py:554
  2.5 6.9 %collective-permute-start.1 = (f32[60,256]{1,0:T(8,128)S(1)}, f32[60,256]{1,0:T(8,128)S(1)}, u32[]{:S(2)}, u32[]{:S(2)}) collective-permute-start(f32[60,256]{1,0:T(8,128)S(1)} %get-tuple-element.49), channel_id=1, source_target_pairs={{0,4},{1,5},{2,6},{3,7},{4,0},{5,1},{6,2},{7,3},{8,12},{9,13},{10,... | collective-permute-start | bytes 184328 | tf_op jit(solution)/shard_map/ppermute | solution.py:554
  9.7 4.2 %collective-permute-start.2 = (f32[40,128]{1,0:T(8,128)S(1)}, f32[40,128]{1,0:T(8,128)S(1)}, u32[]{:S(2)}, u32[]{:S(2)}) collective-permute-start(f32[40,128]{1,0:T(8,128)S(1)} %get-tuple-element.67), channel_id=1, source_target_pairs={{0,1},{2,3},{1,0},{3,2},{4,5},{6,7},{5,4},{7,6},{8,9},{10,11},{9,8... | collective-permute-start | bytes 61448 | tf_op jit(solution)/shard_map/ppermute | solution.py:565
  9.7 4.1 %collective-permute-start.3 = (f32[40,128]{1,0:T(8,128)S(1)}, f32[40,128]{1,0:T(8,128)S(1)}, u32[]{:S(2)}, u32[]{:S(2)}) collective-permute-start(f32[40,128]{1,0:T(8,128)S(1)} %get-tuple-element.68), channel_id=1, source_target_pairs={{1,2},{0,3},{2,1},{3,0},{5,6},{4,7},{6,5},{7,4},{9,10},{8,11},{10,... | collective-permute-start | bytes 61448 | tf_op jit(solution)/shard_map/ppermute | solution.py:565
  21.1 1.3 %collective-permute-start.4 = (f32[72,128]{1,0:T(8,128)S(1)}, f32[72,128]{1,0:T(8,128)S(1)}, u32[]{:S(2)}, u32[]{:S(2)}) collective-permute-start(f32[72,128]{1,0:T(8,128)S(1)} %get-tuple-element.75), channel_id=1, source_target_pairs={{0,1},{1,0},{2,3},{3,2},{4,5},{5,4},{6,7},{7,6},{8,9},{9,8},{10,11... | collective-permute-start | bytes 110600 | tf_op jit(solution)/shard_map/ppermute | solution.py:523
  22.4 3.4 %collective-permute-start.5 = (f32[72,128]{1,0:T(8,128)S(1)}, f32[72,128]{1,0:T(8,128)S(1)}, u32[]{:S(2)}, u32[]{:S(2)}) collective-permute-start(f32[72,128]{1,0:T(8,128)S(1)} %add.15), channel_id=1, source_target_pairs={{0,3},{1,2},{2,1},{3,0},{4,7},{5,6},{6,5},{7,4},{8,11},{9,10},{10,... | collective-permute-start | bytes 110600 | tf_op jit(solution)/shard_map/ppermute | solution.py:523
  25.8 5.2 %collective-permute-start.8 = (f32[72,128]{1,0:T(8,128)S(1)}, f32[72,128]{1,0:T(8,128)S(1)}, u32[]{:S(2)}, u32[]{:S(2)}) collective-permute-start(f32[72,128]{1,0:T(8,128)S(1)} %add.16), channel_id=1, source_target_pairs={{0,13},{1,12},{2,15},{3,14},{4,9},{5,8},{6,11},{7,10},{8,5},{9,4},... | collective-permute-start | bytes 110600 | tf_op jit(solution)/shard_map/ppermute | solution.py:523
  27.8 5.2 %collective-permute-start.7 = (f32[72,128]{1,0:T(8,128)S(1)}, f32[72,128]{1,0:T(8,128)S(1)}, u32[]{:S(2)}, u32[]{:S(2)}) collective-permute-start(f32[72,128]{1,0:T(8,128)S(1)} %add.16), channel_id=1, source_target_pairs={{0,9},{1,8},{2,11},{3,10},{4,13},{5,12},{6,15},{7,14},{8,1},{9,0},... | collective-permute-start | bytes 110600 | tf_op jit(solution)/shard_map/ppermute | solution.py:523
  28.5 4.5 %collective-permute-start.6 = (f32[72,128]{1,0:T(8,128)S(1)}, f32[72,128]{1,0:T(8,128)S(1)}, u32[]{:S(2)}, u32[]{:S(2)}) collective-permute-start(f32[72,128]{1,0:T(8,128)S(1)} %add.16), channel_id=1, source_target_pairs={{0,5},{1,4},{2,7},{3,6},{4,1},{5,0},{6,3},{7,2},{8,13},{9,12},{10,... | collective-permute-start | bytes 110600 | tf_op jit(solution)/shard_map/ppermute | solution.py:523

commit v12 on v11

--- a/solution.py
+++ b/solution.py
@@ -433,7 +433,7 @@
         for _ in itertools.chain(sweeps, back):
             pass
 
-    ahead = [2 * (SWEEPS - number) for number in range(SWEEPS + 1)]
+    ahead = [SWEEPS - number for number in range(SWEEPS + 1)]
     for number in range(1, SWEEPS):
         together([(number, t) for t in range(min(ahead[number] + 1, tiles))], iter(()))
     for t in range(1, tiles - 1):
@@ -522,20 +522,17 @@
         pairs = [(i * num_y + j, (i ^ dx) * num_y + (j ^ dy)) for i in range(num_x) for j in range(num_y)]
         return lax.ppermute(x, ("gx", "gy"), pairs)
 
-    cross = 1 if num_y > 1 else 0
-    if num_y > 1:
-        packed = packed + swapped(packed, 0, 1)
-    step = 2
-    while step < num_y:
-        packed = packed + swapped(packed, 0, step ^ cross)
-        step *= 2
-    step = 1
-    while step < num_x:
-        parts = [packed] + [swapped(packed, k * step, cross) for k in range(1, min(4, num_x // step))]
-        while len(parts) > 1:
-            parts = [a + b for a, b in zip(parts[::2], parts[1::2])]
-        packed = parts[0]
-        step *= 4
+    cross = 0
+    for along_y, count in ((1, num_y), (0, num_x)):
+        step = 1
+        while step < count:
+            shifts = [k * step for k in range(1, min(4, count // step))]
+            parts = [packed] + [swapped(packed, 0, k ^ cross) if along_y else swapped(packed, k, cross) for k in shifts]
+            while len(parts) > 1:
+                parts = [a + b for a, b in zip(parts[::2], parts[1::2])]
+            packed = parts[0]
+            step *= 4
+            cross = cross or along_y
     return packed
 
 

time: 34 us -> 34 us (level)
  starting transfers between devices: 11 us -> 11.4 us
  waiting for transfers between devices: 7.22 us -> 6.82 us
    ppermute x5 -> x6, starting transfers between devices: 4.67 us -> 5.09 us  [swapped(): return lax.ppermute(x, ('gx', 'gy'), pairs)]
    ppermute x5 -> x6, waiting for transfers between devices: 7.21 us -> 6.81 us  [swapped(): return lax.ppermute(x, ('gx', 'gy'), pairs)]
  transfers between devices with their start and end apart: 9 -> 10, of which waited for: 4 -> 5; matrix products, arithmetic and copies ran while one was open for 0% -> 0% of each run, Pallas kernels for 16% -> 16%
where the time goes in v12:
time: 34 us; the launch traced here: 33.9 us
  Pallas kernels  14.8 us (44%)
  starting transfers between devices  11.4 us (34%)
  waiting for transfers between devices  6.82 us (20%)
  between operations  0.76 us (2%)
    pallas_call x1, Pallas kernels, sweeps_and_backward(): pl.pallas_call(functools.partial(adjoint_kernel, num_feat), in_specs=[nea...  7.23 us
    pallas_call x5, Pallas kernels, on_chip(): pl.pallas_call(kernel, in_specs=[here] * len(operands) + [there] * len(fa...  6.81 us
    ppermute x6, waiting for transfers between devices, swapped(): return lax.ppermute(x, ('gx', 'gy'), pairs)  6.81 us
    ppermute x6, starting transfers between devices, swapped(): return lax.ppermute(x, ('gx', 'gy'), pairs)  5.09 us
    ppermute x2, starting transfers between devices, row_swaps(): out.append(lax.ppermute(slab, ('gx', 'gy'), sorted(partner.items())))  4.67 us
    ppermute x2, starting transfers between devices, col_swaps(): out.append(lax.ppermute(slab, 'gy', low + [(b, a) for a, b in low]))  1.68 us
    pallas_call x1, Pallas kernels, clip_all(): pl.pallas_call(clip_kernel, grid=(1,), in_specs=[whole(summed.shape)], ou...  0.81 us
  transfers between devices with their start and end apart: 10, of which 5 were waited for; matrix products, arithmetic and copies ran while one was open for 0% of the time, Pallas kernels for 16%

profile of v12, /device:TPU:0, one launch (start us, length us, event | category | flops | bytes accessed | tf_op | source)
XLA Modules:
  0.0 33.9 jit_solution(2644990779149825095)
XLA Ops:
  0.6 0.0 copy-start
  0.6 1.3 %load.1 = (bf16[5,64,256]{2,1,0:T(8,128)(2,1)S(1)}, bf16[4,64,256]{2,1,0:T(8,128)(2,1)S(1)}, f32[64,256]{1,0:T(8,128)S(1)}, bf16[10,64,256]{2,1,0:T(8,128)(2,1)S...) custom-call(bf16[5,64,256]{2,1,0:T(8,128)(2,1)} %refs_0_.1, ...), custom_call_target="tpu_custom_call" | custom-call | tf_op jit(solution)/shard_map/load/pallas_call | solution.py:35
  2.0 0.5 %collective-permute-start = (f32[60,256]{1,0:T(8,128)S(1)}, f32[60,256]{1,0:T(8,128)S(1)}, u32[]{:S(2)}, u32[]{:S(2)}) collective-permute-start(f32[60,256]{1,0:T(8,128)S(1)} %get-tuple-element.48), channel_id=1, source_target_pairs={{0,1},{1,0},{2,3},{3,2},{4,8},{5,9},{6,10},{7,11},{8,4},{9,5},{10,... | collective-permute-start | bytes 184328 | tf_op jit(solution)/shard_map/ppermute | solution.py:551
  2.5 4.1 %collective-permute-start.1 = (f32[60,256]{1,0:T(8,128)S(1)}, f32[60,256]{1,0:T(8,128)S(1)}, u32[]{:S(2)}, u32[]{:S(2)}) collective-permute-start(f32[60,256]{1,0:T(8,128)S(1)} %get-tuple-element.49), channel_id=1, source_target_pairs={{0,4},{1,5},{2,6},{3,7},{4,0},{5,1},{6,2},{7,3},{8,12},{9,13},{10,... | collective-permute-start | bytes 184328 | tf_op jit(solution)/shard_map/ppermute | solution.py:551
  6.7 0.2 weights.1
  6.9 2.5 %network_forward.2 = (bf16[32,208,256]{2,1,0:T(8,128)(2,1)S(1)}, f32[32,192,256]{2,1,0:T(8,128)S(1)}, f32[32,256]{1,0:T(8,128)S(1)}) custom-call(bf16[10,64,256]{2,1,0:T(8,128)(2,1)S(1)} %get-tuple-element.50.feat, bf16[1280,256]{1,0:T(8,128)(2,1)S(1)} %get-tuple-element.56.w1, bf16[64,64]{1,0:T(8,128)(2,1)S(1)} %get-tuple-element.57.w2, ...), custom_call_target="tpu_custom_call" | custom-call | flops 144703488 | bytes 3571712 | tf_op jit(solution)/shard_map/network_forward/pallas_call | solution.py:35
  9.4 0.0 collective-permute-done.row_second
  9.4 0.0 collective-permute-done.1.row_first
  9.4 0.2 col_slabs.1
  9.7 0.1 collective-permute-start.2
  9.7 1.6 %collective-permute-start.3 = (f32[40,128]{1,0:T(8,128)S(1)}, f32[40,128]{1,0:T(8,128)S(1)}, u32[]{:S(2)}, u32[]{:S(2)}) collective-permute-start(f32[40,128]{1,0:T(8,128)S(1)} %get-tuple-element.68), channel_id=1, source_target_pairs={{1,2},{0,3},{2,1},{3,0},{5,6},{4,7},{6,5},{7,4},{9,10},{8,11},{10,... | collective-permute-start | bytes 61448 | tf_op jit(solution)/shard_map/ppermute | solution.py:562
  11.3 2.5 %network_forward.3 = (bf16[32,208,256]{2,1,0:T(8,128)(2,1)S(1)}, f32[32,192,256]{2,1,0:T(8,128)S(1)}, f32[32,256]{1,0:T(8,128)S(1)}) custom-call(bf16[10,64,256]{2,1,0:T(8,128)(2,1)S(1)} %get-tuple-element.50.feat, bf16[1280,256]{1,0:T(8,128)(2,1)S(1)} %get-tuple-element.56.w1, bf16[64,64]{1,0:T(8,128)(2,1)S(1)} %get-tuple-element.57.w2, ...), custom_call_target="tpu_custom_call" | custom-call | flops 144703488 | bytes 3571712 | tf_op jit(solution)/shard_map/network_forward/pallas_call | solution.py:35
  13.9 0.0 collective-permute-done.2.col_first
  13.9 0.0 collective-permute-done.3.col_second
  13.9 0.0 copy-done
  13.9 7.2 %sweeps_backward.1 = (f32[72,128]{1,0:T(8,128)S(1)}, f32[5,64,256]{2,1,0:T(8,128)}, f32[64,256]{1,0:T(8,128)}) custom-call(bf16[5,64,256]{2,1,0:T(8,128)(2,1)S(1)} %get-tuple-element.44.src, bf16[4,64,256]{2,1,0:T(8,128)(2,1)S(1)} %get-tuple-element.45.cpl, f32[64,256]{1,0:T(8,128)S(1)} %get-tuple-element.46.inv.inverse, ...), custom_call_target="tpu_custom_call" | custom-call | tf_op jit(solution)/shard_map/sweeps_backward/pallas_call | solution.py:464
  21.1 0.7 %collective-permute-start.6 = (f32[72,128]{1,0:T(8,128)S(1)}, f32[72,128]{1,0:T(8,128)S(1)}, u32[]{:S(2)}, u32[]{:S(2)}) collective-permute-start(f32[72,128]{1,0:T(8,128)S(1)} %get-tuple-element.75), channel_id=1, source_target_pairs={{0,3},{1,2},{2,1},{3,0},{4,7},{5,6},{6,5},{7,4},{8,11},{9,10},{10,... | collective-permute-start | bytes 110600 | tf_op jit(solution)/shard_map/ppermute | solution.py:523
  21.9 1.1 %collective-permute-start.5 = (f32[72,128]{1,0:T(8,128)S(1)}, f32[72,128]{1,0:T(8,128)S(1)}, u32[]{:S(2)}, u32[]{:S(2)}) collective-permute-start(f32[72,128]{1,0:T(8,128)S(1)} %get-tuple-element.75), channel_id=1, source_target_pairs={{0,2},{1,3},{2,0},{3,1},{4,6},{5,7},{6,4},{7,5},{8,10},{9,11},{10,... | collective-permute-start | bytes 110600 | tf_op jit(solution)/shard_map/ppermute | solution.py:523
  22.9 0.2 collective-permute-start.4
  23.1 1.7 %collective-permute-done.6 = f32[72,128]{1,0:T(8,128)S(1)} collective-permute-done((f32[72,128]{1,0:T(8,128)S(1)}, f32[72,128]{1,0:T(8,128)S(1)}, u32[]{:S(2)}, u32[]{:S(2)}) %collective-permute-start.6) | collective-permute-done | bytes 36896 | tf_op jit(solution)/shard_map/ppermute | solution.py:523
  24.7 1.1 %collective-permute-done.5 = f32[72,128]{1,0:T(8,128)S(1)} collective-permute-done((f32[72,128]{1,0:T(8,128)S(1)}, f32[72,128]{1,0:T(8,128)S(1)}, u32[]{:S(2)}, u32[]{:S(2)}) %collective-permute-start.5) | collective-permute-done | bytes 36896 | tf_op jit(solution)/shard_map/ppermute | solution.py:523
  25.8 0.0 collective-permute-done.4
  25.8 1.2 %collective-permute-start.9 = (f32[72,128]{1,0:T(8,128)S(1)}, f32[72,128]{1,0:T(8,128)S(1)}, u32[]{:S(2)}, u32[]{:S(2)}) collective-permute-start(f32[72,128]{1,0:T(8,128)S(1)} %add_add_fusion.1), channel_id=1, source_target_pairs={{0,13},{1,12},{2,15},{3,14},{4,9},{5,8},{6,11},{7,10},{8,5},{9,4},... | collective-permute-start | bytes 110600 | tf_op jit(solution)/shard_map/ppermute | solution.py:523
  27.1 1.5 %collective-permute-start.8 = (f32[72,128]{1,0:T(8,128)S(1)}, f32[72,128]{1,0:T(8,128)S(1)}, u32[]{:S(2)}, u32[]{:S(2)}) collective-permute-start(f32[72,128]{1,0:T(8,128)S(1)} %add_add_fusion.1), channel_id=1, source_target_pairs={{0,9},{1,8},{2,11},{3,10},{4,13},{5,12},{6,15},{7,14},{8,1},{9,0},... | collective-permute-start | bytes 110600 | tf_op jit(solution)/shard_map/ppermute | solution.py:523
  28.5 0.4 %collective-permute-start.7 = (f32[72,128]{1,0:T(8,128)S(1)}, f32[72,128]{1,0:T(8,128)S(1)}, u32[]{:S(2)}, u32[]{:S(2)}) collective-permute-start(f32[72,128]{1,0:T(8,128)S(1)} %add_add_fusion.1), channel_id=1, source_target_pairs={{0,5},{1,4},{2,7},{3,6},{4,1},{5,0},{6,3},{7,2},{8,13},{9,12},{10,... | collective-permute-start | bytes 110600 | tf_op jit(solution)/shard_map/ppermute | solution.py:523
  29.0 2.1 %collective-permute-done.9 = f32[72,128]{1,0:T(8,128)S(1)} collective-permute-done((f32[72,128]{1,0:T(8,128)S(1)}, f32[72,128]{1,0:T(8,128)S(1)}, u32[]{:S(2)}, u32[]{:S(2)}) %collective-permute-start.9) | collective-permute-done | bytes 36896 | tf_op jit(solution)/shard_map/ppermute | solution.py:523
  31.1 1.3 %collective-permute-done.8 = f32[72,128]{1,0:T(8,128)S(1)} collective-permute-done((f32[72,128]{1,0:T(8,128)S(1)}, f32[72,128]{1,0:T(8,128)S(1)}, u32[]{:S(2)}, u32[]{:S(2)}) %collective-permute-start.8) | collective-permute-done | bytes 36896 | tf_op jit(solution)/shard_map/ppermute | solution.py:523
  32.4 0.7 %collective-permute-done.7 = f32[72,128]{1,0:T(8,128)S(1)} collective-permute-done((f32[72,128]{1,0:T(8,128)S(1)}, f32[72,128]{1,0:T(8,128)S(1)}, u32[]{:S(2)}, u32[]{:S(2)}) %collective-permute-start.7) | collective-permute-done | bytes 36896 | tf_op jit(solution)/shard_map/ppermute | solution.py:523
  33.1 0.8 %clip.1 = (f32[10,64]{1,0:T(8,128)}, f32[64,64]{1,0:T(8,128)}, f32[64,64]{1,0:T(8,128)}, f32[1,64]{1,0:T(1,128)}, f32[3,64]{1,0:T(4,128)}) custom-call(f32[72,128]{1,0:T(8,128)S(1)} %add_add_fusion.summed), custom_call_target="tpu_custom_call" | custom-call | tf_op jit(solution)/shard_map/clip/pallas_call | solution.py:507
  (2 shorter events, 0.0 us)
Async XLA Ops:
  0.6 13.3 %copy-start = (f32[5,5]{1,0:T(8,128)S(1)}, f32[5,5]{1,0:T(8,128)}, u32[]{:S(2)}) copy-start(f32[5,5]{1,0:T(8,128)} %mix.1) | copy-start | bytes 304
  2.0 7.4 %collective-permute-start = (f32[60,256]{1,0:T(8,128)S(1)}, f32[60,256]{1,0:T(8,128)S(1)}, u32[]{:S(2)}, u32[]{:S(2)}) collective-permute-start(f32[60,256]{1,0:T(8,128)S(1)} %get-tuple-element.48), channel_id=1, source_target_pairs={{0,1},{1,0},{2,3},{3,2},{4,8},{5,9},{6,10},{7,11},{8,4},{9,5},{10,... | collective-permute-start | bytes 184328 | tf_op jit(solution)/shard_map/ppermute | solution.py:551
  2.5 6.9 %collective-permute-start.1 = (f32[60,256]{1,0:T(8,128)S(1)}, f32[60,256]{1,0:T(8,128)S(1)}, u32[]{:S(2)}, u32[]{:S(2)}) collective-permute-start(f32[60,256]{1,0:T(8,128)S(1)} %get-tuple-element.49), channel_id=1, source_target_pairs={{0,4},{1,5},{2,6},{3,7},{4,0},{5,1},{6,2},{7,3},{8,12},{9,13},{10,... | collective-permute-start | bytes 184328 | tf_op jit(solution)/shard_map/ppermute | solution.py:551
  9.7 4.2 %collective-permute-start.2 = (f32[40,128]{1,0:T(8,128)S(1)}, f32[40,128]{1,0:T(8,128)S(1)}, u32[]{:S(2)}, u32[]{:S(2)}) collective-permute-start(f32[40,128]{1,0:T(8,128)S(1)} %get-tuple-element.67), channel_id=1, source_target_pairs={{0,1},{2,3},{1,0},{3,2},{4,5},{6,7},{5,4},{7,6},{8,9},{10,11},{9,8... | collective-permute-start | bytes 61448 | tf_op jit(solution)/shard_map/ppermute | solution.py:562
  9.7 4.1 %collective-permute-start.3 = (f32[40,128]{1,0:T(8,128)S(1)}, f32[40,128]{1,0:T(8,128)S(1)}, u32[]{:S(2)}, u32[]{:S(2)}) collective-permute-start(f32[40,128]{1,0:T(8,128)S(1)} %get-tuple-element.68), channel_id=1, source_target_pairs={{1,2},{0,3},{2,1},{3,0},{5,6},{4,7},{6,5},{7,4},{9,10},{8,11},{10,... | collective-permute-start | bytes 61448 | tf_op jit(solution)/shard_map/ppermute | solution.py:562
  21.1 3.6 %collective-permute-start.6 = (f32[72,128]{1,0:T(8,128)S(1)}, f32[72,128]{1,0:T(8,128)S(1)}, u32[]{:S(2)}, u32[]{:S(2)}) collective-permute-start(f32[72,128]{1,0:T(8,128)S(1)} %get-tuple-element.75), channel_id=1, source_target_pairs={{0,3},{1,2},{2,1},{3,0},{4,7},{5,6},{6,5},{7,4},{8,11},{9,10},{10,... | collective-permute-start | bytes 110600 | tf_op jit(solution)/shard_map/ppermute | solution.py:523
  21.9 4.0 %collective-permute-start.5 = (f32[72,128]{1,0:T(8,128)S(1)}, f32[72,128]{1,0:T(8,128)S(1)}, u32[]{:S(2)}, u32[]{:S(2)}) collective-permute-start(f32[72,128]{1,0:T(8,128)S(1)} %get-tuple-element.75), channel_id=1, source_target_pairs={{0,2},{1,3},{2,0},{3,1},{4,6},{5,7},{6,4},{7,5},{8,10},{9,11},{10,... | collective-permute-start | bytes 110600 | tf_op jit(solution)/shard_map/ppermute | solution.py:523
  22.9 2.9 %collective-permute-start.4 = (f32[72,128]{1,0:T(8,128)S(1)}, f32[72,128]{1,0:T(8,128)S(1)}, u32[]{:S(2)}, u32[]{:S(2)}) collective-permute-start(f32[72,128]{1,0:T(8,128)S(1)} %get-tuple-element.75), channel_id=1, source_target_pairs={{0,1},{1,0},{2,3},{3,2},{4,5},{5,4},{6,7},{7,6},{8,9},{9,8},{10,11... | collective-permute-start | bytes 110600 | tf_op jit(solution)/shard_map/ppermute | solution.py:523
  25.8 5.3 %collective-permute-start.9 = (f32[72,128]{1,0:T(8,128)S(1)}, f32[72,128]{1,0:T(8,128)S(1)}, u32[]{:S(2)}, u32[]{:S(2)}) collective-permute-start(f32[72,128]{1,0:T(8,128)S(1)} %add_add_fusion.1), channel_id=1, source_target_pairs={{0,13},{1,12},{2,15},{3,14},{4,9},{5,8},{6,11},{7,10},{8,5},{9,4},... | collective-permute-start | bytes 110600 | tf_op jit(solution)/shard_map/ppermute | solution.py:523
  27.1 5.3 %collective-permute-start.8 = (f32[72,128]{1,0:T(8,128)S(1)}, f32[72,128]{1,0:T(8,128)S(1)}, u32[]{:S(2)}, u32[]{:S(2)}) collective-permute-start(f32[72,128]{1,0:T(8,128)S(1)} %add_add_fusion.1), channel_id=1, source_target_pairs={{0,9},{1,8},{2,11},{3,10},{4,13},{5,12},{6,15},{7,14},{8,1},{9,0},... | collective-permute-start | bytes 110600 | tf_op jit(solution)/shard_map/ppermute | solution.py:523
  28.5 4.5 %collective-permute-start.7 = (f32[72,128]{1,0:T(8,128)S(1)}, f32[72,128]{1,0:T(8,128)S(1)}, u32[]{:S(2)}, u32[]{:S(2)}) collective-permute-start(f32[72,128]{1,0:T(8,128)S(1)} %add_add_fusion.1), channel_id=1, source_target_pairs={{0,5},{1,4},{2,7},{3,6},{4,1},{5,0},{6,3},{7,2},{8,13},{9,12},{10,... | collective-permute-start | bytes 110600 | tf_op jit(solution)/shard_map/ppermute | solution.py:523

commit v13 on v12

--- a/solution.py
+++ b/solution.py
@@ -204,38 +204,48 @@
     hidden = w2.shape[0]
     step_rows, blk, per = hidden + 16, 16, 4
     x1[...] = jnp.zeros(x1.shape, BF16)
-
-    @pl.loop(0, acts.shape[0] // blk)
-    def _(block):
-        start = pl.multiple_of(block * blk, blk)
-        x1[0 : nf * blk] = feat[:, pl.ds(first_row + start, blk), :].reshape(nf * blk, cols)
-        b1, b2, b3, wo = (across(cst[k], cols) for k in range(4))
-        lines = []
-        first = jnp.dot(w1[...], x1[...], preferred_element_type=F32)
-        for g in range(blk // per):
-            ones = []
-            for q in range(g * per, (g + 1) * per):
-                part = first[q * step_rows : (q + 1) * step_rows]
+    b1, b2, b3, wo = (across(cst[k], cols) for k in range(4))
+
+    def product(weight, parts):
+        return jnp.dot(weight, jnp.concatenate(parts, axis=1), preferred_element_type=F32)
+
+    groups = acts.shape[0] // per
+    ones, twos, lines = {}, {}, []
+    for s in range(groups + 2):
+        rows = [range((s - lag) * per, (s - lag + 1) * per) for lag in range(3)]
+        if s < groups and s * per % blk == 0:
+            block = s * per // blk
+            cells = feat[:, first_row + s * per : first_row + s * per + blk, :]
+            x1[block, 0 : nf * blk] = cells.reshape(nf * blk, cols)
+            first = jnp.dot(w1[...], x1[block], preferred_element_type=F32)
+        second = product(w2[...], ones.pop(s - 1)) if 1 <= s <= groups else None
+        third = product(w3[...], twos.pop(s - 2)) if s >= 2 else None
+        if s < groups:
+            ones[s] = []
+            for r in rows[0]:
+                part = first[r % blk * step_rows : (r % blk + 1) * step_rows]
                 one = jnp.tanh(part[:hidden] + b1).astype(BF16)
-                slopes[start + q, 0:hidden] = slope(one.astype(F32))
-                acts[start + q, 0:hidden] = one
-                acts[start + q, 2 * hidden : 2 * hidden + 16] = part[hidden:].astype(BF16)
-                ones.append(one)
-            second = jnp.dot(w2[...], jnp.concatenate(ones, axis=1), preferred_element_type=F32)
-            twos = []
-            for q in range(per):
+                slopes[r, 0:hidden] = slope(one.astype(F32))
+                acts[r, 0:hidden] = one
+                acts[r, 2 * hidden : 2 * hidden + 16] = part[hidden:].astype(BF16)
+                ones[s].append(one)
+        if second is not None:
+            twos[s - 1] = []
+            for q, r in enumerate(rows[1]):
                 two = jnp.tanh(second[:, q * cols : (q + 1) * cols] + b2).astype(BF16)
-                slopes[start + (g * per + q), hidden : 2 * hidden] = slope(two.astype(F32))
-                acts[start + (g * per + q), hidden : 2 * hidden] = two
-                twos.append(two)
-            third = jnp.dot(w3[...], jnp.concatenate(twos, axis=1), preferred_element_type=F32)
-            for q in range(per):
+                slopes[r, hidden : 2 * hidden] = slope(two.astype(F32))
+                acts[r, hidden : 2 * hidden] = two
+                twos[s - 1].append(two)
+        if third is not None:
+            for q, r in enumerate(rows[2]):
                 three = jnp.tanh(third[:, q * cols : (q + 1) * cols] + b3).astype(BF16)
-                acts[start + (g * per + q), 2 * hidden + 16 :] = three
+                acts[r, 2 * hidden + 16 :] = three
                 three = three.astype(F32)
-                slopes[start + (g * per + q), 2 * hidden :] = wo * slope(three)
+                slopes[r, 2 * hidden :] = wo * slope(three)
                 lines.append(1.0 + jnp.sum(three * wo, axis=0, keepdims=True))
-        beta[pl.ds(start, blk), :] = jnp.concatenate(lines, axis=0)
+                if len(lines) == SUB:
+                    beta[r + 1 - SUB : r + 1, :] = jnp.concatenate(lines, axis=0)
+                    lines = []
 
 
 def forward(features, prepared, first_row, count):
@@ -247,7 +257,7 @@
         functools.partial(forward_kernel, first_row),
         [features, *prepared],
         [((count, high, cols), BF16), ((count, 3 * hidden, cols), F32), ((count, cols), F32)],
-        [pltpu.VMEM((w1.shape[1], cols), BF16)],
+        [pltpu.VMEM((count // 16, w1.shape[1], cols), BF16)],
         cost_estimate=pl.CostEstimate(
             flops=2 * count * cols * (nf + 2 * hidden) * hidden,
             bytes_accessed=2 * count * cols * (high + nf),

time: 34 us -> 33.7 us (level)
  Pallas kernels: 14.8 us -> 13.7 us
  waiting for transfers between devices: 6.82 us -> 7.63 us
    pallas_call x5, Pallas kernels: 6.81 us -> 5.62 us  [on_chip(): pl.pallas_call(kernel, in_specs=[here] * len(operands) + [there] * len(fa...]
    ppermute x6, waiting for transfers between devices: 6.81 us -> 7.56 us  [swapped(): return lax.ppermute(x, ('gx', 'gy'), pairs)]
  transfers between devices with their start and end apart: 10 -> 10, of which waited for: 5 -> 6; matrix products, arithmetic and copies ran while one was open for 0% -> 0% of each run, Pallas kernels for 16% -> 12%
where the time goes in v13:
time: 33.7 us; the launch traced here: 33.6 us
  Pallas kernels  13.7 us (41%)
  starting transfers between devices  11.5 us (34%)
  waiting for transfers between devices  7.63 us (23%)
  between operations  0.74 us (2%)
    ppermute x6, waiting for transfers between devices, swapped(): return lax.ppermute(x, ('gx', 'gy'), pairs)  7.56 us
    pallas_call x1, Pallas kernels, sweeps_and_backward(): pl.pallas_call(functools.partial(adjoint_kernel, num_feat), in_specs=[nea...  7.23 us
    pallas_call x5, Pallas kernels, on_chip(): pl.pallas_call(kernel, in_specs=[here] * len(operands) + [there] * len(fa...  5.62 us
    ppermute x6, starting transfers between devices, swapped(): return lax.ppermute(x, ('gx', 'gy'), pairs)  5.2 us
    ppermute x2, starting transfers between devices, row_swaps(): out.append(lax.ppermute(slab, ('gx', 'gy'), sorted(partner.items())))  4.67 us
    ppermute x2, starting transfers between devices, col_swaps(): out.append(lax.ppermute(slab, 'gy', low + [(b, a) for a, b in low]))  1.68 us
    pallas_call x1, Pallas kernels, clip_all(): pl.pallas_call(clip_kernel, grid=(1,), in_specs=[whole(summed.shape)], ou...  0.81 us
  transfers between devices with their start and end apart: 10, of which 6 were waited for; matrix products, arithmetic and copies ran while one was open for 0% of the time, Pallas kernels for 12%

profile of v13, /device:TPU:0, one launch (start us, length us, event | category | flops | bytes accessed | tf_op | source)
XLA Modules:
  0.0 33.6 jit_solution(1540206155961226462)
XLA Ops:
  0.6 0.0 copy-start
  0.6 1.3 %load.1 = (bf16[5,64,256]{2,1,0:T(8,128)(2,1)S(1)}, bf16[4,64,256]{2,1,0:T(8,128)(2,1)S(1)}, f32[64,256]{1,0:T(8,128)S(1)}, bf16[10,64,256]{2,1,0:T(8,128)(2,1)S...) custom-call(bf16[5,64,256]{2,1,0:T(8,128)(2,1)} %refs_0_.1, ...), custom_call_target="tpu_custom_call" | custom-call | tf_op jit(solution)/shard_map/load/pallas_call | solution.py:35
  2.0 0.5 %collective-permute-start = (f32[60,256]{1,0:T(8,128)S(1)}, f32[60,256]{1,0:T(8,128)S(1)}, u32[]{:S(2)}, u32[]{:S(2)}) collective-permute-start(f32[60,256]{1,0:T(8,128)S(1)} %get-tuple-element.48), channel_id=1, source_target_pairs={{0,1},{1,0},{2,3},{3,2},{4,8},{5,9},{6,10},{7,11},{8,4},{9,5},{10,... | collective-permute-start | bytes 184328 | tf_op jit(solution)/shard_map/ppermute | solution.py:561
  2.5 4.1 %collective-permute-start.1 = (f32[60,256]{1,0:T(8,128)S(1)}, f32[60,256]{1,0:T(8,128)S(1)}, u32[]{:S(2)}, u32[]{:S(2)}) collective-permute-start(f32[60,256]{1,0:T(8,128)S(1)} %get-tuple-element.49), channel_id=1, source_target_pairs={{0,4},{1,5},{2,6},{3,7},{4,0},{5,1},{6,2},{7,3},{8,12},{9,13},{10,... | collective-permute-start | bytes 184328 | tf_op jit(solution)/shard_map/ppermute | solution.py:561
  6.7 0.2 weights.1
  6.9 1.9 %network_forward.2 = (bf16[32,208,256]{2,1,0:T(8,128)(2,1)S(1)}, f32[32,192,256]{2,1,0:T(8,128)S(1)}, f32[32,256]{1,0:T(8,128)S(1)}) custom-call(bf16[10,64,256]{2,1,0:T(8,128)(2,1)S(1)} %get-tuple-element.50.feat, bf16[1280,256]{1,0:T(8,128)(2,1)S(1)} %get-tuple-element.56.w1, bf16[64,64]{1,0:T(8,128)(2,1)S(1)} %get-tuple-element.57.w2, ...), custom_call_target="tpu_custom_call" | custom-call | flops 144703488 | bytes 3571712 | tf_op jit(solution)/shard_map/network_forward/pallas_call | solution.py:35
  8.8 0.0 collective-permute-done.row_second
  8.8 0.1 collective-permute-done.1.row_first
  8.9 0.2 col_slabs.1
  9.1 0.1 collective-permute-start.2
  9.2 1.6 %collective-permute-start.3 = (f32[40,128]{1,0:T(8,128)S(1)}, f32[40,128]{1,0:T(8,128)S(1)}, u32[]{:S(2)}, u32[]{:S(2)}) collective-permute-start(f32[40,128]{1,0:T(8,128)S(1)} %get-tuple-element.68), channel_id=1, source_target_pairs={{1,2},{0,3},{2,1},{3,0},{5,6},{4,7},{6,5},{7,4},{9,10},{8,11},{10,... | collective-permute-start | bytes 61448 | tf_op jit(solution)/shard_map/ppermute | solution.py:572
  10.8 1.9 %network_forward.3 = (bf16[32,208,256]{2,1,0:T(8,128)(2,1)S(1)}, f32[32,192,256]{2,1,0:T(8,128)S(1)}, f32[32,256]{1,0:T(8,128)S(1)}) custom-call(bf16[10,64,256]{2,1,0:T(8,128)(2,1)S(1)} %get-tuple-element.50.feat, bf16[1280,256]{1,0:T(8,128)(2,1)S(1)} %get-tuple-element.56.w1, bf16[64,64]{1,0:T(8,128)(2,1)S(1)} %get-tuple-element.57.w2, ...), custom_call_target="tpu_custom_call" | custom-call | flops 144703488 | bytes 3571712 | tf_op jit(solution)/shard_map/network_forward/pallas_call | solution.py:35
  12.7 0.0 collective-permute-done.2.col_first
  12.7 0.0 collective-permute-done.3.col_second
  12.7 0.0 copy-done
  12.8 7.2 %sweeps_backward.1 = (f32[72,128]{1,0:T(8,128)S(1)}, f32[5,64,256]{2,1,0:T(8,128)}, f32[64,256]{1,0:T(8,128)}) custom-call(bf16[5,64,256]{2,1,0:T(8,128)(2,1)S(1)} %get-tuple-element.44.src, bf16[4,64,256]{2,1,0:T(8,128)(2,1)S(1)} %get-tuple-element.45.cpl, f32[64,256]{1,0:T(8,128)S(1)} %get-tuple-element.46.inv.inverse, ...), custom_call_target="tpu_custom_call" | custom-call | tf_op jit(solution)/shard_map/sweeps_backward/pallas_call | solution.py:474
  20.0 1.3 %collective-permute-start.6 = (f32[72,128]{1,0:T(8,128)S(1)}, f32[72,128]{1,0:T(8,128)S(1)}, u32[]{:S(2)}, u32[]{:S(2)}) collective-permute-start(f32[72,128]{1,0:T(8,128)S(1)} %get-tuple-element.75), channel_id=1, source_target_pairs={{0,3},{1,2},{2,1},{3,0},{4,7},{5,6},{6,5},{7,4},{8,11},{9,10},{10,... | collective-permute-start | bytes 110600 | tf_op jit(solution)/shard_map/ppermute | solution.py:533
  21.3 0.6 %collective-permute-start.5 = (f32[72,128]{1,0:T(8,128)S(1)}, f32[72,128]{1,0:T(8,128)S(1)}, u32[]{:S(2)}, u32[]{:S(2)}) collective-permute-start(f32[72,128]{1,0:T(8,128)S(1)} %get-tuple-element.75), channel_id=1, source_target_pairs={{0,2},{1,3},{2,0},{3,1},{4,6},{5,7},{6,4},{7,5},{8,10},{9,11},{10,... | collective-permute-start | bytes 110600 | tf_op jit(solution)/shard_map/ppermute | solution.py:533
  21.8 0.1 collective-permute-start.4
  21.9 1.6 %collective-permute-done.6 = f32[72,128]{1,0:T(8,128)S(1)} collective-permute-done((f32[72,128]{1,0:T(8,128)S(1)}, f32[72,128]{1,0:T(8,128)S(1)}, u32[]{:S(2)}, u32[]{:S(2)}) %collective-permute-start.6) | collective-permute-done | bytes 36896 | tf_op jit(solution)/shard_map/ppermute | solution.py:533
  23.5 1.8 %collective-permute-done.5 = f32[72,128]{1,0:T(8,128)S(1)} collective-permute-done((f32[72,128]{1,0:T(8,128)S(1)}, f32[72,128]{1,0:T(8,128)S(1)}, u32[]{:S(2)}, u32[]{:S(2)}) %collective-permute-start.5) | collective-permute-done | bytes 36896 | tf_op jit(solution)/shard_map/ppermute | solution.py:533
  25.3 0.0 collective-permute-done.4
  25.3 1.3 %collective-permute-start.9 = (f32[72,128]{1,0:T(8,128)S(1)}, f32[72,128]{1,0:T(8,128)S(1)}, u32[]{:S(2)}, u32[]{:S(2)}) collective-permute-start(f32[72,128]{1,0:T(8,128)S(1)} %add_add_fusion.1), channel_id=1, source_target_pairs={{0,13},{1,12},{2,15},{3,14},{4,9},{5,8},{6,11},{7,10},{8,5},{9,4},... | collective-permute-start | bytes 110600 | tf_op jit(solution)/shard_map/ppermute | solution.py:533
  26.6 2.0 %collective-permute-start.8 = (f32[72,128]{1,0:T(8,128)S(1)}, f32[72,128]{1,0:T(8,128)S(1)}, u32[]{:S(2)}, u32[]{:S(2)}) collective-permute-start(f32[72,128]{1,0:T(8,128)S(1)} %add_add_fusion.1), channel_id=1, source_target_pairs={{0,9},{1,8},{2,11},{3,10},{4,13},{5,12},{6,15},{7,14},{8,1},{9,0},... | collective-permute-start | bytes 110600 | tf_op jit(solution)/shard_map/ppermute | solution.py:533
  28.5 0.0 collective-permute-start.7
  28.5 2.0 %collective-permute-done.9 = f32[72,128]{1,0:T(8,128)S(1)} collective-permute-done((f32[72,128]{1,0:T(8,128)S(1)}, f32[72,128]{1,0:T(8,128)S(1)}, u32[]{:S(2)}, u32[]{:S(2)}) %collective-permute-start.9) | collective-permute-done | bytes 36896 | tf_op jit(solution)/shard_map/ppermute | solution.py:533
  30.6 1.4 %collective-permute-done.8 = f32[72,128]{1,0:T(8,128)S(1)} collective-permute-done((f32[72,128]{1,0:T(8,128)S(1)}, f32[72,128]{1,0:T(8,128)S(1)}, u32[]{:S(2)}, u32[]{:S(2)}) %collective-permute-start.8) | collective-permute-done | bytes 36896 | tf_op jit(solution)/shard_map/ppermute | solution.py:533
  32.0 0.8 %collective-permute-done.7 = f32[72,128]{1,0:T(8,128)S(1)} collective-permute-done((f32[72,128]{1,0:T(8,128)S(1)}, f32[72,128]{1,0:T(8,128)S(1)}, u32[]{:S(2)}, u32[]{:S(2)}) %collective-permute-start.7) | collective-permute-done | bytes 36896 | tf_op jit(solution)/shard_map/ppermute | solution.py:533
  32.8 0.8 %clip.1 = (f32[10,64]{1,0:T(8,128)}, f32[64,64]{1,0:T(8,128)}, f32[64,64]{1,0:T(8,128)}, f32[1,64]{1,0:T(1,128)}, f32[3,64]{1,0:T(4,128)}) custom-call(f32[72,128]{1,0:T(8,128)S(1)} %add_add_fusion.summed), custom_call_target="tpu_custom_call" | custom-call | tf_op jit(solution)/shard_map/clip/pallas_call | solution.py:517
  (2 shorter events, 0.0 us)
Async XLA Ops:
  0.6 12.1 %copy-start = (f32[5,5]{1,0:T(8,128)S(1)}, f32[5,5]{1,0:T(8,128)}, u32[]{:S(2)}) copy-start(f32[5,5]{1,0:T(8,128)} %mix.1) | copy-start | bytes 304
  2.0 6.8 %collective-permute-start = (f32[60,256]{1,0:T(8,128)S(1)}, f32[60,256]{1,0:T(8,128)S(1)}, u32[]{:S(2)}, u32[]{:S(2)}) collective-permute-start(f32[60,256]{1,0:T(8,128)S(1)} %get-tuple-element.48), channel_id=1, source_target_pairs={{0,1},{1,0},{2,3},{3,2},{4,8},{5,9},{6,10},{7,11},{8,4},{9,5},{10,... | collective-permute-start | bytes 184328 | tf_op jit(solution)/shard_map/ppermute | solution.py:561
  2.5 6.4 %collective-permute-start.1 = (f32[60,256]{1,0:T(8,128)S(1)}, f32[60,256]{1,0:T(8,128)S(1)}, u32[]{:S(2)}, u32[]{:S(2)}) collective-permute-start(f32[60,256]{1,0:T(8,128)S(1)} %get-tuple-element.49), channel_id=1, source_target_pairs={{0,4},{1,5},{2,6},{3,7},{4,0},{5,1},{6,2},{7,3},{8,12},{9,13},{10,... | collective-permute-start | bytes 184328 | tf_op jit(solution)/shard_map/ppermute | solution.py:561
  9.1 3.6 %collective-permute-start.2 = (f32[40,128]{1,0:T(8,128)S(1)}, f32[40,128]{1,0:T(8,128)S(1)}, u32[]{:S(2)}, u32[]{:S(2)}) collective-permute-start(f32[40,128]{1,0:T(8,128)S(1)} %get-tuple-element.67), channel_id=1, source_target_pairs={{0,1},{2,3},{1,0},{3,2},{4,5},{6,7},{5,4},{7,6},{8,9},{10,11},{9,8... | collective-permute-start | bytes 61448 | tf_op jit(solution)/shard_map/ppermute | solution.py:572
  9.2 3.5 %collective-permute-start.3 = (f32[40,128]{1,0:T(8,128)S(1)}, f32[40,128]{1,0:T(8,128)S(1)}, u32[]{:S(2)}, u32[]{:S(2)}) collective-permute-start(f32[40,128]{1,0:T(8,128)S(1)} %get-tuple-element.68), channel_id=1, source_target_pairs={{1,2},{0,3},{2,1},{3,0},{5,6},{4,7},{6,5},{7,4},{9,10},{8,11},{10,... | collective-permute-start | bytes 61448 | tf_op jit(solution)/shard_map/ppermute | solution.py:572
  20.0 3.5 %collective-permute-start.6 = (f32[72,128]{1,0:T(8,128)S(1)}, f32[72,128]{1,0:T(8,128)S(1)}, u32[]{:S(2)}, u32[]{:S(2)}) collective-permute-start(f32[72,128]{1,0:T(8,128)S(1)} %get-tuple-element.75), channel_id=1, source_target_pairs={{0,3},{1,2},{2,1},{3,0},{4,7},{5,6},{6,5},{7,4},{8,11},{9,10},{10,... | collective-permute-start | bytes 110600 | tf_op jit(solution)/shard_map/ppermute | solution.py:533
  21.3 4.0 %collective-permute-start.5 = (f32[72,128]{1,0:T(8,128)S(1)}, f32[72,128]{1,0:T(8,128)S(1)}, u32[]{:S(2)}, u32[]{:S(2)}) collective-permute-start(f32[72,128]{1,0:T(8,128)S(1)} %get-tuple-element.75), channel_id=1, source_target_pairs={{0,2},{1,3},{2,0},{3,1},{4,6},{5,7},{6,4},{7,5},{8,10},{9,11},{10,... | collective-permute-start | bytes 110600 | tf_op jit(solution)/shard_map/ppermute | solution.py:533
  21.8 3.4 %collective-permute-start.4 = (f32[72,128]{1,0:T(8,128)S(1)}, f32[72,128]{1,0:T(8,128)S(1)}, u32[]{:S(2)}, u32[]{:S(2)}) collective-permute-start(f32[72,128]{1,0:T(8,128)S(1)} %get-tuple-element.75), channel_id=1, source_target_pairs={{0,1},{1,0},{2,3},{3,2},{4,5},{5,4},{6,7},{7,6},{8,9},{9,8},{10,11... | collective-permute-start | bytes 110600 | tf_op jit(solution)/shard_map/ppermute | solution.py:533
  25.3 5.3 %collective-permute-start.9 = (f32[72,128]{1,0:T(8,128)S(1)}, f32[72,128]{1,0:T(8,128)S(1)}, u32[]{:S(2)}, u32[]{:S(2)}) collective-permute-start(f32[72,128]{1,0:T(8,128)S(1)} %add_add_fusion.1), channel_id=1, source_target_pairs={{0,13},{1,12},{2,15},{3,14},{4,9},{5,8},{6,11},{7,10},{8,5},{9,4},... | collective-permute-start | bytes 110600 | tf_op jit(solution)/shard_map/ppermute | solution.py:533
  26.6 5.4 %collective-permute-start.8 = (f32[72,128]{1,0:T(8,128)S(1)}, f32[72,128]{1,0:T(8,128)S(1)}, u32[]{:S(2)}, u32[]{:S(2)}) collective-permute-start(f32[72,128]{1,0:T(8,128)S(1)} %add_add_fusion.1), channel_id=1, source_target_pairs={{0,9},{1,8},{2,11},{3,10},{4,13},{5,12},{6,15},{7,14},{8,1},{9,0},... | collective-permute-start | bytes 110600 | tf_op jit(solution)/shard_map/ppermute | solution.py:533
  28.5 4.2 %collective-permute-start.7 = (f32[72,128]{1,0:T(8,128)S(1)}, f32[72,128]{1,0:T(8,128)S(1)}, u32[]{:S(2)}, u32[]{:S(2)}) collective-permute-start(f32[72,128]{1,0:T(8,128)S(1)} %add_add_fusion.1), channel_id=1, source_target_pairs={{0,5},{1,4},{2,7},{3,6},{4,1},{5,0},{6,3},{7,2},{8,13},{9,12},{10,... | collective-permute-start | bytes 110600 | tf_op jit(solution)/shard_map/ppermute | solution.py:533
